TPU v7x, 256 devices: a whole 4x4x8 slice. The times are simulated.
256 devices in a mesh: dp: 16 (over y_lo, z), tensor: 16 (over x, y_hi, core).
Axes of the slice: x: 4, y: 4 (y_hi: 2, y_lo: 2; y = y_hi * 2 + y_lo), z: 8, core: 2. Of those that a mesh axis runs over, the one named last changes fastest.
Arguments:
- tokens: bfloat16 [12288, 8192], P('dp', 'tensor'), may hold values from -40 to 40
- gain: float32 [8192], P('tensor'), may hold values from 0.1 to 1.9
- w_first: bfloat16 [32, 256, 512], P('tensor'), may hold values from -0.375 to 0.375
- w_second: bfloat16 [16, 1024, 1024], P('tensor'), may hold values from -0.1875 to 0.1875
- w_third: bfloat16 [16, 1024, 1024], P('tensor'), may hold values from -0.1875 to 0.1875
- w_fourth: bfloat16 [32, 512, 256], P('tensor'), may hold values from -0.25 to 0.25
- cotangent: bfloat16 [12288, 8192], P('dp', 'tensor'), may hold values from -5 to 5
Outputs:
- output: bfloat16 [12288, 8192], P('dp', 'tensor')
- token_gradient: bfloat16 [12288, 8192], P('dp', 'tensor')
- grad_first: float32 [32, 256, 512], P('tensor', 'dp')
- grad_second: float32 [16, 1024, 1024], P('tensor', 'dp')
- grad_third: float32 [16, 1024, 1024], P('tensor', 'dp')
- grad_fourth: float32 [32, 512, 256], P('tensor', 'dp')
All inputs are finite; a program needn't handle non-finite values.
Results may differ from a plain program's by a relative error of at most 0.023.
Values may be sent and summed in bfloat16 or wider, within the bound.
No kernel may reach another device: no remote copies, remote signals or barrier semaphores. Data moves between devices by JAX's collectives and lax.ppermute only.
A program may use at most 128 MiB of HBM per device.

v0:
```python
import math

import jax
import jax.numpy as jnp
from jax import lax
from jax.sharding import PartitionSpec as P

MODEL_WIDTH = 8192
DIAGONAL_BLOCKS = 32
HBS = 1024
HB = 16


epsilon = 1e-05
root_scale = math.sqrt(2.0 / math.pi)
cubic_term = 0.044715


def gelu_value(value):
    return 0.5 * value * (1.0 + jnp.tanh(root_scale * (value + cubic_term * value * value * value)))


def gelu_slope(value):
    hyper = jnp.tanh(root_scale * (value + cubic_term * value * value * value))
    return 0.5 * (1.0 + hyper) + 0.5 * value * (1.0 - hyper * hyper) * root_scale * (
        1.0 + 3.0 * cubic_term * value * value
    )


def shards(tokens, gain, w_first, w_second, w_third, w_fourth, cotangent):
    element_count, local_width = tokens.shape
    model_width_shard = w_first.shape[0]
    diagonal_block_width = w_first.shape[1]
    hidden_local = w_second.shape[0]
    eb_size = HBS // DIAGONAL_BLOCKS
    scale = 1.0 / math.sqrt(element_count * lax.axis_size("dp"))
    single_precision = jnp.float32
    complete_input = tokens.astype(single_precision)
    squares = lax.psum(jnp.sum(complete_input * complete_input, axis=1), "tensor")
    reciprocal_norm = lax.rsqrt(squares / MODEL_WIDTH + epsilon)[:, None]
    centered_input = complete_input * reciprocal_norm
    normalized_input = (
        (centered_input * gain)
        .astype(jnp.bfloat16)
        .reshape(element_count, model_width_shard, diagonal_block_width)
    )
    first = jnp.einsum(
        "tak,akh->tah", normalized_input, w_first, preferred_element_type=single_precision
    ).astype(jnp.bfloat16)
    send_first = (
        first.reshape(element_count, model_width_shard, HB, eb_size)
        .transpose(0, 2, 1, 3)
        .reshape(element_count, HB, model_width_shard * eb_size)
    )
    mixed_piece = lax.all_to_all(send_first, "tensor", split_axis=1, concat_axis=2, tiled=True)
    pre = jnp.einsum("tck,ckf->tcf", mixed_piece, w_second, preferred_element_type=single_precision)
    act = gelu_value(pre).astype(jnp.bfloat16)
    third = jnp.einsum(
        "tcf,cfm->tcm", act, w_third, preferred_element_type=single_precision
    ).astype(jnp.bfloat16)
    send_third = (
        third.reshape(element_count, hidden_local, DIAGONAL_BLOCKS, eb_size)
        .transpose(0, 2, 1, 3)
        .reshape(element_count, DIAGONAL_BLOCKS, hidden_local * eb_size)
    )
    gathered_piece = lax.all_to_all(send_third, "tensor", split_axis=1, concat_axis=2, tiled=True)
    branch = jnp.einsum(
        "tak,ako->tao", gathered_piece, w_fourth, preferred_element_type=single_precision
    )
    output = (complete_input + branch.reshape(element_count, local_width)).astype(jnp.bfloat16)
    dy_blocks = cotangent.reshape(element_count, model_width_shard, diagonal_block_width)
    grad_fourth = jnp.einsum(
        "tak,tao->ako", gathered_piece, dy_blocks, preferred_element_type=single_precision
    )
    dgathered = jnp.einsum(
        "tao,ako->tak", dy_blocks, w_fourth, preferred_element_type=single_precision
    ).astype(jnp.bfloat16)
    piece = lax.all_to_all(dgathered, "tensor", split_axis=2, concat_axis=1, tiled=True)
    piece_rows = piece.shape[0]
    dthird_piece = (
        piece.reshape(piece_rows, DIAGONAL_BLOCKS, hidden_local, eb_size)
        .transpose(0, 2, 1, 3)
        .reshape(piece_rows, hidden_local, DIAGONAL_BLOCKS * eb_size)
    )
    dact = jnp.einsum(
        "tcm,cfm->tcf", dthird_piece, w_third, preferred_element_type=single_precision
    )
    dpre = (dact * gelu_slope(pre)).astype(jnp.bfloat16)
    dmixed = jnp.einsum(
        "tcf,ckf->tck", dpre, w_second, preferred_element_type=single_precision
    ).astype(jnp.bfloat16)
    send_back = (
        dmixed.reshape(element_count, hidden_local, DIAGONAL_BLOCKS, eb_size)
        .transpose(0, 2, 1, 3)
        .reshape(element_count, DIAGONAL_BLOCKS, hidden_local * eb_size)
    )
    grad_third = jnp.einsum(
        "tcf,tcm->cfm", act, dthird_piece, preferred_element_type=single_precision
    )
    grad_second = jnp.einsum(
        "tck,tcf->ckf", mixed_piece, dpre, preferred_element_type=single_precision
    )
    piece = lax.all_to_all(send_back, "tensor", split_axis=1, concat_axis=2, tiled=True)
    dnormed = jnp.einsum("tah,akh->tak", piece, w_first, preferred_element_type=single_precision)
    grad_first = jnp.einsum(
        "tak,tah->akh", normalized_input, piece, preferred_element_type=single_precision
    )
    grad_first, grad_second, grad_third, grad_fourth = (
        lax.psum_scatter(
            grad_first.astype(jnp.bfloat16), "dp", scatter_dimension=1, tiled=True
        ).astype(jnp.float32),
        lax.psum_scatter(
            grad_second.astype(jnp.bfloat16), "dp", scatter_dimension=1, tiled=True
        ).astype(jnp.float32),
        lax.psum_scatter(
            grad_third.astype(jnp.bfloat16), "dp", scatter_dimension=1, tiled=True
        ).astype(jnp.float32),
        lax.psum_scatter(
            grad_fourth.astype(jnp.bfloat16), "dp", scatter_dimension=1, tiled=True
        ).astype(jnp.float32),
    )
    scaled_gradient = dnormed.reshape(element_count, local_width) * gain
    inner_product = (
        lax.psum(jnp.sum(scaled_gradient * centered_input, axis=1), "tensor")[:, None] / MODEL_WIDTH
    )
    token_gradient = (
        cotangent.astype(single_precision)
        + reciprocal_norm * (scaled_gradient - centered_input * inner_product)
    ).astype(jnp.bfloat16)
    return (
        output,
        token_gradient,
        grad_first * scale,
        grad_second * scale,
        grad_third * scale,
        grad_fourth * scale,
    )


def solution(mesh):
    return jax.shard_map(
        shards,
        mesh=mesh,
        in_specs=(
            P("dp", "tensor"),
            P("tensor"),
            P("tensor", None, None),
            P("tensor", None, None),
            P("tensor", None, None),
            P("tensor", None, None),
            P("dp", "tensor"),
        ),
        out_specs=(
            P("dp", "tensor"),
            P("dp", "tensor"),
            P("tensor", "dp", None),
            P("tensor", "dp", None),
            P("tensor", "dp", None),
            P("tensor", "dp", None),
        ),
        check_vma=False,
    )
```

profile of v0, /device:TPU:18, one launch (start us, length us, event | category | flops | bytes accessed | tf_op | source)
XLA Modules:
  0.0 441.2 jit_solution(691373398110219180)
XLA Ops:
  7.2 0.0 copy-start
  7.2 1.5 fusion.32
  8.7 26.6 %psum.14 = f32[768]{0:T(1024)S(1)} all-reduce(f32[768]{0:T(1024)S(1)} %fusion.32), channel_id=1, replica_groups=mesh['dp'=16,'tensor'=16] {'tensor'}, use_global_device_ids=true, to_apply=%region_1.0 | all-reduce | flops 768 | bytes 6144 | tf_op jit(solution)/shard_map/psum | solution.py:39
  35.4 2.3 fusion.26
  37.7 1.4 copy.82
  39.1 0.6 convolution_convert_fusion.1
  39.7 1.3 copy.60
  41.0 15.9 %all-to-all-start = ((bf16[768,16,64]{0,2,1:T(8,128)(2,1)}), bf16[768,16,64]{0,2,1:T(8,128)(2,1)}, u32[]{:S(2)}, u32[]{:S(2)}) async-start(bf16[768,16,64]{0,2,1:T(8,128)(2,1)} %bitcast.136), calls=%async_computation | async-start | bytes 3145728 | tf_op jit(solution)/shard_map/all_to_all | solution.py:55
  57.0 1.7 fusion.38
  58.7 2.8 copy.67
  61.5 14.6 %all-to-all-done = bf16[768,16,64]{0,2,1:T(8,128)(2,1)} async-done(((bf16[768,16,64]{0,2,1:T(8,128)(2,1)}), bf16[768,16,64]{0,2,1:T(8,128)(2,1)}, u32[]{:S(2)}, u32[]{:S(2)}) %all-to-all-start) | async-done | bytes 1572896 | tf_op jit(solution)/shard_map/all_to_all | solution.py:55
  76.2 8.8 %all-to-all-start.2 = ((bf16[768,2,512]{0,1,2:T(2,128)(2,1)}), bf16[768,2,512]{0,1,2:T(2,128)(2,1)}, u32[]{:S(2)}, u32[]{:S(2)}) async-start(bf16[768,2,512]{0,1,2:T(2,128)(2,1)} %copy.67), calls=%async_computation.2 | async-start | bytes 3145728 | tf_op jit(solution)/shard_map/all_to_all | solution.py:78
  85.0 3.9 fusion.16
  88.9 0.0 copy-start.4
  88.9 1.6 copy-done.4
  90.5 0.0 copy-done
  90.5 3.2 fusion.39
  93.7 2.6 copy.61
  96.3 7.9 %all-to-all-done.2 = bf16[768,2,512]{0,1,2:T(2,128)(2,1)} async-done(((bf16[768,2,512]{0,1,2:T(2,128)(2,1)}), bf16[768,2,512]{0,1,2:T(2,128)(2,1)}, u32[]{:S(2)}, u32[]{:S(2)}) %all-to-all-start.2) | async-done | bytes 1572896 | tf_op jit(solution)/shard_map/all_to_all | solution.py:78
  104.2 8.8 %all-to-all-start.1 = ((bf16[768,32,32]{0,2,1:T(8,128)(2,1)}), bf16[768,32,32]{0,2,1:T(8,128)(2,1)}, u32[]{:S(2)}, u32[]{:S(2)}) async-start(bf16[768,32,32]{0,2,1:T(8,128)(2,1)} %bitcast.135), calls=%async_computation.1 | async-start | bytes 3145728 | tf_op jit(solution)/shard_map/all_to_all | solution.py:66
  113.0 1.6 copy.68
  114.6 0.1 copy.69
  114.8 2.3 copy-done.5
  117.1 3.5 fusion.6
  120.6 1.2 copy-done.13
  121.7 3.0 fusion.44
  124.7 2.6 copy.70
  127.4 4.8 %all-to-all-done.1 = bf16[768,32,32]{0,2,1:T(8,128)(2,1)} async-done(((bf16[768,32,32]{0,2,1:T(8,128)(2,1)}), bf16[768,32,32]{0,2,1:T(8,128)(2,1)}, u32[]{:S(2)}, u32[]{:S(2)}) %all-to-all-start.1) | async-done | bytes 1572896 | tf_op jit(solution)/shard_map/all_to_all | solution.py:66
  132.2 8.8 %all-to-all-start.3 = ((bf16[768,32,32]{0,2,1:T(8,128)(2,1)}), bf16[768,32,32]{0,2,1:T(8,128)(2,1)}, u32[]{:S(2)}, u32[]{:S(2)}) async-start(bf16[768,32,32]{0,2,1:T(8,128)(2,1)} %bitcast.134), calls=%async_computation.3 | async-start | bytes 3145728 | tf_op jit(solution)/shard_map/all_to_all | solution.py:103
  141.0 0.0 reduce-scatter.11.cloned.1.call-start
  141.1 0.0 copy-start.6
  141.1 1.6 copy.62
  142.7 0.0 copy-start.3
  142.7 1.1 copy-done.3
  143.8 0.0 copy-done.6
  143.8 1.4 convolution_convert_fusion.2
  145.2 0.0 reduce-scatter.11.cloned.1.call-update
  145.2 0.0 reduce-scatter.5.cloned.1.call-start
  145.3 14.9 %all-to-all-done.3 = bf16[768,32,32]{0,2,1:T(8,128)(2,1)} async-done(((bf16[768,32,32]{0,2,1:T(8,128)(2,1)}), bf16[768,32,32]{0,2,1:T(8,128)(2,1)}, u32[]{:S(2)}, u32[]{:S(2)}) %all-to-all-start.3) | async-done | bytes 1572896 | tf_op jit(solution)/shard_map/all_to_all | solution.py:103
  160.2 1.5 copy.71
  161.7 0.0 copy-start.1
  161.8 1.2 copy-done.1
  163.0 1.4 convolution_convert_fusion.3
  164.4 0.0 reduce-scatter.5.cloned.1.call-update
  164.4 0.0 reduce-scatter.9.cloned.1.call-start
  164.5 5.9 %convert_bitcast_fusion = bf16[1,1024,1024]{2,1,0:T(8,128)(2,1)} fusion(bf16[768,1024]{0,1:T(8,128)(2,1)} %bitcast.144, f32[768,1024]{1,0:T(8,128)} %copy-done.4), kind=kOutput, calls=%fused_computation.25 | convolution fusion | flops 1618739200 | bytes 6815744 | tf_op jit(solution)/shard_map/tcf,tcm->cfm/dot_general | solution.py:97
  170.4 0.0 reduce-scatter.9.cloned.1.call-update
  170.4 0.0 reduce-scatter.7.cloned.1.call-start
  170.4 5.0 %convert_bitcast_fusion.1 = bf16[1,1024,1024]{2,1,0:T(8,128)(2,1)} fusion(bf16[768,1024]{0,1:T(8,128)(2,1)} %bitcast.4, bf16[768,1,1024]{2,0,1:T(8,128)(2,1)} %copy-done.13), kind=kOutput, calls=%fused_computation.26 | convolution fusion | flops 1611661312 | bytes 5242880 | tf_op jit(solution)/shard_map/tck,tcf->ckf/dot_general | solution.py:100
  175.4 0.0 reduce-scatter.7.cloned.1.call-update
  175.5 3.2 fusion.61
  178.7 3.1 copy.65
  181.8 3.2 fusion.62
  185.0 3.1 copy.73
  188.1 1.9 fusion.27
  190.0 29.6 %psum.15 = f32[768]{0:T(1024)S(1)} all-reduce(f32[768]{0:T(1024)S(1)} %fusion.27), channel_id=1, replica_groups=mesh['dp'=16,'tensor'=16] {'tensor'}, use_global_device_ids=true, to_apply=%region_3.0 | all-reduce | flops 768 | bytes 6144 | tf_op jit(solution)/shard_map/psum | solution.py:124
  219.6 3.8 fusion.31
  223.4 1.4 convert_multiply_fusion.4
  224.8 62.4 %reduce-scatter.5.cloned.1.call-done = bf16[2,16,512]{2,1,0:T(8,128)(2,1)} async-done(((bf16[2,256,512]{2,1,0:T(8,128)(2,1)}), bf16[2,16,512]{2,1,0:T(8,128)(2,1)}) %reduce-scatter.5.cloned.1.call-update) | async-done | bytes 32784 | tf_op jit(solution)/shard_map/reduce_scatter | solution.py:109
  287.2 1.4 convert_multiply_fusion.5
  288.6 71.6 %reduce-scatter.9.cloned.1.call-done = bf16[1,64,1024]{2,1,0:T(8,128)(2,1)} async-done(((bf16[1,1024,1024]{2,1,0:T(8,128)(2,1)}), bf16[1,64,1024]{2,1,0:T(8,128)(2,1)}) %reduce-scatter.9.cloned.1.call-update) | async-done | bytes 131088 | tf_op jit(solution)/shard_map/reduce_scatter | solution.py:115
  360.2 1.6 convert_multiply_fusion.2
  361.9 71.2 %reduce-scatter.7.cloned.1.call-done = bf16[1,64,1024]{2,1,0:T(8,128)(2,1)} async-done(((bf16[1,1024,1024]{2,1,0:T(8,128)(2,1)}), bf16[1,64,1024]{2,1,0:T(8,128)(2,1)}) %reduce-scatter.7.cloned.1.call-update) | async-done | bytes 131088 | tf_op jit(solution)/shard_map/reduce_scatter | solution.py:112
  433.1 1.6 convert_multiply_fusion.3
  (19 shorter events, 0.0 us)
Async XLA Ops:
  7.2 83.4 %copy-start = (bf16[1,1024,1024]{2,1,0:T(8,128)(2,1)S(1)}, bf16[1,1024,1024]{2,1,0:T(8,128)(2,1)}, u32[]{:S(2)}) copy-start(bf16[1,1024,1024]{2,1,0:T(8,128)(2,1)} %param.11) | copy-start | bytes 6291460
  35.3 3.7 copy-start.9
  41.0 15.9 %copy-start.8 = (bf16[2,512,256]{2,1,0:T(8,128)(2,1)S(1)}, bf16[2,512,256]{2,1,0:T(8,128)(2,1)}, u32[]{:S(2)}) copy-start(bf16[2,512,256]{2,1,0:T(8,128)(2,1)} %param.12) | copy-start | bytes 1572868
  41.0 35.1 %all-to-all-start = ((bf16[768,16,64]{0,2,1:T(8,128)(2,1)}), bf16[768,16,64]{0,2,1:T(8,128)(2,1)}, u32[]{:S(2)}, u32[]{:S(2)}) async-start(bf16[768,16,64]{0,2,1:T(8,128)(2,1)} %bitcast.136), calls=%async_computation | async-start | bytes 3145728 | tf_op jit(solution)/shard_map/all_to_all | solution.py:55
  76.2 28.0 %all-to-all-start.2 = ((bf16[768,2,512]{0,1,2:T(2,128)(2,1)}), bf16[768,2,512]{0,1,2:T(2,128)(2,1)}, u32[]{:S(2)}, u32[]{:S(2)}) async-start(bf16[768,2,512]{0,1,2:T(2,128)(2,1)} %copy.67), calls=%async_computation.2 | async-start | bytes 3145728 | tf_op jit(solution)/shard_map/all_to_all | solution.py:78
  88.9 1.6 copy-start.4
  104.2 28.0 %all-to-all-start.1 = ((bf16[768,32,32]{0,2,1:T(8,128)(2,1)}), bf16[768,32,32]{0,2,1:T(8,128)(2,1)}, u32[]{:S(2)}, u32[]{:S(2)}) async-start(bf16[768,32,32]{0,2,1:T(8,128)(2,1)} %bitcast.135), calls=%async_computation.1 | async-start | bytes 3145728 | tf_op jit(solution)/shard_map/all_to_all | solution.py:66
  114.6 2.5 copy-start.5
  114.7 5.8 %copy-start.11 = (bf16[768,16,2,32]{0,3,2,1:T(8,128)(2,1)}, bf16[768,16,2,32]{0,3,2,1:T(8,128)(2,1)S(1)}, u32[]{:S(2)}) copy-start(bf16[768,16,2,32]{0,3,2,1:T(8,128)(2,1)S(1)} %copy.69) | copy-start | bytes 4718596
  117.1 4.7 %copy-start.7 = (bf16[1,1024,1024]{2,1,0:T(8,128)(2,1)S(1)}, bf16[1,1024,1024]{2,1,0:T(8,128)(2,1)}, u32[]{:S(2)}) copy-start(bf16[1,1024,1024]{2,1,0:T(8,128)(2,1)} %param.10) | copy-start | bytes 6291460
  120.6 1.2 copy-start.13
  132.2 28.0 %all-to-all-start.3 = ((bf16[768,32,32]{0,2,1:T(8,128)(2,1)}), bf16[768,32,32]{0,2,1:T(8,128)(2,1)}, u32[]{:S(2)}, u32[]{:S(2)}) async-start(bf16[768,32,32]{0,2,1:T(8,128)(2,1)} %bitcast.134), calls=%async_computation.3 | async-start | bytes 3145728 | tf_op jit(solution)/shard_map/all_to_all | solution.py:103
  141.0 82.4 %reduce-scatter.11.cloned.1.call-start = ((), (), s32[]{:S(2)}) async-start(), calls=%async_computation.11 | async-start | bytes 557056 | tf_op jit(solution)/shard_map/reduce_scatter | solution.py:118
  141.1 2.7 copy-start.6
  142.7 1.1 copy-start.3
  145.2 142.0 %reduce-scatter.5.cloned.1.call-start = ((), (), s32[]{:S(2)}) async-start(), calls=%async_computation.8 | async-start | bytes 557056 | tf_op jit(solution)/shard_map/reduce_scatter | solution.py:109
  161.7 1.2 copy-start.1
  164.4 195.8 %reduce-scatter.9.cloned.1.call-start = ((), (), s32[]{:S(2)}) async-start(), calls=%async_computation.10 | async-start | bytes 2228224 | tf_op jit(solution)/shard_map/reduce_scatter | solution.py:115
  170.4 262.7 %reduce-scatter.7.cloned.1.call-start = ((), (), s32[]{:S(2)}) async-start(), calls=%async_computation.9 | async-start | bytes 2228224 | tf_op jit(solution)/shard_map/reduce_scatter | solution.py:112
  178.7 3.1 copy-start.10
  185.0 3.1 copy-start.2
  185.0 3.1 copy-start.12
Sparse Core Ops, SparseCore 0:
  145.3 72.7 reduce-scatter.10
  220.8 66.3 reduce-scatter.4
  289.8 70.4 reduce-scatter.8
  362.6 70.3 reduce-scatter.6
where the time goes:
time: 443 us; the launch traced here: 441 us
  waiting for transfers between devices  248 us (56%)
  blocking collectives  56.2 us (13%)
  starting transfers between devices  42.6 us (10%)
  matrix products  36 us (8%)
  local copies, waits for them, and re-layouts  29.3 us (7%)
  other arithmetic  15.6 us (4%)
  between operations  13.9 us (3%)
    reduce_scatter x1, waiting for transfers between devices, shards(): lax.psum_scatter(grad_third.astype(jnp.bfloat16), 'dp', scatter_dimension...  71.6 us
    reduce_scatter x1, waiting for transfers between devices, shards(): lax.psum_scatter(grad_second.astype(jnp.bfloat16), 'dp', scatter_dimensio...  71.2 us
    reduce_scatter x1, waiting for transfers between devices, shards(): lax.psum_scatter(grad_first.astype(jnp.bfloat16), 'dp', scatter_dimension...  62.4 us
    psum x1, blocking collectives, shards(): lax.psum(jnp.sum(scaled_gradient * centered_input, axis=1), 'tensor')  29.6 us
    psum x1, blocking collectives, shards(): lax.psum(jnp.sum(complete_input * complete_input, axis=1), 'tensor')  26.6 us
    all_to_all x1, starting transfers between devices, shards(): lax.all_to_all(send_first, 'tensor', split_axis=1, concat_axis=2, tiled=T...  15.9 us
    all_to_all x1, waiting for transfers between devices, shards(): lax.all_to_all(send_back, 'tensor', split_axis=1, concat_axis=2, tiled=True)  14.9 us
    all_to_all x1, waiting for transfers between devices, shards(): lax.all_to_all(send_first, 'tensor', split_axis=1, concat_axis=2, tiled=T...  14.6 us
  transfers between devices with their start and end apart: 8, of which 7 were waited for; matrix products, arithmetic and copies ran while one was open for 15% of the time, Pallas kernels for 0%

commit v1 on v0

v1 whole, which is shorter than its diff:
```python
import math

import jax
import jax.numpy as jnp
from jax import lax
from jax.experimental import pallas as pl
from jax.experimental.pallas import tpu as pltpu
from jax.sharding import PartitionSpec as P

MODEL_WIDTH = 8192
DIAGONAL_BLOCKS = 32
HBS = 1024
HB = 16
BS = 256
EB = 32
PEERS = 16
PAIR = 2 * EB
LANES = 128
STATS = 16

epsilon = 1e-05
root_scale = math.sqrt(2.0 / math.pi)
cubic_term = 0.044715

F32 = jnp.float32
BF16 = jnp.bfloat16

NN = (((1,), (0,)), ((), ()))
NT = (((1,), (1,)), ((), ()))
TN = (((0,), (0,)), ((), ()))
TT = (((0,), (1,)), ((), ()))


def dot(a, b, dims):
    return lax.dot_general(a, b, dims, preferred_element_type=F32)


def call(kernel, out_shape, args, scratch=(), flops=0, **extra):
    outs = out_shape if isinstance(out_shape, (list, tuple)) else [out_shape]
    moved = sum(a.size * a.dtype.itemsize for a in args) + sum(
        math.prod(o.shape) * o.dtype.itemsize for o in outs
    )
    return pl.pallas_call(
        kernel,
        out_shape=out_shape,
        in_specs=[pl.BlockSpec(memory_space=pltpu.VMEM)] * len(args),
        out_specs=jax.tree.map(lambda _: pl.BlockSpec(memory_space=pltpu.VMEM), out_shape),
        scratch_shapes=list(scratch),
        compiler_params=pltpu.CompilerParams(vmem_limit_bytes=48 * 1024 * 1024),
        cost_estimate=pl.CostEstimate(flops=int(flops), bytes_accessed=int(moved), transcendentals=0),
        **extra,
    )(*args)


def stat_rows(value, chunks):
    high = value.astype(BF16).astype(F32)
    low = value - high
    rows = []
    for i in range(chunks):
        part = slice(i * LANES, (i + 1) * LANES)
        rows += [high[:, part], low[:, part]]
    rows.append(jnp.zeros((STATS - 2 * chunks, LANES), F32))
    return jnp.concatenate(rows, axis=0).astype(BF16)


def stat_sum(rows):
    return jnp.sum(rows.astype(F32), axis=0)


def head_kernel(x_ref, gain_ref, w1_ref, w4_ref, cot_ref, out_ref):
    tokens = x_ref.shape[0]
    chunks = tokens // LANES
    for a in range(2):
        feats = slice(a * BS, (a + 1) * BS)
        scaled = (x_ref[:, feats].astype(F32) * gain_ref[:, feats]).astype(BF16)
        first = dot(w1_ref[a].T, scaled, NT).astype(BF16)
        dgathered = dot(w4_ref[a], cot_ref[:, feats], NT).astype(BF16)
        for i in range(chunks):
            part = slice(i * LANES, (i + 1) * LANES)
            base = i * 2 * PAIR + a * EB
            out_ref[:, base : base + EB, :] = first[:, part].reshape(PEERS, EB, LANES)
            base += PAIR
            out_ref[:, base : base + EB, :] = dgathered[:, part].reshape(PEERS, EB, LANES)
    x = x_ref[...].astype(F32)
    squares = x * x
    width = squares.shape[1]
    folded = squares[:, :LANES]
    for i in range(1, width // LANES):
        folded = folded + squares[:, i * LANES : (i + 1) * LANES]
    total = jnp.sum(folded.T, axis=0, keepdims=True)
    rows = stat_rows(total, chunks)
    out_ref[:, chunks * 2 * PAIR :, :] = jnp.broadcast_to(rows[None], (PEERS, STATS, LANES))


def reciprocals(stats, chunks):
    rows = [stats[2 * i : 2 * i + 1] + stats[2 * i + 1 : 2 * i + 2] for i in range(chunks)]
    return lax.rsqrt(jnp.concatenate(rows, axis=1) / MODEL_WIDTH + epsilon)


def hidden_rows(ref, chunk, offset, stride):
    start = chunk * stride + offset
    return ref[:, start : start + PAIR, :].reshape(HBS, LANES)


def turn_kernel(w2_ref, w3_ref, w2t_ref, w3t_ref):
    w2t_ref[...] = w2_ref[0].T
    w3t_ref[...] = w3_ref[0].T


def forward_kernel(recv_ref, w2t_ref, w3t_ref, pre_ref, act_ref, out_ref):
    chunks = (recv_ref.shape[1] - STATS) // (2 * PAIR)
    stats = stat_sum(recv_ref[:, chunks * 2 * PAIR :, :])
    inverse = reciprocals(stats, chunks)
    for i in range(0, chunks, 2):
        part = slice(i * LANES, (i + 2) * LANES)
        mixed = jnp.concatenate([hidden_rows(recv_ref, i + k, 0, 2 * PAIR) for k in range(2)], axis=1)
        pre = dot(w2t_ref[...], mixed, NN) * inverse[:, part]
        pre_ref[:, part] = pre
        hyper = jnp.tanh(root_scale * (pre + cubic_term * pre * pre * pre))
        act = (0.5 * pre * (1.0 + hyper)).astype(BF16)
        act_ref[:, part] = act
        third = dot(w3t_ref[...], act, NN).astype(BF16)
        for k in range(2):
            rows = slice((i + k) * PAIR, (i + k + 1) * PAIR)
            out_ref[:, rows, :] = third[:, k * LANES : (k + 1) * LANES].reshape(PEERS, PAIR, LANES)


def backward_kernel(recv_ref, pre_ref, w2_ref, w3_ref, dpre_ref, out_ref):
    chunks = (recv_ref.shape[1] - STATS) // (2 * PAIR)
    stats = stat_sum(recv_ref[:, chunks * 2 * PAIR :, :])
    inverse = reciprocals(stats, chunks)
    inner = []
    for i in range(0, chunks, 2):
        part = slice(i * LANES, (i + 2) * LANES)
        dthird = jnp.concatenate([hidden_rows(recv_ref, i + k, PAIR, 2 * PAIR) for k in range(2)], axis=1)
        dact = dot(w3_ref[0], dthird, NN)
        pre = pre_ref[:, part]
        hyper = jnp.tanh(root_scale * (pre + cubic_term * pre * pre * pre))
        slope = 0.5 * (1.0 + hyper) + 0.5 * pre * (1.0 - hyper * hyper) * root_scale * (
            1.0 + 3.0 * cubic_term * pre * pre
        )
        dpre = dact * slope
        inner.append(jnp.sum(dpre * pre, axis=0, keepdims=True))
        dpre_ref[:, part] = (dpre * inverse[:, part]).astype(BF16)
        dmixed = dot(w2_ref[0], dpre.astype(BF16), NN).astype(BF16)
        for k in range(2):
            rows = slice((i + k) * PAIR, (i + k + 1) * PAIR)
            out_ref[:, rows, :] = dmixed[:, k * LANES : (k + 1) * LANES].reshape(PEERS, PAIR, LANES)
    rows = stat_rows(jnp.concatenate(inner, axis=1), chunks)
    out_ref[:, chunks * PAIR :, :] = jnp.broadcast_to(rows[None], (PEERS, STATS, LANES))


def hidden_grads_kernel(recv_ref, act_ref, dpre_ref, out_ref):
    chunks = (recv_ref.shape[1] - STATS) // (2 * PAIR)
    mixed = jnp.concatenate([hidden_rows(recv_ref, i, 0, 2 * PAIR) for i in range(chunks)], axis=1)
    dthird = jnp.concatenate([hidden_rows(recv_ref, i, PAIR, 2 * PAIR) for i in range(chunks)], axis=1)
    z_size, y_size, rows, _ = out_ref.shape
    half = z_size // 2
    step = half * rows
    for i in range(2 * y_size):
        part = slice(i * step, (i + 1) * step)
        z = slice((i % 2) * half, (i % 2 + 1) * half)
        second = dot(mixed[part], dpre_ref[...], NT).astype(BF16)
        out_ref[z, i // 2, :, :HBS] = second.reshape(half, rows, HBS)
        third = dot(act_ref[part, :], dthird, NT).astype(BF16)
        out_ref[z, i // 2, :, HBS:] = third.reshape(half, rows, HBS)


def model_rows(ref, chunks, a, stride):
    parts = []
    for i in range(chunks):
        start = i * stride + a * EB
        parts.append(ref[:, start : start + EB, :].reshape(HB * EB, LANES))
    return jnp.concatenate(parts, axis=1)


def columns(stats, chunks):
    turned = stats.T
    parts = [turned[:, 2 * i : 2 * i + 1] + turned[:, 2 * i + 1 : 2 * i + 2] for i in range(chunks)]
    return jnp.concatenate(parts, axis=0)


def norm_kernel(x_ref, gain_ref, stats_ref, normed_ref):
    chunks = x_ref.shape[0] // LANES
    inverse = lax.rsqrt(columns(stat_sum(stats_ref[...]), chunks) / MODEL_WIDTH + epsilon)
    normed_ref[...] = (x_ref[...].astype(F32) * inverse * gain_ref[...]).astype(BF16)


def output_kernel(recv_ref, x_ref, w4_ref, out_ref):
    chunks = x_ref.shape[0] // LANES
    for a in range(2):
        feats = slice(a * BS, (a + 1) * BS)
        gathered = model_rows(recv_ref, chunks, a, PAIR)
        branch = dot(gathered, w4_ref[a], TN)
        out_ref[:, feats] = (x_ref[:, feats].astype(F32) + branch).astype(BF16)


def grad_fourth_kernel(recv_ref, cot_ref, out_ref):
    chunks = cot_ref.shape[0] // LANES
    for a in range(2):
        gathered = model_rows(recv_ref, chunks, a, PAIR)
        grad = dot(gathered, cot_ref[:, a * BS : (a + 1) * BS], NN).astype(BF16)
        out_ref[:, a, :, :] = grad.reshape(PEERS, HB * EB // PEERS, BS)


def grad_first_kernel(recv_ref, normed_ref, out_ref):
    chunks = normed_ref.shape[0] // LANES
    for a in range(2):
        dfirst = model_rows(recv_ref, chunks, a, PAIR)
        grad = dot(dfirst, normed_ref[:, a * BS : (a + 1) * BS], NN).astype(BF16)
        out_ref[:, a, :, :] = grad.T.reshape(PEERS, BS // PEERS, HB * EB)


def token_kernel(recv_ref, squares_ref, x_ref, gain_ref, w1_ref, cot_ref, out_ref):
    chunks = x_ref.shape[0] // LANES
    inverse = lax.rsqrt(columns(stat_sum(squares_ref[...]), chunks) / MODEL_WIDTH + epsilon)
    inner = columns(stat_sum(recv_ref[:, chunks * PAIR :, :]), chunks) / MODEL_WIDTH
    for a in range(2):
        feats = slice(a * BS, (a + 1) * BS)
        dfirst = model_rows(recv_ref, chunks, a, PAIR)
        dnormed = dot(dfirst, w1_ref[a], TT)
        xhat = x_ref[:, feats].astype(F32) * inverse
        change = dnormed * gain_ref[:, feats] - xhat * inner
        out_ref[:, feats] = (cot_ref[:, feats].astype(F32) + inverse * change).astype(BF16)


def shards(tokens, gain, w_first, w_second, w_third, w_fourth, cotangent):
    element_count, local_width = tokens.shape
    dp = lax.axis_size("dp")
    scale = 1.0 / math.sqrt(element_count * dp)
    chunks = element_count // LANES
    gain_row = gain[None, :]
    z_size = dp // 2
    z_groups = [[y * z_size + z for z in range(z_size)] for y in range(2)]
    y_index = lax.axis_index("dp") // z_size
    shape = jax.ShapeDtypeStruct
    hidden_flops = 2 * HBS * HBS * element_count
    model_flops = 2 * local_width * HB * EB * element_count

    def exchange(value, axis):
        return lax.all_to_all(value, axis, 0, 0, tiled=True)

    send = call(
        head_kernel,
        shape((PEERS, chunks * 2 * PAIR + STATS, LANES), BF16),
        (tokens, gain_row, w_first, w_fourth, cotangent),
        flops=2 * model_flops,
    )
    recv = exchange(send, "tensor")
    turned = shape((HBS, HBS), BF16)
    w_second_t, w_third_t = call(turn_kernel, [turned, turned], (w_second, w_third))
    pre, act, send = call(
        forward_kernel,
        [
            shape((HBS, element_count), F32),
            shape((HBS, element_count), BF16),
            shape((PEERS, chunks * PAIR, LANES), BF16),
        ],
        (recv, w_second_t, w_third_t),
        flops=2 * hidden_flops,
    )
    third = exchange(send, "tensor")
    dpre, send = call(
        backward_kernel,
        [shape((HBS, element_count), BF16), shape((PEERS, chunks * PAIR + STATS, LANES), BF16)],
        (recv, pre, w_second, w_third),
        flops=2 * hidden_flops,
    )
    hidden = call(
        hidden_grads_kernel,
        shape((z_size, 2, HBS // dp, 2 * HBS), BF16),
        (recv, act, dpre),
        flops=2 * hidden_flops,
    )
    hidden = lax.psum_scatter(hidden, "dp", scatter_dimension=0, axis_index_groups=z_groups, tiled=True)[0]
    back = exchange(send, "tensor")

    squares = recv[:, chunks * 2 * PAIR :, :]
    normed = call(norm_kernel, shape(tokens.shape, BF16), (tokens, gain_row, squares))
    output = call(output_kernel, shape(tokens.shape, BF16), (third, tokens, w_fourth), flops=model_flops)
    fourth = call(
        grad_fourth_kernel,
        shape((PEERS, 2, HB * EB // PEERS, BS), BF16),
        (third, cotangent),
        flops=model_flops,
    )
    first = call(
        grad_first_kernel,
        shape((PEERS, 2, BS // PEERS, HB * EB), BF16),
        (back, normed),
        flops=model_flops,
    )
    fourth = exchange(fourth, "dp")
    first = exchange(first, "dp")
    token_gradient = call(
        token_kernel,
        shape(tokens.shape, BF16),
        (back, squares, tokens, gain_row, w_first, cotangent),
        flops=model_flops,
    )
    grad_first = (jnp.sum(first.astype(F32), axis=0)) * scale
    grad_fourth = (jnp.sum(fourth.astype(F32), axis=0)) * scale

    other = lax.ppermute(
        lax.dynamic_index_in_dim(hidden, 1 - y_index, 0, keepdims=False),
        "dp",
        [(i, (i + z_size) % dp) for i in range(dp)],
    )
    own = lax.dynamic_index_in_dim(hidden, y_index, 0, keepdims=False)
    hidden = (own.astype(F32) + other.astype(F32)) * scale
    return (
        output,
        token_gradient,
        grad_first,
        hidden[None, :, :HBS],
        hidden[None, :, HBS:],
        grad_fourth,
    )


def solution(mesh):
    return jax.shard_map(
        shards,
        mesh=mesh,
        in_specs=(
            P("dp", "tensor"),
            P("tensor"),
            P("tensor", None, None),
            P("tensor", None, None),
            P("tensor", None, None),
            P("tensor", None, None),
            P("dp", "tensor"),
        ),
        out_specs=(
            P("dp", "tensor"),
            P("dp", "tensor"),
            P("tensor", "dp", None),
            P("tensor", "dp", None),
            P("tensor", "dp", None),
            P("tensor", "dp", None),
        ),
        check_vma=False,
    )
```

time: 443 us -> 209 us (0.47)
  waiting for transfers between devices: 248 us -> 66.6 us
  matrix products: 36 us -> 0 us
  Pallas kernels: 0 us -> 35.9 us
  blocking collectives: 56.2 us -> 31.5 us
  other arithmetic: 15.6 us -> 4.55 us
  starting transfers between devices: 42.6 us -> 31.8 us
  local copies, waits for them, and re-layouts: 29.3 us -> 20.9 us
    reduce_scatter x4 -> x1, waiting for transfers between devices: 205 us -> 0.01 us  [shards(): lax.psum_scatter(hidden, 'dp', scatter_dimension=0, axis_index_groups=z_g...]
    psum x2 -> x0, blocking collectives: 56.2 us -> none  [the longest x1 29.6 us: shards(): lax.psum(jnp.sum(scaled_gradient * centered_input, axis=1), 'tensor')]
    dot_general x12 -> x0, matrix products: 36 us -> none  [the longest x1 5.9 us: shards(): jnp.einsum('tcf,tcm->cfm', act, dthird_piece, preferred_element_type=sing...]
    pallas_call x0 -> x10, Pallas kernels: none -> 35.9 us  [call(): pl.pallas_call(kernel, out_shape=out_shape, in_specs=[pl.BlockSpec(memory...]
    all_to_all x0 -> x1, blocking collectives: none -> 31.5 us  [exchange(): return lax.all_to_all(value, axis, 0, 0, tiled=True)]
    all_to_all x4, waiting for transfers between devices: 42.3 us -> 65.7 us  [exchange(): return lax.all_to_all(value, axis, 0, 0, tiled=True)]
    all_to_all x4, starting transfers between devices: 42.4 us -> 29.8 us  [exchange(): return lax.all_to_all(value, axis, 0, 0, tiled=True)]
    unnamed x28 -> x40, local copies, waits for them, and re-layouts: 7.48 us -> 18.2 us
  transfers between devices with their start and end apart: 8 -> 6, of which waited for: 7 -> 5; matrix products, arithmetic and copies ran while one was open for 15% -> 3% of each run, Pallas kernels for 0% -> 4%
where the time goes in v1:
time: 209 us; the launch traced here: 205 us
  waiting for transfers between devices  66.6 us (32%)
  Pallas kernels  35.9 us (17%)
  starting transfers between devices  31.8 us (15%)
  blocking collectives  31.5 us (15%)
  local copies, waits for them, and re-layouts  20.9 us (10%)
  between operations  14.2 us (7%)
  other arithmetic  4.55 us (2%)
    all_to_all x4, waiting for transfers between devices, exchange(): return lax.all_to_all(value, axis, 0, 0, tiled=True)  65.7 us
    pallas_call x10, Pallas kernels, call(): pl.pallas_call(kernel, out_shape=out_shape, in_specs=[pl.BlockSpec(memory...  35.9 us
    all_to_all x1, blocking collectives, exchange(): return lax.all_to_all(value, axis, 0, 0, tiled=True)  31.5 us
    all_to_all x4, starting transfers between devices, exchange(): return lax.all_to_all(value, axis, 0, 0, tiled=True)  29.8 us
    unnamed x40, local copies, waits for them, and re-layouts  18.2 us
  transfers between devices with their start and end apart: 6, of which 5 were waited for; matrix products, arithmetic and copies ran while one was open for 3% of the time, Pallas kernels for 4%

profile of v1, /device:TPU:18, one launch (start us, length us, event | category | flops | bytes accessed | tf_op | source)
XLA Modules:
  0.0 205.4 jit_solution(15734604099005495235)
XLA Ops:
  7.2 0.0 copy-start
  7.2 1.1 copy-done
  8.3 0.0 copy-start.3
  8.3 1.1 copy-done.3
  9.4 0.0 copy-start.9
  9.4 1.0 copy-done.9
  10.5 0.0 copy-start.11
  10.5 1.0 copy-done.11
  11.5 0.0 copy-start.14
  11.5 0.7 copy-done.14
  12.2 2.7 %shard_map.118 = bf16[16,784,128]{2,1,0:T(8,128)(2,1)} custom-call(bf16[768,512]{1,0:T(8,128)(2,1)S(1)} %copy-done, f32[1,512]{1,0:T(1,128)S(1)} %bitcast.10, bf16[2,256,512]{2,1,0:T(8,128)(2,1)S(1)} %copy-done.11, bf16[2,512,256]{2,1,0:T(8,128)(2,1)S(1)} %copy-done.9, bf16[768,512]{1,0:T(8,128)(2,1)S(1)} %copy-done.3), custom_call_target="tpu_custom_call" | custom-call | flops 805306368 | bytes 5834752 | tf_op jit(solution)/shard_map/pallas_call | solution.py:43
  14.9 7.3 %all-to-all-start = ((bf16[16,784,128]{2,1,0:T(8,128)(2,1)}), bf16[16,784,128]{2,1,0:T(8,128)(2,1)S(1)}, u32[]{:S(2)}, u32[]{:S(2)}) async-start(bf16[16,784,128]{2,1,0:T(8,128)(2,1)} %shard_map.118), calls=%async_computation | async-start | bytes 6422528 | tf_op jit(solution)/shard_map/all_to_all | solution.py:241
  22.1 0.0 reduce-scatter.2.cloned.1.call-start
  22.2 3.5 %shard_map.119 = (bf16[1024,1024]{1,0:T(8,128)(2,1)S(1)}, bf16[1024,1024]{1,0:T(8,128)(2,1)S(1)}) custom-call(bf16[1,1024,1024]{2,1,0:T(8,128)(2,1)} %w2_ref.3, bf16[1,1024,1024]{2,1,0:T(8,128)(2,1)} %w3_ref.3), custom_call_target="tpu_custom_call" | custom-call | bytes 8388608 | tf_op jit(solution)/shard_map/pallas_call | solution.py:43
  25.6 0.0 copy-start.16
  25.6 1.3 copy-done.16
  27.0 0.0 copy-start.18
  27.0 1.3 copy-done.18
  28.3 31.3 %all-to-all-done.recv_ref = bf16[16,784,128]{2,1,0:T(8,128)(2,1)S(1)} async-done(((bf16[16,784,128]{2,1,0:T(8,128)(2,1)}), bf16[16,784,128]{2,1,0:T(8,128)(2,1)S(1)}, u32[]{:S(2)}, u32[]{:S(2)}) %all-to-all-start) | async-done | bytes 3211296 | tf_op jit(solution)/shard_map/all_to_all | solution.py:241
  59.6 0.0 copy-start.19
  59.6 1.7 copy-done.19
  61.2 0.0 copy-start.17
  61.2 1.6 copy-done.17
  62.8 8.0 %shard_map.120 = (f32[1024,768]{1,0:T(8,128)}, bf16[1024,768]{1,0:T(8,128)(2,1)S(1)}, bf16[16,384,128]{2,1,0:T(8,128)(2,1)S(1)}) custom-call(bf16[16,784,128]{2,1,0:T(8,128)(2,1)} %copy-done.19, bf16[1024,1024]{1,0:T(8,128)(2,1)S(1)} %copy-done.17, bf16[1024,1024]{1,0:T(8,128)(2,1)} %copy-done.18), custom_call_target="tpu_custom_call" | custom-call | flops 3221225472 | bytes 13697024 | tf_op jit(solution)/shard_map/pallas_call | solution.py:43
  70.8 0.0 copy-done.6
  70.8 9.0 %shard_map.122 = (bf16[1024,768]{1,0:T(8,128)(2,1)S(1)}, bf16[16,400,128]{2,1,0:T(8,128)(2,1)S(1)}) custom-call(bf16[16,784,128]{2,1,0:T(8,128)(2,1)} %copy-done.19, f32[1024,768]{1,0:T(8,128)} %get-tuple-element.16.pre_ref, bf16[1,1024,1024]{2,1,0:T(8,128)(2,1)S(1)} %copy-done.6, bf16[1,1024,1024]{2,1,0:T(8,128)(2,1)} %w3_ref.3), custom_call_target="tpu_custom_call" | custom-call | flops 3221225472 | bytes 13762560 | tf_op jit(solution)/shard_map/pallas_call | solution.py:43
  79.9 0.0 copy-start.13
  79.9 1.3 copy-done.13
  81.1 7.3 %shard_map.126 = bf16[8,2,64,2048]{3,2,1,0:T(8,128)(2,1)} custom-call(bf16[16,784,128]{2,1,0:T(8,128)(2,1)} %copy-done.19, bf16[1024,768]{1,0:T(8,128)(2,1)S(1)} %get-tuple-element.18.act_ref, bf16[1024,768]{1,0:T(8,128)(2,1)S(1)} %get-tuple-element.19.dpre_ref), custom_call_target="tpu_custom_call" | custom-call | flops 3221225472 | bytes 10551296 | tf_op jit(solution)/shard_map/pallas_call | solution.py:43
  88.5 0.0 reduce-scatter.2.cloned.1.call-update
  88.5 31.5 %all_to_all.25.recv_ref = bf16[16,384,128]{2,1,0:T(8,128)(2,1)S(1)} all-to-all(bf16[16,384,128]{2,1,0:T(8,128)(2,1)S(1)} %get-tuple-element.15), channel_id=1, replica_groups=mesh['dp'=16,'tensor'=16] {'tensor'}, dimensions={0} | all-to-all | bytes 3145728 | tf_op jit(solution)/shard_map/all_to_all | solution.py:241
  120.0 8.4 %all-to-all-start.2 = ((bf16[16,400,128]{2,1,0:T(8,128)(2,1)}), bf16[16,400,128]{2,1,0:T(8,128)(2,1)S(1)}, u32[]{:S(2)}, u32[]{:S(2)}) async-start(bf16[16,400,128]{2,1,0:T(8,128)(2,1)} %copy-done.13), calls=%async_computation.2 | async-start | bytes 3276800 | tf_op jit(solution)/shard_map/all_to_all | solution.py:241
  128.3 1.1 copy-done.4
  129.5 0.6 shard_map.127
  130.0 0.0 copy-start.8
  130.0 0.8 copy-done.8
  130.8 17.4 %all-to-all-done.2.recv_ref = bf16[16,400,128]{2,1,0:T(8,128)(2,1)S(1)} async-done(((bf16[16,400,128]{2,1,0:T(8,128)(2,1)}), bf16[16,400,128]{2,1,0:T(8,128)(2,1)S(1)}, u32[]{:S(2)}, u32[]{:S(2)}) %all-to-all-start.2) | async-done | bytes 1638432 | tf_op jit(solution)/shard_map/all_to_all | solution.py:241
  148.2 9.4 %all-to-all-start.4 = ((bf16[16,2,32,256]{3,2,1,0:T(8,128)(2,1)}), bf16[16,2,32,256]{3,2,1,0:T(8,128)(2,1)}, u32[]{:S(2)}, u32[]{:S(2)}) async-start(bf16[16,2,32,256]{3,2,1,0:T(8,128)(2,1)} %copy-done.8), calls=%async_computation.5 | async-start | bytes 1048576 | tf_op jit(solution)/shard_map/all_to_all | solution.py:241
  157.6 0.9 slice.12.squares_ref.stats_ref
  158.4 0.0 copy-done.15
  158.4 1.1 copy-done.1
  159.6 0.5 shard_map.124.normed_ref
  160.0 0.6 shard_map.125
  160.7 0.0 copy-start.7
  160.7 0.8 copy-done.7
  161.5 11.9 %all-to-all-done.4 = bf16[16,2,32,256]{3,2,1,0:T(8,128)(2,1)} async-done(((bf16[16,2,32,256]{3,2,1,0:T(8,128)(2,1)}), bf16[16,2,32,256]{3,2,1,0:T(8,128)(2,1)}, u32[]{:S(2)}, u32[]{:S(2)}) %all-to-all-start.4) | async-done | bytes 524320 | tf_op jit(solution)/shard_map/all_to_all | solution.py:241
  173.4 4.9 %all-to-all-start.3 = ((bf16[16,2,16,512]{3,2,1,0:T(8,128)(2,1)}), bf16[16,2,16,512]{3,2,1,0:T(8,128)(2,1)}, u32[]{:S(2)}, u32[]{:S(2)}) async-start(bf16[16,2,16,512]{3,2,1,0:T(8,128)(2,1)} %copy-done.7), calls=%async_computation.3 | async-start | bytes 1048576 | tf_op jit(solution)/shard_map/all_to_all | solution.py:241
  178.3 0.0 copy-start.2
  178.3 1.1 copy-done.2
  179.5 1.0 copy-done.10
  180.5 1.5 shard_map.121
  182.0 0.0 copy-done.5
  182.0 0.0 copy-done.12
  182.0 2.2 %shard_map.123 = bf16[768,512]{1,0:T(8,128)(2,1)} custom-call(bf16[16,400,128]{2,1,0:T(8,128)(2,1)S(1)} %all-to-all-done.2.recv_ref, bf16[16,16,128]{2,1,0:T(8,128)(2,1)S(1)} %slice.12.squares_ref.stats_ref, bf16[768,512]{1,0:T(8,128)(2,1)S(1)} %copy-done.2, f32[1,512]{1,0:T(1,128)S(1)} %bitcast.12, bf16[2,256,512]{2,1,0:T(8,128)(2,1)S(1)} %copy-done.12, ...), custom_call_target="tpu_custom_call" | custom-call | flops 402653184 | bytes 4589568 | tf_op jit(solution)/shard_map/pallas_call | solution.py:43
  184.2 1.1 convert_reduce_fusion
  185.4 0.6 broadcast_multiply_fusion
  186.0 1.0 dynamic-slice_bitcast_fusion
  187.0 1.9 collective-permute-start
  188.9 5.1 %all-to-all-done.3 = bf16[16,2,16,512]{3,2,1,0:T(8,128)(2,1)} async-done(((bf16[16,2,16,512]{3,2,1,0:T(8,128)(2,1)}), bf16[16,2,16,512]{3,2,1,0:T(8,128)(2,1)}, u32[]{:S(2)}, u32[]{:S(2)}) %all-to-all-start.3) | async-done | bytes 524320 | tf_op jit(solution)/shard_map/all_to_all | solution.py:241
  194.0 1.1 convert_reduce_fusion.1
  195.1 0.6 broadcast_multiply_fusion.1
  195.8 0.9 collective-permute-done
  196.7 1.0 fusion
  197.7 0.8 slice_bitcast_fusion
  (8 shorter events, 0.0 us)
Async XLA Ops:
  7.2 1.1 copy-start
  8.3 1.1 copy-start.3
  9.4 1.0 copy-start.9
  10.5 1.0 copy-start.11
  11.5 0.7 copy-start.14
  14.9 44.7 %all-to-all-start = ((bf16[16,784,128]{2,1,0:T(8,128)(2,1)}), bf16[16,784,128]{2,1,0:T(8,128)(2,1)S(1)}, u32[]{:S(2)}, u32[]{:S(2)}) async-start(bf16[16,784,128]{2,1,0:T(8,128)(2,1)} %shard_map.118), calls=%async_computation | async-start | bytes 6422528 | tf_op jit(solution)/shard_map/all_to_all | solution.py:241
  22.1 163.9 %reduce-scatter.2.cloned.1.call-start = ((), (), s32[]{:S(2)}) async-start(), calls=%async_computation.6 | async-start | bytes 4718592 | tf_op jit(solution)/shard_map/reduce_scatter | solution.py:275
  25.6 1.3 copy-start.16
  27.0 1.3 copy-start.18
  59.6 1.7 copy-start.19
  61.2 1.6 copy-start.17
  62.8 8.0 %copy-start.6 = (bf16[1,1024,1024]{2,1,0:T(8,128)(2,1)S(1)}, bf16[1,1024,1024]{2,1,0:T(8,128)(2,1)}, u32[]{:S(2)}) copy-start(bf16[1,1024,1024]{2,1,0:T(8,128)(2,1)} %w2_ref.3) | copy-start | bytes 6291460
  79.9 1.3 copy-start.13
  120.0 28.2 %all-to-all-start.2 = ((bf16[16,400,128]{2,1,0:T(8,128)(2,1)}), bf16[16,400,128]{2,1,0:T(8,128)(2,1)S(1)}, u32[]{:S(2)}, u32[]{:S(2)}) async-start(bf16[16,400,128]{2,1,0:T(8,128)(2,1)} %copy-done.13), calls=%async_computation.2 | async-start | bytes 3276800 | tf_op jit(solution)/shard_map/all_to_all | solution.py:241
  128.3 1.1 copy-start.4
  129.5 29.0 %copy-start.15 = (f32[512]{0:T(512)S(1)}, f32[512]{0:T(512)}, u32[]{:S(2)}) copy-start(f32[512]{0:T(512)} %param.8) | copy-start | bytes 6148
  130.0 0.8 copy-start.8
  148.2 25.2 %all-to-all-start.4 = ((bf16[16,2,32,256]{3,2,1,0:T(8,128)(2,1)}), bf16[16,2,32,256]{3,2,1,0:T(8,128)(2,1)}, u32[]{:S(2)}, u32[]{:S(2)}) async-start(bf16[16,2,32,256]{3,2,1,0:T(8,128)(2,1)} %copy-done.8), calls=%async_computation.5 | async-start | bytes 1048576 | tf_op jit(solution)/shard_map/all_to_all | solution.py:241
  158.4 1.1 copy-start.1
  160.7 0.8 copy-start.7
  173.4 20.6 %all-to-all-start.3 = ((bf16[16,2,16,512]{3,2,1,0:T(8,128)(2,1)}), bf16[16,2,16,512]{3,2,1,0:T(8,128)(2,1)}, u32[]{:S(2)}, u32[]{:S(2)}) async-start(bf16[16,2,16,512]{3,2,1,0:T(8,128)(2,1)} %copy-done.7), calls=%async_computation.3 | async-start | bytes 1048576 | tf_op jit(solution)/shard_map/all_to_all | solution.py:241
  178.3 1.1 copy-start.2
  179.5 1.0 copy-start.10
  180.5 1.5 copy-start.5
  180.5 1.5 copy-start.12
  187.0 9.7 %collective-permute-start = (bf16[64,2048]{1,0:T(8,128)(2,1)S(1)}, bf16[64,2048]{1,0:T(8,128)(2,1)S(1)}, u32[]{:S(2)}, u32[]{:S(2)}) collective-permute-start(bf16[64,2048]{1,0:T(8,128)(2,1)S(1)} %dynamic-slice_bitcast_fusion), channel_id=1, source_target_pairs={{0,128},{16,144},{32,160},{48,176},{64,192},{80,208},{96,224},{112... | collective-permute-start | bytes 786440 | tf_op jit(solution)/shard_map/ppermute | solution.py:304
Sparse Core Ops, SparseCore 0:
  88.6 63.6 reduce-scatter.1

commit v2 on v1

v2 whole, which is shorter than its diff:
```python
import functools
import math

import jax
import jax.numpy as jnp
from jax import lax
from jax.experimental import pallas as pl
from jax.experimental.pallas import tpu as pltpu
from jax.sharding import PartitionSpec as P

MODEL_WIDTH = 8192
DIAGONAL_BLOCKS = 32
HBS = 1024
HB = 16
BS = 256
EB = 32
PEERS = 16
PAIR = 2 * EB
LANES = 128
STATS = 16
LATE = 1000
VMEM = 58 * 1024 * 1024

epsilon = 1e-05
root_scale = math.sqrt(2.0 / math.pi)
cubic_term = 0.044715

F32 = jnp.float32
BF16 = jnp.bfloat16

NN = (((1,), (0,)), ((), ()))
NT = (((1,), (1,)), ((), ()))
TN = (((0,), (0,)), ((), ()))
TT = (((0,), (1,)), ((), ()))


def dot(a, b, dims):
    return lax.dot_general(a, b, dims, preferred_element_type=F32)


def call(kernel, out_shape, args, scratch=(), flops=0, **extra):
    outs = out_shape if isinstance(out_shape, (list, tuple)) else [out_shape]
    moved = sum(a.size * a.dtype.itemsize for a in args) + sum(
        math.prod(o.shape) * o.dtype.itemsize for o in outs
    )
    return pl.pallas_call(
        kernel,
        out_shape=out_shape,
        in_specs=[pl.BlockSpec(memory_space=pltpu.VMEM)] * len(args),
        out_specs=jax.tree.map(lambda _: pl.BlockSpec(memory_space=pltpu.VMEM), out_shape),
        scratch_shapes=list(scratch),
        compiler_params=pltpu.CompilerParams(vmem_limit_bytes=VMEM),
        cost_estimate=pl.CostEstimate(flops=int(flops), bytes_accessed=int(moved), transcendentals=0),
        **extra,
    )(*args)


def stat_rows(value, chunks):
    high = value.astype(BF16).astype(F32)
    low = value - high
    rows = []
    for i in range(chunks):
        part = slice(i * LANES, (i + 1) * LANES)
        rows += [high[:, part], low[:, part]]
    rows.append(jnp.zeros((STATS - 2 * chunks, LANES), F32))
    return jnp.concatenate(rows, axis=0).astype(BF16)


def stat_sum(rows):
    return jnp.sum(rows.astype(F32), axis=0)


def first_kernel(x_ref, gain_ref, w1_ref, out_ref, squares_ref):
    a = pl.program_id(0)
    chunks = x_ref.shape[0] // LANES
    x = x_ref[...].astype(F32)
    first = dot(w1_ref[0].T, (x * gain_ref[...]).astype(BF16), NT).astype(BF16)
    base = pl.multiple_of(a * EB, EB)
    for i in range(chunks):
        part = slice(i * LANES, (i + 1) * LANES)
        out_ref[:, pl.ds(i * PAIR + base, EB), :] = first[:, part].reshape(PEERS, EB, LANES)
    squares = x * x
    total = jnp.sum((squares[:, :LANES] + squares[:, LANES:]).T, axis=0, keepdims=True)

    @pl.when(a == 0)
    def _():
        squares_ref[...] = total

    @pl.when(a == 1)
    def _():
        rows = stat_rows(squares_ref[...] + total, chunks)
        out_ref[:, chunks * PAIR :, :] = jnp.broadcast_to(rows[None], (PEERS, STATS, LANES))


def dgathered_kernel(w4_ref, cot_ref, out_ref):
    chunks = cot_ref.shape[0] // LANES
    for a in range(2):
        dgathered = dot(w4_ref[a], cot_ref[:, a * BS : (a + 1) * BS], NT).astype(BF16)
        for i in range(chunks):
            part = slice(i * LANES, (i + 1) * LANES)
            base = i * PAIR + a * EB
            out_ref[:, base : base + EB, :] = dgathered[:, part].reshape(PEERS, EB, LANES)


def reciprocals(stats, chunks):
    rows = [stats[2 * i : 2 * i + 1] + stats[2 * i + 1 : 2 * i + 2] for i in range(chunks)]
    return lax.rsqrt(jnp.concatenate(rows, axis=1) / MODEL_WIDTH + epsilon)


def hidden_rows(ref, first, last):
    parts = [ref[:, i * PAIR : (i + 1) * PAIR, :].reshape(HBS, LANES) for i in range(first, last)]
    return jnp.concatenate(parts, axis=1)


def store_rows(ref, value, first):
    for k in range(value.shape[1] // LANES):
        rows = slice((first + k) * PAIR, (first + k + 1) * PAIR)
        ref[:, rows, :] = value[:, k * LANES : (k + 1) * LANES].reshape(PEERS, PAIR, LANES)


def turn_kernel(w2_ref, w3_ref, w2t_ref, w3t_ref):
    w2t_ref[...] = w2_ref[0].T
    w3t_ref[...] = w3_ref[0].T


def forward_kernel(recv_ref, w2t_ref, w3t_ref, pre_ref, act_ref, out_ref):
    chunks = (recv_ref.shape[1] - STATS) // PAIR
    inverse = reciprocals(stat_sum(recv_ref[:, chunks * PAIR :, :]), chunks)
    for i in range(0, chunks, 2):
        part = slice(i * LANES, (i + 2) * LANES)
        pre = dot(w2t_ref[...], hidden_rows(recv_ref, i, i + 2), NN) * inverse[:, part]
        pre_ref[:, part] = pre
        hyper = jnp.tanh(root_scale * (pre + cubic_term * pre * pre * pre))
        act = (0.5 * pre * (1.0 + hyper)).astype(BF16)
        act_ref[:, part] = act
        store_rows(out_ref, dot(w3t_ref[...], act, NN).astype(BF16), i)


def backward_kernel(recv_ref, stats_ref, pre_ref, w2_ref, w3_ref, scaled_ref, out_ref):
    chunks = recv_ref.shape[1] // PAIR
    inverse = reciprocals(stat_sum(stats_ref[...]), chunks)
    inner = []
    for i in range(0, chunks, 2):
        part = slice(i * LANES, (i + 2) * LANES)
        dact = dot(w3_ref[0], hidden_rows(recv_ref, i, i + 2), NN)
        pre = pre_ref[:, part]
        hyper = jnp.tanh(root_scale * (pre + cubic_term * pre * pre * pre))
        slope = 0.5 * (1.0 + hyper) + 0.5 * pre * (1.0 - hyper * hyper) * root_scale * (
            1.0 + 3.0 * cubic_term * pre * pre
        )
        dpre = dact * slope
        inner.append(jnp.sum(dpre * pre, axis=0, keepdims=True))
        scaled_ref[:, part] = (dpre * inverse[:, part]).astype(BF16)
        store_rows(out_ref, dot(w2_ref[0], dpre.astype(BF16), NN).astype(BF16), i)
    rows = stat_rows(jnp.concatenate(inner, axis=1), chunks)
    out_ref[:, chunks * PAIR :, :] = jnp.broadcast_to(rows[None], (PEERS, STATS, LANES))


def hidden_grads_kernel(recv_ref, dthird_ref, act_ref, scaled_ref, out_ref):
    chunks = dthird_ref.shape[1] // PAIR
    mixed = hidden_rows(recv_ref, 0, chunks)
    dthird = hidden_rows(dthird_ref, 0, chunks)
    z_size, y_size, rows, _ = out_ref.shape
    half = z_size // 2
    step = half * rows
    for i in range(2 * y_size):
        part = slice(i * step, (i + 1) * step)
        z = slice((i % 2) * half, (i % 2 + 1) * half)
        second = dot(mixed[part], scaled_ref[...], NT).astype(BF16)
        out_ref[z, i // 2, :, :HBS] = second.reshape(half, rows, HBS)
        third = dot(act_ref[part, :], dthird, NT).astype(BF16)
        out_ref[z, i // 2, :, HBS:] = third.reshape(half, rows, HBS)


def model_rows(ref, chunks, a, stride):
    parts = []
    for i in range(chunks):
        start = i * stride + a * EB
        parts.append(ref[:, start : start + EB, :].reshape(HB * EB, LANES))
    return jnp.concatenate(parts, axis=1)


def columns(stats, chunks):
    turned = stats.T
    parts = [turned[:, 2 * i : 2 * i + 1] + turned[:, 2 * i + 1 : 2 * i + 2] for i in range(chunks)]
    return jnp.concatenate(parts, axis=0)


def norm_kernel(x_ref, gain_ref, stats_ref, normed_ref):
    chunks = x_ref.shape[0] // LANES
    inverse = lax.rsqrt(columns(stat_sum(stats_ref[...]), chunks) / MODEL_WIDTH + epsilon)
    normed_ref[...] = (x_ref[...].astype(F32) * inverse * gain_ref[...]).astype(BF16)


def output_kernel(recv_ref, x_ref, w4_ref, out_ref):
    chunks = x_ref.shape[0] // LANES
    for a in range(2):
        feats = slice(a * BS, (a + 1) * BS)
        gathered = model_rows(recv_ref, chunks, a, PAIR)
        branch = dot(gathered, w4_ref[a], TN)
        out_ref[:, feats] = (x_ref[:, feats].astype(F32) + branch).astype(BF16)


def grad_fourth_kernel(recv_ref, cot_ref, out_ref):
    chunks = cot_ref.shape[0] // LANES
    rows = HB * EB // PEERS
    for a in range(2):
        gathered = model_rows(recv_ref, chunks, a, PAIR)
        grad = dot(gathered, cot_ref[:, a * BS : (a + 1) * BS], NN).astype(BF16)
        out_ref[:, a * rows : (a + 1) * rows, :] = grad.reshape(PEERS, rows, BS)


def grad_first_kernel(recv_ref, normed_ref, fourth_ref, out_ref):
    chunks = normed_ref.shape[0] // LANES
    rows = BS // PEERS
    for a in range(2):
        dfirst = model_rows(recv_ref, chunks, a, PAIR)
        grad = dot(dfirst, normed_ref[:, a * BS : (a + 1) * BS], NN).astype(BF16).T
        for half in range(2):
            base = (2 * a + half) * rows
            part = grad[:, half * BS : (half + 1) * BS]
            out_ref[:, base : base + rows, :] = part.reshape(PEERS, rows, BS)
    out_ref[:, 4 * rows :, :] = fourth_ref[...]


def sum_kernel(scale, recv_ref, first_ref, fourth_ref):
    total = jnp.sum(recv_ref[...].astype(F32), axis=0) * scale
    _, rows, _ = first_ref.shape
    for a in range(2):
        for half in range(2):
            base = (2 * a + half) * rows
            first_ref[a, :, half * BS : (half + 1) * BS] = total[base : base + rows]
    fourth_ref[...] = total[4 * rows :].reshape(fourth_ref.shape)


def finish_kernel(scale, own_ref, other_ref, second_ref, third_ref):
    total = (own_ref[...].astype(F32) + other_ref[...].astype(F32)) * scale
    second_ref[0] = total[:, :HBS]
    third_ref[0] = total[:, HBS:]


def token_kernel(recv_ref, squares_ref, x_ref, gain_ref, w1_ref, cot_ref, out_ref):
    chunks = x_ref.shape[0] // LANES
    inverse = lax.rsqrt(columns(stat_sum(squares_ref[...]), chunks) / MODEL_WIDTH + epsilon)
    inner = columns(stat_sum(recv_ref[:, chunks * PAIR :, :]), chunks) / MODEL_WIDTH
    for a in range(2):
        feats = slice(a * BS, (a + 1) * BS)
        dfirst = model_rows(recv_ref, chunks, a, PAIR)
        dnormed = dot(dfirst, w1_ref[a], TT)
        xhat = x_ref[:, feats].astype(F32) * inverse
        change = dnormed * gain_ref[:, feats] - xhat * inner
        out_ref[:, feats] = (cot_ref[:, feats].astype(F32) + inverse * change).astype(BF16)


def shards(tokens, gain, w_first, w_second, w_third, w_fourth, cotangent):
    element_count, local_width = tokens.shape
    dp = lax.axis_size("dp")
    scale = 1.0 / math.sqrt(element_count * dp)
    chunks = element_count // LANES
    gain_row = gain[None, :]
    z_size = dp // 2
    z_groups = [[y * z_size + z for z in range(z_size)] for y in range(2)]
    y_index = lax.axis_index("dp") // z_size
    shape = jax.ShapeDtypeStruct
    hidden_flops = 2 * HBS * HBS * element_count
    model_flops = 2 * local_width * HB * EB * element_count

    def exchange(value, axis):
        return lax.all_to_all(value, axis, 0, 0, tiled=True)

    def after(value, other):
        return lax.optimization_barrier((value, other))[0]

    rows = chunks * PAIR
    send = pl.pallas_call(
        first_kernel,
        out_shape=shape((PEERS, rows + STATS, LANES), BF16),
        grid=(2,),
        in_specs=[
            pl.BlockSpec((element_count, BS), lambda a: (0, a)),
            pl.BlockSpec((1, BS), lambda a: (0, a)),
            pl.BlockSpec((1, BS, HB * EB), lambda a: (a, 0, 0)),
        ],
        out_specs=pl.BlockSpec((PEERS, rows + STATS, LANES), lambda a: (0, 0, 0)),
        scratch_shapes=[pltpu.VMEM((1, element_count), F32)],
        compiler_params=pltpu.CompilerParams(vmem_limit_bytes=VMEM),
    )(tokens, gain_row, w_first)
    first = exchange(send, "tensor")
    send = call(dgathered_kernel, shape((PEERS, rows, LANES), BF16), (w_fourth, cotangent), flops=model_flops)
    dthird = exchange(after(send, first), "tensor")
    turned = shape((HBS, HBS), BF16)
    w_second_t, w_third_t = call(turn_kernel, [turned, turned], (w_second, w_third))
    wide = (HBS, element_count)
    pre, act, send = call(
        forward_kernel,
        [shape(wide, F32), shape(wide, BF16), shape((PEERS, rows, LANES), BF16)],
        (first, w_second_t, w_third_t),
        flops=2 * hidden_flops,
    )
    third = exchange(after(send, dthird), "tensor")
    squares = first[:, rows:, :]
    scaled, send = call(
        backward_kernel,
        [shape(wide, BF16), shape((PEERS, rows + STATS, LANES), BF16)],
        (dthird, squares, pre, w_second, w_third),
        flops=2 * hidden_flops,
    )
    hidden = call(
        hidden_grads_kernel,
        shape((z_size, 2, HBS // dp, 2 * HBS), BF16),
        (first, dthird, act, scaled),
        flops=2 * hidden_flops,
    )
    hidden = lax.psum_scatter(hidden, "dp", scatter_dimension=0, axis_index_groups=z_groups, tiled=True)[0]
    back = exchange(after(send, third), "tensor")

    normed = call(norm_kernel, shape(tokens.shape, BF16), (tokens, gain_row, after(squares, third)))
    output = call(
        output_kernel, shape(tokens.shape, BF16), (third, tokens, w_fourth), flops=LATE * model_flops
    )
    fourth = call(
        grad_fourth_kernel, shape((PEERS, 64, BS), BF16), (third, cotangent), flops=model_flops
    )
    both = call(
        grad_first_kernel, shape((PEERS, 128, BS), BF16), (back, normed, fourth), flops=model_flops
    )
    both = exchange(both, "dp")
    token_gradient = call(
        token_kernel,
        shape(tokens.shape, BF16),
        (back, squares, tokens, gain_row, w_first, cotangent),
        flops=LATE * model_flops,
    )
    grad_first, grad_fourth = call(
        functools.partial(sum_kernel, scale),
        [shape((2, BS // dp, HB * EB), F32), shape((2, HB * EB // dp, BS), F32)],
        (both,),
    )
    other = lax.ppermute(
        lax.dynamic_index_in_dim(hidden, 1 - y_index, 0, keepdims=False),
        "dp",
        [(i, (i + z_size) % dp) for i in range(dp)],
    )
    own = lax.dynamic_index_in_dim(hidden, y_index, 0, keepdims=False)
    part = shape((1, HBS // dp, HBS), F32)
    grad_second, grad_third = call(functools.partial(finish_kernel, scale), [part, part], (own, other))
    return output, token_gradient, grad_first, grad_second, grad_third, grad_fourth


def solution(mesh):
    return jax.shard_map(
        shards,
        mesh=mesh,
        in_specs=(
            P("dp", "tensor"),
            P("tensor"),
            P("tensor", None, None),
            P("tensor", None, None),
            P("tensor", None, None),
            P("tensor", None, None),
            P("dp", "tensor"),
        ),
        out_specs=(
            P("dp", "tensor"),
            P("dp", "tensor"),
            P("tensor", "dp", None),
            P("tensor", "dp", None),
            P("tensor", "dp", None),
            P("tensor", "dp", None),
        ),
        check_vma=False,
    )
```

time: 209 us -> 195 us (0.933); the launches traced: 205 us -> 194 us
  blocking collectives: 31.5 us -> 0 us
  Pallas kernels: 35.9 us -> 59.2 us
  local copies, waits for them, and re-layouts: 20.9 us -> 5.61 us
  starting transfers between devices: 31.8 us -> 42.4 us
  waiting for transfers between devices: 66.6 us -> 72.8 us
  other arithmetic: 4.55 us -> 0 us
    reduce_scatter x1, waiting for transfers between devices: 0.01 us -> 38.7 us  [shards(): lax.psum_scatter(hidden, 'dp', scatter_dimension=0, axis_index_groups=z_g...]
    all_to_all x4 -> x5, waiting for transfers between devices: 65.7 us -> 33.1 us  [exchange(): return lax.all_to_all(value, axis, 0, 0, tiled=True)]
    all_to_all x1 -> x0, blocking collectives: 31.5 us -> none  [exchange(): return lax.all_to_all(value, axis, 0, 0, tiled=True)]
    pallas_call x10 -> x12, Pallas kernels: 35.9 us -> 56 us  [call(): pl.pallas_call(kernel, out_shape=out_shape, in_specs=[pl.BlockSpec(memory...]
    unnamed x40 -> x6, local copies, waits for them, and re-layouts: 18.2 us -> 2.27 us
    all_to_all x4 -> x5, starting transfers between devices: 29.8 us -> 41.2 us  [exchange(): return lax.all_to_all(value, axis, 0, 0, tiled=True)]
    pallas_call x0 -> x1, Pallas kernels: none -> 3.22 us  [shards(): pl.pallas_call(first_kernel, out_shape=shape((PEERS, rows + STATS, LANES)...]
    mul x3 -> x0, other arithmetic: 2.29 us -> none  [the longest x1 1.02 us: shards(): hidden = (own.astype(F32) + other.astype(F32)) * scale]
  transfers between devices with their start and end apart: 6 -> 7, of which waited for: 5 -> 5; matrix products, arithmetic and copies ran while one was open for 3% -> 2% of each run, Pallas kernels for 4% -> 28%
where the time goes in v2:
time: 195 us; the launch traced here: 194 us
  waiting for transfers between devices  72.8 us (37%)
  Pallas kernels  59.2 us (30%)
  starting transfers between devices  42.4 us (22%)
  between operations  14.1 us (7%)
  local copies, waits for them, and re-layouts  5.61 us (3%)
    pallas_call x12, Pallas kernels, call(): pl.pallas_call(kernel, out_shape=out_shape, in_specs=[pl.BlockSpec(memory...  56 us
    all_to_all x5, starting transfers between devices, exchange(): return lax.all_to_all(value, axis, 0, 0, tiled=True)  41.2 us
    reduce_scatter x1, waiting for transfers between devices, shards(): lax.psum_scatter(hidden, 'dp', scatter_dimension=0, axis_index_groups=z_g...  38.7 us
    all_to_all x5, waiting for transfers between devices, exchange(): return lax.all_to_all(value, axis, 0, 0, tiled=True)  33.1 us
  transfers between devices with their start and end apart: 7, of which 5 were waited for; matrix products, arithmetic and copies ran while one was open for 2% of the time, Pallas kernels for 28%

profile of v2, /device:TPU:18, one launch (start us, length us, event | category | flops | bytes accessed | tf_op | source)
XLA Modules:
  0.0 194.1 jit_solution(15446688986886318129)
XLA Ops:
  7.2 3.2 %shard_map.118 = bf16[16,400,128]{2,1,0:T(8,128)(2,1)} custom-call(bf16[768,512]{1,0:T(8,128)(2,1)} %x_ref.7, f32[1,512]{1,0:T(1,128)} %bitcast.5, bf16[2,256,512]{2,1,0:T(8,128)(2,1)} %w1_ref.3), custom_call_target="tpu_custom_call" | custom-call | tf_op jit(solution)/shard_map/pallas_call | solution.py:275
  10.4 7.3 %all-to-all-start = ((bf16[16,400,128]{2,1,0:T(8,128)(2,1)}), bf16[16,400,128]{2,1,0:T(8,128)(2,1)S(1)}, u32[]{:S(2)}, u32[]{:S(2)}) async-start(bf16[16,400,128]{2,1,0:T(8,128)(2,1)} %shard_map.118), calls=%async_computation | async-start | bytes 3276800 | tf_op jit(solution)/shard_map/all_to_all | solution.py:269
  17.6 3.1 %shard_map.121 = bf16[16,384,128]{2,1,0:T(8,128)(2,1)} custom-call(bf16[2,512,256]{2,1,0:T(8,128)(2,1)} %w4_ref.3, bf16[768,512]{1,0:T(8,128)(2,1)} %cot_ref.5), custom_call_target="tpu_custom_call" | custom-call | flops 402653184 | bytes 2883584 | tf_op jit(solution)/shard_map/pallas_call | solution.py:46
  20.8 16.7 %all-to-all-done.recv_ref = bf16[16,400,128]{2,1,0:T(8,128)(2,1)S(1)} async-done(((bf16[16,400,128]{2,1,0:T(8,128)(2,1)}), bf16[16,400,128]{2,1,0:T(8,128)(2,1)S(1)}, u32[]{:S(2)}, u32[]{:S(2)}) %all-to-all-start) | async-done | bytes 1638432 | tf_op jit(solution)/shard_map/all_to_all | solution.py:269
  37.5 0.0 copy-start.1
  37.5 8.6 %all-to-all-start.1 = ((bf16[16,384,128]{2,1,0:T(8,128)(2,1)}), bf16[16,384,128]{2,1,0:T(8,128)(2,1)S(1)}, u32[]{:S(2)}, u32[]{:S(2)}) async-start(bf16[16,384,128]{2,1,0:T(8,128)(2,1)} %shard_map.121), calls=%async_computation.1 | async-start | bytes 3145728 | tf_op jit(solution)/shard_map/all_to_all | solution.py:269
  46.1 4.9 %shard_map.119 = (bf16[1024,1024]{1,0:T(8,128)(2,1)}, bf16[1024,1024]{1,0:T(8,128)(2,1)}) custom-call(bf16[1,1024,1024]{2,1,0:T(8,128)(2,1)} %w2_ref.3, bf16[1,1024,1024]{2,1,0:T(8,128)(2,1)} %w3_ref.3), custom_call_target="tpu_custom_call" | custom-call | bytes 8388608 | tf_op jit(solution)/shard_map/pallas_call | solution.py:46
  51.0 0.0 copy-done.1
  51.0 9.0 %shard_map.120 = (f32[1024,768]{1,0:T(8,128)}, bf16[1024,768]{1,0:T(8,128)(2,1)}, bf16[16,384,128]{2,1,0:T(8,128)(2,1)}) custom-call(bf16[16,400,128]{2,1,0:T(8,128)(2,1)} %copy-done.1, bf16[1024,1024]{1,0:T(8,128)(2,1)} %get-tuple-element.21.w2t_ref, bf16[1024,1024]{1,0:T(8,128)(2,1)} %get-tuple-element.22.w3t_ref), custom_call_target="tpu_custom_call" | custom-call | flops 3221225472 | bytes 12124160 | tf_op jit(solution)/shard_map/pallas_call | solution.py:46
  60.0 5.2 %all-to-all-done.1.recv_ref.dthird_ref = bf16[16,384,128]{2,1,0:T(8,128)(2,1)S(1)} async-done(((bf16[16,384,128]{2,1,0:T(8,128)(2,1)}), bf16[16,384,128]{2,1,0:T(8,128)(2,1)S(1)}, u32[]{:S(2)}, u32[]{:S(2)}) %all-to-all-start.1) | async-done | bytes 1572896 | tf_op jit(solution)/shard_map/all_to_all | solution.py:269
  65.2 0.0 copy-start.2
  65.2 1.1 copy-done.2
  66.3 8.6 %all-to-all-start.2 = ((bf16[16,384,128]{2,1,0:T(8,128)(2,1)}), bf16[16,384,128]{2,1,0:T(8,128)(2,1)S(1)}, u32[]{:S(2)}, u32[]{:S(2)}) async-start(bf16[16,384,128]{2,1,0:T(8,128)(2,1)} %get-tuple-element.25), calls=%async_computation.2 | async-start | bytes 3145728 | tf_op jit(solution)/shard_map/all_to_all | solution.py:269
  74.9 0.2 reduce-scatter.2.cloned.1.call-start
  75.1 1.5 slice.4.stats_ref.squares_ref
  76.6 10.4 %shard_map.123 = (bf16[1024,768]{1,0:T(8,128)(2,1)}, bf16[16,400,128]{2,1,0:T(8,128)(2,1)}) custom-call(bf16[16,384,128]{2,1,0:T(8,128)(2,1)} %copy-done.2, bf16[16,16,128]{2,1,0:T(8,128)(2,1)} %slice.4.stats_ref.squares_ref, f32[1024,768]{1,0:T(8,128)} %get-tuple-element.26.pre_ref, bf16[1,1024,1024]{2,1,0:T(8,128)(2,1)} %w2_ref.3, ...), custom_call_target="tpu_custom_call" | custom-call | flops 3221225472 | bytes 12189696 | tf_op jit(solution)/shard_map/pallas_call | solution.py:46
  87.0 8.3 %shard_map.129 = bf16[8,2,64,2048]{3,2,1,0:T(8,128)(2,1)} custom-call(bf16[16,400,128]{2,1,0:T(8,128)(2,1)} %copy-done.1, bf16[16,384,128]{2,1,0:T(8,128)(2,1)} %copy-done.2, bf16[1024,768]{1,0:T(8,128)(2,1)} %get-tuple-element.31.act_ref, bf16[1024,768]{1,0:T(8,128)(2,1)} %get-tuple-element.32.scaled_ref), custom_call_target="tpu_custom_call" | custom-call | flops 3221225472 | bytes 10551296 | tf_op jit(solution)/shard_map/pallas_call | solution.py:46
  95.2 0.0 reduce-scatter.2.cloned.1.call-update
  95.3 0.0 all-to-all-done.2.recv_ref
  95.3 0.0 copy-start
  95.3 1.1 copy-done
  96.4 7.5 %all-to-all-start.3 = ((bf16[16,400,128]{2,1,0:T(8,128)(2,1)}), bf16[16,400,128]{2,1,0:T(8,128)(2,1)}, u32[]{:S(2)}, u32[]{:S(2)}) async-start(bf16[16,400,128]{2,1,0:T(8,128)(2,1)} %get-tuple-element.28), calls=%async_computation.3 | async-start | bytes 3276800 | tf_op jit(solution)/shard_map/all_to_all | solution.py:269
  103.9 3.3 %shard_map.122 = bf16[768,512]{1,0:T(8,128)(2,1)} custom-call(bf16[16,384,128]{2,1,0:T(8,128)(2,1)} %copy-done, bf16[768,512]{1,0:T(8,128)(2,1)} %x_ref.7, bf16[2,512,256]{2,1,0:T(8,128)(2,1)} %w4_ref.3), custom_call_target="tpu_custom_call" | custom-call | flops 402653184000 | bytes 3670016 | tf_op jit(solution)/shard_map/pallas_call | solution.py:46
  107.1 2.5 %shard_map.125.normed_ref = bf16[768,512]{1,0:T(8,128)(2,1)} custom-call(bf16[768,512]{1,0:T(8,128)(2,1)} %x_ref.7, f32[1,512]{1,0:T(1,128)} %bitcast.6, bf16[16,16,128]{2,1,0:T(8,128)(2,1)} %slice.4.stats_ref.squares_ref), custom_call_target="tpu_custom_call" | custom-call | bytes 1640448 | tf_op jit(solution)/shard_map/pallas_call | solution.py:46
  109.6 3.0 %shard_map.126.fourth_ref = bf16[16,64,256]{2,1,0:T(8,128)(2,1)} custom-call(bf16[16,384,128]{2,1,0:T(8,128)(2,1)} %copy-done, bf16[768,512]{1,0:T(8,128)(2,1)} %cot_ref.5), custom_call_target="tpu_custom_call" | custom-call | flops 402653184 | bytes 2883584 | tf_op jit(solution)/shard_map/pallas_call | solution.py:46
  112.7 11.1 %all-to-all-done.3.recv_ref = bf16[16,400,128]{2,1,0:T(8,128)(2,1)} async-done(((bf16[16,400,128]{2,1,0:T(8,128)(2,1)}), bf16[16,400,128]{2,1,0:T(8,128)(2,1)}, u32[]{:S(2)}, u32[]{:S(2)}) %all-to-all-start.3) | async-done | bytes 1638432 | tf_op jit(solution)/shard_map/all_to_all | solution.py:269
  123.8 3.4 %shard_map.127 = bf16[16,128,256]{2,1,0:T(8,128)(2,1)} custom-call(bf16[16,400,128]{2,1,0:T(8,128)(2,1)} %all-to-all-done.3.recv_ref, bf16[768,512]{1,0:T(8,128)(2,1)} %shard_map.125.normed_ref, bf16[16,64,256]{2,1,0:T(8,128)(2,1)} %shard_map.126.fourth_ref), custom_call_target="tpu_custom_call" | custom-call | flops 402653184 | bytes 3997696 | tf_op jit(solution)/shard_map/pallas_call | solution.py:46
  127.2 9.4 %all-to-all-start.4 = ((bf16[16,128,256]{2,1,0:T(8,128)(2,1)}), bf16[16,128,256]{2,1,0:T(8,128)(2,1)}, u32[]{:S(2)}, u32[]{:S(2)}) async-start(bf16[16,128,256]{2,1,0:T(8,128)(2,1)} %shard_map.127), calls=%async_computation.4 | async-start | bytes 2097152 | tf_op jit(solution)/shard_map/all_to_all | solution.py:269
  136.6 38.7 %reduce-scatter.2.cloned.1.call-done = bf16[1,2,64,2048]{3,2,1,0:T(8,128)(2,1)} async-done(((bf16[8,2,64,2048]{3,2,1,0:T(8,128)(2,1)}), bf16[1,2,64,2048]{3,2,1,0:T(8,128)(2,1)}) %reduce-scatter.2.cloned.1.call-update) | async-done | bytes 524304 | tf_op jit(solution)/shard_map/reduce_scatter | solution.py:314
  175.3 1.9 dynamic-slice_bitcast_fusion
  177.1 1.0 collective-permute-start
  178.1 4.3 %shard_map.124 = bf16[768,512]{1,0:T(8,128)(2,1)} custom-call(bf16[16,400,128]{2,1,0:T(8,128)(2,1)} %all-to-all-done.3.recv_ref, bf16[16,16,128]{2,1,0:T(8,128)(2,1)} %slice.4.stats_ref.squares_ref, bf16[768,512]{1,0:T(8,128)(2,1)} %x_ref.7, f32[1,512]{1,0:T(1,128)} %bitcast.7, bf16[2,256,512]{2,1,0:T(8,128)(2,1)} %w1_ref.3, bf16[768,512]{1,0:T(8,128)(2,1)} %cot_ref.5), custom_call_target="tpu_custom_call" | custom-call | flops 402653184000 | bytes 4589568 | tf_op jit(solution)/shard_map/pallas_call | solution.py:46
  182.4 0.0 all-to-all-done.4.recv_ref
  182.4 2.0 %shard_map.128 = (f32[2,16,512]{2,1,0:T(8,128)}, f32[2,32,256]{2,1,0:T(8,128)}) custom-call(bf16[16,128,256]{2,1,0:T(8,128)(2,1)} %all-to-all-done.4.recv_ref), custom_call_target="tpu_custom_call" | custom-call | bytes 1179648 | tf_op jit(solution)/shard_map/pallas_call | solution.py:46
  184.4 1.0 collective-permute-done.other_ref
  185.4 1.9 shard_map.130
Async XLA Ops:
  10.4 27.1 %all-to-all-start = ((bf16[16,400,128]{2,1,0:T(8,128)(2,1)}), bf16[16,400,128]{2,1,0:T(8,128)(2,1)S(1)}, u32[]{:S(2)}, u32[]{:S(2)}) async-start(bf16[16,400,128]{2,1,0:T(8,128)(2,1)} %shard_map.118), calls=%async_computation | async-start | bytes 3276800 | tf_op jit(solution)/shard_map/all_to_all | solution.py:269
  37.5 13.5 %copy-start.1 = (bf16[16,400,128]{2,1,0:T(8,128)(2,1)}, bf16[16,400,128]{2,1,0:T(8,128)(2,1)S(1)}, u32[]{:S(2)}) copy-start(bf16[16,400,128]{2,1,0:T(8,128)(2,1)S(1)} %all-to-all-done.recv_ref) | copy-start | bytes 4915204
  37.5 27.7 %all-to-all-start.1 = ((bf16[16,384,128]{2,1,0:T(8,128)(2,1)}), bf16[16,384,128]{2,1,0:T(8,128)(2,1)S(1)}, u32[]{:S(2)}, u32[]{:S(2)}) async-start(bf16[16,384,128]{2,1,0:T(8,128)(2,1)} %shard_map.121), calls=%async_computation.1 | async-start | bytes 3145728 | tf_op jit(solution)/shard_map/all_to_all | solution.py:269
  65.2 1.1 copy-start.2
  66.3 29.0 %all-to-all-start.2 = ((bf16[16,384,128]{2,1,0:T(8,128)(2,1)}), bf16[16,384,128]{2,1,0:T(8,128)(2,1)S(1)}, u32[]{:S(2)}, u32[]{:S(2)}) async-start(bf16[16,384,128]{2,1,0:T(8,128)(2,1)} %get-tuple-element.25), calls=%async_computation.2 | async-start | bytes 3145728 | tf_op jit(solution)/shard_map/all_to_all | solution.py:269
  74.9 100.4 %reduce-scatter.2.cloned.1.call-start = ((), (), s32[]{:S(2)}) async-start(), calls=%async_computation.6 | async-start | bytes 4718592 | tf_op jit(solution)/shard_map/reduce_scatter | solution.py:314
  95.3 1.1 copy-start
  96.4 27.4 %all-to-all-start.3 = ((bf16[16,400,128]{2,1,0:T(8,128)(2,1)}), bf16[16,400,128]{2,1,0:T(8,128)(2,1)}, u32[]{:S(2)}, u32[]{:S(2)}) async-start(bf16[16,400,128]{2,1,0:T(8,128)(2,1)} %get-tuple-element.28), calls=%async_computation.3 | async-start | bytes 3276800 | tf_op jit(solution)/shard_map/all_to_all | solution.py:269
  127.2 55.2 %all-to-all-start.4 = ((bf16[16,128,256]{2,1,0:T(8,128)(2,1)}), bf16[16,128,256]{2,1,0:T(8,128)(2,1)}, u32[]{:S(2)}, u32[]{:S(2)}) async-start(bf16[16,128,256]{2,1,0:T(8,128)(2,1)} %shard_map.127), calls=%async_computation.4 | async-start | bytes 2097152 | tf_op jit(solution)/shard_map/all_to_all | solution.py:269
  177.1 8.3 %collective-permute-start = (bf16[64,2048]{1,0:T(8,128)(2,1)}, bf16[64,2048]{1,0:T(8,128)(2,1)}, u32[]{:S(2)}, u32[]{:S(2)}) collective-permute-start(bf16[64,2048]{1,0:T(8,128)(2,1)} %get-tuple-element.36), channel_id=1, source_target_pairs={{0,128},{16,144},{32,160},{48,176},{64,192},{80,208},{96,224},{112... | collective-permute-start | bytes 786440 | tf_op jit(solution)/shard_map/ppermute | solution.py:339
Sparse Core Ops, SparseCore 0:
  95.4 79.8 reduce-scatter.1

commit v3 on v2

--- a/solution.py
+++ b/solution.py
@@ -70,15 +70,17 @@
     return jnp.sum(rows.astype(F32), axis=0)
 
 
-def first_kernel(x_ref, gain_ref, w1_ref, out_ref, squares_ref):
+def head_kernel(x_ref, gain_ref, w1_ref, w4_ref, cot_ref, out_ref, squares_ref):
     a = pl.program_id(0)
     chunks = x_ref.shape[0] // LANES
     x = x_ref[...].astype(F32)
     first = dot(w1_ref[0].T, (x * gain_ref[...]).astype(BF16), NT).astype(BF16)
+    dgathered = dot(w4_ref[0], cot_ref[...], NT).astype(BF16)
     base = pl.multiple_of(a * EB, EB)
     for i in range(chunks):
         part = slice(i * LANES, (i + 1) * LANES)
         out_ref[:, pl.ds(i * PAIR + base, EB), :] = first[:, part].reshape(PEERS, EB, LANES)
+        out_ref[:, pl.ds((chunks + i) * PAIR + base, EB), :] = dgathered[:, part].reshape(PEERS, EB, LANES)
     squares = x * x
     total = jnp.sum((squares[:, :LANES] + squares[:, LANES:]).T, axis=0, keepdims=True)
 
@@ -89,33 +91,21 @@
     @pl.when(a == 1)
     def _():
         rows = stat_rows(squares_ref[...] + total, chunks)
-        out_ref[:, chunks * PAIR :, :] = jnp.broadcast_to(rows[None], (PEERS, STATS, LANES))
-
-
-def dgathered_kernel(w4_ref, cot_ref, out_ref):
-    chunks = cot_ref.shape[0] // LANES
-    for a in range(2):
-        dgathered = dot(w4_ref[a], cot_ref[:, a * BS : (a + 1) * BS], NT).astype(BF16)
-        for i in range(chunks):
-            part = slice(i * LANES, (i + 1) * LANES)
-            base = i * PAIR + a * EB
-            out_ref[:, base : base + EB, :] = dgathered[:, part].reshape(PEERS, EB, LANES)
-
-
-def reciprocals(stats, chunks):
-    rows = [stats[2 * i : 2 * i + 1] + stats[2 * i + 1 : 2 * i + 2] for i in range(chunks)]
-    return lax.rsqrt(jnp.concatenate(rows, axis=1) / MODEL_WIDTH + epsilon)
-
-
-def hidden_rows(ref, first, last):
-    parts = [ref[:, i * PAIR : (i + 1) * PAIR, :].reshape(HBS, LANES) for i in range(first, last)]
+        out_ref[:, 2 * chunks * PAIR :, :] = jnp.broadcast_to(rows[None], (PEERS, STATS, LANES))
+
+
+def reciprocal(stats, i):
+    rows = stats[pl.ds(4 * i, 4), :]
+    total = jnp.concatenate([rows[0:1] + rows[1:2], rows[2:3] + rows[3:4]], axis=1)
+    return lax.rsqrt(total / MODEL_WIDTH + epsilon)
+
+
+def hidden_rows(ref):
+    sources, rows, _ = ref.shape
+    parts = [
+        ref[:, i * PAIR : (i + 1) * PAIR, :].reshape(sources * PAIR, LANES) for i in range(rows // PAIR)
+    ]
     return jnp.concatenate(parts, axis=1)
-
-
-def store_rows(ref, value, first):
-    for k in range(value.shape[1] // LANES):
-        rows = slice((first + k) * PAIR, (first + k + 1) * PAIR)
-        ref[:, rows, :] = value[:, k * LANES : (k + 1) * LANES].reshape(PEERS, PAIR, LANES)
 
 
 def turn_kernel(w2_ref, w3_ref, w2t_ref, w3t_ref):
@@ -123,53 +113,69 @@
     w3t_ref[...] = w3_ref[0].T
 
 
-def forward_kernel(recv_ref, w2t_ref, w3t_ref, pre_ref, act_ref, out_ref):
-    chunks = (recv_ref.shape[1] - STATS) // PAIR
-    inverse = reciprocals(stat_sum(recv_ref[:, chunks * PAIR :, :]), chunks)
-    for i in range(0, chunks, 2):
-        part = slice(i * LANES, (i + 2) * LANES)
-        pre = dot(w2t_ref[...], hidden_rows(recv_ref, i, i + 2), NN) * inverse[:, part]
-        pre_ref[:, part] = pre
-        hyper = jnp.tanh(root_scale * (pre + cubic_term * pre * pre * pre))
-        act = (0.5 * pre * (1.0 + hyper)).astype(BF16)
-        act_ref[:, part] = act
-        store_rows(out_ref, dot(w3t_ref[...], act, NN).astype(BF16), i)
-
-
-def backward_kernel(recv_ref, stats_ref, pre_ref, w2_ref, w3_ref, scaled_ref, out_ref):
-    chunks = recv_ref.shape[1] // PAIR
-    inverse = reciprocals(stat_sum(stats_ref[...]), chunks)
-    inner = []
-    for i in range(0, chunks, 2):
-        part = slice(i * LANES, (i + 2) * LANES)
-        dact = dot(w3_ref[0], hidden_rows(recv_ref, i, i + 2), NN)
-        pre = pre_ref[:, part]
-        hyper = jnp.tanh(root_scale * (pre + cubic_term * pre * pre * pre))
-        slope = 0.5 * (1.0 + hyper) + 0.5 * pre * (1.0 - hyper * hyper) * root_scale * (
-            1.0 + 3.0 * cubic_term * pre * pre
-        )
-        dpre = dact * slope
-        inner.append(jnp.sum(dpre * pre, axis=0, keepdims=True))
-        scaled_ref[:, part] = (dpre * inverse[:, part]).astype(BF16)
-        store_rows(out_ref, dot(w2_ref[0], dpre.astype(BF16), NN).astype(BF16), i)
-    rows = stat_rows(jnp.concatenate(inner, axis=1), chunks)
-    out_ref[:, chunks * PAIR :, :] = jnp.broadcast_to(rows[None], (PEERS, STATS, LANES))
-
-
-def hidden_grads_kernel(recv_ref, dthird_ref, act_ref, scaled_ref, out_ref):
-    chunks = dthird_ref.shape[1] // PAIR
-    mixed = hidden_rows(recv_ref, 0, chunks)
-    dthird = hidden_rows(dthird_ref, 0, chunks)
-    z_size, y_size, rows, _ = out_ref.shape
-    half = z_size // 2
-    step = half * rows
-    for i in range(2 * y_size):
-        part = slice(i * step, (i + 1) * step)
-        z = slice((i % 2) * half, (i % 2 + 1) * half)
-        second = dot(mixed[part], scaled_ref[...], NT).astype(BF16)
-        out_ref[z, i // 2, :, :HBS] = second.reshape(half, rows, HBS)
-        third = dot(act_ref[part, :], dthird, NT).astype(BF16)
-        out_ref[z, i // 2, :, HBS:] = third.reshape(half, rows, HBS)
+def by_peer(value):
+    parts = [value[:, k * LANES : (k + 1) * LANES].reshape(PEERS, PAIR, LANES) for k in range(2)]
+    return jnp.concatenate(parts, axis=1)
+
+
+def forward_kernel(recv_ref, stats_ref, w2t_ref, w3t_ref, pre_ref, act_ref, out_ref, total_ref):
+    i = pl.program_id(0)
+
+    @pl.when(i == 0)
+    def _():
+        total_ref[...] = stat_sum(stats_ref[...])
+
+    pre = dot(w2t_ref[...], hidden_rows(recv_ref), NN) * reciprocal(total_ref, i)
+    pre_ref[...] = pre
+    hyper = jnp.tanh(root_scale * (pre + cubic_term * pre * pre * pre))
+    act = (0.5 * pre * (1.0 + hyper)).astype(BF16)
+    act_ref[...] = act
+    out_ref[...] = by_peer(dot(w3t_ref[...], act, NN).astype(BF16))
+
+
+def backward_kernel(recv_ref, stats_ref, pre_ref, w2_ref, w3_ref, scaled_ref, out_ref, total_ref, inner_ref):
+    i = pl.program_id(0)
+    steps = pl.num_programs(0)
+
+    @pl.when(i == 0)
+    def _():
+        total_ref[...] = stat_sum(stats_ref[...])
+        inner_ref[...] = jnp.zeros_like(inner_ref)
+
+    dact = dot(w3_ref[0], hidden_rows(recv_ref), NN)
+    pre = pre_ref[...]
+    hyper = jnp.tanh(root_scale * (pre + cubic_term * pre * pre * pre))
+    slope = 0.5 * (1.0 + hyper) + 0.5 * pre * (1.0 - hyper * hyper) * root_scale * (
+        1.0 + 3.0 * cubic_term * pre * pre
+    )
+    dpre = dact * slope
+    inner = jnp.sum(dpre * pre, axis=0, keepdims=True)
+    scaled_ref[...] = (dpre * reciprocal(total_ref, i)).astype(BF16)
+    dmixed = dot(w2_ref[0], dpre.astype(BF16), NN).astype(BF16)
+    out_ref[:, pl.ds(pl.multiple_of(i * 2 * PAIR, 2 * PAIR), 2 * PAIR), :] = by_peer(dmixed)
+    high = inner.astype(BF16).astype(F32)
+    low = inner - high
+    rows = [high[:, :LANES], low[:, :LANES], high[:, LANES:], low[:, LANES:]]
+    inner_ref[pl.ds(4 * i, 4), :] = jnp.concatenate(rows, axis=0)
+
+    @pl.when(i == steps - 1)
+    def _():
+        stats = jnp.broadcast_to(inner_ref[...].astype(BF16)[None], (PEERS, STATS, LANES))
+        out_ref[:, out_ref.shape[1] - STATS :, :] = stats
+
+
+def hidden_grads_kernel(y_ref, mixed_ref, dthird_ref, act_ref, scaled_ref, out_ref, turned_ref):
+    del y_ref
+
+    @pl.when(pl.program_id(0) == 0)
+    def _():
+        turned_ref[...] = hidden_rows(dthird_ref)
+
+    shape = (out_ref.shape[0], out_ref.shape[2], HBS)
+    second = dot(hidden_rows(mixed_ref), scaled_ref[...], NT).astype(BF16)
+    out_ref[:, 0, :, :HBS] = second.reshape(shape)
+    third = dot(act_ref[...], turned_ref[...], NT).astype(BF16)
+    out_ref[:, 0, :, HBS:] = third.reshape(shape)
 
 
 def model_rows(ref, chunks, a, stride):
@@ -234,7 +240,7 @@
 
 
 def finish_kernel(scale, own_ref, other_ref, second_ref, third_ref):
-    total = (own_ref[...].astype(F32) + other_ref[...].astype(F32)) * scale
+    total = (own_ref[0, 0].astype(F32) + other_ref[...].astype(F32)) * scale
     second_ref[0] = total[:, :HBS]
     third_ref[0] = total[:, HBS:]
 
@@ -272,46 +278,89 @@
         return lax.optimization_barrier((value, other))[0]
 
     rows = chunks * PAIR
+    wide = (HBS, element_count)
+    step = 2 * LANES
+    steps = element_count // step
+    params = pltpu.CompilerParams(vmem_limit_bytes=VMEM)
+
+    def cost(flops):
+        return pl.CostEstimate(flops=int(flops), bytes_accessed=8 << 20, transcendentals=0)
+
+    def whole(*dims):
+        return pl.BlockSpec(dims, lambda i, *_: (0,) * len(dims))
+
     send = pl.pallas_call(
-        first_kernel,
-        out_shape=shape((PEERS, rows + STATS, LANES), BF16),
+        head_kernel,
+        out_shape=shape((PEERS, 2 * rows + STATS, LANES), BF16),
         grid=(2,),
         in_specs=[
             pl.BlockSpec((element_count, BS), lambda a: (0, a)),
             pl.BlockSpec((1, BS), lambda a: (0, a)),
             pl.BlockSpec((1, BS, HB * EB), lambda a: (a, 0, 0)),
+            pl.BlockSpec((1, HB * EB, BS), lambda a: (a, 0, 0)),
+            pl.BlockSpec((element_count, BS), lambda a: (0, a)),
         ],
-        out_specs=pl.BlockSpec((PEERS, rows + STATS, LANES), lambda a: (0, 0, 0)),
+        out_specs=whole(PEERS, 2 * rows + STATS, LANES),
         scratch_shapes=[pltpu.VMEM((1, element_count), F32)],
-        compiler_params=pltpu.CompilerParams(vmem_limit_bytes=VMEM),
-    )(tokens, gain_row, w_first)
-    first = exchange(send, "tensor")
-    send = call(dgathered_kernel, shape((PEERS, rows, LANES), BF16), (w_fourth, cotangent), flops=model_flops)
-    dthird = exchange(after(send, first), "tensor")
+        compiler_params=params,
+        cost_estimate=cost(2 * model_flops),
+    )(tokens, gain_row, w_first, w_fourth, cotangent)
+    recv = exchange(send, "tensor")
     turned = shape((HBS, HBS), BF16)
     w_second_t, w_third_t = call(turn_kernel, [turned, turned], (w_second, w_third))
-    wide = (HBS, element_count)
-    pre, act, send = call(
+    by_tokens = pl.BlockSpec((HBS, step), lambda i: (0, i))
+    peer_rows = pl.BlockSpec((PEERS, 2 * PAIR, LANES), lambda i: (0, i, 0))
+    stats_spec = pl.BlockSpec((PEERS, STATS, LANES), lambda i: (0, 2 * rows // STATS, 0))
+    pre, act, send = pl.pallas_call(
         forward_kernel,
-        [shape(wide, F32), shape(wide, BF16), shape((PEERS, rows, LANES), BF16)],
-        (first, w_second_t, w_third_t),
-        flops=2 * hidden_flops,
-    )
-    third = exchange(after(send, dthird), "tensor")
-    squares = first[:, rows:, :]
-    scaled, send = call(
+        out_shape=[shape(wide, F32), shape(wide, BF16), shape((PEERS, rows, LANES), BF16)],
+        grid=(steps,),
+        in_specs=[peer_rows, stats_spec, whole(HBS, HBS), whole(HBS, HBS)],
+        out_specs=[by_tokens, by_tokens, peer_rows],
+        scratch_shapes=[pltpu.VMEM((STATS, LANES), F32)],
+        compiler_params=params,
+        cost_estimate=cost(2 * hidden_flops),
+    )(recv, recv, w_second_t, w_third_t)
+    third = exchange(send, "tensor")
+    scaled, send = pl.pallas_call(
         backward_kernel,
-        [shape(wide, BF16), shape((PEERS, rows + STATS, LANES), BF16)],
-        (dthird, squares, pre, w_second, w_third),
-        flops=2 * hidden_flops,
-    )
-    hidden = call(
+        out_shape=[shape(wide, BF16), shape((PEERS, rows + STATS, LANES), BF16)],
+        grid=(steps,),
+        in_specs=[
+            pl.BlockSpec((PEERS, 2 * PAIR, LANES), lambda i: (0, steps + i, 0)),
+            stats_spec,
+            by_tokens,
+            whole(1, HBS, HBS),
+            whole(1, HBS, HBS),
+        ],
+        out_specs=[by_tokens, whole(PEERS, rows + STATS, LANES)],
+        scratch_shapes=[pltpu.VMEM((STATS, LANES), F32)] * 2,
+        compiler_params=params,
+        cost_estimate=cost(2 * hidden_flops),
+    )(recv, recv, pre, w_second, w_third)
+    quarter = z_size // 2
+    hidden = pl.pallas_call(
         hidden_grads_kernel,
-        shape((z_size, 2, HBS // dp, 2 * HBS), BF16),
-        (first, dthird, act, scaled),
-        flops=2 * hidden_flops,
-    )
-    hidden = lax.psum_scatter(hidden, "dp", scatter_dimension=0, axis_index_groups=z_groups, tiled=True)[0]
+        out_shape=shape((z_size, 2, HBS // dp, 2 * HBS), BF16),
+        grid_spec=pltpu.PrefetchScalarGridSpec(
+            num_scalar_prefetch=1,
+            grid=(4,),
+            in_specs=[
+                pl.BlockSpec((PEERS // 4, rows, LANES), lambda i, y: (i, 0, 0)),
+                pl.BlockSpec((PEERS, rows, LANES), lambda i, y: (0, 1, 0)),
+                pl.BlockSpec((HBS // 4, element_count), lambda i, y: (i, 0)),
+                whole(*wide),
+            ],
+            out_specs=pl.BlockSpec(
+                (quarter, 1, HBS // dp, 2 * HBS), lambda i, y: (i % 2, (i // 2 + y[0]) % 2, 0, 0)
+            ),
+            scratch_shapes=[pltpu.VMEM(wide, BF16)],
+        ),
+        compiler_params=params,
+        cost_estimate=cost(2 * hidden_flops),
+    )(y_index.astype(jnp.int32)[None], recv, recv, act, scaled)
+    hidden = lax.psum_scatter(hidden, "dp", scatter_dimension=0, axis_index_groups=z_groups, tiled=True)
+    squares = recv[:, 2 * rows :, :]
     back = exchange(after(send, third), "tensor")
 
     normed = call(norm_kernel, shape(tokens.shape, BF16), (tokens, gain_row, after(squares, third)))
@@ -336,14 +385,9 @@
         [shape((2, BS // dp, HB * EB), F32), shape((2, HB * EB // dp, BS), F32)],
         (both,),
     )
-    other = lax.ppermute(
-        lax.dynamic_index_in_dim(hidden, 1 - y_index, 0, keepdims=False),
-        "dp",
-        [(i, (i + z_size) % dp) for i in range(dp)],
-    )
-    own = lax.dynamic_index_in_dim(hidden, y_index, 0, keepdims=False)
+    other = lax.ppermute(hidden[0, 1], "dp", [(i, (i + z_size) % dp) for i in range(dp)])
     part = shape((1, HBS // dp, HBS), F32)
-    grad_second, grad_third = call(functools.partial(finish_kernel, scale), [part, part], (own, other))
+    grad_second, grad_third = call(functools.partial(finish_kernel, scale), [part, part], (hidden, other))
     return output, token_gradient, grad_first, grad_second, grad_third, grad_fourth
 
 

time: 195 us -> 201 us (1.031)
  waiting for transfers between devices: 72.8 us -> 83.1 us
  starting transfers between devices: 42.4 us -> 37.7 us
    pallas_call x1 -> x4, Pallas kernels: 3.22 us -> 35.3 us  [the longest x1 12.4 us: shards(): pl.pallas_call(backward_kernel, out_shape=[shape(wide, BF16), shape((PEER...]
    pallas_call x12 -> x8, Pallas kernels: 56 us -> 25.4 us  [call(): pl.pallas_call(kernel, out_shape=out_shape, in_specs=[pl.BlockSpec(memory...]
    all_to_all x5 -> x4, waiting for transfers between devices: 33.1 us -> 43.6 us  [exchange(): return lax.all_to_all(value, axis, 0, 0, tiled=True)]
    all_to_all x5 -> x4, starting transfers between devices: 41.2 us -> 36.7 us  [exchange(): return lax.all_to_all(value, axis, 0, 0, tiled=True)]
  transfers between devices with their start and end apart: 7 -> 6, of which waited for: 5 -> 4; matrix products, arithmetic and copies ran while one was open for 2% -> 2% of each run, Pallas kernels for 28% -> 22%
where the time goes in v3:
time: 201 us; the launch traced here: 200 us
  waiting for transfers between devices  83.1 us (41%)
  Pallas kernels  60.7 us (30%)
  starting transfers between devices  37.7 us (19%)
  between operations  14.1 us (7%)
  local copies, waits for them, and re-layouts  4.85 us (2%)
    all_to_all x4, waiting for transfers between devices, exchange(): return lax.all_to_all(value, axis, 0, 0, tiled=True)  43.6 us
    reduce_scatter x1, waiting for transfers between devices, shards(): lax.psum_scatter(hidden, 'dp', scatter_dimension=0, axis_index_groups=z_g...  38.5 us
    all_to_all x4, starting transfers between devices, exchange(): return lax.all_to_all(value, axis, 0, 0, tiled=True)  36.7 us
    pallas_call x8, Pallas kernels, call(): pl.pallas_call(kernel, out_shape=out_shape, in_specs=[pl.BlockSpec(memory...  25.4 us
    pallas_call x1, Pallas kernels, shards(): pl.pallas_call(backward_kernel, out_shape=[shape(wide, BF16), shape((PEER...  12.4 us
    pallas_call x1, Pallas kernels, shards(): pl.pallas_call(forward_kernel, out_shape=[shape(wide, F32), shape(wide, B...  10.3 us
    pallas_call x1, Pallas kernels, shards(): pl.pallas_call(hidden_grads_kernel, out_shape=shape((z_size, 2, HBS // dp...  8.11 us
    pallas_call x1, Pallas kernels, shards(): pl.pallas_call(head_kernel, out_shape=shape((PEERS, 2 * rows + STATS, LAN...  4.52 us
  transfers between devices with their start and end apart: 6, of which 4 were waited for; matrix products, arithmetic and copies ran while one was open for 2% of the time, Pallas kernels for 22%

profile of v3, /device:TPU:18, one launch (start us, length us, event | category | flops | bytes accessed | tf_op | source)
XLA Modules:
  0.0 200.4 jit_solution(7191946241435374220)
XLA Ops:
  7.2 4.5 %shard_map.118 = bf16[16,784,128]{2,1,0:T(8,128)(2,1)} custom-call(bf16[768,512]{1,0:T(8,128)(2,1)} %x_ref.7, f32[1,512]{1,0:T(1,128)} %bitcast.4, bf16[2,256,512]{2,1,0:T(8,128)(2,1)} %w1_ref.3, bf16[2,512,256]{2,1,0:T(8,128)(2,1)} %w4_ref.3, bf16[768,512]{1,0:T(8,128)(2,1)} %cot_ref.5), custom_call_target="tpu_custom_call" | custom-call | flops 805306368 | bytes 8388608 | tf_op jit(solution)/shard_map/pallas_call | solution.py:292
  11.7 7.2 %all-to-all-start = ((bf16[16,784,128]{2,1,0:T(8,128)(2,1)}), bf16[16,784,128]{2,1,0:T(8,128)(2,1)S(1)}, u32[]{:S(2)}, u32[]{:S(2)}) async-start(bf16[16,784,128]{2,1,0:T(8,128)(2,1)} %shard_map.118), calls=%async_computation | async-start | bytes 6422528 | tf_op jit(solution)/shard_map/all_to_all | solution.py:275
  18.9 4.9 %shard_map.119 = (bf16[1024,1024]{1,0:T(8,128)(2,1)}, bf16[1024,1024]{1,0:T(8,128)(2,1)}) custom-call(bf16[1,1024,1024]{2,1,0:T(8,128)(2,1)} %w2_ref.3, bf16[1,1024,1024]{2,1,0:T(8,128)(2,1)} %w3_ref.3), custom_call_target="tpu_custom_call" | custom-call | bytes 8388608 | tf_op jit(solution)/shard_map/pallas_call | solution.py:46
  23.9 32.5 %all-to-all-done.recv_ref.stats_ref.mixed_ref.dthird_ref = bf16[16,784,128]{2,1,0:T(8,128)(2,1)S(1)} async-done(((bf16[16,784,128]{2,1,0:T(8,128)(2,1)}), bf16[16,784,128]{2,1,0:T(8,128)(2,1)S(1)}, u32[]{:S(2)}, u32[]{:S(2)}) %all-to-all-start) | async-done | bytes 3211296 | tf_op jit(solution)/shard_map/all_to_all | solution.py:275
  56.4 0.0 copy-start
  56.4 1.7 copy-done
  58.1 10.3 %shard_map.120 = (f32[1024,768]{1,0:T(8,128)}, bf16[1024,768]{1,0:T(8,128)(2,1)}, bf16[16,384,128]{2,1,0:T(8,128)(2,1)}) custom-call(bf16[16,784,128]{2,1,0:T(8,128)(2,1)} %copy-done, bf16[16,784,128]{2,1,0:T(8,128)(2,1)} %copy-done, bf16[1024,1024]{1,0:T(8,128)(2,1)} %get-tuple-element.19.w2t_ref, bf16[1024,1024]{1,0:T(8,128)(2,1)} %get-tuple-element.20.w3t_ref), custom_call_target="tpu_custom_call" | custom-call | flops 3221225472 | bytes 8388608 | tf_op jit(solution)/shard_map/pallas_call | solution.py:314
  68.4 12.8 %all-to-all-start.1 = ((bf16[16,384,128]{2,1,0:T(8,128)(2,1)}), bf16[16,384,128]{2,1,0:T(8,128)(2,1)S(1)}, u32[]{:S(2)}, u32[]{:S(2)}) async-start(bf16[16,384,128]{2,1,0:T(8,128)(2,1)} %get-tuple-element.21), calls=%async_computation.1 | async-start | bytes 3145728 | tf_op jit(solution)/shard_map/all_to_all | solution.py:275
  81.2 0.0 reduce-scatter.2.cloned.1.call-start
  81.2 12.4 %shard_map.122 = (bf16[1024,768]{1,0:T(8,128)(2,1)}, bf16[16,400,128]{2,1,0:T(8,128)(2,1)}) custom-call(bf16[16,784,128]{2,1,0:T(8,128)(2,1)} %copy-done, bf16[16,784,128]{2,1,0:T(8,128)(2,1)} %copy-done, f32[1024,768]{1,0:T(8,128)} %get-tuple-element.22.pre_ref, bf16[1,1024,1024]{2,1,0:T(8,128)(2,1)} %w2_ref.3, bf16[1,1024,1024]{2,1,0:T(8,128)(2,1)} %w3_ref.3), custom_call_target="tpu_custom_call" | custom-call | flops 3221225472 | bytes 8388608 | tf_op jit(solution)/shard_map/pallas_call | solution.py:325
  93.7 8.1 %shard_map.128 = bf16[8,2,64,2048]{3,2,1,0:T(8,128)(2,1)} custom-call(s32[1]{0:T(128)} %bitcast.1.y_ref, bf16[16,784,128]{2,1,0:T(8,128)(2,1)} %copy-done, bf16[16,784,128]{2,1,0:T(8,128)(2,1)} %copy-done, bf16[1024,768]{1,0:T(8,128)(2,1)} %get-tuple-element.27.act_ref, bf16[1024,768]{1,0:T(8,128)(2,1)} %get-tuple-element.28.scaled_ref), custom_call_target="tpu_custom_call" | custom-call | flops 3221225472 | bytes 8388608 | tf_op jit(solution)/shard_map/pallas_call | solution.py:342
  101.8 0.0 reduce-scatter.2.cloned.1.call-update
  101.8 1.5 slice.8.squares_ref.stats_ref
  103.3 0.0 all-to-all-done.1.recv_ref
  103.3 0.0 copy-start.1
  103.3 7.2 %all-to-all-start.2 = ((bf16[16,400,128]{2,1,0:T(8,128)(2,1)}), bf16[16,400,128]{2,1,0:T(8,128)(2,1)}, u32[]{:S(2)}, u32[]{:S(2)}) async-start(bf16[16,400,128]{2,1,0:T(8,128)(2,1)} %get-tuple-element.24), calls=%async_computation.2 | async-start | bytes 3276800 | tf_op jit(solution)/shard_map/all_to_all | solution.py:275
  110.5 0.0 copy-done.1
  110.5 3.3 %shard_map.121 = bf16[768,512]{1,0:T(8,128)(2,1)} custom-call(bf16[16,384,128]{2,1,0:T(8,128)(2,1)} %copy-done.1, bf16[768,512]{1,0:T(8,128)(2,1)} %x_ref.7, bf16[2,512,256]{2,1,0:T(8,128)(2,1)} %w4_ref.3), custom_call_target="tpu_custom_call" | custom-call | flops 402653184000 | bytes 3670016 | tf_op jit(solution)/shard_map/pallas_call | solution.py:46
  113.8 2.5 %shard_map.124.normed_ref = bf16[768,512]{1,0:T(8,128)(2,1)} custom-call(bf16[768,512]{1,0:T(8,128)(2,1)} %x_ref.7, f32[1,512]{1,0:T(1,128)} %bitcast.5, bf16[16,16,128]{2,1,0:T(8,128)(2,1)} %slice.8.squares_ref.stats_ref), custom_call_target="tpu_custom_call" | custom-call | bytes 1640448 | tf_op jit(solution)/shard_map/pallas_call | solution.py:46
  116.3 3.0 %shard_map.125.fourth_ref = bf16[16,64,256]{2,1,0:T(8,128)(2,1)} custom-call(bf16[16,384,128]{2,1,0:T(8,128)(2,1)} %copy-done.1, bf16[768,512]{1,0:T(8,128)(2,1)} %cot_ref.5), custom_call_target="tpu_custom_call" | custom-call | flops 402653184 | bytes 2883584 | tf_op jit(solution)/shard_map/pallas_call | solution.py:46
  119.3 11.1 %all-to-all-done.2.recv_ref = bf16[16,400,128]{2,1,0:T(8,128)(2,1)} async-done(((bf16[16,400,128]{2,1,0:T(8,128)(2,1)}), bf16[16,400,128]{2,1,0:T(8,128)(2,1)}, u32[]{:S(2)}, u32[]{:S(2)}) %all-to-all-start.2) | async-done | bytes 1638432 | tf_op jit(solution)/shard_map/all_to_all | solution.py:275
  130.4 3.4 %shard_map.126 = bf16[16,128,256]{2,1,0:T(8,128)(2,1)} custom-call(bf16[16,400,128]{2,1,0:T(8,128)(2,1)} %all-to-all-done.2.recv_ref, bf16[768,512]{1,0:T(8,128)(2,1)} %shard_map.124.normed_ref, bf16[16,64,256]{2,1,0:T(8,128)(2,1)} %shard_map.125.fourth_ref), custom_call_target="tpu_custom_call" | custom-call | flops 402653184 | bytes 3997696 | tf_op jit(solution)/shard_map/pallas_call | solution.py:46
  133.8 9.4 %all-to-all-start.3 = ((bf16[16,128,256]{2,1,0:T(8,128)(2,1)}), bf16[16,128,256]{2,1,0:T(8,128)(2,1)}, u32[]{:S(2)}, u32[]{:S(2)}) async-start(bf16[16,128,256]{2,1,0:T(8,128)(2,1)} %shard_map.126), calls=%async_computation.3 | async-start | bytes 2097152 | tf_op jit(solution)/shard_map/all_to_all | solution.py:275
  143.2 38.5 %reduce-scatter.2.cloned.1.call-done.own_ref = bf16[1,2,64,2048]{3,2,1,0:T(8,128)(2,1)} async-done(((bf16[8,2,64,2048]{3,2,1,0:T(8,128)(2,1)}), bf16[1,2,64,2048]{3,2,1,0:T(8,128)(2,1)}) %reduce-scatter.2.cloned.1.call-update) | async-done | bytes 524304 | tf_op jit(solution)/shard_map/reduce_scatter | solution.py:362
  181.7 1.7 slice_bitcast_fusion
  183.4 1.0 collective-permute-start
  184.4 4.3 %shard_map.123 = bf16[768,512]{1,0:T(8,128)(2,1)} custom-call(bf16[16,400,128]{2,1,0:T(8,128)(2,1)} %all-to-all-done.2.recv_ref, bf16[16,16,128]{2,1,0:T(8,128)(2,1)} %slice.8.squares_ref.stats_ref, bf16[768,512]{1,0:T(8,128)(2,1)} %x_ref.7, f32[1,512]{1,0:T(1,128)} %bitcast.6, bf16[2,256,512]{2,1,0:T(8,128)(2,1)} %w1_ref.3, bf16[768,512]{1,0:T(8,128)(2,1)} %cot_ref.5), custom_call_target="tpu_custom_call" | custom-call | flops 402653184000 | bytes 4589568 | tf_op jit(solution)/shard_map/pallas_call | solution.py:46
  188.7 0.0 all-to-all-done.3.recv_ref
  188.7 2.0 shard_map.127
  190.7 0.9 collective-permute-done.other_ref
  191.6 1.9 shard_map.129
Async XLA Ops:
  11.7 44.7 %all-to-all-start = ((bf16[16,784,128]{2,1,0:T(8,128)(2,1)}), bf16[16,784,128]{2,1,0:T(8,128)(2,1)S(1)}, u32[]{:S(2)}, u32[]{:S(2)}) async-start(bf16[16,784,128]{2,1,0:T(8,128)(2,1)} %shard_map.118), calls=%async_computation | async-start | bytes 6422528 | tf_op jit(solution)/shard_map/all_to_all | solution.py:275
  56.4 1.7 copy-start
  68.4 34.9 %all-to-all-start.1 = ((bf16[16,384,128]{2,1,0:T(8,128)(2,1)}), bf16[16,384,128]{2,1,0:T(8,128)(2,1)S(1)}, u32[]{:S(2)}, u32[]{:S(2)}) async-start(bf16[16,384,128]{2,1,0:T(8,128)(2,1)} %get-tuple-element.21), calls=%async_computation.1 | async-start | bytes 3145728 | tf_op jit(solution)/shard_map/all_to_all | solution.py:275
  81.2 100.5 %reduce-scatter.2.cloned.1.call-start = ((), (), s32[]{:S(2)}) async-start(), calls=%async_computation.5 | async-start | bytes 4718592 | tf_op jit(solution)/shard_map/reduce_scatter | solution.py:362
  103.3 7.2 %copy-start.1 = (bf16[16,384,128]{2,1,0:T(8,128)(2,1)}, bf16[16,384,128]{2,1,0:T(8,128)(2,1)S(1)}, u32[]{:S(2)}) copy-start(bf16[16,384,128]{2,1,0:T(8,128)(2,1)S(1)} %all-to-all-done.1.recv_ref) | copy-start | bytes 4718596
  103.3 27.1 %all-to-all-start.2 = ((bf16[16,400,128]{2,1,0:T(8,128)(2,1)}), bf16[16,400,128]{2,1,0:T(8,128)(2,1)}, u32[]{:S(2)}, u32[]{:S(2)}) async-start(bf16[16,400,128]{2,1,0:T(8,128)(2,1)} %get-tuple-element.24), calls=%async_computation.2 | async-start | bytes 3276800 | tf_op jit(solution)/shard_map/all_to_all | solution.py:275
  133.8 54.9 %all-to-all-start.3 = ((bf16[16,128,256]{2,1,0:T(8,128)(2,1)}), bf16[16,128,256]{2,1,0:T(8,128)(2,1)}, u32[]{:S(2)}, u32[]{:S(2)}) async-start(bf16[16,128,256]{2,1,0:T(8,128)(2,1)} %shard_map.126), calls=%async_computation.3 | async-start | bytes 2097152 | tf_op jit(solution)/shard_map/all_to_all | solution.py:275
  183.4 8.3 %collective-permute-start = (bf16[64,2048]{1,0:T(8,128)(2,1)}, bf16[64,2048]{1,0:T(8,128)(2,1)}, u32[]{:S(2)}, u32[]{:S(2)}) collective-permute-start(bf16[64,2048]{1,0:T(8,128)(2,1)} %slice_bitcast_fusion), channel_id=1, source_target_pairs={{0,128},{16,144},{32,160},{48,176},{64,192},{80,208},{96,224},{112... | collective-permute-start | bytes 786440 | tf_op jit(solution)/shard_map/ppermute | solution.py:388
Sparse Core Ops, SparseCore 0:
  101.9 79.7 reduce-scatter.1

commit v4 on v3

v4 whole, which is shorter than its diff:
```python
import functools
import math

import jax
import jax.numpy as jnp
from jax import lax
from jax.experimental import pallas as pl
from jax.experimental.pallas import tpu as pltpu
from jax.sharding import PartitionSpec as P

MODEL_WIDTH = 8192
DIAGONAL_BLOCKS = 32
HBS = 1024
HB = 16
BS = 256
EB = 32
PEERS = 16
PAIR = 2 * EB
LANES = 128
STATS = 16
STEP = 256
LATE = 1000
VMEM = 58 * 1024 * 1024
ROOM = 3407872

epsilon = 1e-05
root_scale = math.sqrt(2.0 / math.pi)
cubic_term = 0.044715

F32 = jnp.float32
BF16 = jnp.bfloat16

NN = (((1,), (0,)), ((), ()))
NT = (((1,), (1,)), ((), ()))
TN = (((0,), (0,)), ((), ()))
TT = (((0,), (1,)), ((), ()))


def dot(a, b, dims):
    return lax.dot_general(a, b, dims, preferred_element_type=F32)


def call(kernel, out_shape, args, scratch=(), flops=0, **extra):
    outs = out_shape if isinstance(out_shape, (list, tuple)) else [out_shape]
    moved = sum(a.size * a.dtype.itemsize for a in args) + sum(
        math.prod(o.shape) * o.dtype.itemsize for o in outs
    )
    return pl.pallas_call(
        kernel,
        out_shape=out_shape,
        in_specs=[pl.BlockSpec(memory_space=pltpu.VMEM)] * len(args),
        out_specs=jax.tree.map(lambda _: pl.BlockSpec(memory_space=pltpu.VMEM), out_shape),
        scratch_shapes=list(scratch),
        compiler_params=pltpu.CompilerParams(vmem_limit_bytes=VMEM),
        cost_estimate=pl.CostEstimate(flops=int(flops), bytes_accessed=int(moved), transcendentals=0),
        **extra,
    )(*args)


def stat_rows(value, chunks):
    high = value.astype(BF16).astype(F32)
    low = value - high
    rows = []
    for i in range(chunks):
        part = slice(i * LANES, (i + 1) * LANES)
        rows += [high[:, part], low[:, part]]
    rows.append(jnp.zeros((STATS - 2 * chunks, LANES), F32))
    return jnp.concatenate(rows, axis=0).astype(BF16)


def stat_sum(rows):
    return jnp.sum(rows.astype(F32), axis=0)


def head_kernel(
    x_hbm, cot_hbm, gain_ref, w1_hbm, w4_hbm, out_hbm, x_ref, cot_ref, w1_ref, w4_ref, out_ref, in_sems, out_sems
):
    steps = x_ref.shape[0] // STEP
    rows = steps * 2 * PAIR
    loads, stores = [], []
    weights = [
        pltpu.make_async_copy(source, target, in_sems.at[2 * steps + k])
        for k, (source, target) in enumerate(((w1_hbm, w1_ref), (w4_hbm, w4_ref)))
    ]
    weights[0].start()
    for i in range(steps):
        part = pl.ds(i * STEP, STEP)
        for k, (source, target) in enumerate(((x_hbm, x_ref), (cot_hbm, cot_ref))):
            loads.append(pltpu.make_async_copy(source.at[part], target.at[part], in_sems.at[2 * i + k]))
    loads[0].start()

    def store(base, size):
        part = pl.ds(base, size)
        copy = pltpu.make_async_copy(out_ref.at[:, part], out_hbm.at[:, part], out_sems.at[len(stores)])
        copy.start()
        stores.append(copy)

    weights[0].wait()
    weights[1].start()
    for copy in loads[1:]:
        copy.start()
    turned = [w1_ref[a].T for a in range(2)]
    totals = []
    for i in range(steps):
        part = slice(i * STEP, (i + 1) * STEP)
        loads[2 * i].wait()
        x = x_ref[part, :].astype(F32)
        scaled = (x * gain_ref[...]).astype(BF16)
        base = i * 2 * PAIR
        for a in range(2):
            first = dot(turned[a], scaled[:, a * BS : (a + 1) * BS], NT).astype(BF16)
            for k in range(2):
                start = base + k * PAIR + a * EB
                value = first[:, k * LANES : (k + 1) * LANES]
                out_ref[:, start : start + EB, :] = value.reshape(PEERS, EB, LANES)
        store(base, 2 * PAIR)
        loads[2 * i + 1].wait()
        if i == 0:
            weights[1].wait()
        for a in range(2):
            dgathered = dot(w4_ref[a], cot_ref[part, a * BS : (a + 1) * BS], NT).astype(BF16)
            for k in range(2):
                start = rows + base + k * PAIR + a * EB
                value = dgathered[:, k * LANES : (k + 1) * LANES]
                out_ref[:, start : start + EB, :] = value.reshape(PEERS, EB, LANES)
        store(rows + base, 2 * PAIR)
        squares = x * x
        folded = squares[:, :LANES]
        for k in range(1, squares.shape[1] // LANES):
            folded = folded + squares[:, k * LANES : (k + 1) * LANES]
        totals.append(jnp.sum(folded.T, axis=0, keepdims=True))
    stats = stat_rows(jnp.concatenate(totals, axis=1), 2 * steps)
    out_ref[:, 2 * rows :, :] = jnp.broadcast_to(stats[None], (PEERS, STATS, LANES))
    store(2 * rows, STATS)
    for copy in stores:
        copy.wait()


def reciprocal(stats, i):
    rows = stats[4 * i : 4 * i + 4]
    total = jnp.concatenate([rows[0:1] + rows[1:2], rows[2:3] + rows[3:4]], axis=1)
    return lax.rsqrt(total / MODEL_WIDTH + epsilon)


def hidden_rows(ref):
    sources, rows, _ = ref.shape
    parts = [
        ref[:, i * PAIR : (i + 1) * PAIR, :].reshape(sources * PAIR, LANES) for i in range(rows // PAIR)
    ]
    return jnp.concatenate(parts, axis=1)


def turn_kernel(w2_ref, w3_ref, w2t_ref, w3t_ref):
    w2t_ref[...] = w2_ref[0].T
    w3t_ref[...] = w3_ref[0].T


def by_peer(value):
    parts = [value[:, k * LANES : (k + 1) * LANES].reshape(PEERS, PAIR, LANES) for k in range(2)]
    return jnp.concatenate(parts, axis=1)


def middle_kernel(
    recv_hbm, w2t_hbm, w3t_hbm, w2_hbm, w3_hbm, act_hbm, scaled_hbm, out_hbm,
    recv_ref, w2t_ref, w3t_ref, w2_ref, w3_ref, pre_ref, act_ref, dpre_ref, scaled_ref, out_ref, in_sems, out_sems,
):
    steps = act_ref.shape[0]
    rows = steps * 2 * PAIR
    loads, stores = {}, []

    def load(key, source, target):
        copy = pltpu.make_async_copy(source, target, in_sems.at[len(loads)])
        copy.start()
        loads[key] = copy

    def load_rows(base, size):
        part = pl.ds(base, size)
        load(base, recv_hbm.at[:, part], recv_ref.at[:, part])

    def store(source, target):
        copy = pltpu.make_async_copy(source, target, out_sems.at[len(stores)])
        copy.start()
        stores.append(copy)

    def peer_rows(base):
        return hidden_rows(recv_ref.at[:, pl.ds(base, 2 * PAIR)])

    def send_rows(base, value):
        out_ref[:, base : base + 2 * PAIR, :] = by_peer(value.astype(BF16))
        part = pl.ds(base, 2 * PAIR)
        store(out_ref.at[:, part], out_hbm.at[:, part])

    load_rows(2 * rows, STATS)
    load_rows(0, 2 * PAIR)
    load("w2t", w2t_hbm, w2t_ref)
    for i in range(1, steps):
        load_rows(i * 2 * PAIR, 2 * PAIR)
    load("w3", w3_hbm, w3_ref)
    for i in range(steps):
        load_rows(rows + i * 2 * PAIR, 2 * PAIR)
    load("w3t", w3t_hbm, w3t_ref)
    load("w2", w2_hbm, w2_ref)
    loads[2 * rows].wait()
    stats = stat_sum(recv_ref[:, 2 * rows :, :])
    inverses = [reciprocal(stats, i) for i in range(steps)]
    loads["w2t"].wait()
    for i in range(steps):
        loads[i * 2 * PAIR].wait()
        pre_ref[i] = dot(w2t_ref[...], peer_rows(i * 2 * PAIR), NN) * inverses[i]
    loads["w3"].wait()
    for i in range(steps):
        loads[rows + i * 2 * PAIR].wait()
    inner = []
    for i in range(steps):
        dact = dot(w3_ref[0], peer_rows(rows + i * 2 * PAIR), NN)
        pre = pre_ref[i]
        square = pre * pre
        hyper = jnp.tanh(pre * (root_scale + (root_scale * cubic_term) * square))
        half = 0.5 * pre
        act_ref[i] = (half + half * hyper).astype(BF16)
        slope = (0.5 + 0.5 * hyper) + half * (1.0 - hyper * hyper) * (
            root_scale + (3.0 * root_scale * cubic_term) * square
        )
        dpre = dact * slope
        inner.append(jnp.sum(dpre * pre, axis=0, keepdims=True))
        dpre_ref[i] = dpre.astype(BF16)
        scaled_ref[i] = (dpre * inverses[i]).astype(BF16)
    store(act_ref, act_hbm)
    store(scaled_ref, scaled_hbm)
    loads["w3t"].wait()
    for i in range(steps):
        send_rows(i * 2 * PAIR, dot(w3t_ref[...], act_ref[i], NN))
    loads["w2"].wait()
    for i in range(steps):
        send_rows(rows + i * 2 * PAIR, dot(w2_ref[0], dpre_ref[i], NN))
    rest = stat_rows(jnp.concatenate(inner, axis=1), 2 * steps)
    out_ref[:, 2 * rows :, :] = jnp.broadcast_to(rest[None], (PEERS, STATS, LANES))
    part = pl.ds(2 * rows, STATS)
    store(out_ref.at[:, part], out_hbm.at[:, part])
    for copy in stores:
        copy.wait()


def hidden_grads_kernel(y_ref, mixed_ref, dthird_ref, act_ref, scaled_ref, out_ref, turned_ref):
    del y_ref

    @pl.when(pl.program_id(0) == 0)
    def _():
        turned_ref[...] = hidden_rows(dthird_ref)

    shape = (out_ref.shape[0], out_ref.shape[2], HBS)
    scaled = jnp.concatenate([scaled_ref[i] for i in range(scaled_ref.shape[0])], axis=1)
    act = jnp.concatenate([act_ref[i] for i in range(act_ref.shape[0])], axis=1)
    second = dot(hidden_rows(mixed_ref), scaled, NT).astype(BF16)
    out_ref[:, 0, :, :HBS] = second.reshape(shape)
    third = dot(act, turned_ref[...], NT).astype(BF16)
    out_ref[:, 0, :, HBS:] = third.reshape(shape)


def model_rows(ref, chunks, a, offset):
    parts = []
    for i in range(chunks):
        start = offset + i * PAIR + a * EB
        parts.append(ref[:, start : start + EB, :].reshape(HB * EB, LANES))
    return jnp.concatenate(parts, axis=1)


def columns(stats, chunks):
    turned = stats.T
    parts = [turned[:, 2 * i : 2 * i + 1] + turned[:, 2 * i + 1 : 2 * i + 2] for i in range(chunks)]
    return jnp.concatenate(parts, axis=0)


def norm_kernel(x_ref, gain_ref, stats_ref, normed_ref):
    chunks = x_ref.shape[0] // LANES
    inverse = lax.rsqrt(columns(stat_sum(stats_ref[...]), chunks) / MODEL_WIDTH + epsilon)
    normed_ref[...] = (x_ref[...].astype(F32) * inverse * gain_ref[...]).astype(BF16)


def output_kernel(recv_ref, x_ref, w4_ref, out_ref):
    chunks = x_ref.shape[0] // LANES
    for a in range(2):
        feats = slice(a * BS, (a + 1) * BS)
        gathered = model_rows(recv_ref, chunks, a, 0)
        branch = dot(gathered, w4_ref[a], TN)
        out_ref[:, feats] = (x_ref[:, feats].astype(F32) + branch).astype(BF16)


def model_grads_kernel(
    recv_hbm, normed_hbm, cot_hbm, out_hbm, recv_ref, normed_ref, cot_ref, out_ref, sems, out_sems
):
    chunks = normed_ref.shape[0] // LANES
    rows = chunks * PAIR
    loads = []
    for source, target in (
        (recv_hbm.at[:, pl.ds(rows, rows)], recv_ref.at[:, pl.ds(rows, rows)]),
        (normed_hbm, normed_ref),
        (recv_hbm.at[:, pl.ds(0, rows)], recv_ref.at[:, pl.ds(0, rows)]),
        (cot_hbm, cot_ref),
    ):
        loads.append(pltpu.make_async_copy(source, target, sems.at[len(loads)]))
        loads[-1].start()
    first_rows, fourth_rows = BS // PEERS, HB * EB // PEERS
    stores = []

    def store(k):
        part = pl.ds(k * 4 * first_rows, 4 * first_rows)
        copy = pltpu.make_async_copy(out_ref.at[:, part], out_hbm.at[:, part], out_sems.at[k])
        copy.start()
        stores.append(copy)

    loads[0].wait()
    loads[1].wait()
    for a in range(2):
        dfirst = model_rows(recv_ref, chunks, a, rows)
        grad = dot(dfirst, normed_ref[:, a * BS : (a + 1) * BS], NN).astype(BF16).T
        for half in range(2):
            part = grad[:, half * BS : (half + 1) * BS]
            base = (2 * a + half) * first_rows
            out_ref[:, base : base + first_rows, :] = part.reshape(PEERS, first_rows, BS)
    store(0)
    loads[2].wait()
    loads[3].wait()
    for a in range(2):
        gathered = model_rows(recv_ref, chunks, a, 0)
        grad = dot(gathered, cot_ref[:, a * BS : (a + 1) * BS], NN).astype(BF16)
        base = 4 * first_rows + a * fourth_rows
        out_ref[:, base : base + fourth_rows, :] = grad.reshape(PEERS, fourth_rows, BS)
    store(1)
    for copy in stores:
        copy.wait()


def token_kernel(recv_ref, stats_ref, x_ref, gain_ref, w1_ref, cot_ref, out_ref):
    chunks = x_ref.shape[0] // LANES
    inverse = lax.rsqrt(columns(stat_sum(stats_ref[...]), chunks) / MODEL_WIDTH + epsilon)
    inner = columns(stat_sum(recv_ref[:, 2 * chunks * PAIR :, :]), chunks) / MODEL_WIDTH
    for a in range(2):
        feats = slice(a * BS, (a + 1) * BS)
        dfirst = model_rows(recv_ref, chunks, a, chunks * PAIR)
        dnormed = dot(dfirst, w1_ref[a], TT)
        xhat = x_ref[:, feats].astype(F32) * inverse
        change = dnormed * gain_ref[:, feats] - xhat * inner
        out_ref[:, feats] = (cot_ref[:, feats].astype(F32) + inverse * change).astype(BF16)


def sum_kernel(scale, recv_ref, first_ref, fourth_ref):
    total = jnp.sum(recv_ref[...].astype(F32), axis=0) * scale
    _, rows, _ = first_ref.shape
    for a in range(2):
        for half in range(2):
            base = (2 * a + half) * rows
            first_ref[a, :, half * BS : (half + 1) * BS] = total[base : base + rows]
    fourth_ref[...] = total[4 * rows :].reshape(fourth_ref.shape)


def finish_kernel(scale, own_ref, other_ref, second_ref, third_ref):
    total = (own_ref[0, 0].astype(F32) + other_ref[...].astype(F32)) * scale
    second_ref[0] = total[:, :HBS]
    third_ref[0] = total[:, HBS:]


def shards(tokens, gain, w_first, w_second, w_third, w_fourth, cotangent):
    element_count, local_width = tokens.shape
    dp = lax.axis_size("dp")
    scale = 1.0 / math.sqrt(element_count * dp)
    gain_row = gain[None, :]
    z_size = dp // 2
    z_groups = [[y * z_size + z for z in range(z_size)] for y in range(2)]
    y_pairs = [(i, (i + z_size) % dp) for i in range(dp)]
    y_index = (lax.axis_index("dp") // z_size).astype(jnp.int32)[None]
    shape = jax.ShapeDtypeStruct
    hidden_flops = 2 * HBS * HBS * element_count
    model_flops = 2 * local_width * HB * EB * element_count
    steps = element_count // STEP
    rows = steps * 2 * PAIR
    sent = shape((PEERS, 2 * rows + STATS, LANES), BF16)
    stepped = shape((steps, HBS, STEP), BF16)
    hbm = pl.BlockSpec(memory_space=pltpu.HBM)
    vmem = pl.BlockSpec(memory_space=pltpu.VMEM)
    params = pltpu.CompilerParams(vmem_limit_bytes=VMEM)
    beside = pltpu.CompilerParams(vmem_limit_bytes=VMEM - ROOM)

    def cost(flops):
        return pl.CostEstimate(flops=int(flops), bytes_accessed=8 << 20, transcendentals=0)

    def whole(*dims):
        return pl.BlockSpec(dims, lambda i, *_: (0,) * len(dims))

    send = pl.pallas_call(
        head_kernel,
        out_shape=sent,
        in_specs=[hbm, hbm, vmem, hbm, hbm],
        out_specs=hbm,
        scratch_shapes=[
            pltpu.VMEM(tokens.shape, BF16),
            pltpu.VMEM(tokens.shape, BF16),
            pltpu.VMEM(w_first.shape, BF16),
            pltpu.VMEM(w_fourth.shape, BF16),
            pltpu.VMEM(sent.shape, BF16),
            pltpu.SemaphoreType.DMA((2 * steps + 2,)),
            pltpu.SemaphoreType.DMA((2 * steps + 1,)),
        ],
        compiler_params=params,
        cost_estimate=cost(2 * model_flops),
    )(tokens, cotangent, gain_row, w_first, w_fourth)
    recv = lax.all_to_all(send, "tensor", 0, 0, tiled=True)
    turned = shape((HBS, HBS), BF16)
    w_second_t, w_third_t = call(turn_kernel, [turned, turned], (w_second, w_third))
    act, scaled, send = pl.pallas_call(
        middle_kernel,
        out_shape=[stepped, stepped, sent],
        in_specs=[hbm] * 5,
        out_specs=[hbm, hbm, hbm],
        scratch_shapes=[
            pltpu.VMEM(sent.shape, BF16),
            pltpu.VMEM(turned.shape, BF16),
            pltpu.VMEM(turned.shape, BF16),
            pltpu.VMEM(w_second.shape, BF16),
            pltpu.VMEM(w_third.shape, BF16),
            pltpu.VMEM(stepped.shape, F32),
            pltpu.VMEM(stepped.shape, BF16),
            pltpu.VMEM(stepped.shape, BF16),
            pltpu.VMEM(stepped.shape, BF16),
            pltpu.VMEM(sent.shape, BF16),
            pltpu.SemaphoreType.DMA((2 * steps + 5,)),
            pltpu.SemaphoreType.DMA((2 * steps + 3,)),
        ],
        compiler_params=beside,
        cost_estimate=cost(4 * hidden_flops),
    )(recv, w_second_t, w_third_t, w_second, w_third)
    back = lax.all_to_all(send, "tensor", 0, 0, tiled=True)
    quarter = z_size // 2
    hidden = pl.pallas_call(
        hidden_grads_kernel,
        out_shape=shape((z_size, 2, HBS // dp, 2 * HBS), BF16),
        grid_spec=pltpu.PrefetchScalarGridSpec(
            num_scalar_prefetch=1,
            grid=(4,),
            in_specs=[
                pl.BlockSpec((PEERS // 4, rows, LANES), lambda i, y: (i, 0, 0)),
                pl.BlockSpec((PEERS, rows, LANES), lambda i, y: (0, 1, 0)),
                pl.BlockSpec((steps, HBS // 4, STEP), lambda i, y: (0, i, 0)),
                whole(steps, HBS, STEP),
            ],
            out_specs=pl.BlockSpec(
                (quarter, 1, HBS // dp, 2 * HBS), lambda i, y: (i % 2, (i // 2 + y[0]) % 2, 0, 0)
            ),
            scratch_shapes=[pltpu.VMEM((HBS, element_count), BF16)],
        ),
        compiler_params=params,
        cost_estimate=cost(2 * hidden_flops),
    )(y_index, recv, recv, act, scaled)
    hidden = lax.psum_scatter(hidden, "dp", scatter_dimension=0, axis_index_groups=z_groups, tiled=True)

    stats_spec = pl.BlockSpec((PEERS, STATS, LANES), lambda i: (0, 2 * rows // STATS, 0))
    normed = pl.pallas_call(
        norm_kernel,
        out_shape=shape(tokens.shape, BF16),
        grid=(1,),
        in_specs=[whole(*tokens.shape), whole(1, local_width), stats_spec],
        out_specs=whole(*tokens.shape),
        compiler_params=params,
        cost_estimate=cost(model_flops),
    )(tokens, gain_row, recv)
    both = shape((PEERS, 2 * PAIR, BS), BF16)
    both = pl.pallas_call(
        model_grads_kernel,
        out_shape=both,
        in_specs=[hbm, hbm, hbm],
        out_specs=hbm,
        scratch_shapes=[
            pltpu.VMEM((PEERS, 2 * rows, LANES), BF16),
            pltpu.VMEM(tokens.shape, BF16),
            pltpu.VMEM(tokens.shape, BF16),
            pltpu.VMEM(both.shape, BF16),
            pltpu.SemaphoreType.DMA((4,)),
            pltpu.SemaphoreType.DMA((2,)),
        ],
        compiler_params=beside,
        cost_estimate=cost(2 * model_flops),
    )(back, normed, cotangent)
    both = lax.all_to_all(both, "dp", 0, 0, tiled=True)
    output = call(output_kernel, shape(tokens.shape, BF16), (back, tokens, w_fourth), flops=LATE * model_flops)
    token_gradient = pl.pallas_call(
        token_kernel,
        out_shape=shape(tokens.shape, BF16),
        grid=(1,),
        in_specs=[
            whole(*sent.shape),
            stats_spec,
            whole(*tokens.shape),
            whole(1, local_width),
            whole(*w_first.shape),
            whole(*tokens.shape),
        ],
        out_specs=whole(*tokens.shape),
        compiler_params=params,
        cost_estimate=cost(LATE * model_flops),
    )(back, recv, tokens, gain_row, w_first, cotangent)
    grad_first, grad_fourth = call(
        functools.partial(sum_kernel, scale),
        [shape((2, BS // dp, HB * EB), F32), shape((2, HB * EB // dp, BS), F32)],
        (both,),
    )
    other = lax.ppermute(hidden[0, 1], "dp", y_pairs)
    part = shape((1, HBS // dp, HBS), F32)
    grad_second, grad_third = call(functools.partial(finish_kernel, scale), [part, part], (hidden, other))
    return output, token_gradient, grad_first, grad_second, grad_third, grad_fourth


def solution(mesh):
    return jax.shard_map(
        shards,
        mesh=mesh,
        in_specs=(
            P("dp", "tensor"),
            P("tensor"),
            P("tensor", None, None),
            P("tensor", None, None),
            P("tensor", None, None),
            P("tensor", None, None),
            P("dp", "tensor"),
        ),
        out_specs=(
            P("dp", "tensor"),
            P("dp", "tensor"),
            P("tensor", "dp", None),
            P("tensor", "dp", None),
            P("tensor", "dp", None),
            P("tensor", "dp", None),
        ),
        check_vma=False,
    )
```

time: 201 us -> 194 us (0.965)
  waiting for transfers between devices: 83.1 us -> 91.6 us
  Pallas kernels: 60.7 us -> 52.5 us
  starting transfers between devices: 37.7 us -> 30.5 us
    all_to_all x4 -> x3, waiting for transfers between devices: 43.6 us -> 59.3 us  [the longest x1 32.6 us: shards(): recv = lax.all_to_all(send, 'tensor', 0, 0, tiled=True)]
    pallas_call x8 -> x4, Pallas kernels: 25.4 us -> 12.6 us  [call(): pl.pallas_call(kernel, out_shape=out_shape, in_specs=[pl.BlockSpec(memory...]
    all_to_all x4 -> x3, starting transfers between devices: 36.7 us -> 29.6 us  [the longest x1 13 us: shards(): back = lax.all_to_all(send, 'tensor', 0, 0, tiled=True)]
    reduce_scatter x1, waiting for transfers between devices: 38.5 us -> 32.2 us  [shards(): lax.psum_scatter(hidden, 'dp', scatter_dimension=0, axis_index_groups=z_g...]
    pallas_call x3 -> x5, Pallas kernels: 27.2 us -> 31.7 us  [the longest x1 15.1 us: shards(): pl.pallas_call(middle_kernel, out_shape=[stepped, stepped, sent], in_spec...]
  transfers between devices with their start and end apart: 6 -> 5, of which waited for: 4 -> 4; matrix products, arithmetic and copies ran while one was open for 2% -> 1% of each run, Pallas kernels for 22% -> 15%
where the time goes in v4:
time: 194 us
  waiting for transfers between devices  91.6 us (47%)
  Pallas kernels  52.5 us (27%)
  starting transfers between devices  30.5 us (16%)
  between operations  14.1 us (7%)
  local copies, waits for them, and re-layouts  5.12 us (3%)
    all_to_all x1, waiting for transfers between devices, shards(): recv = lax.all_to_all(send, 'tensor', 0, 0, tiled=True)  32.6 us
    reduce_scatter x1, waiting for transfers between devices, shards(): lax.psum_scatter(hidden, 'dp', scatter_dimension=0, axis_index_groups=z_g...  32.2 us
    all_to_all x1, waiting for transfers between devices, shards(): back = lax.all_to_all(send, 'tensor', 0, 0, tiled=True)  26.7 us
    pallas_call x1, Pallas kernels, shards(): pl.pallas_call(middle_kernel, out_shape=[stepped, stepped, sent], in_spec...  15.1 us
    all_to_all x1, starting transfers between devices, shards(): back = lax.all_to_all(send, 'tensor', 0, 0, tiled=True)  13 us
    pallas_call x4, Pallas kernels, call(): pl.pallas_call(kernel, out_shape=out_shape, in_specs=[pl.BlockSpec(memory...  12.6 us
    all_to_all x1, starting transfers between devices, shards(): both = lax.all_to_all(both, 'dp', 0, 0, tiled=True)  9.3 us
    pallas_call x1, Pallas kernels, shards(): pl.pallas_call(hidden_grads_kernel, out_shape=shape((z_size, 2, HBS // dp...  8.12 us
  transfers between devices with their start and end apart: 5, of which 4 were waited for; matrix products, arithmetic and copies ran while one was open for 1% of the time, Pallas kernels for 15%

profile of v4, /device:TPU:18, one launch (start us, length us, event | category | flops | bytes accessed | tf_op | source)
XLA Modules:
  0.0 193.9 jit_solution(499957156146698265)
XLA Ops:
  7.2 5.5 %shard_map.118 = bf16[16,784,128]{2,1,0:T(8,128)(2,1)} custom-call(bf16[768,512]{1,0:T(8,128)(2,1)} %x_ref.5, bf16[768,512]{1,0:T(8,128)(2,1)} %cot_hbm.3, f32[1,512]{1,0:T(1,128)} %bitcast.4, bf16[2,256,512]{2,1,0:T(8,128)(2,1)} %w1_ref.1, bf16[2,512,256]{2,1,0:T(8,128)(2,1)} %w4_ref.1), custom_call_target="tpu_custom_call" | custom-call | flops 805306368 | bytes 8388608 | tf_op jit(solution)/shard_map/pallas_call | solution.py:390
  12.7 7.3 %all-to-all-start = ((bf16[16,784,128]{2,1,0:T(8,128)(2,1)}), bf16[16,784,128]{2,1,0:T(8,128)(2,1)S(1)}, u32[]{:S(2)}, u32[]{:S(2)}) async-start(bf16[16,784,128]{2,1,0:T(8,128)(2,1)} %shard_map.118), calls=%async_computation | async-start | bytes 6422528 | tf_op jit(solution)/shard_map/all_to_all | solution.py:407
  20.0 4.9 %shard_map.119 = (bf16[1024,1024]{1,0:T(8,128)(2,1)}, bf16[1024,1024]{1,0:T(8,128)(2,1)}) custom-call(bf16[1,1024,1024]{2,1,0:T(8,128)(2,1)} %w2_hbm.1, bf16[1,1024,1024]{2,1,0:T(8,128)(2,1)} %w3_hbm.1), custom_call_target="tpu_custom_call" | custom-call | bytes 8388608 | tf_op jit(solution)/shard_map/pallas_call | solution.py:48
  24.9 32.6 %all-to-all-done.recv_hbm.stats_ref.mixed_ref.dthird_ref = bf16[16,784,128]{2,1,0:T(8,128)(2,1)S(1)} async-done(((bf16[16,784,128]{2,1,0:T(8,128)(2,1)}), bf16[16,784,128]{2,1,0:T(8,128)(2,1)S(1)}, u32[]{:S(2)}, u32[]{:S(2)}) %all-to-all-start) | async-done | bytes 3211296 | tf_op jit(solution)/shard_map/all_to_all | solution.py:407
  57.4 0.0 copy-start
  57.4 1.7 copy-done
  59.1 15.1 %shard_map.120 = (bf16[3,1024,256]{2,1,0:T(8,128)(2,1)}, bf16[3,1024,256]{2,1,0:T(8,128)(2,1)}, bf16[16,784,128]{2,1,0:T(8,128)(2,1)}) custom-call(bf16[16,784,128]{2,1,0:T(8,128)(2,1)} %copy-done, bf16[1024,1024]{1,0:T(8,128)(2,1)} %get-tuple-element.15.w2t_hbm, bf16[1024,1024]{1,0:T(8,128)(2,1)} %get-tuple-element.16.w3t_hbm, ...), custom_call_target="tpu_custom_call" | custom-call | flops 6442450944 | bytes 8388608 | tf_op jit(solution)/shard_map/pallas_call | solution.py:410
  74.2 13.0 %all-to-all-start.1 = ((bf16[16,784,128]{2,1,0:T(8,128)(2,1)}), bf16[16,784,128]{2,1,0:T(8,128)(2,1)S(1)}, u32[]{:S(2)}, u32[]{:S(2)}) async-start(bf16[16,784,128]{2,1,0:T(8,128)(2,1)} %get-tuple-element.17), calls=%async_computation.1 | async-start | bytes 6422528 | tf_op jit(solution)/shard_map/all_to_all | solution.py:432
  87.2 0.0 reduce-scatter.2.cloned.1.call-start
  87.3 8.1 %shard_map.126 = bf16[8,2,64,2048]{3,2,1,0:T(8,128)(2,1)} custom-call(s32[1]{0:T(128)} %bitcast.1.y_ref, bf16[16,784,128]{2,1,0:T(8,128)(2,1)} %copy-done, bf16[16,784,128]{2,1,0:T(8,128)(2,1)} %copy-done, bf16[3,1024,256]{2,1,0:T(8,128)(2,1)} %get-tuple-element.19.act_ref, bf16[3,1024,256]{2,1,0:T(8,128)(2,1)} %get-tuple-element.20.scaled_ref), custom_call_target="tpu_custom_call" | custom-call | flops 3221225472 | bytes 8388608 | tf_op jit(solution)/shard_map/pallas_call | solution.py:434
  95.4 0.0 reduce-scatter.2.cloned.1.call-update
  95.4 2.5 %shard_map.123.normed_hbm = bf16[768,512]{1,0:T(8,128)(2,1)} custom-call(bf16[768,512]{1,0:T(8,128)(2,1)} %x_ref.5, f32[1,512]{1,0:T(1,128)} %bitcast.5, bf16[16,784,128]{2,1,0:T(8,128)(2,1)} %copy-done), custom_call_target="tpu_custom_call" | custom-call | flops 402653184 | bytes 8388608 | tf_op jit(solution)/shard_map/pallas_call | solution.py:457
  97.9 26.7 %all-to-all-done.1.recv_ref.recv_hbm = bf16[16,784,128]{2,1,0:T(8,128)(2,1)S(1)} async-done(((bf16[16,784,128]{2,1,0:T(8,128)(2,1)}), bf16[16,784,128]{2,1,0:T(8,128)(2,1)S(1)}, u32[]{:S(2)}, u32[]{:S(2)}) %all-to-all-start.1) | async-done | bytes 3211296 | tf_op jit(solution)/shard_map/all_to_all | solution.py:432
  124.7 0.0 copy-start.1
  124.7 1.8 copy-done.1
  126.5 3.8 %shard_map.124 = bf16[16,128,256]{2,1,0:T(8,128)(2,1)} custom-call(bf16[16,784,128]{2,1,0:T(8,128)(2,1)} %copy-done.1, bf16[768,512]{1,0:T(8,128)(2,1)} %shard_map.123.normed_hbm, bf16[768,512]{1,0:T(8,128)(2,1)} %cot_hbm.3), custom_call_target="tpu_custom_call" | custom-call | flops 805306368 | bytes 8388608 | tf_op jit(solution)/shard_map/pallas_call | solution.py:467
  130.3 9.3 %all-to-all-start.2 = ((bf16[16,128,256]{2,1,0:T(8,128)(2,1)}), bf16[16,128,256]{2,1,0:T(8,128)(2,1)}, u32[]{:S(2)}, u32[]{:S(2)}) async-start(bf16[16,128,256]{2,1,0:T(8,128)(2,1)} %shard_map.124), calls=%async_computation.2 | async-start | bytes 2097152 | tf_op jit(solution)/shard_map/all_to_all | solution.py:483
  139.6 3.8 %shard_map.121 = bf16[768,512]{1,0:T(8,128)(2,1)} custom-call(bf16[16,784,128]{2,1,0:T(8,128)(2,1)} %copy-done.1, bf16[768,512]{1,0:T(8,128)(2,1)} %x_ref.5, bf16[2,512,256]{2,1,0:T(8,128)(2,1)} %w4_ref.1), custom_call_target="tpu_custom_call" | custom-call | flops 402653184000 | bytes 5308416 | tf_op jit(solution)/shard_map/pallas_call | solution.py:48
  143.4 32.2 %reduce-scatter.2.cloned.1.call-done.own_ref = bf16[1,2,64,2048]{3,2,1,0:T(8,128)(2,1)} async-done(((bf16[8,2,64,2048]{3,2,1,0:T(8,128)(2,1)}), bf16[1,2,64,2048]{3,2,1,0:T(8,128)(2,1)}) %reduce-scatter.2.cloned.1.call-update) | async-done | bytes 524304 | tf_op jit(solution)/shard_map/reduce_scatter | solution.py:454
  175.7 1.7 slice_bitcast_fusion
  177.3 0.9 collective-permute-start
  178.2 4.8 %shard_map.122 = bf16[768,512]{1,0:T(8,128)(2,1)} custom-call(bf16[16,784,128]{2,1,0:T(8,128)(2,1)} %copy-done.1, bf16[16,784,128]{2,1,0:T(8,128)(2,1)} %copy-done, bf16[768,512]{1,0:T(8,128)(2,1)} %x_ref.5, f32[1,512]{1,0:T(1,128)} %bitcast.6, bf16[2,256,512]{2,1,0:T(8,128)(2,1)} %w1_ref.1, bf16[768,512]{1,0:T(8,128)(2,1)} %cot_hbm.3), custom_call_target="tpu_custom_call" | custom-call | flops 402653184000 | bytes 8388608 | tf_op jit(solution)/shard_map/pallas_call | solution.py:485
  183.0 0.0 all-to-all-done.2.recv_ref
  183.0 2.0 %shard_map.125 = (f32[2,16,512]{2,1,0:T(8,128)}, f32[2,32,256]{2,1,0:T(8,128)}) custom-call(bf16[16,128,256]{2,1,0:T(8,128)(2,1)} %all-to-all-done.2.recv_ref), custom_call_target="tpu_custom_call" | custom-call | bytes 1179648 | tf_op jit(solution)/shard_map/pallas_call | solution.py:48
  185.0 0.1 collective-permute-done.other_ref
  185.1 1.9 shard_map.127
Async XLA Ops:
  12.7 44.7 %all-to-all-start = ((bf16[16,784,128]{2,1,0:T(8,128)(2,1)}), bf16[16,784,128]{2,1,0:T(8,128)(2,1)S(1)}, u32[]{:S(2)}, u32[]{:S(2)}) async-start(bf16[16,784,128]{2,1,0:T(8,128)(2,1)} %shard_map.118), calls=%async_computation | async-start | bytes 6422528 | tf_op jit(solution)/shard_map/all_to_all | solution.py:407
  57.4 1.7 copy-start
  74.2 50.4 %all-to-all-start.1 = ((bf16[16,784,128]{2,1,0:T(8,128)(2,1)}), bf16[16,784,128]{2,1,0:T(8,128)(2,1)S(1)}, u32[]{:S(2)}, u32[]{:S(2)}) async-start(bf16[16,784,128]{2,1,0:T(8,128)(2,1)} %get-tuple-element.17), calls=%async_computation.1 | async-start | bytes 6422528 | tf_op jit(solution)/shard_map/all_to_all | solution.py:432
  87.2 88.4 %reduce-scatter.2.cloned.1.call-start = ((), (), s32[]{:S(2)}) async-start(), calls=%async_computation.4 | async-start | bytes 4718592 | tf_op jit(solution)/shard_map/reduce_scatter | solution.py:454
  124.7 1.8 copy-start.1
  130.3 52.7 %all-to-all-start.2 = ((bf16[16,128,256]{2,1,0:T(8,128)(2,1)}), bf16[16,128,256]{2,1,0:T(8,128)(2,1)}, u32[]{:S(2)}, u32[]{:S(2)}) async-start(bf16[16,128,256]{2,1,0:T(8,128)(2,1)} %shard_map.124), calls=%async_computation.2 | async-start | bytes 2097152 | tf_op jit(solution)/shard_map/all_to_all | solution.py:483
  177.3 7.8 %collective-permute-start = (bf16[64,2048]{1,0:T(8,128)(2,1)}, bf16[64,2048]{1,0:T(8,128)(2,1)}, u32[]{:S(2)}, u32[]{:S(2)}) collective-permute-start(bf16[64,2048]{1,0:T(8,128)(2,1)} %slice_bitcast_fusion), channel_id=1, source_target_pairs={{0,128},{16,144},{32,160},{48,176},{64,192},{80,208},{96,224},{112... | collective-permute-start | bytes 786440 | tf_op jit(solution)/shard_map/ppermute | solution.py:506
Sparse Core Ops, SparseCore 0:
  95.6 80.0 reduce-scatter.1

commit v5 on v4

v5 whole, which is shorter than its diff:
```python
import functools
import math

import jax
import jax.numpy as jnp
from jax import lax
from jax.experimental import pallas as pl
from jax.experimental.pallas import tpu as pltpu
from jax.sharding import PartitionSpec as P

MODEL_WIDTH = 8192
DIAGONAL_BLOCKS = 32
HBS = 1024
HB = 16
BS = 256
EB = 32
PEERS = 16
PAIR = 2 * EB
LANES = 128
STATS = 16
STEP = 256
LATE = 1000
VMEM = 58 * 1024 * 1024

epsilon = 1e-05
root_scale = math.sqrt(2.0 / math.pi)
cubic_term = 0.044715

F32 = jnp.float32
BF16 = jnp.bfloat16

NN = (((1,), (0,)), ((), ()))
NT = (((1,), (1,)), ((), ()))
TN = (((0,), (0,)), ((), ()))
TT = (((0,), (1,)), ((), ()))


def dot(a, b, dims):
    return lax.dot_general(a, b, dims, preferred_element_type=F32)


def call(kernel, out_shape, args, scratch=(), flops=0, **extra):
    outs = out_shape if isinstance(out_shape, (list, tuple)) else [out_shape]
    moved = sum(a.size * a.dtype.itemsize for a in args) + sum(
        math.prod(o.shape) * o.dtype.itemsize for o in outs
    )
    return pl.pallas_call(
        kernel,
        out_shape=out_shape,
        in_specs=[pl.BlockSpec(memory_space=pltpu.VMEM)] * len(args),
        out_specs=jax.tree.map(lambda _: pl.BlockSpec(memory_space=pltpu.VMEM), out_shape),
        scratch_shapes=list(scratch),
        compiler_params=pltpu.CompilerParams(vmem_limit_bytes=VMEM),
        cost_estimate=pl.CostEstimate(flops=int(flops), bytes_accessed=int(moved), transcendentals=0),
        **extra,
    )(*args)


def stat_rows(value, chunks):
    high = value.astype(BF16).astype(F32)
    low = value - high
    rows = []
    for i in range(chunks):
        part = slice(i * LANES, (i + 1) * LANES)
        rows += [high[:, part], low[:, part]]
    rows.append(jnp.zeros((STATS - 2 * chunks, LANES), F32))
    return jnp.concatenate(rows, axis=0).astype(BF16)


def stat_sum(rows):
    return jnp.sum(rows.astype(F32), axis=0)


def head_kernel(
    x_hbm, cot_hbm, gain_ref, w1_hbm, w4_hbm, out_hbm, x_ref, cot_ref, w1_ref, w4_ref, out_ref, in_sems, out_sems
):
    steps = x_ref.shape[0] // STEP
    rows = steps * 2 * PAIR
    loads, stores = [], []
    weights = [
        pltpu.make_async_copy(source, target, in_sems.at[2 * steps + k])
        for k, (source, target) in enumerate(((w1_hbm, w1_ref), (w4_hbm, w4_ref)))
    ]
    weights[0].start()
    for i in range(steps):
        part = pl.ds(i * STEP, STEP)
        for k, (source, target) in enumerate(((x_hbm, x_ref), (cot_hbm, cot_ref))):
            loads.append(pltpu.make_async_copy(source.at[part], target.at[part], in_sems.at[2 * i + k]))
    loads[0].start()

    def store(base, size):
        part = pl.ds(base, size)
        copy = pltpu.make_async_copy(out_ref.at[:, part], out_hbm.at[:, part], out_sems.at[len(stores)])
        copy.start()
        stores.append(copy)

    weights[0].wait()
    weights[1].start()
    for copy in loads[1:]:
        copy.start()
    turned = [w1_ref[a].T for a in range(2)]
    totals = []
    for i in range(steps):
        part = slice(i * STEP, (i + 1) * STEP)
        loads[2 * i].wait()
        x = x_ref[part, :].astype(F32)
        scaled = (x * gain_ref[...]).astype(BF16)
        base = i * 2 * PAIR
        for a in range(2):
            first = dot(turned[a], scaled[:, a * BS : (a + 1) * BS], NT).astype(BF16)
            for k in range(2):
                start = base + k * PAIR + a * EB
                value = first[:, k * LANES : (k + 1) * LANES]
                out_ref[:, start : start + EB, :] = value.reshape(PEERS, EB, LANES)
        store(base, 2 * PAIR)
        loads[2 * i + 1].wait()
        if i == 0:
            weights[1].wait()
        for a in range(2):
            dgathered = dot(w4_ref[a], cot_ref[part, a * BS : (a + 1) * BS], NT).astype(BF16)
            for k in range(2):
                start = rows + base + k * PAIR + a * EB
                value = dgathered[:, k * LANES : (k + 1) * LANES]
                out_ref[:, start : start + EB, :] = value.reshape(PEERS, EB, LANES)
        store(rows + base, 2 * PAIR)
        squares = x * x
        folded = squares[:, :LANES]
        for k in range(1, squares.shape[1] // LANES):
            folded = folded + squares[:, k * LANES : (k + 1) * LANES]
        totals.append(jnp.sum(folded.T, axis=0, keepdims=True))
    stats = stat_rows(jnp.concatenate(totals, axis=1), 2 * steps)
    out_ref[:, 2 * rows :, :] = jnp.broadcast_to(stats[None], (PEERS, STATS, LANES))
    store(2 * rows, STATS)
    for copy in stores:
        copy.wait()


def reciprocal(stats, i):
    rows = stats[4 * i : 4 * i + 4]
    total = jnp.concatenate([rows[0:1] + rows[1:2], rows[2:3] + rows[3:4]], axis=1)
    return lax.rsqrt(total / MODEL_WIDTH + epsilon)


def hidden_rows(ref):
    sources, rows, _ = ref.shape
    parts = [
        ref[:, i * PAIR : (i + 1) * PAIR, :].reshape(sources * PAIR, LANES) for i in range(rows // PAIR)
    ]
    return jnp.concatenate(parts, axis=1)


def turn_kernel(w2_ref, w3_ref, w2t_ref, w3t_ref):
    w2t_ref[...] = w2_ref[0].T
    w3t_ref[...] = w3_ref[0].T


def by_peer(value):
    parts = [value[:, k * LANES : (k + 1) * LANES].reshape(PEERS, PAIR, LANES) for k in range(2)]
    return jnp.concatenate(parts, axis=1)


class Copies:
    def __init__(self, sems):
        self.sems = sems
        self.started = []

    def start(self, source, target):
        copy = pltpu.make_async_copy(source, target, self.sems.at[len(self.started)])
        copy.start()
        self.started.append(copy)
        return copy

    def wait(self):
        for copy in self.started:
            copy.wait()


def forward_kernel(
    recv_hbm, w2t_hbm, w3t_hbm, pre_hbm, act_hbm, out_hbm,
    recv_ref, w2t_ref, w3t_ref, pre_ref, act_ref, out_ref, in_sems, out_sems,
):
    steps = act_ref.shape[0]
    rows = steps * 2 * PAIR
    loads, stores = Copies(in_sems), Copies(out_sems)
    parts = [pl.ds(i * 2 * PAIR, 2 * PAIR) for i in range(steps)]
    rest = pl.ds(2 * rows, STATS)
    stats_load = loads.start(recv_hbm.at[:, rest], recv_ref.at[:, pl.ds(rows, STATS)])
    row_loads = [loads.start(recv_hbm.at[:, parts[0]], recv_ref.at[:, parts[0]])]
    w2t_load = loads.start(w2t_hbm, w2t_ref)
    for part in parts[1:]:
        row_loads.append(loads.start(recv_hbm.at[:, part], recv_ref.at[:, part]))
    w3t_load = loads.start(w3t_hbm, w3t_ref)
    stats_load.wait()
    stats = stat_sum(recv_ref[:, rows:, :])
    w2t_load.wait()
    for i in range(steps):
        row_loads[i].wait()
        pre = dot(w2t_ref[...], hidden_rows(recv_ref.at[:, parts[i]]), NN) * reciprocal(stats, i)
        pre_ref[i] = pre
        stores.start(pre_ref.at[i], pre_hbm.at[i])
        hyper = jnp.tanh(pre * (root_scale + (root_scale * cubic_term) * (pre * pre)))
        half = 0.5 * pre
        act_ref[i] = (half + half * hyper).astype(BF16)
    w3t_load.wait()
    for i in range(steps):
        third = dot(w3t_ref[...], act_ref[i], NN).astype(BF16)
        out_ref[:, i * 2 * PAIR : (i + 1) * 2 * PAIR, :] = by_peer(third)
        stores.start(out_ref.at[:, parts[i]], out_hbm.at[:, parts[i]])
    stores.start(act_ref, act_hbm)
    stores.wait()


def backward_kernel(
    y_ref, recv_hbm, pre_hbm, act_hbm, w3_hbm, grads_hbm, dpre_hbm, inner_ref,
    recv_ref, pre_ref, act_ref, w3_ref, dpre_ref, scaled_ref, grads_ref, in_sems, out_sems,
):
    steps = act_ref.shape[0]
    rows = steps * 2 * PAIR
    y = y_ref[0]
    loads, stores = Copies(in_sems), Copies(out_sems)

    def load_rows(base, size):
        part = pl.ds(base, size)
        return loads.start(recv_hbm.at[:, part], recv_ref.at[:, part])

    stats_load = load_rows(2 * rows, STATS)
    w3_load = loads.start(w3_hbm, w3_ref)
    third_loads = [load_rows(rows + i * 2 * PAIR, 2 * PAIR) for i in range(steps)]
    pre_loads = [loads.start(pre_hbm.at[i], pre_ref.at[i]) for i in range(steps)]
    act_load = loads.start(act_hbm, act_ref)
    mixed_load = load_rows(0, rows)
    stats_load.wait()
    stats = stat_sum(recv_ref[:, 2 * rows :, :])
    w3_load.wait()
    for i in range(steps):
        third_loads[i].wait()
        pre_loads[i].wait()
        dact = dot(w3_ref[0], hidden_rows(recv_ref.at[:, pl.ds(rows + i * 2 * PAIR, 2 * PAIR)]), NN)
        pre = pre_ref[i]
        square = pre * pre
        hyper = jnp.tanh(pre * (root_scale + (root_scale * cubic_term) * square))
        slope = (0.5 + 0.5 * hyper) + (0.5 * pre) * (1.0 - hyper * hyper) * (
            root_scale + (3.0 * root_scale * cubic_term) * square
        )
        dpre = dact * slope
        inner_ref[:, i * STEP : (i + 1) * STEP] = jnp.sum(dpre * pre, axis=0, keepdims=True)
        dpre_ref[i] = dpre.astype(BF16)
        scaled_ref[i] = (dpre * reciprocal(stats, i)).astype(BF16)
    act_load.wait()
    mixed_load.wait()
    dthird = hidden_rows(recv_ref.at[:, pl.ds(rows, rows)])
    scaled = jnp.concatenate([scaled_ref[i] for i in range(steps)], axis=1)
    z_size, y_size, part_rows, _ = grads_ref.shape
    half = z_size // 2
    size = half * part_rows
    for r in range(2 * y_size):
        z = pl.ds(r % 2 * half, half)
        act = jnp.concatenate([act_ref[i, r * size : (r + 1) * size, :] for i in range(steps)], axis=1)
        third = dot(act, dthird, NT).astype(BF16)
        grads_ref[z, r // 2, :, HBS:] = third.reshape(half, part_rows, HBS)
        sources = pl.ds(r * (size // PAIR), size // PAIR)
        mixed = hidden_rows(recv_ref.at[sources, pl.ds(0, rows)])
        second = dot(mixed, scaled, NT).astype(BF16)
        grads_ref[z, r // 2, :, :HBS] = second.reshape(half, part_rows, HBS)
        stores.start(grads_ref.at[z, r // 2], grads_hbm.at[z, lax.rem(r // 2 + y, y_size)])
    stores.start(dpre_ref, dpre_hbm)
    stores.wait()


def dmixed_kernel(dpre_ref, inner_ref, w2_ref, out_ref):
    steps = dpre_ref.shape[0]
    for i in range(steps):
        dmixed = dot(w2_ref[0], dpre_ref[i], NN).astype(BF16)
        out_ref[:, i * 2 * PAIR : (i + 1) * 2 * PAIR, :] = by_peer(dmixed)
    rest = stat_rows(inner_ref[...], 2 * steps)
    out_ref[:, steps * 2 * PAIR :, :] = jnp.broadcast_to(rest[None], (PEERS, STATS, LANES))


def model_rows(ref, chunks, a):
    parts = []
    for i in range(chunks):
        start = i * PAIR + a * EB
        parts.append(ref[:, start : start + EB, :].reshape(HB * EB, LANES))
    return jnp.concatenate(parts, axis=1)


def columns(stats, chunks):
    turned = stats.T
    parts = [turned[:, 2 * i : 2 * i + 1] + turned[:, 2 * i + 1 : 2 * i + 2] for i in range(chunks)]
    return jnp.concatenate(parts, axis=0)


def output_kernel(recv_ref, x_ref, w4_ref, out_ref):
    chunks = x_ref.shape[0] // LANES
    for a in range(2):
        feats = slice(a * BS, (a + 1) * BS)
        branch = dot(model_rows(recv_ref, chunks, a), w4_ref[a], TN)
        out_ref[:, feats] = (x_ref[:, feats].astype(F32) + branch).astype(BF16)


def fourth_kernel(y_ref, recv_ref, cot_ref, x_ref, gain_ref, stats_ref, own_ref, other_ref, normed_ref):
    chunks = cot_ref.shape[0] // LANES
    z_size = own_ref.shape[0]
    rows = HB * EB // PEERS
    for a in range(2):
        grad = dot(model_rows(recv_ref, chunks, a), cot_ref[:, a * BS : (a + 1) * BS], NN).astype(BF16)
        grad = grad.reshape(PEERS, rows, BS)
        part = slice(a * rows, (a + 1) * rows)
        own_ref[:, part, :] = jnp.where(y_ref[0] == 0, grad[:z_size], grad[z_size:])
        other_ref[:, part, :] = jnp.where(y_ref[0] == 0, grad[z_size:], grad[:z_size])
    inverse = lax.rsqrt(columns(stat_sum(stats_ref[...]), chunks) / MODEL_WIDTH + epsilon)
    normed_ref[...] = (x_ref[...].astype(F32) * inverse * gain_ref[...]).astype(BF16)


def pair_kernel(z_ref, own_ref, other_ref, *out_refs):
    size = len(out_refs)
    for k, out_ref in enumerate(out_refs):
        z = lax.rem(z_ref[0] + k, size)
        out_ref[...] = (own_ref[z].astype(F32) + other_ref[z].astype(F32)).astype(BF16)


def fourth_sum_kernel(scale, *refs):
    total = refs[0][...].astype(F32)
    for ref in refs[1:-1]:
        total = total + ref[...].astype(F32)
    refs[-1][...] = (total * scale).reshape(refs[-1].shape)


def first_kernel(recv_hbm, normed_hbm, out_ref, recv_ref, normed_ref, sems):
    chunks = normed_ref.shape[0] // LANES
    loads = Copies(sems)
    for a in range(2):
        feats = pl.ds(a * BS, BS)
        loads.start(normed_hbm.at[:, feats], normed_ref.at[:, feats])
    part = pl.ds(0, chunks * PAIR)
    loads.start(recv_hbm.at[:, part], recv_ref)
    loads.wait()
    rows = BS // PEERS
    for a in range(2):
        dfirst = model_rows(recv_ref, chunks, a)
        grad = dot(dfirst, normed_ref[:, a * BS : (a + 1) * BS], NN).astype(BF16).T
        for half in range(2):
            base = (2 * a + half) * rows
            value = grad[:, half * BS : (half + 1) * BS]
            out_ref[:, base : base + rows, :] = value.reshape(PEERS, rows, BS)


def token_kernel(recv_ref, stats_ref, x_ref, gain_ref, w1_ref, cot_ref, out_ref):
    chunks = x_ref.shape[0] // LANES
    inverse = lax.rsqrt(columns(stat_sum(stats_ref[...]), chunks) / MODEL_WIDTH + epsilon)
    inner = columns(stat_sum(recv_ref[:, chunks * PAIR :, :]), chunks) / MODEL_WIDTH
    for a in range(2):
        feats = slice(a * BS, (a + 1) * BS)
        dfirst = model_rows(recv_ref, chunks, a)
        dnormed = dot(dfirst, w1_ref[a], TT)
        xhat = x_ref[:, feats].astype(F32) * inverse
        change = dnormed * gain_ref[:, feats] - xhat * inner
        out_ref[:, feats] = (cot_ref[:, feats].astype(F32) + inverse * change).astype(BF16)


def first_sum_kernel(scale, recv_ref, first_ref):
    total = jnp.sum(recv_ref[...].astype(F32), axis=0) * scale
    _, rows, _ = first_ref.shape
    for a in range(2):
        for half in range(2):
            base = (2 * a + half) * rows
            first_ref[a, :, half * BS : (half + 1) * BS] = total[base : base + rows]


def finish_kernel(scale, own_ref, other_ref, second_ref, third_ref):
    total = (own_ref[0, 0].astype(F32) + other_ref[...].astype(F32)) * scale
    second_ref[0] = total[:, :HBS]
    third_ref[0] = total[:, HBS:]


def shards(tokens, gain, w_first, w_second, w_third, w_fourth, cotangent):
    element_count, local_width = tokens.shape
    dp = lax.axis_size("dp")
    scale = 1.0 / math.sqrt(element_count * dp)
    gain_row = gain[None, :]
    z_size = dp // 2
    z_groups = [[y * z_size + z for z in range(z_size)] for y in range(2)]
    y_pairs = [(i, (i + z_size) % dp) for i in range(dp)]
    y_index = (lax.axis_index("dp") // z_size).astype(jnp.int32)[None]
    z_index = (lax.axis_index("dp") % z_size).astype(jnp.int32)[None]
    shape = jax.ShapeDtypeStruct
    hidden_flops = 2 * HBS * HBS * element_count
    model_flops = 2 * local_width * HB * EB * element_count
    steps = element_count // STEP
    rows = steps * 2 * PAIR
    sent = shape((PEERS, 2 * rows + STATS, LANES), BF16)
    stepped = shape((steps, HBS, STEP), BF16)
    hbm = pl.BlockSpec(memory_space=pltpu.HBM)
    vmem = pl.BlockSpec(memory_space=pltpu.VMEM)
    smem = pl.BlockSpec(memory_space=pltpu.SMEM)
    params = pltpu.CompilerParams(vmem_limit_bytes=VMEM)

    def cost(flops):
        return pl.CostEstimate(flops=int(flops), bytes_accessed=8 << 20, transcendentals=0)

    def whole(*dims):
        return pl.BlockSpec(dims, lambda i, *_: (0,) * len(dims))

    send = pl.pallas_call(
        head_kernel,
        out_shape=sent,
        in_specs=[hbm, hbm, vmem, hbm, hbm],
        out_specs=hbm,
        scratch_shapes=[
            pltpu.VMEM(tokens.shape, BF16),
            pltpu.VMEM(tokens.shape, BF16),
            pltpu.VMEM(w_first.shape, BF16),
            pltpu.VMEM(w_fourth.shape, BF16),
            pltpu.VMEM(sent.shape, BF16),
            pltpu.SemaphoreType.DMA((2 * steps + 2,)),
            pltpu.SemaphoreType.DMA((2 * steps + 1,)),
        ],
        compiler_params=params,
        cost_estimate=cost(2 * model_flops),
    )(tokens, cotangent, gain_row, w_first, w_fourth)
    recv = lax.all_to_all(send, "tensor", 0, 0, tiled=True)
    turned = shape((HBS, HBS), BF16)
    w_second_t, w_third_t = call(turn_kernel, [turned, turned], (w_second, w_third))
    third_sent = shape((PEERS, rows, LANES), BF16)
    back_sent = shape((PEERS, rows + STATS, LANES), BF16)
    pre_shape = shape(stepped.shape, F32)
    pre, act, send = pl.pallas_call(
        forward_kernel,
        out_shape=[pre_shape, stepped, third_sent],
        in_specs=[hbm] * 3,
        out_specs=[hbm] * 3,
        scratch_shapes=[
            pltpu.VMEM(back_sent.shape, BF16),
            pltpu.VMEM(turned.shape, BF16),
            pltpu.VMEM(turned.shape, BF16),
            pltpu.VMEM(stepped.shape, F32),
            pltpu.VMEM(stepped.shape, BF16),
            pltpu.VMEM(third_sent.shape, BF16),
            pltpu.SemaphoreType.DMA((steps + 3,)),
            pltpu.SemaphoreType.DMA((2 * steps + 1,)),
        ],
        compiler_params=params,
        cost_estimate=cost(2 * hidden_flops),
    )(recv, w_second_t, w_third_t)
    third = lax.all_to_all(send, "tensor", 0, 0, tiled=True)
    grads = shape((z_size, 2, HBS // dp, 2 * HBS), BF16)
    hidden, dpre, inner = pl.pallas_call(
        backward_kernel,
        out_shape=[grads, stepped, shape((1, element_count), F32)],
        in_specs=[smem] + [hbm] * 4,
        out_specs=[hbm, hbm, vmem],
        scratch_shapes=[
            pltpu.VMEM(sent.shape, BF16),
            pltpu.VMEM(stepped.shape, F32),
            pltpu.VMEM(stepped.shape, BF16),
            pltpu.VMEM(w_third.shape, BF16),
            pltpu.VMEM(stepped.shape, BF16),
            pltpu.VMEM(stepped.shape, BF16),
            pltpu.VMEM(grads.shape, BF16),
            pltpu.SemaphoreType.DMA((2 * steps + 4,)),
            pltpu.SemaphoreType.DMA((5,)),
        ],
        compiler_params=params,
        cost_estimate=cost(3 * hidden_flops),
    )(y_index, recv, pre, act, w_third)
    hidden = lax.psum_scatter(hidden, "dp", scatter_dimension=0, axis_index_groups=z_groups, tiled=True)
    send = call(dmixed_kernel, back_sent, (dpre, inner, w_second), flops=hidden_flops)
    send, third = lax.optimization_barrier((send, third))
    back = lax.all_to_all(send, "tensor", 0, 0, tiled=True)

    stats_spec = pl.BlockSpec((PEERS, STATS, LANES), lambda i: (0, 2 * rows // STATS, 0))
    all_tokens = whole(*tokens.shape)
    row = whole(1, local_width)
    part = shape((z_size, PAIR, BS), BF16)
    own, other, normed = pl.pallas_call(
        fourth_kernel,
        out_shape=[part, part, shape(tokens.shape, BF16)],
        grid=(1,),
        in_specs=[smem, whole(*third_sent.shape), all_tokens, all_tokens, row, stats_spec],
        out_specs=[whole(*part.shape), whole(*part.shape), all_tokens],
        compiler_params=params,
        cost_estimate=cost(model_flops),
    )(y_index, third, cotangent, tokens, gain_row, recv)
    other = lax.ppermute(other, "dp", y_pairs)
    block = shape((PAIR, BS), BF16)
    blocks = pl.pallas_call(
        pair_kernel,
        out_shape=[block] * z_size,
        in_specs=[smem, vmem, vmem],
        out_specs=[vmem] * z_size,
        compiler_params=params,
        cost_estimate=cost(0),
    )(z_index, own, other)
    blocks, back = lax.optimization_barrier((blocks, back))
    blocks = [blocks[0]] + [
        lax.ppermute(
            blocks[k], "dp", [(g[z], g[(z + k) % z_size]) for g in z_groups for z in range(z_size)]
        )
        for k in range(1, z_size)
    ]
    output = call(output_kernel, shape(tokens.shape, BF16), (third, tokens, w_fourth), flops=LATE * model_flops)
    first = shape((PEERS, PAIR, BS), BF16)
    first = pl.pallas_call(
        first_kernel,
        out_shape=first,
        in_specs=[hbm, hbm],
        out_specs=vmem,
        scratch_shapes=[
            pltpu.VMEM(third_sent.shape, BF16),
            pltpu.VMEM(tokens.shape, BF16),
            pltpu.SemaphoreType.DMA((3,)),
        ],
        compiler_params=params,
        cost_estimate=cost(model_flops),
    )(back, normed)
    first = lax.all_to_all(first, "dp", 0, 0, tiled=True)
    token_gradient = pl.pallas_call(
        token_kernel,
        out_shape=shape(tokens.shape, BF16),
        grid=(1,),
        in_specs=[whole(*back_sent.shape), stats_spec, all_tokens, row, whole(*w_first.shape), all_tokens],
        out_specs=all_tokens,
        compiler_params=params,
        cost_estimate=cost(LATE * model_flops),
    )(back, recv, tokens, gain_row, w_first, cotangent)
    grad_fourth = call(
        functools.partial(fourth_sum_kernel, scale), shape((2, HB * EB // dp, BS), F32), tuple(blocks)
    )
    grad_first = call(functools.partial(first_sum_kernel, scale), shape((2, BS // dp, HB * EB), F32), (first,))
    hidden, grad_fourth = lax.optimization_barrier((hidden, grad_fourth))
    other = lax.ppermute(hidden[0, 1], "dp", y_pairs)
    part = shape((1, HBS // dp, HBS), F32)
    grad_second, grad_third = call(functools.partial(finish_kernel, scale), [part, part], (hidden, other))
    return output, token_gradient, grad_first, grad_second, grad_third, grad_fourth


def solution(mesh):
    return jax.shard_map(
        shards,
        mesh=mesh,
        in_specs=(
            P("dp", "tensor"),
            P("tensor"),
            P("tensor", None, None),
            P("tensor", None, None),
            P("tensor", None, None),
            P("tensor", None, None),
            P("dp", "tensor"),
        ),
        out_specs=(
            P("dp", "tensor"),
            P("dp", "tensor"),
            P("tensor", "dp", None),
            P("tensor", "dp", None),
            P("tensor", "dp", None),
            P("tensor", "dp", None),
        ),
        check_vma=False,
    )
```

time: 194 us -> 209 us (1.077)
  starting transfers between devices: 30.5 us -> 53.9 us
  waiting for transfers between devices: 91.6 us -> 74.9 us
  Pallas kernels: 52.5 us -> 59.6 us
    all_to_all x1, waiting for transfers between devices: 26.7 us -> 0.01 us  [shards(): back = lax.all_to_all(send, 'tensor', 0, 0, tiled=True)]
    ppermute x0 -> x8, waiting for transfers between devices: none -> 20.8 us  [the longest x1 20.8 us: shards(): other = lax.ppermute(other, 'dp', y_pairs)]
    ppermute x0 -> x8, starting transfers between devices: none -> 19.7 us  [the longest x7 18.4 us: shards(): lax.ppermute(blocks[k], 'dp', [(g[z], g[(z + k) % z_size]) for g in z_gro...]
    reduce_scatter x1, waiting for transfers between devices: 32.2 us -> 19.7 us  [shards(): lax.psum_scatter(hidden, 'dp', scatter_dimension=0, axis_index_groups=z_g...]
    all_to_all x1 -> x2, starting transfers between devices: 9.3 us -> 17.1 us  [the longest x1 12.8 us: shards(): third = lax.all_to_all(send, 'tensor', 0, 0, tiled=True)]
    pallas_call x4 -> x6, Pallas kernels: 12.6 us -> 18.5 us  [call(): pl.pallas_call(kernel, out_shape=out_shape, in_specs=[pl.BlockSpec(memory...]
    all_to_all x1, starting transfers between devices: 13 us -> 8.56 us  [shards(): back = lax.all_to_all(send, 'tensor', 0, 0, tiled=True)]
    pallas_call x4 -> x5, Pallas kernels: 29.5 us -> 31.3 us  [the longest x1 13.4 us: shards(): pl.pallas_call(backward_kernel, out_shape=[grads, stepped, shape((1, elem...]
  transfers between devices with their start and end apart: 5 -> 14, of which waited for: 4 -> 5; matrix products, arithmetic and copies ran while one was open for 1% -> 1% of each run, Pallas kernels for 15% -> 20%
where the time goes in v5:
time: 209 us; the launch traced here: 208 us
  waiting for transfers between devices  74.9 us (36%)
  Pallas kernels  59.6 us (29%)
  starting transfers between devices  53.9 us (26%)
  between operations  14.2 us (7%)
  local copies, waits for them, and re-layouts  5.24 us (3%)
    all_to_all x1, waiting for transfers between devices, shards(): recv = lax.all_to_all(send, 'tensor', 0, 0, tiled=True)  32.6 us
    ppermute x1, waiting for transfers between devices, shards(): other = lax.ppermute(other, 'dp', y_pairs)  20.8 us
    reduce_scatter x1, waiting for transfers between devices, shards(): lax.psum_scatter(hidden, 'dp', scatter_dimension=0, axis_index_groups=z_g...  19.7 us
    pallas_call x6, Pallas kernels, call(): pl.pallas_call(kernel, out_shape=out_shape, in_specs=[pl.BlockSpec(memory...  18.5 us
    ppermute x7, starting transfers between devices, shards(): lax.ppermute(blocks[k], 'dp', [(g[z], g[(z + k) % z_size]) for g in z_gro...  18.4 us
    pallas_call x1, Pallas kernels, shards(): pl.pallas_call(backward_kernel, out_shape=[grads, stepped, shape((1, elem...  13.4 us
    all_to_all x1, starting transfers between devices, shards(): third = lax.all_to_all(send, 'tensor', 0, 0, tiled=True)  12.8 us
    pallas_call x1, Pallas kernels, shards(): pl.pallas_call(forward_kernel, out_shape=[pre_shape, stepped, third_sent]...  9.55 us
  transfers between devices with their start and end apart: 14, of which 5 were waited for; matrix products, arithmetic and copies ran while one was open for 1% of the time, Pallas kernels for 20%

profile of v5, /device:TPU:18, one launch (start us, length us, event | category | flops | bytes accessed | tf_op | source)
XLA Modules:
  0.0 207.8 jit_solution(8005504634265294983)
XLA Ops:
  7.2 5.5 %shard_map.118 = bf16[16,784,128]{2,1,0:T(8,128)(2,1)} custom-call(bf16[768,512]{1,0:T(8,128)(2,1)} %x_ref.5, bf16[768,512]{1,0:T(8,128)(2,1)} %cot_ref.3, f32[1,512]{1,0:T(1,128)} %bitcast.5, bf16[2,256,512]{2,1,0:T(8,128)(2,1)} %w1_ref.1, bf16[2,512,256]{2,1,0:T(8,128)(2,1)} %w4_ref.1), custom_call_target="tpu_custom_call" | custom-call | flops 805306368 | bytes 8388608 | tf_op jit(solution)/shard_map/pallas_call | solution.py:404
  12.7 7.3 %all-to-all-start = ((bf16[16,784,128]{2,1,0:T(8,128)(2,1)}), bf16[16,784,128]{2,1,0:T(8,128)(2,1)S(1)}, u32[]{:S(2)}, u32[]{:S(2)}) async-start(bf16[16,784,128]{2,1,0:T(8,128)(2,1)} %shard_map.118), calls=%async_computation | async-start | bytes 6422528 | tf_op jit(solution)/shard_map/all_to_all | solution.py:421
  20.0 4.8 %shard_map.119 = (bf16[1024,1024]{1,0:T(8,128)(2,1)}, bf16[1024,1024]{1,0:T(8,128)(2,1)}) custom-call(bf16[1,1024,1024]{2,1,0:T(8,128)(2,1)} %w2_ref.3, bf16[1,1024,1024]{2,1,0:T(8,128)(2,1)} %w3_hbm.1), custom_call_target="tpu_custom_call" | custom-call | bytes 8388608 | tf_op jit(solution)/shard_map/pallas_call | solution.py:47
  24.8 32.6 %all-to-all-done.recv_hbm.stats_ref = bf16[16,784,128]{2,1,0:T(8,128)(2,1)S(1)} async-done(((bf16[16,784,128]{2,1,0:T(8,128)(2,1)}), bf16[16,784,128]{2,1,0:T(8,128)(2,1)S(1)}, u32[]{:S(2)}, u32[]{:S(2)}) %all-to-all-start) | async-done | bytes 3211296 | tf_op jit(solution)/shard_map/all_to_all | solution.py:421
  57.4 0.0 copy-start
  57.4 1.7 copy-done
  59.1 9.5 %shard_map.120 = (f32[3,1024,256]{2,1,0:T(8,128)}, bf16[3,1024,256]{2,1,0:T(8,128)(2,1)}, bf16[16,384,128]{2,1,0:T(8,128)(2,1)}) custom-call(bf16[16,784,128]{2,1,0:T(8,128)(2,1)} %copy-done, bf16[1024,1024]{1,0:T(8,128)(2,1)} %get-tuple-element.40.w2t_hbm, bf16[1024,1024]{1,0:T(8,128)(2,1)} %get-tuple-element.41.w3t_hbm), custom_call_target="tpu_custom_call" | custom-call | flops 3221225472 | bytes 8388608 | tf_op jit(solution)/shard_map/pallas_call | solution.py:427
  68.6 12.8 %all-to-all-start.1 = ((bf16[16,384,128]{2,1,0:T(8,128)(2,1)}), bf16[16,384,128]{2,1,0:T(8,128)(2,1)S(1)}, u32[]{:S(2)}, u32[]{:S(2)}) async-start(bf16[16,384,128]{2,1,0:T(8,128)(2,1)} %get-tuple-element.46), calls=%async_computation.1 | async-start | bytes 3145728 | tf_op jit(solution)/shard_map/all_to_all | solution.py:445
  81.5 13.4 %shard_map.121 = (bf16[8,2,64,2048]{3,2,1,0:T(8,128)(2,1)}, bf16[3,1024,256]{2,1,0:T(8,128)(2,1)}, f32[1,768]{1,0:T(1,128)}) custom-call(s32[1]{0:T(128)} %bitcast.y_ref, bf16[16,784,128]{2,1,0:T(8,128)(2,1)} %copy-done, f32[3,1024,256]{2,1,0:T(8,128)} %get-tuple-element.42.pre_hbm, bf16[3,1024,256]{2,1,0:T(8,128)(2,1)} %get-tuple-element.43.act_hbm, ...), custom_call_target="tpu_custom_call" | custom-call | flops 4831838208 | bytes 8388608 | tf_op jit(solution)/shard_map/pallas_call | solution.py:447
  94.8 5.1 %shard_map.122 = bf16[16,400,128]{2,1,0:T(8,128)(2,1)} custom-call(bf16[3,1024,256]{2,1,0:T(8,128)(2,1)} %get-tuple-element.44.dpre_ref, f32[1,768]{1,0:T(1,128)} %get-tuple-element.45.inner_ref, bf16[1,1024,1024]{2,1,0:T(8,128)(2,1)} %w2_ref.3), custom_call_target="tpu_custom_call" | custom-call | flops 1610612736 | bytes 5311488 | tf_op jit(solution)/shard_map/pallas_call | solution.py:47
  99.9 0.6 all-to-all-done.1.recv_ref
  100.6 0.0 copy-start.2
  100.6 8.6 %all-to-all-start.2 = ((bf16[16,400,128]{2,1,0:T(8,128)(2,1)}), bf16[16,400,128]{2,1,0:T(8,128)(2,1)S(1)}, u32[]{:S(2)}, u32[]{:S(2)}) async-start(bf16[16,400,128]{2,1,0:T(8,128)(2,1)} %shard_map.122), calls=%async_computation.2 | async-start | bytes 3276800 | tf_op jit(solution)/shard_map/all_to_all | solution.py:469
  109.1 0.0 reduce-scatter.2.cloned.1.call-start
  109.2 0.0 copy-done.2
  109.2 3.5 %shard_map.124 = (bf16[8,64,256]{2,1,0:T(8,128)(2,1)}, bf16[8,64,256]{2,1,0:T(8,128)(2,1)}, bf16[768,512]{1,0:T(8,128)(2,1)}) custom-call(s32[1]{0:T(128)} %bitcast.y_ref, bf16[16,384,128]{2,1,0:T(8,128)(2,1)} %copy-done.2, bf16[768,512]{1,0:T(8,128)(2,1)} %cot_ref.3, bf16[768,512]{1,0:T(8,128)(2,1)} %x_ref.5, f32[1,512]{1,0:T(1,128)} %bitcast.6, ...), custom_call_target="tpu_custom_call" | custom-call | flops 402653184 | bytes 8388608 | tf_op jit(solution)/shard_map/pallas_call | solution.py:475
  112.7 1.3 collective-permute-start
  114.0 0.0 reduce-scatter.2.cloned.1.call-update
  114.0 20.8 %collective-permute-done.other_ref = bf16[8,64,256]{2,1,0:T(8,128)(2,1)S(1)} collective-permute-done((bf16[8,64,256]{2,1,0:T(8,128)(2,1)}, bf16[8,64,256]{2,1,0:T(8,128)(2,1)S(1)}, u32[]{:S(2)}, u32[]{:S(2)}) %collective-permute-start) | collective-permute-done | bytes 262176 | tf_op jit(solution)/shard_map/ppermute | solution.py:484
  134.8 0.7 copy-done.3
  135.5 1.7 shard_map.125
  137.2 0.0 all-to-all-done.2.recv_ref.recv_hbm
  137.2 1.9 collective-permute-start.1
  139.2 3.3 %collective-permute-start.2 = (bf16[64,256]{1,0:T(8,128)(2,1)}, bf16[64,256]{1,0:T(8,128)(2,1)}, u32[]{:S(2)}, u32[]{:S(2)}) collective-permute-start(bf16[64,256]{1,0:T(8,128)(2,1)} %get-tuple-element.64), channel_id=1, source_target_pairs={{0,32},{16,48},{32,64},{48,80},{64,96},{80,112},{96,0},{112,16},{1... | collective-permute-start | bytes 98312 | tf_op jit(solution)/shard_map/ppermute | solution.py:496
  142.5 0.0 copy-start.9
  142.5 3.3 %shard_map.123 = bf16[768,512]{1,0:T(8,128)(2,1)} custom-call(bf16[16,384,128]{2,1,0:T(8,128)(2,1)} %copy-done.2, bf16[768,512]{1,0:T(8,128)(2,1)} %x_ref.5, bf16[2,512,256]{2,1,0:T(8,128)(2,1)} %w4_ref.1), custom_call_target="tpu_custom_call" | custom-call | flops 402653184000 | bytes 3670016 | tf_op jit(solution)/shard_map/pallas_call | solution.py:47
  145.8 0.0 copy-done.1
  145.8 0.0 copy-done.13
  145.8 4.0 %collective-permute-start.3 = (bf16[64,256]{1,0:T(8,128)(2,1)S(1)}, bf16[64,256]{1,0:T(8,128)(2,1)S(1)}, u32[]{:S(2)}, u32[]{:S(2)}) collective-permute-start(bf16[64,256]{1,0:T(8,128)(2,1)S(1)} %copy-done.13), channel_id=1, source_target_pairs={{0,48},{16,64},{32,80},{48,96},{64,112},{80,0},{96,16},{112,32},{1... | collective-permute-start | bytes 98312 | tf_op jit(solution)/shard_map/ppermute | solution.py:496
  149.9 0.0 copy-done.12
  149.9 0.6 collective-permute-start.4
  150.4 0.0 copy-done.11
  150.4 4.9 %collective-permute-start.5 = (bf16[64,256]{1,0:T(8,128)(2,1)S(1)}, bf16[64,256]{1,0:T(8,128)(2,1)S(1)}, u32[]{:S(2)}, u32[]{:S(2)}) collective-permute-start(bf16[64,256]{1,0:T(8,128)(2,1)S(1)} %copy-done.11), channel_id=1, source_target_pairs={{0,80},{16,96},{32,112},{48,0},{64,16},{80,32},{96,48},{112,64},{1... | collective-permute-start | bytes 98312 | tf_op jit(solution)/shard_map/ppermute | solution.py:496
  155.4 0.0 collective-permute-done.1.refs_1_
  155.4 0.0 copy-done.10
  155.4 2.7 %collective-permute-start.6 = (bf16[64,256]{1,0:T(8,128)(2,1)S(1)}, bf16[64,256]{1,0:T(8,128)(2,1)S(1)}, u32[]{:S(2)}, u32[]{:S(2)}) collective-permute-start(bf16[64,256]{1,0:T(8,128)(2,1)S(1)} %copy-done.10), channel_id=1, source_target_pairs={{0,96},{16,112},{32,0},{48,16},{64,32},{80,48},{96,64},{112,80},{1... | collective-permute-start | bytes 98312 | tf_op jit(solution)/shard_map/ppermute | solution.py:496
  158.1 0.0 collective-permute-done.2.refs_2_
  158.1 0.0 copy-done.9
  158.1 0.9 collective-permute-start.7
  159.0 3.2 %shard_map.127 = bf16[16,64,256]{2,1,0:T(8,128)(2,1)} custom-call(bf16[16,400,128]{2,1,0:T(8,128)(2,1)} %copy-done.1, bf16[768,512]{1,0:T(8,128)(2,1)} %get-tuple-element.60.normed_hbm), custom_call_target="tpu_custom_call" | custom-call | flops 402653184 | bytes 8388608 | tf_op jit(solution)/shard_map/pallas_call | solution.py:503
  162.2 4.3 %all-to-all-start.3 = ((bf16[16,64,256]{2,1,0:T(8,128)(2,1)}), bf16[16,64,256]{2,1,0:T(8,128)(2,1)}, u32[]{:S(2)}, u32[]{:S(2)}) async-start(bf16[16,64,256]{2,1,0:T(8,128)(2,1)} %shard_map.127), calls=%async_computation.3 | async-start | bytes 1048576 | tf_op jit(solution)/shard_map/all_to_all | solution.py:516
  166.5 0.0 collective-permute-done.3.refs_3_
  166.5 0.0 copy-start.4
  166.5 0.0 collective-permute-done.4.refs_4_
  166.5 0.0 copy-start.5
  166.5 0.0 collective-permute-done.5.refs_5_
  166.5 0.0 copy-start.6
  166.5 0.0 collective-permute-done.6.refs_6_
  166.5 0.0 copy-start.7
  166.5 0.0 collective-permute-done.7.refs_7_
  166.6 0.5 copy-done.4
  167.1 0.0 copy-done.5
  167.1 0.0 copy-done.6
  167.1 0.0 copy-done.7
  167.1 0.6 copy-done.8
  167.7 1.5 shard_map.129
  169.3 19.7 %reduce-scatter.2.cloned.1.call-done.own_ref = bf16[1,2,64,2048]{3,2,1,0:T(8,128)(2,1)} async-done(((bf16[8,2,64,2048]{3,2,1,0:T(8,128)(2,1)}), bf16[1,2,64,2048]{3,2,1,0:T(8,128)(2,1)}) %reduce-scatter.2.cloned.1.call-update) | async-done | bytes 524304 | tf_op jit(solution)/shard_map/reduce_scatter | solution.py:466
  189.0 1.7 slice_bitcast_fusion
  190.7 1.2 collective-permute-start.8
  191.9 4.3 %shard_map.126 = bf16[768,512]{1,0:T(8,128)(2,1)} custom-call(bf16[16,400,128]{2,1,0:T(8,128)(2,1)} %copy-done.1, bf16[16,784,128]{2,1,0:T(8,128)(2,1)} %copy-done, bf16[768,512]{1,0:T(8,128)(2,1)} %x_ref.5, f32[1,512]{1,0:T(1,128)} %bitcast.7, bf16[2,256,512]{2,1,0:T(8,128)(2,1)} %w1_ref.1, bf16[768,512]{1,0:T(8,128)(2,1)} %cot_ref.3), custom_call_target="tpu_custom_call" | custom-call | flops 402653184000 | bytes 8388608 | tf_op jit(solution)/shard_map/pallas_call | solution.py:517
  196.2 0.0 all-to-all-done.3.recv_ref
  196.2 1.7 shard_map.128
  197.9 1.2 collective-permute-done.8.other_ref
  199.1 1.9 shard_map.130
  (7 shorter events, 0.0 us)
Async XLA Ops:
  12.7 44.7 %all-to-all-start = ((bf16[16,784,128]{2,1,0:T(8,128)(2,1)}), bf16[16,784,128]{2,1,0:T(8,128)(2,1)S(1)}, u32[]{:S(2)}, u32[]{:S(2)}) async-start(bf16[16,784,128]{2,1,0:T(8,128)(2,1)} %shard_map.118), calls=%async_computation | async-start | bytes 6422528 | tf_op jit(solution)/shard_map/all_to_all | solution.py:421
  57.4 1.7 copy-start
  68.6 31.9 %all-to-all-start.1 = ((bf16[16,384,128]{2,1,0:T(8,128)(2,1)}), bf16[16,384,128]{2,1,0:T(8,128)(2,1)S(1)}, u32[]{:S(2)}, u32[]{:S(2)}) async-start(bf16[16,384,128]{2,1,0:T(8,128)(2,1)} %get-tuple-element.46), calls=%async_computation.1 | async-start | bytes 3145728 | tf_op jit(solution)/shard_map/all_to_all | solution.py:445
  100.6 8.6 %copy-start.2 = (bf16[16,384,128]{2,1,0:T(8,128)(2,1)}, bf16[16,384,128]{2,1,0:T(8,128)(2,1)S(1)}, u32[]{:S(2)}) copy-start(bf16[16,384,128]{2,1,0:T(8,128)(2,1)S(1)} %all-to-all-done.1.recv_ref) | copy-start | bytes 4718596
  100.6 36.7 %all-to-all-start.2 = ((bf16[16,400,128]{2,1,0:T(8,128)(2,1)}), bf16[16,400,128]{2,1,0:T(8,128)(2,1)S(1)}, u32[]{:S(2)}, u32[]{:S(2)}) async-start(bf16[16,400,128]{2,1,0:T(8,128)(2,1)} %shard_map.122), calls=%async_computation.2 | async-start | bytes 3276800 | tf_op jit(solution)/shard_map/all_to_all | solution.py:469
  109.1 79.9 %reduce-scatter.2.cloned.1.call-start = ((), (), s32[]{:S(2)}) async-start(), calls=%async_computation.5 | async-start | bytes 4718592 | tf_op jit(solution)/shard_map/reduce_scatter | solution.py:466
  112.7 22.1 %collective-permute-start = (bf16[8,64,256]{2,1,0:T(8,128)(2,1)}, bf16[8,64,256]{2,1,0:T(8,128)(2,1)S(1)}, u32[]{:S(2)}, u32[]{:S(2)}) collective-permute-start(bf16[8,64,256]{2,1,0:T(8,128)(2,1)} %get-tuple-element.49), channel_id=1, source_target_pairs={{0,128},{16,144},{32,160},{48,176},{64,192},{80,208},{96,224},{112... | collective-permute-start | bytes 786440 | tf_op jit(solution)/shard_map/ppermute | solution.py:484
  134.8 0.7 copy-start.3
  137.2 8.6 %copy-start.1 = (bf16[16,400,128]{2,1,0:T(8,128)(2,1)}, bf16[16,400,128]{2,1,0:T(8,128)(2,1)S(1)}, u32[]{:S(2)}) copy-start(bf16[16,400,128]{2,1,0:T(8,128)(2,1)S(1)} %all-to-all-done.2.recv_ref.recv_hbm) | copy-start | bytes 4915204
  137.2 18.1 %collective-permute-start.1 = (bf16[64,256]{1,0:T(8,128)(2,1)}, bf16[64,256]{1,0:T(8,128)(2,1)}, u32[]{:S(2)}, u32[]{:S(2)}) collective-permute-start(bf16[64,256]{1,0:T(8,128)(2,1)} %get-tuple-element.63), channel_id=1, source_target_pairs={{0,16},{16,32},{32,48},{48,64},{64,80},{80,96},{96,112},{112,0},{1... | collective-permute-start | bytes 98312 | tf_op jit(solution)/shard_map/ppermute | solution.py:496
  139.2 18.9 %collective-permute-start.2 = (bf16[64,256]{1,0:T(8,128)(2,1)}, bf16[64,256]{1,0:T(8,128)(2,1)}, u32[]{:S(2)}, u32[]{:S(2)}) collective-permute-start(bf16[64,256]{1,0:T(8,128)(2,1)} %get-tuple-element.64), channel_id=1, source_target_pairs={{0,32},{16,48},{32,64},{48,80},{64,96},{80,112},{96,0},{112,16},{1... | collective-permute-start | bytes 98312 | tf_op jit(solution)/shard_map/ppermute | solution.py:496
  142.5 3.3 %copy-start.13 = (bf16[64,256]{1,0:T(8,128)(2,1)S(1)}, bf16[64,256]{1,0:T(8,128)(2,1)}, u32[]{:S(2)}) copy-start(bf16[64,256]{1,0:T(8,128)(2,1)} %get-tuple-element.65) | copy-start | bytes 98308
  142.5 7.4 %copy-start.12 = (bf16[64,256]{1,0:T(8,128)(2,1)S(1)}, bf16[64,256]{1,0:T(8,128)(2,1)}, u32[]{:S(2)}) copy-start(bf16[64,256]{1,0:T(8,128)(2,1)} %get-tuple-element.66) | copy-start | bytes 98308
  142.5 7.9 %copy-start.11 = (bf16[64,256]{1,0:T(8,128)(2,1)S(1)}, bf16[64,256]{1,0:T(8,128)(2,1)}, u32[]{:S(2)}) copy-start(bf16[64,256]{1,0:T(8,128)(2,1)} %get-tuple-element.67) | copy-start | bytes 98308
  142.5 12.9 %copy-start.10 = (bf16[64,256]{1,0:T(8,128)(2,1)S(1)}, bf16[64,256]{1,0:T(8,128)(2,1)}, u32[]{:S(2)}) copy-start(bf16[64,256]{1,0:T(8,128)(2,1)} %get-tuple-element.68) | copy-start | bytes 98308
  142.5 15.6 %copy-start.9 = (bf16[64,256]{1,0:T(8,128)(2,1)S(1)}, bf16[64,256]{1,0:T(8,128)(2,1)}, u32[]{:S(2)}) copy-start(bf16[64,256]{1,0:T(8,128)(2,1)} %get-tuple-element.69) | copy-start | bytes 98308
  145.8 20.6 %collective-permute-start.3 = (bf16[64,256]{1,0:T(8,128)(2,1)S(1)}, bf16[64,256]{1,0:T(8,128)(2,1)S(1)}, u32[]{:S(2)}, u32[]{:S(2)}) collective-permute-start(bf16[64,256]{1,0:T(8,128)(2,1)S(1)} %copy-done.13), channel_id=1, source_target_pairs={{0,48},{16,64},{32,80},{48,96},{64,112},{80,0},{96,16},{112,32},{1... | collective-permute-start | bytes 98312 | tf_op jit(solution)/shard_map/ppermute | solution.py:496
  149.9 16.6 %collective-permute-start.4 = (bf16[64,256]{1,0:T(8,128)(2,1)S(1)}, bf16[64,256]{1,0:T(8,128)(2,1)S(1)}, u32[]{:S(2)}, u32[]{:S(2)}) collective-permute-start(bf16[64,256]{1,0:T(8,128)(2,1)S(1)} %copy-done.12), channel_id=1, source_target_pairs={{0,64},{16,80},{32,96},{48,112},{64,0},{80,16},{96,32},{112,48},{1... | collective-permute-start | bytes 98312 | tf_op jit(solution)/shard_map/ppermute | solution.py:496
  150.4 16.1 %collective-permute-start.5 = (bf16[64,256]{1,0:T(8,128)(2,1)S(1)}, bf16[64,256]{1,0:T(8,128)(2,1)S(1)}, u32[]{:S(2)}, u32[]{:S(2)}) collective-permute-start(bf16[64,256]{1,0:T(8,128)(2,1)S(1)} %copy-done.11), channel_id=1, source_target_pairs={{0,80},{16,96},{32,112},{48,0},{64,16},{80,32},{96,48},{112,64},{1... | collective-permute-start | bytes 98312 | tf_op jit(solution)/shard_map/ppermute | solution.py:496
  155.4 11.2 %collective-permute-start.6 = (bf16[64,256]{1,0:T(8,128)(2,1)S(1)}, bf16[64,256]{1,0:T(8,128)(2,1)S(1)}, u32[]{:S(2)}, u32[]{:S(2)}) collective-permute-start(bf16[64,256]{1,0:T(8,128)(2,1)S(1)} %copy-done.10), channel_id=1, source_target_pairs={{0,96},{16,112},{32,0},{48,16},{64,32},{80,48},{96,64},{112,80},{1... | collective-permute-start | bytes 98312 | tf_op jit(solution)/shard_map/ppermute | solution.py:496
  158.1 8.5 %collective-permute-start.7 = (bf16[64,256]{1,0:T(8,128)(2,1)S(1)}, bf16[64,256]{1,0:T(8,128)(2,1)S(1)}, u32[]{:S(2)}, u32[]{:S(2)}) collective-permute-start(bf16[64,256]{1,0:T(8,128)(2,1)S(1)} %copy-done.9), channel_id=1, source_target_pairs={{0,112},{16,0},{32,16},{48,32},{64,48},{80,64},{96,80},{112,96},{1... | collective-permute-start | bytes 98312 | tf_op jit(solution)/shard_map/ppermute | solution.py:496
  162.2 34.0 %all-to-all-start.3 = ((bf16[16,64,256]{2,1,0:T(8,128)(2,1)}), bf16[16,64,256]{2,1,0:T(8,128)(2,1)}, u32[]{:S(2)}, u32[]{:S(2)}) async-start(bf16[16,64,256]{2,1,0:T(8,128)(2,1)} %shard_map.127), calls=%async_computation.3 | async-start | bytes 1048576 | tf_op jit(solution)/shard_map/all_to_all | solution.py:516
  166.5 0.6 copy-start.4
  166.5 0.6 copy-start.5
  166.5 0.6 copy-start.6
  166.5 0.6 copy-start.7
  167.1 0.6 copy-start.8
  190.7 8.4 %collective-permute-start.8 = (bf16[64,2048]{1,0:T(8,128)(2,1)}, bf16[64,2048]{1,0:T(8,128)(2,1)}, u32[]{:S(2)}, u32[]{:S(2)}) collective-permute-start(bf16[64,2048]{1,0:T(8,128)(2,1)} %slice_bitcast_fusion), channel_id=1, source_target_pairs={{0,128},{16,144},{32,160},{48,176},{64,192},{80,208},{96,224},{112... | collective-permute-start | bytes 786440 | tf_op jit(solution)/shard_map/ppermute | solution.py:531
Sparse Core Ops, SparseCore 0:
  114.1 74.8 reduce-scatter.1

commit v6 on v5

--- a/solution.py
+++ b/solution.py
@@ -19,7 +19,7 @@
 LANES = 128
 STATS = 16
 STEP = 256
-LATE = 1000
+LATE = 160
 VMEM = 58 * 1024 * 1024
 
 epsilon = 1e-05
@@ -86,7 +86,8 @@
         part = pl.ds(i * STEP, STEP)
         for k, (source, target) in enumerate(((x_hbm, x_ref), (cot_hbm, cot_ref))):
             loads.append(pltpu.make_async_copy(source.at[part], target.at[part], in_sems.at[2 * i + k]))
-    loads[0].start()
+    for copy in loads[:1] + weights[1:] + loads[1:]:
+        copy.start()
 
     def store(base, size):
         part = pl.ds(base, size)
@@ -95,9 +96,6 @@
         stores.append(copy)
 
     weights[0].wait()
-    weights[1].start()
-    for copy in loads[1:]:
-        copy.start()
     turned = [w1_ref[a].T for a in range(2)]
     totals = []
     for i in range(steps):
@@ -312,28 +310,17 @@
     normed_ref[...] = (x_ref[...].astype(F32) * inverse * gain_ref[...]).astype(BF16)
 
 
-def pair_kernel(z_ref, own_ref, other_ref, *out_refs):
-    size = len(out_refs)
-    for k, out_ref in enumerate(out_refs):
-        z = lax.rem(z_ref[0] + k, size)
-        out_ref[...] = (own_ref[z].astype(F32) + other_ref[z].astype(F32)).astype(BF16)
-
-
-def fourth_sum_kernel(scale, *refs):
-    total = refs[0][...].astype(F32)
-    for ref in refs[1:-1]:
-        total = total + ref[...].astype(F32)
-    refs[-1][...] = (total * scale).reshape(refs[-1].shape)
-
-
-def first_kernel(recv_hbm, normed_hbm, out_ref, recv_ref, normed_ref, sems):
+def pair_kernel(first_own, first_other, fourth_own, fourth_other, out_ref):
+    out_ref[:, :PAIR, :] = (first_own[...].astype(F32) + first_other[...].astype(F32)).astype(BF16)
+    out_ref[:, PAIR:, :] = (fourth_own[...].astype(F32) + fourth_other[...].astype(F32)).astype(BF16)
+
+
+def first_kernel(y_ref, recv_hbm, normed_hbm, own_ref, other_ref, recv_ref, normed_ref, sems):
     chunks = normed_ref.shape[0] // LANES
+    z_size = own_ref.shape[0]
     loads = Copies(sems)
-    for a in range(2):
-        feats = pl.ds(a * BS, BS)
-        loads.start(normed_hbm.at[:, feats], normed_ref.at[:, feats])
-    part = pl.ds(0, chunks * PAIR)
-    loads.start(recv_hbm.at[:, part], recv_ref)
+    loads.start(normed_hbm, normed_ref)
+    loads.start(recv_hbm.at[:, pl.ds(0, chunks * PAIR)], recv_ref)
     loads.wait()
     rows = BS // PEERS
     for a in range(2):
@@ -341,8 +328,10 @@
         grad = dot(dfirst, normed_ref[:, a * BS : (a + 1) * BS], NN).astype(BF16).T
         for half in range(2):
             base = (2 * a + half) * rows
-            value = grad[:, half * BS : (half + 1) * BS]
-            out_ref[:, base : base + rows, :] = value.reshape(PEERS, rows, BS)
+            value = grad[:, half * BS : (half + 1) * BS].reshape(PEERS, rows, BS)
+            part = slice(base, base + rows)
+            own_ref[:, part, :] = jnp.where(y_ref[0] == 0, value[:z_size], value[z_size:])
+            other_ref[:, part, :] = jnp.where(y_ref[0] == 0, value[z_size:], value[:z_size])
 
 
 def token_kernel(recv_ref, stats_ref, x_ref, gain_ref, w1_ref, cot_ref, out_ref):
@@ -358,13 +347,14 @@
         out_ref[:, feats] = (cot_ref[:, feats].astype(F32) + inverse * change).astype(BF16)
 
 
-def first_sum_kernel(scale, recv_ref, first_ref):
+def sum_kernel(scale, recv_ref, first_ref, fourth_ref):
     total = jnp.sum(recv_ref[...].astype(F32), axis=0) * scale
     _, rows, _ = first_ref.shape
     for a in range(2):
         for half in range(2):
             base = (2 * a + half) * rows
             first_ref[a, :, half * BS : (half + 1) * BS] = total[base : base + rows]
+    fourth_ref[...] = total[PAIR:].reshape(fourth_ref.shape)
 
 
 def finish_kernel(scale, own_ref, other_ref, second_ref, third_ref):
@@ -382,7 +372,6 @@
     z_groups = [[y * z_size + z for z in range(z_size)] for y in range(2)]
     y_pairs = [(i, (i + z_size) % dp) for i in range(dp)]
     y_index = (lax.axis_index("dp") // z_size).astype(jnp.int32)[None]
-    z_index = (lax.axis_index("dp") % z_size).astype(jnp.int32)[None]
     shape = jax.ShapeDtypeStruct
     hidden_flops = 2 * HBS * HBS * element_count
     model_flops = 2 * local_width * HB * EB * element_count
@@ -481,39 +470,24 @@
         compiler_params=params,
         cost_estimate=cost(model_flops),
     )(y_index, third, cotangent, tokens, gain_row, recv)
-    other = lax.ppermute(other, "dp", y_pairs)
-    block = shape((PAIR, BS), BF16)
-    blocks = pl.pallas_call(
-        pair_kernel,
-        out_shape=[block] * z_size,
-        in_specs=[smem, vmem, vmem],
-        out_specs=[vmem] * z_size,
-        compiler_params=params,
-        cost_estimate=cost(0),
-    )(z_index, own, other)
-    blocks, back = lax.optimization_barrier((blocks, back))
-    blocks = [blocks[0]] + [
-        lax.ppermute(
-            blocks[k], "dp", [(g[z], g[(z + k) % z_size]) for g in z_groups for z in range(z_size)]
-        )
-        for k in range(1, z_size)
-    ]
+    fourths = (own, lax.ppermute(other, "dp", y_pairs))
     output = call(output_kernel, shape(tokens.shape, BF16), (third, tokens, w_fourth), flops=LATE * model_flops)
-    first = shape((PEERS, PAIR, BS), BF16)
-    first = pl.pallas_call(
+    own, other = pl.pallas_call(
         first_kernel,
-        out_shape=first,
-        in_specs=[hbm, hbm],
-        out_specs=vmem,
+        out_shape=[part, part],
+        in_specs=[smem, hbm, hbm],
+        out_specs=[vmem, vmem],
         scratch_shapes=[
             pltpu.VMEM(third_sent.shape, BF16),
             pltpu.VMEM(tokens.shape, BF16),
-            pltpu.SemaphoreType.DMA((3,)),
+            pltpu.SemaphoreType.DMA((2,)),
         ],
         compiler_params=params,
         cost_estimate=cost(model_flops),
-    )(back, normed)
-    first = lax.all_to_all(first, "dp", 0, 0, tiled=True)
+    )(y_index, back, normed)
+    firsts = (own, lax.ppermute(other, "dp", y_pairs))
+    both = call(pair_kernel, shape((z_size, 2 * PAIR, BS), BF16), firsts + fourths)
+    both = lax.all_to_all(both, "dp", 0, 0, axis_index_groups=z_groups, tiled=True)
     token_gradient = pl.pallas_call(
         token_kernel,
         out_shape=shape(tokens.shape, BF16),
@@ -523,11 +497,11 @@
         compiler_params=params,
         cost_estimate=cost(LATE * model_flops),
     )(back, recv, tokens, gain_row, w_first, cotangent)
-    grad_fourth = call(
-        functools.partial(fourth_sum_kernel, scale), shape((2, HB * EB // dp, BS), F32), tuple(blocks)
+    grad_first, grad_fourth = call(
+        functools.partial(sum_kernel, scale),
+        [shape((2, BS // dp, HB * EB), F32), shape((2, HB * EB // dp, BS), F32)],
+        (both,),
     )
-    grad_first = call(functools.partial(first_sum_kernel, scale), shape((2, BS // dp, HB * EB), F32), (first,))
-    hidden, grad_fourth = lax.optimization_barrier((hidden, grad_fourth))
     other = lax.ppermute(hidden[0, 1], "dp", y_pairs)
     part = shape((1, HBS // dp, HBS), F32)
     grad_second, grad_third = call(functools.partial(finish_kernel, scale), [part, part], (hidden, other))

time: 209 us -> 185 us (0.89)
  starting transfers between devices: 53.9 us -> 41.3 us
  waiting for transfers between devices: 74.9 us -> 63.2 us
    reduce_scatter x1, waiting for transfers between devices: 19.7 us -> 0.01 us  [shards(): lax.psum_scatter(hidden, 'dp', scatter_dimension=0, axis_index_groups=z_g...]
    ppermute x8 -> x2, starting transfers between devices: 19.7 us -> 2.6 us  [the longest x1 1.37 us: shards(): firsts = (own, lax.ppermute(other, 'dp', y_pairs))]
    ppermute x8 -> x2, waiting for transfers between devices: 20.8 us -> 4.35 us  [the longest x1 4.34 us: shards(): firsts = (own, lax.ppermute(other, 'dp', y_pairs))]
    all_to_all x1, waiting for transfers between devices: 0.01 us -> 15 us  [shards(): back = lax.all_to_all(send, 'tensor', 0, 0, tiled=True)]
    all_to_all x1, waiting for transfers between devices: 0.01 us -> 10.8 us  [shards(): lax.all_to_all(both, 'dp', 0, 0, axis_index_groups=z_groups, tiled=True)]
    all_to_all x1, starting transfers between devices: 4.25 us -> 8.44 us  [shards(): lax.all_to_all(both, 'dp', 0, 0, axis_index_groups=z_groups, tiled=True)]
    pallas_call x2 -> x1, Pallas kernels: 4.91 us -> 3.14 us  [shards(): pl.pallas_call(first_kernel, out_shape=[part, part], in_specs=[smem, hbm,...]
    unnamed x28 -> x14, local copies, waits for them, and re-layouts: 3.57 us -> 5.13 us
  transfers between devices with their start and end apart: 14 -> 8, of which waited for: 5 -> 5; matrix products, arithmetic and copies ran while one was open for 1% -> 1% of each run, Pallas kernels for 20% -> 23%
where the time goes in v6:
time: 185 us; the launch traced here: 183 us
  waiting for transfers between devices  63.2 us (34%)
  Pallas kernels  57.9 us (31%)
  starting transfers between devices  41.3 us (22%)
  between operations  14.1 us (8%)
  local copies, waits for them, and re-layouts  6.1 us (3%)
    all_to_all x1, waiting for transfers between devices, shards(): recv = lax.all_to_all(send, 'tensor', 0, 0, tiled=True)  32.6 us
    pallas_call x6, Pallas kernels, call(): pl.pallas_call(kernel, out_shape=out_shape, in_specs=[pl.BlockSpec(memory...  19 us
    all_to_all x1, waiting for transfers between devices, shards(): back = lax.all_to_all(send, 'tensor', 0, 0, tiled=True)  15 us
    pallas_call x1, Pallas kernels, shards(): pl.pallas_call(backward_kernel, out_shape=[grads, stepped, shape((1, elem...  13.4 us
    all_to_all x1, starting transfers between devices, shards(): third = lax.all_to_all(send, 'tensor', 0, 0, tiled=True)  12.8 us
    all_to_all x1, waiting for transfers between devices, shards(): lax.all_to_all(both, 'dp', 0, 0, axis_index_groups=z_groups, tiled=True)  10.8 us
    pallas_call x1, Pallas kernels, shards(): pl.pallas_call(forward_kernel, out_shape=[pre_shape, stepped, third_sent]...  9.46 us
    all_to_all x1, starting transfers between devices, shards(): back = lax.all_to_all(send, 'tensor', 0, 0, tiled=True)  8.56 us
  transfers between devices with their start and end apart: 8, of which 5 were waited for; matrix products, arithmetic and copies ran while one was open for 1% of the time, Pallas kernels for 23%

profile of v6, /device:TPU:18, one launch (start us, length us, event | category | flops | bytes accessed | tf_op | source)
XLA Modules:
  0.0 182.5 jit_solution(15410861026544372546)
XLA Ops:
  7.2 4.9 %shard_map.118 = bf16[16,784,128]{2,1,0:T(8,128)(2,1)} custom-call(bf16[768,512]{1,0:T(8,128)(2,1)} %x_ref.5, bf16[768,512]{1,0:T(8,128)(2,1)} %cot_ref.3, f32[1,512]{1,0:T(1,128)} %bitcast.4, bf16[2,256,512]{2,1,0:T(8,128)(2,1)} %w1_ref.1, bf16[2,512,256]{2,1,0:T(8,128)(2,1)} %w4_ref.1), custom_call_target="tpu_custom_call" | custom-call | flops 805306368 | bytes 8388608 | tf_op jit(solution)/shard_map/pallas_call | solution.py:393
  12.1 7.3 %all-to-all-start = ((bf16[16,784,128]{2,1,0:T(8,128)(2,1)}), bf16[16,784,128]{2,1,0:T(8,128)(2,1)S(1)}, u32[]{:S(2)}, u32[]{:S(2)}) async-start(bf16[16,784,128]{2,1,0:T(8,128)(2,1)} %shard_map.118), calls=%async_computation | async-start | bytes 6422528 | tf_op jit(solution)/shard_map/all_to_all | solution.py:410
  19.4 4.9 %shard_map.119 = (bf16[1024,1024]{1,0:T(8,128)(2,1)}, bf16[1024,1024]{1,0:T(8,128)(2,1)}) custom-call(bf16[1,1024,1024]{2,1,0:T(8,128)(2,1)} %w2_ref.3, bf16[1,1024,1024]{2,1,0:T(8,128)(2,1)} %w3_hbm.1), custom_call_target="tpu_custom_call" | custom-call | bytes 8388608 | tf_op jit(solution)/shard_map/pallas_call | solution.py:47
  24.2 32.6 %all-to-all-done.recv_hbm.stats_ref = bf16[16,784,128]{2,1,0:T(8,128)(2,1)S(1)} async-done(((bf16[16,784,128]{2,1,0:T(8,128)(2,1)}), bf16[16,784,128]{2,1,0:T(8,128)(2,1)S(1)}, u32[]{:S(2)}, u32[]{:S(2)}) %all-to-all-start) | async-done | bytes 3211296 | tf_op jit(solution)/shard_map/all_to_all | solution.py:410
  56.8 0.0 copy-start
  56.8 1.6 copy-done
  58.4 9.5 %shard_map.120 = (f32[3,1024,256]{2,1,0:T(8,128)}, bf16[3,1024,256]{2,1,0:T(8,128)(2,1)}, bf16[16,384,128]{2,1,0:T(8,128)(2,1)}) custom-call(bf16[16,784,128]{2,1,0:T(8,128)(2,1)} %copy-done, bf16[1024,1024]{1,0:T(8,128)(2,1)} %get-tuple-element.25.w2t_hbm, bf16[1024,1024]{1,0:T(8,128)(2,1)} %get-tuple-element.26.w3t_hbm), custom_call_target="tpu_custom_call" | custom-call | flops 3221225472 | bytes 8388608 | tf_op jit(solution)/shard_map/pallas_call | solution.py:416
  67.9 12.8 %all-to-all-start.1 = ((bf16[16,384,128]{2,1,0:T(8,128)(2,1)}), bf16[16,384,128]{2,1,0:T(8,128)(2,1)S(1)}, u32[]{:S(2)}, u32[]{:S(2)}) async-start(bf16[16,384,128]{2,1,0:T(8,128)(2,1)} %get-tuple-element.31), calls=%async_computation.1 | async-start | bytes 3145728 | tf_op jit(solution)/shard_map/all_to_all | solution.py:434
  80.7 0.2 reduce-scatter.2.cloned.1.call-start
  81.0 13.4 %shard_map.121 = (bf16[8,2,64,2048]{3,2,1,0:T(8,128)(2,1)}, bf16[3,1024,256]{2,1,0:T(8,128)(2,1)}, f32[1,768]{1,0:T(1,128)}) custom-call(s32[1]{0:T(128)} %bitcast.y_ref, bf16[16,784,128]{2,1,0:T(8,128)(2,1)} %copy-done, f32[3,1024,256]{2,1,0:T(8,128)} %get-tuple-element.27.pre_hbm, bf16[3,1024,256]{2,1,0:T(8,128)(2,1)} %get-tuple-element.28.act_hbm, ...), custom_call_target="tpu_custom_call" | custom-call | flops 4831838208 | bytes 8388608 | tf_op jit(solution)/shard_map/pallas_call | solution.py:436
  94.4 0.0 reduce-scatter.2.cloned.1.call-update
  94.4 5.1 %shard_map.122 = bf16[16,400,128]{2,1,0:T(8,128)(2,1)} custom-call(bf16[3,1024,256]{2,1,0:T(8,128)(2,1)} %get-tuple-element.29.dpre_ref, f32[1,768]{1,0:T(1,128)} %get-tuple-element.30.inner_ref, bf16[1,1024,1024]{2,1,0:T(8,128)(2,1)} %w2_ref.3), custom_call_target="tpu_custom_call" | custom-call | flops 1610612736 | bytes 5311488 | tf_op jit(solution)/shard_map/pallas_call | solution.py:47
  99.5 0.3 all-to-all-done.1.recv_ref
  99.8 0.0 copy-start.2
  99.8 8.6 %all-to-all-start.2 = ((bf16[16,400,128]{2,1,0:T(8,128)(2,1)}), bf16[16,400,128]{2,1,0:T(8,128)(2,1)S(1)}, u32[]{:S(2)}, u32[]{:S(2)}) async-start(bf16[16,400,128]{2,1,0:T(8,128)(2,1)} %shard_map.122), calls=%async_computation.2 | async-start | bytes 3276800 | tf_op jit(solution)/shard_map/all_to_all | solution.py:458
  108.4 0.0 copy-done.2
  108.4 3.6 %shard_map.125 = (bf16[8,64,256]{2,1,0:T(8,128)(2,1)}, bf16[8,64,256]{2,1,0:T(8,128)(2,1)}, bf16[768,512]{1,0:T(8,128)(2,1)}) custom-call(s32[1]{0:T(128)} %bitcast.y_ref, bf16[16,384,128]{2,1,0:T(8,128)(2,1)} %copy-done.2, bf16[768,512]{1,0:T(8,128)(2,1)} %cot_ref.3, bf16[768,512]{1,0:T(8,128)(2,1)} %x_ref.5, f32[1,512]{1,0:T(1,128)} %bitcast.5, ...), custom_call_target="tpu_custom_call" | custom-call | flops 402653184 | bytes 8388608 | tf_op jit(solution)/shard_map/pallas_call | solution.py:464
  112.0 1.2 collective-permute-start.1
  113.3 15.0 %all-to-all-done.2.recv_ref.recv_hbm = bf16[16,400,128]{2,1,0:T(8,128)(2,1)S(1)} async-done(((bf16[16,400,128]{2,1,0:T(8,128)(2,1)}), bf16[16,400,128]{2,1,0:T(8,128)(2,1)S(1)}, u32[]{:S(2)}, u32[]{:S(2)}) %all-to-all-start.2) | async-done | bytes 1638432 | tf_op jit(solution)/shard_map/all_to_all | solution.py:458
  128.3 0.0 copy-start.1
  128.3 1.3 copy-done.1
  129.6 3.1 %shard_map.126 = (bf16[8,64,256]{2,1,0:T(8,128)(2,1)}, bf16[8,64,256]{2,1,0:T(8,128)(2,1)}) custom-call(s32[1]{0:T(128)} %bitcast.y_ref, bf16[16,400,128]{2,1,0:T(8,128)(2,1)} %copy-done.1, bf16[768,512]{1,0:T(8,128)(2,1)} %get-tuple-element.34.normed_hbm), custom_call_target="tpu_custom_call" | custom-call | flops 402653184 | bytes 8388608 | tf_op jit(solution)/shard_map/pallas_call | solution.py:475
  132.7 1.4 collective-permute-start
  134.1 3.3 %shard_map.123 = bf16[768,512]{1,0:T(8,128)(2,1)} custom-call(bf16[16,384,128]{2,1,0:T(8,128)(2,1)} %copy-done.2, bf16[768,512]{1,0:T(8,128)(2,1)} %x_ref.5, bf16[2,512,256]{2,1,0:T(8,128)(2,1)} %w4_ref.1), custom_call_target="tpu_custom_call" | custom-call | flops 64424509440 | bytes 3670016 | tf_op jit(solution)/shard_map/pallas_call | solution.py:47
  137.4 0.0 collective-permute-done.1.fourth_other
  137.4 0.0 copy-start.5
  137.4 4.3 %collective-permute-done.first_other = bf16[8,64,256]{2,1,0:T(8,128)(2,1)S(1)} collective-permute-done((bf16[8,64,256]{2,1,0:T(8,128)(2,1)}, bf16[8,64,256]{2,1,0:T(8,128)(2,1)S(1)}, u32[]{:S(2)}, u32[]{:S(2)}) %collective-permute-start) | collective-permute-done | bytes 262176 | tf_op jit(solution)/shard_map/ppermute | solution.py:488
  141.7 0.0 copy-start.6
  141.7 0.0 copy-done.5
  141.7 0.7 copy-done.6
  142.4 2.1 %shard_map.127 = bf16[8,128,256]{2,1,0:T(8,128)(2,1)} custom-call(bf16[8,64,256]{2,1,0:T(8,128)(2,1)} %get-tuple-element.35.first_own, bf16[8,64,256]{2,1,0:T(8,128)(2,1)} %copy-done.6, bf16[8,64,256]{2,1,0:T(8,128)(2,1)} %get-tuple-element.37.fourth_own, bf16[8,64,256]{2,1,0:T(8,128)(2,1)} %copy-done.5), custom_call_target="tpu_custom_call" | custom-call | bytes 1572864 | tf_op jit(solution)/shard_map/pallas_call | solution.py:47
  144.5 8.4 %all-to-all-start.3 = ((bf16[8,128,256]{2,1,0:T(8,128)(2,1)}), bf16[8,128,256]{2,1,0:T(8,128)(2,1)S(1)}, u32[]{:S(2)}, u32[]{:S(2)}) async-start(bf16[8,128,256]{2,1,0:T(8,128)(2,1)} %shard_map.127), calls=%async_computation.3 | async-start | bytes 1048576 | tf_op jit(solution)/shard_map/all_to_all | solution.py:490
  153.0 0.0 reduce-scatter.2.cloned.1.call-done.own_ref
  153.0 1.0 slice_bitcast_fusion
  154.0 1.4 collective-permute-start.2
  155.3 4.3 %shard_map.124 = bf16[768,512]{1,0:T(8,128)(2,1)} custom-call(bf16[16,400,128]{2,1,0:T(8,128)(2,1)} %copy-done.1, bf16[16,784,128]{2,1,0:T(8,128)(2,1)} %copy-done, bf16[768,512]{1,0:T(8,128)(2,1)} %x_ref.5, f32[1,512]{1,0:T(1,128)} %bitcast.6, bf16[2,256,512]{2,1,0:T(8,128)(2,1)} %w1_ref.1, bf16[768,512]{1,0:T(8,128)(2,1)} %cot_ref.3), custom_call_target="tpu_custom_call" | custom-call | flops 64424509440 | bytes 8388608 | tf_op jit(solution)/shard_map/pallas_call | solution.py:491
  159.6 10.8 %all-to-all-done.3.recv_ref = bf16[8,128,256]{2,1,0:T(8,128)(2,1)S(1)} async-done(((bf16[8,128,256]{2,1,0:T(8,128)(2,1)}), bf16[8,128,256]{2,1,0:T(8,128)(2,1)S(1)}, u32[]{:S(2)}, u32[]{:S(2)}) %all-to-all-start.3) | async-done | bytes 524320 | tf_op jit(solution)/shard_map/all_to_all | solution.py:490
  170.5 0.0 copy-start.3
  170.5 0.8 copy-done.3
  171.3 1.7 shard_map.128
  173.0 0.0 collective-permute-done.2.other_ref
  173.0 0.0 copy-start.4
  173.0 0.7 copy-done.4
  173.7 1.9 %shard_map.129 = (f32[1,64,1024]{2,1,0:T(8,128)}, f32[1,64,1024]{2,1,0:T(8,128)}) custom-call(bf16[1,2,64,2048]{3,2,1,0:T(8,128)(2,1)} %reduce-scatter.2.cloned.1.call-done.own_ref, bf16[64,2048]{1,0:T(8,128)(2,1)} %copy-done.4), custom_call_target="tpu_custom_call" | custom-call | bytes 1310720 | tf_op jit(solution)/shard_map/pallas_call | solution.py:47
Async XLA Ops:
  12.1 44.7 %all-to-all-start = ((bf16[16,784,128]{2,1,0:T(8,128)(2,1)}), bf16[16,784,128]{2,1,0:T(8,128)(2,1)S(1)}, u32[]{:S(2)}, u32[]{:S(2)}) async-start(bf16[16,784,128]{2,1,0:T(8,128)(2,1)} %shard_map.118), calls=%async_computation | async-start | bytes 6422528 | tf_op jit(solution)/shard_map/all_to_all | solution.py:410
  56.8 1.7 copy-start
  67.9 31.9 %all-to-all-start.1 = ((bf16[16,384,128]{2,1,0:T(8,128)(2,1)}), bf16[16,384,128]{2,1,0:T(8,128)(2,1)S(1)}, u32[]{:S(2)}, u32[]{:S(2)}) async-start(bf16[16,384,128]{2,1,0:T(8,128)(2,1)} %get-tuple-element.31), calls=%async_computation.1 | async-start | bytes 3145728 | tf_op jit(solution)/shard_map/all_to_all | solution.py:434
  80.7 72.3 %reduce-scatter.2.cloned.1.call-start = ((), (), s32[]{:S(2)}) async-start(), calls=%async_computation.5 | async-start | bytes 4718592 | tf_op jit(solution)/shard_map/reduce_scatter | solution.py:455
  99.8 8.6 %copy-start.2 = (bf16[16,384,128]{2,1,0:T(8,128)(2,1)}, bf16[16,384,128]{2,1,0:T(8,128)(2,1)S(1)}, u32[]{:S(2)}) copy-start(bf16[16,384,128]{2,1,0:T(8,128)(2,1)S(1)} %all-to-all-done.1.recv_ref) | copy-start | bytes 4718596
  99.8 28.5 %all-to-all-start.2 = ((bf16[16,400,128]{2,1,0:T(8,128)(2,1)}), bf16[16,400,128]{2,1,0:T(8,128)(2,1)S(1)}, u32[]{:S(2)}, u32[]{:S(2)}) async-start(bf16[16,400,128]{2,1,0:T(8,128)(2,1)} %shard_map.122), calls=%async_computation.2 | async-start | bytes 3276800 | tf_op jit(solution)/shard_map/all_to_all | solution.py:458
  112.0 25.4 %collective-permute-start.1 = (bf16[8,64,256]{2,1,0:T(8,128)(2,1)}, bf16[8,64,256]{2,1,0:T(8,128)(2,1)S(1)}, u32[]{:S(2)}, u32[]{:S(2)}) collective-permute-start(bf16[8,64,256]{2,1,0:T(8,128)(2,1)} %get-tuple-element.38), channel_id=1, source_target_pairs={{0,128},{16,144},{32,160},{48,176},{64,192},{80,208},{96,224},{112... | collective-permute-start | bytes 786440 | tf_op jit(solution)/shard_map/ppermute | solution.py:473
  128.3 1.3 copy-start.1
  132.7 9.0 %collective-permute-start = (bf16[8,64,256]{2,1,0:T(8,128)(2,1)}, bf16[8,64,256]{2,1,0:T(8,128)(2,1)S(1)}, u32[]{:S(2)}, u32[]{:S(2)}) collective-permute-start(bf16[8,64,256]{2,1,0:T(8,128)(2,1)} %get-tuple-element.36), channel_id=1, source_target_pairs={{0,128},{16,144},{32,160},{48,176},{64,192},{80,208},{96,224},{112... | collective-permute-start | bytes 786440 | tf_op jit(solution)/shard_map/ppermute | solution.py:488
  137.4 4.4 %copy-start.5 = (bf16[8,64,256]{2,1,0:T(8,128)(2,1)}, bf16[8,64,256]{2,1,0:T(8,128)(2,1)S(1)}, u32[]{:S(2)}) copy-start(bf16[8,64,256]{2,1,0:T(8,128)(2,1)S(1)} %collective-permute-done.1.fourth_other) | copy-start | bytes 786436
  141.7 0.7 copy-start.6
  144.5 25.9 %all-to-all-start.3 = ((bf16[8,128,256]{2,1,0:T(8,128)(2,1)}), bf16[8,128,256]{2,1,0:T(8,128)(2,1)S(1)}, u32[]{:S(2)}, u32[]{:S(2)}) async-start(bf16[8,128,256]{2,1,0:T(8,128)(2,1)} %shard_map.127), calls=%async_computation.3 | async-start | bytes 1048576 | tf_op jit(solution)/shard_map/all_to_all | solution.py:490
  154.0 19.1 %collective-permute-start.2 = (bf16[64,2048]{1,0:T(8,128)(2,1)S(1)}, bf16[64,2048]{1,0:T(8,128)(2,1)S(1)}, u32[]{:S(2)}, u32[]{:S(2)}) collective-permute-start(bf16[64,2048]{1,0:T(8,128)(2,1)S(1)} %slice_bitcast_fusion), channel_id=1, source_target_pairs={{0,128},{16,144},{32,160},{48,176},{64,192},{80,208},{96,224},{112... | collective-permute-start | bytes 786440 | tf_op jit(solution)/shard_map/ppermute | solution.py:505
  170.5 0.8 copy-start.3
  173.0 0.7 copy-start.4
Sparse Core Ops, SparseCore 0:
  94.5 58.0 reduce-scatter.1

commit v7 on v6

--- a/solution.py
+++ b/solution.py
@@ -71,37 +71,34 @@
     return jnp.sum(rows.astype(F32), axis=0)
 
 
-def head_kernel(
-    x_hbm, cot_hbm, gain_ref, w1_hbm, w4_hbm, out_hbm, x_ref, cot_ref, w1_ref, w4_ref, out_ref, in_sems, out_sems
-):
+class Copies:
+    def __init__(self, sems):
+        self.sems = sems
+        self.started = []
+
+    def start(self, source, target):
+        copy = pltpu.make_async_copy(source, target, self.sems.at[len(self.started)])
+        copy.start()
+        self.started.append(copy)
+        return copy
+
+    def wait(self):
+        for copy in self.started:
+            copy.wait()
+
+
+def head_kernel(x_hbm, gain_ref, w1_hbm, out_hbm, x_ref, w1_ref, out_ref, in_sems, out_sems):
     steps = x_ref.shape[0] // STEP
-    rows = steps * 2 * PAIR
-    loads, stores = [], []
-    weights = [
-        pltpu.make_async_copy(source, target, in_sems.at[2 * steps + k])
-        for k, (source, target) in enumerate(((w1_hbm, w1_ref), (w4_hbm, w4_ref)))
-    ]
-    weights[0].start()
-    for i in range(steps):
-        part = pl.ds(i * STEP, STEP)
-        for k, (source, target) in enumerate(((x_hbm, x_ref), (cot_hbm, cot_ref))):
-            loads.append(pltpu.make_async_copy(source.at[part], target.at[part], in_sems.at[2 * i + k]))
-    for copy in loads[:1] + weights[1:] + loads[1:]:
-        copy.start()
-
-    def store(base, size):
-        part = pl.ds(base, size)
-        copy = pltpu.make_async_copy(out_ref.at[:, part], out_hbm.at[:, part], out_sems.at[len(stores)])
-        copy.start()
-        stores.append(copy)
-
-    weights[0].wait()
+    loads, stores = Copies(in_sems), Copies(out_sems)
+    w1_load = loads.start(w1_hbm, w1_ref)
+    parts = [pl.ds(i * STEP, STEP) for i in range(steps)]
+    x_loads = [loads.start(x_hbm.at[part], x_ref.at[part]) for part in parts]
+    w1_load.wait()
     turned = [w1_ref[a].T for a in range(2)]
     totals = []
     for i in range(steps):
-        part = slice(i * STEP, (i + 1) * STEP)
-        loads[2 * i].wait()
-        x = x_ref[part, :].astype(F32)
+        x_loads[i].wait()
+        x = x_ref[parts[i], :].astype(F32)
         scaled = (x * gain_ref[...]).astype(BF16)
         base = i * 2 * PAIR
         for a in range(2):
@@ -110,27 +107,29 @@
                 start = base + k * PAIR + a * EB
                 value = first[:, k * LANES : (k + 1) * LANES]
                 out_ref[:, start : start + EB, :] = value.reshape(PEERS, EB, LANES)
-        store(base, 2 * PAIR)
-        loads[2 * i + 1].wait()
-        if i == 0:
-            weights[1].wait()
-        for a in range(2):
-            dgathered = dot(w4_ref[a], cot_ref[part, a * BS : (a + 1) * BS], NT).astype(BF16)
-            for k in range(2):
-                start = rows + base + k * PAIR + a * EB
-                value = dgathered[:, k * LANES : (k + 1) * LANES]
-                out_ref[:, start : start + EB, :] = value.reshape(PEERS, EB, LANES)
-        store(rows + base, 2 * PAIR)
+        part = pl.ds(base, 2 * PAIR)
+        stores.start(out_ref.at[:, part], out_hbm.at[:, part])
         squares = x * x
         folded = squares[:, :LANES]
         for k in range(1, squares.shape[1] // LANES):
             folded = folded + squares[:, k * LANES : (k + 1) * LANES]
         totals.append(jnp.sum(folded.T, axis=0, keepdims=True))
+    rows = steps * 2 * PAIR
     stats = stat_rows(jnp.concatenate(totals, axis=1), 2 * steps)
-    out_ref[:, 2 * rows :, :] = jnp.broadcast_to(stats[None], (PEERS, STATS, LANES))
-    store(2 * rows, STATS)
-    for copy in stores:
-        copy.wait()
+    out_ref[:, rows:, :] = jnp.broadcast_to(stats[None], (PEERS, STATS, LANES))
+    part = pl.ds(rows, STATS)
+    stores.start(out_ref.at[:, part], out_hbm.at[:, part])
+    stores.wait()
+
+
+def dgathered_kernel(w4_ref, cot_ref, out_ref):
+    chunks = cot_ref.shape[0] // LANES
+    for a in range(2):
+        dgathered = dot(w4_ref[a], cot_ref[:, a * BS : (a + 1) * BS], NT).astype(BF16)
+        for i in range(chunks):
+            start = i * PAIR + a * EB
+            value = dgathered[:, i * LANES : (i + 1) * LANES]
+            out_ref[:, start : start + EB, :] = value.reshape(PEERS, EB, LANES)
 
 
 def reciprocal(stats, i):
@@ -155,22 +154,6 @@
 def by_peer(value):
     parts = [value[:, k * LANES : (k + 1) * LANES].reshape(PEERS, PAIR, LANES) for k in range(2)]
     return jnp.concatenate(parts, axis=1)
-
-
-class Copies:
-    def __init__(self, sems):
-        self.sems = sems
-        self.started = []
-
-    def start(self, source, target):
-        copy = pltpu.make_async_copy(source, target, self.sems.at[len(self.started)])
-        copy.start()
-        self.started.append(copy)
-        return copy
-
-    def wait(self):
-        for copy in self.started:
-            copy.wait()
 
 
 def forward_kernel(
@@ -181,8 +164,8 @@
     rows = steps * 2 * PAIR
     loads, stores = Copies(in_sems), Copies(out_sems)
     parts = [pl.ds(i * 2 * PAIR, 2 * PAIR) for i in range(steps)]
-    rest = pl.ds(2 * rows, STATS)
-    stats_load = loads.start(recv_hbm.at[:, rest], recv_ref.at[:, pl.ds(rows, STATS)])
+    rest = pl.ds(rows, STATS)
+    stats_load = loads.start(recv_hbm.at[:, rest], recv_ref.at[:, rest])
     row_loads = [loads.start(recv_hbm.at[:, parts[0]], recv_ref.at[:, parts[0]])]
     w2t_load = loads.start(w2t_hbm, w2t_ref)
     for part in parts[1:]:
@@ -199,41 +182,39 @@
         hyper = jnp.tanh(pre * (root_scale + (root_scale * cubic_term) * (pre * pre)))
         half = 0.5 * pre
         act_ref[i] = (half + half * hyper).astype(BF16)
+    stores.start(act_ref, act_hbm)
     w3t_load.wait()
     for i in range(steps):
         third = dot(w3t_ref[...], act_ref[i], NN).astype(BF16)
         out_ref[:, i * 2 * PAIR : (i + 1) * 2 * PAIR, :] = by_peer(third)
         stores.start(out_ref.at[:, parts[i]], out_hbm.at[:, parts[i]])
-    stores.start(act_ref, act_hbm)
     stores.wait()
 
 
 def backward_kernel(
-    y_ref, recv_hbm, pre_hbm, act_hbm, w3_hbm, grads_hbm, dpre_hbm, inner_ref,
-    recv_ref, pre_ref, act_ref, w3_ref, dpre_ref, scaled_ref, grads_ref, in_sems, out_sems,
+    y_ref, recv_hbm, dthird_hbm, pre_hbm, act_hbm, w3_hbm, grads_hbm, dpre_hbm, inner_ref,
+    recv_ref, dthird_ref, pre_ref, act_ref, w3_ref, dpre_ref, scaled_ref, grads_ref, in_sems, out_sems,
 ):
     steps = act_ref.shape[0]
     rows = steps * 2 * PAIR
     y = y_ref[0]
     loads, stores = Copies(in_sems), Copies(out_sems)
 
-    def load_rows(base, size):
-        part = pl.ds(base, size)
-        return loads.start(recv_hbm.at[:, part], recv_ref.at[:, part])
-
-    stats_load = load_rows(2 * rows, STATS)
+    parts = [pl.ds(i * 2 * PAIR, 2 * PAIR) for i in range(steps)]
+    rest = pl.ds(rows, STATS)
+    stats_load = loads.start(recv_hbm.at[:, rest], recv_ref.at[:, rest])
     w3_load = loads.start(w3_hbm, w3_ref)
-    third_loads = [load_rows(rows + i * 2 * PAIR, 2 * PAIR) for i in range(steps)]
+    third_loads = [loads.start(dthird_hbm.at[:, part], dthird_ref.at[:, part]) for part in parts]
     pre_loads = [loads.start(pre_hbm.at[i], pre_ref.at[i]) for i in range(steps)]
     act_load = loads.start(act_hbm, act_ref)
-    mixed_load = load_rows(0, rows)
+    mixed_load = loads.start(recv_hbm.at[:, pl.ds(0, rows)], recv_ref.at[:, pl.ds(0, rows)])
     stats_load.wait()
-    stats = stat_sum(recv_ref[:, 2 * rows :, :])
+    stats = stat_sum(recv_ref[:, rows:, :])
     w3_load.wait()
     for i in range(steps):
         third_loads[i].wait()
         pre_loads[i].wait()
-        dact = dot(w3_ref[0], hidden_rows(recv_ref.at[:, pl.ds(rows + i * 2 * PAIR, 2 * PAIR)]), NN)
+        dact = dot(w3_ref[0], hidden_rows(dthird_ref.at[:, parts[i]]), NN)
         pre = pre_ref[i]
         square = pre * pre
         hyper = jnp.tanh(pre * (root_scale + (root_scale * cubic_term) * square))
@@ -246,7 +227,7 @@
         scaled_ref[i] = (dpre * reciprocal(stats, i)).astype(BF16)
     act_load.wait()
     mixed_load.wait()
-    dthird = hidden_rows(recv_ref.at[:, pl.ds(rows, rows)])
+    dthird = hidden_rows(dthird_ref)
     scaled = jnp.concatenate([scaled_ref[i] for i in range(steps)], axis=1)
     z_size, y_size, part_rows, _ = grads_ref.shape
     half = z_size // 2
@@ -377,7 +358,8 @@
     model_flops = 2 * local_width * HB * EB * element_count
     steps = element_count // STEP
     rows = steps * 2 * PAIR
-    sent = shape((PEERS, 2 * rows + STATS, LANES), BF16)
+    plain_sent = shape((PEERS, rows, LANES), BF16)
+    stats_sent = shape((PEERS, rows + STATS, LANES), BF16)
     stepped = shape((steps, HBS, STEP), BF16)
     hbm = pl.BlockSpec(memory_space=pltpu.HBM)
     vmem = pl.BlockSpec(memory_space=pltpu.VMEM)
@@ -390,56 +372,58 @@
     def whole(*dims):
         return pl.BlockSpec(dims, lambda i, *_: (0,) * len(dims))
 
+    def exchange(value):
+        return lax.all_to_all(value, "tensor", 0, 0, tiled=True)
+
     send = pl.pallas_call(
         head_kernel,
-        out_shape=sent,
-        in_specs=[hbm, hbm, vmem, hbm, hbm],
+        out_shape=stats_sent,
+        in_specs=[hbm, vmem, hbm],
         out_specs=hbm,
         scratch_shapes=[
             pltpu.VMEM(tokens.shape, BF16),
-            pltpu.VMEM(tokens.shape, BF16),
             pltpu.VMEM(w_first.shape, BF16),
-            pltpu.VMEM(w_fourth.shape, BF16),
-            pltpu.VMEM(sent.shape, BF16),
-            pltpu.SemaphoreType.DMA((2 * steps + 2,)),
-            pltpu.SemaphoreType.DMA((2 * steps + 1,)),
+            pltpu.VMEM(stats_sent.shape, BF16),
+            pltpu.SemaphoreType.DMA((steps + 1,)),
+            pltpu.SemaphoreType.DMA((steps + 1,)),
         ],
         compiler_params=params,
-        cost_estimate=cost(2 * model_flops),
-    )(tokens, cotangent, gain_row, w_first, w_fourth)
-    recv = lax.all_to_all(send, "tensor", 0, 0, tiled=True)
+        cost_estimate=cost(model_flops),
+    )(tokens, gain_row, w_first)
+    recv = exchange(send)
+    send = call(dgathered_kernel, plain_sent, (w_fourth, cotangent), flops=model_flops)
+    dthird = exchange(lax.optimization_barrier((send, recv))[0])
     turned = shape((HBS, HBS), BF16)
     w_second_t, w_third_t = call(turn_kernel, [turned, turned], (w_second, w_third))
-    third_sent = shape((PEERS, rows, LANES), BF16)
-    back_sent = shape((PEERS, rows + STATS, LANES), BF16)
     pre_shape = shape(stepped.shape, F32)
     pre, act, send = pl.pallas_call(
         forward_kernel,
-        out_shape=[pre_shape, stepped, third_sent],
+        out_shape=[pre_shape, stepped, plain_sent],
         in_specs=[hbm] * 3,
         out_specs=[hbm] * 3,
         scratch_shapes=[
-            pltpu.VMEM(back_sent.shape, BF16),
+            pltpu.VMEM(stats_sent.shape, BF16),
             pltpu.VMEM(turned.shape, BF16),
             pltpu.VMEM(turned.shape, BF16),
             pltpu.VMEM(stepped.shape, F32),
             pltpu.VMEM(stepped.shape, BF16),
-            pltpu.VMEM(third_sent.shape, BF16),
+            pltpu.VMEM(plain_sent.shape, BF16),
             pltpu.SemaphoreType.DMA((steps + 3,)),
             pltpu.SemaphoreType.DMA((2 * steps + 1,)),
         ],
         compiler_params=params,
         cost_estimate=cost(2 * hidden_flops),
     )(recv, w_second_t, w_third_t)
-    third = lax.all_to_all(send, "tensor", 0, 0, tiled=True)
+    third = exchange(lax.optimization_barrier((send, dthird))[0])
     grads = shape((z_size, 2, HBS // dp, 2 * HBS), BF16)
     hidden, dpre, inner = pl.pallas_call(
         backward_kernel,
         out_shape=[grads, stepped, shape((1, element_count), F32)],
-        in_specs=[smem] + [hbm] * 4,
+        in_specs=[smem] + [hbm] * 5,
         out_specs=[hbm, hbm, vmem],
         scratch_shapes=[
-            pltpu.VMEM(sent.shape, BF16),
+            pltpu.VMEM(stats_sent.shape, BF16),
+            pltpu.VMEM(plain_sent.shape, BF16),
             pltpu.VMEM(stepped.shape, F32),
             pltpu.VMEM(stepped.shape, BF16),
             pltpu.VMEM(w_third.shape, BF16),
@@ -451,13 +435,13 @@
         ],
         compiler_params=params,
         cost_estimate=cost(3 * hidden_flops),
-    )(y_index, recv, pre, act, w_third)
+    )(y_index, recv, dthird, pre, act, w_third)
     hidden = lax.psum_scatter(hidden, "dp", scatter_dimension=0, axis_index_groups=z_groups, tiled=True)
-    send = call(dmixed_kernel, back_sent, (dpre, inner, w_second), flops=hidden_flops)
+    send = call(dmixed_kernel, stats_sent, (dpre, inner, w_second), flops=hidden_flops)
     send, third = lax.optimization_barrier((send, third))
-    back = lax.all_to_all(send, "tensor", 0, 0, tiled=True)
-
-    stats_spec = pl.BlockSpec((PEERS, STATS, LANES), lambda i: (0, 2 * rows // STATS, 0))
+    back = exchange(send)
+
+    stats_spec = pl.BlockSpec((PEERS, STATS, LANES), lambda i: (0, rows // STATS, 0))
     all_tokens = whole(*tokens.shape)
     row = whole(1, local_width)
     part = shape((z_size, PAIR, BS), BF16)
@@ -465,7 +449,7 @@
         fourth_kernel,
         out_shape=[part, part, shape(tokens.shape, BF16)],
         grid=(1,),
-        in_specs=[smem, whole(*third_sent.shape), all_tokens, all_tokens, row, stats_spec],
+        in_specs=[smem, whole(*plain_sent.shape), all_tokens, all_tokens, row, stats_spec],
         out_specs=[whole(*part.shape), whole(*part.shape), all_tokens],
         compiler_params=params,
         cost_estimate=cost(model_flops),
@@ -478,7 +462,7 @@
         in_specs=[smem, hbm, hbm],
         out_specs=[vmem, vmem],
         scratch_shapes=[
-            pltpu.VMEM(third_sent.shape, BF16),
+            pltpu.VMEM(plain_sent.shape, BF16),
             pltpu.VMEM(tokens.shape, BF16),
             pltpu.SemaphoreType.DMA((2,)),
         ],
@@ -492,19 +476,20 @@
         token_kernel,
         out_shape=shape(tokens.shape, BF16),
         grid=(1,),
-        in_specs=[whole(*back_sent.shape), stats_spec, all_tokens, row, whole(*w_first.shape), all_tokens],
+        in_specs=[whole(*stats_sent.shape), stats_spec, all_tokens, row, whole(*w_first.shape), all_tokens],
         out_specs=all_tokens,
         compiler_params=params,
         cost_estimate=cost(LATE * model_flops),
     )(back, recv, tokens, gain_row, w_first, cotangent)
+    other = lax.ppermute(hidden[0, 1], "dp", y_pairs)
+    part = shape((1, HBS // dp, HBS), F32)
+    grad_second, grad_third = call(functools.partial(finish_kernel, scale), [part, part], (hidden, other))
+    both, grad_second, grad_third = lax.optimization_barrier((both, grad_second, grad_third))
     grad_first, grad_fourth = call(
         functools.partial(sum_kernel, scale),
         [shape((2, BS // dp, HB * EB), F32), shape((2, HB * EB // dp, BS), F32)],
         (both,),
     )
-    other = lax.ppermute(hidden[0, 1], "dp", y_pairs)
-    part = shape((1, HBS // dp, HBS), F32)
-    grad_second, grad_third = call(functools.partial(finish_kernel, scale), [part, part], (hidden, other))
     return output, token_gradient, grad_first, grad_second, grad_third, grad_fourth
 
 

time: 185 us -> 177 us (0.957)
  waiting for transfers between devices: 63.2 us -> 50.3 us
  starting transfers between devices: 41.3 us -> 45.7 us
    all_to_all x3 -> x4, waiting for transfers between devices: 48 us -> 37.7 us  [exchange(): return lax.all_to_all(value, 'tensor', 0, 0, tiled=True)]
    all_to_all x1, waiting for transfers between devices: 10.8 us -> 6 us  [shards(): lax.all_to_all(both, 'dp', 0, 0, axis_index_groups=z_groups, tiled=True)]
    all_to_all x3 -> x4, starting transfers between devices: 28.7 us -> 33 us  [exchange(): return lax.all_to_all(value, 'tensor', 0, 0, tiled=True)]
    pallas_call x6 -> x7, Pallas kernels: 19 us -> 22.1 us  [call(): pl.pallas_call(kernel, out_shape=out_shape, in_specs=[pl.BlockSpec(memory...]
    ppermute x1, waiting for transfers between devices: 0.01 us -> 2.23 us  [shards(): other = lax.ppermute(hidden[0, 1], 'dp', y_pairs)]
    unnamed x14 -> x16, local copies, waits for them, and re-layouts: 5.13 us -> 4.6 us
  transfers between devices with their start and end apart: 8 -> 9, of which waited for: 5 -> 7; matrix products, arithmetic and copies ran while one was open for 1% -> 1% of each run, Pallas kernels for 23% -> 31%
where the time goes in v7:
time: 177 us; the launch traced here: 175 us
  Pallas kernels  59.1 us (33%)
  waiting for transfers between devices  50.3 us (28%)
  starting transfers between devices  45.7 us (26%)
  between operations  14.1 us (8%)
  local copies, waits for them, and re-layouts  5.57 us (3%)
    all_to_all x4, waiting for transfers between devices, exchange(): return lax.all_to_all(value, 'tensor', 0, 0, tiled=True)  37.7 us
    all_to_all x4, starting transfers between devices, exchange(): return lax.all_to_all(value, 'tensor', 0, 0, tiled=True)  33 us
    pallas_call x7, Pallas kernels, call(): pl.pallas_call(kernel, out_shape=out_shape, in_specs=[pl.BlockSpec(memory...  22.1 us
    pallas_call x1, Pallas kernels, shards(): pl.pallas_call(backward_kernel, out_shape=[grads, stepped, shape((1, elem...  13.3 us
    pallas_call x1, Pallas kernels, shards(): pl.pallas_call(forward_kernel, out_shape=[pre_shape, stepped, plain_sent]...  8.93 us
    all_to_all x1, starting transfers between devices, shards(): lax.all_to_all(both, 'dp', 0, 0, axis_index_groups=z_groups, tiled=True)  8.46 us
    all_to_all x1, waiting for transfers between devices, shards(): lax.all_to_all(both, 'dp', 0, 0, axis_index_groups=z_groups, tiled=True)  6 us
    unnamed x16, local copies, waits for them, and re-layouts  4.6 us
  transfers between devices with their start and end apart: 9, of which 7 were waited for; matrix products, arithmetic and copies ran while one was open for 1% of the time, Pallas kernels for 31%

profile of v7, /device:TPU:18, one launch (start us, length us, event | category | flops | bytes accessed | tf_op | source)
XLA Modules:
  0.0 174.8 jit_solution(186855030518241691)
XLA Ops:
  7.2 3.9 %shard_map.118 = bf16[16,400,128]{2,1,0:T(8,128)(2,1)} custom-call(bf16[768,512]{1,0:T(8,128)(2,1)} %x_ref.5, f32[1,512]{1,0:T(1,128)} %bitcast.4, bf16[2,256,512]{2,1,0:T(8,128)(2,1)} %w1_ref.1), custom_call_target="tpu_custom_call" | custom-call | flops 402653184 | bytes 8388608 | tf_op jit(solution)/shard_map/pallas_call | solution.py:378
  11.0 7.3 %all-to-all-start = ((bf16[16,400,128]{2,1,0:T(8,128)(2,1)}), bf16[16,400,128]{2,1,0:T(8,128)(2,1)S(1)}, u32[]{:S(2)}, u32[]{:S(2)}) async-start(bf16[16,400,128]{2,1,0:T(8,128)(2,1)} %shard_map.118), calls=%async_computation | async-start | bytes 3276800 | tf_op jit(solution)/shard_map/all_to_all | solution.py:376
  18.3 3.0 %shard_map.119 = bf16[16,384,128]{2,1,0:T(8,128)(2,1)} custom-call(bf16[2,512,256]{2,1,0:T(8,128)(2,1)} %w4_ref.3, bf16[768,512]{1,0:T(8,128)(2,1)} %cot_ref.5), custom_call_target="tpu_custom_call" | custom-call | flops 402653184 | bytes 2883584 | tf_op jit(solution)/shard_map/pallas_call | solution.py:47
  21.4 16.8 %all-to-all-done.recv_hbm.stats_ref = bf16[16,400,128]{2,1,0:T(8,128)(2,1)S(1)} async-done(((bf16[16,400,128]{2,1,0:T(8,128)(2,1)}), bf16[16,400,128]{2,1,0:T(8,128)(2,1)S(1)}, u32[]{:S(2)}, u32[]{:S(2)}) %all-to-all-start) | async-done | bytes 1638432 | tf_op jit(solution)/shard_map/all_to_all | solution.py:376
  38.2 0.0 copy-start
  38.2 8.6 %all-to-all-start.1 = ((bf16[16,384,128]{2,1,0:T(8,128)(2,1)}), bf16[16,384,128]{2,1,0:T(8,128)(2,1)S(1)}, u32[]{:S(2)}, u32[]{:S(2)}) async-start(bf16[16,384,128]{2,1,0:T(8,128)(2,1)} %shard_map.119), calls=%async_computation.1 | async-start | bytes 3145728 | tf_op jit(solution)/shard_map/all_to_all | solution.py:376
  46.7 4.8 %shard_map.120 = (bf16[1024,1024]{1,0:T(8,128)(2,1)}, bf16[1024,1024]{1,0:T(8,128)(2,1)}) custom-call(bf16[1,1024,1024]{2,1,0:T(8,128)(2,1)} %w2_ref.3, bf16[1,1024,1024]{2,1,0:T(8,128)(2,1)} %w3_hbm.1), custom_call_target="tpu_custom_call" | custom-call | bytes 8388608 | tf_op jit(solution)/shard_map/pallas_call | solution.py:47
  51.6 0.0 copy-done
  51.6 8.9 %shard_map.121 = (f32[3,1024,256]{2,1,0:T(8,128)}, bf16[3,1024,256]{2,1,0:T(8,128)(2,1)}, bf16[16,384,128]{2,1,0:T(8,128)(2,1)}) custom-call(bf16[16,400,128]{2,1,0:T(8,128)(2,1)} %copy-done, bf16[1024,1024]{1,0:T(8,128)(2,1)} %get-tuple-element.31.w2t_hbm, bf16[1024,1024]{1,0:T(8,128)(2,1)} %get-tuple-element.32.w3t_hbm), custom_call_target="tpu_custom_call" | custom-call | flops 3221225472 | bytes 8388608 | tf_op jit(solution)/shard_map/pallas_call | solution.py:399
  60.5 5.3 %all-to-all-done.1.dthird_hbm = bf16[16,384,128]{2,1,0:T(8,128)(2,1)S(1)} async-done(((bf16[16,384,128]{2,1,0:T(8,128)(2,1)}), bf16[16,384,128]{2,1,0:T(8,128)(2,1)S(1)}, u32[]{:S(2)}, u32[]{:S(2)}) %all-to-all-start.1) | async-done | bytes 1572896 | tf_op jit(solution)/shard_map/all_to_all | solution.py:376
  65.8 0.0 copy-start.4
  65.8 8.6 %all-to-all-start.2 = ((bf16[16,384,128]{2,1,0:T(8,128)(2,1)}), bf16[16,384,128]{2,1,0:T(8,128)(2,1)S(1)}, u32[]{:S(2)}, u32[]{:S(2)}) async-start(bf16[16,384,128]{2,1,0:T(8,128)(2,1)} %get-tuple-element.38), calls=%async_computation.2 | async-start | bytes 3145728 | tf_op jit(solution)/shard_map/all_to_all | solution.py:376
  74.4 0.2 reduce-scatter.2.cloned.1.call-start
  74.6 0.0 copy-done.4
  74.6 13.3 %shard_map.122 = (bf16[8,2,64,2048]{3,2,1,0:T(8,128)(2,1)}, bf16[3,1024,256]{2,1,0:T(8,128)(2,1)}, f32[1,768]{1,0:T(1,128)}) custom-call(s32[1]{0:T(128)} %bitcast.y_ref, bf16[16,400,128]{2,1,0:T(8,128)(2,1)} %copy-done, bf16[16,384,128]{2,1,0:T(8,128)(2,1)} %copy-done.4, f32[3,1024,256]{2,1,0:T(8,128)} %get-tuple-element.33.pre_hbm, ...), custom_call_target="tpu_custom_call" | custom-call | flops 4831838208 | bytes 8388608 | tf_op jit(solution)/shard_map/pallas_call | solution.py:419
  88.0 0.0 reduce-scatter.2.cloned.1.call-update
  88.0 5.1 %shard_map.123 = bf16[16,400,128]{2,1,0:T(8,128)(2,1)} custom-call(bf16[3,1024,256]{2,1,0:T(8,128)(2,1)} %get-tuple-element.35.dpre_ref, f32[1,768]{1,0:T(1,128)} %get-tuple-element.36.inner_ref, bf16[1,1024,1024]{2,1,0:T(8,128)(2,1)} %w2_ref.3), custom_call_target="tpu_custom_call" | custom-call | flops 1610612736 | bytes 5311488 | tf_op jit(solution)/shard_map/pallas_call | solution.py:47
  93.1 0.4 all-to-all-done.2.recv_ref
  93.5 0.0 copy-start.2
  93.5 1.2 copy-done.2
  94.7 8.6 %all-to-all-start.3 = ((bf16[16,400,128]{2,1,0:T(8,128)(2,1)}), bf16[16,400,128]{2,1,0:T(8,128)(2,1)S(1)}, u32[]{:S(2)}, u32[]{:S(2)}) async-start(bf16[16,400,128]{2,1,0:T(8,128)(2,1)} %shard_map.123), calls=%async_computation.3 | async-start | bytes 3276800 | tf_op jit(solution)/shard_map/all_to_all | solution.py:376
  103.2 3.5 %shard_map.126 = (bf16[8,64,256]{2,1,0:T(8,128)(2,1)}, bf16[8,64,256]{2,1,0:T(8,128)(2,1)}, bf16[768,512]{1,0:T(8,128)(2,1)}) custom-call(s32[1]{0:T(128)} %bitcast.y_ref, bf16[16,384,128]{2,1,0:T(8,128)(2,1)} %copy-done.2, bf16[768,512]{1,0:T(8,128)(2,1)} %cot_ref.5, bf16[768,512]{1,0:T(8,128)(2,1)} %x_ref.5, f32[1,512]{1,0:T(1,128)} %bitcast.5, ...), custom_call_target="tpu_custom_call" | custom-call | flops 402653184 | bytes 8388608 | tf_op jit(solution)/shard_map/pallas_call | solution.py:448
  106.7 1.3 collective-permute-start.1
  108.0 15.1 %all-to-all-done.3.recv_ref.recv_hbm = bf16[16,400,128]{2,1,0:T(8,128)(2,1)S(1)} async-done(((bf16[16,400,128]{2,1,0:T(8,128)(2,1)}), bf16[16,400,128]{2,1,0:T(8,128)(2,1)S(1)}, u32[]{:S(2)}, u32[]{:S(2)}) %all-to-all-start.3) | async-done | bytes 1638432 | tf_op jit(solution)/shard_map/all_to_all | solution.py:376
  123.1 0.0 copy-start.1
  123.1 1.2 copy-done.1
  124.3 3.2 %shard_map.127 = (bf16[8,64,256]{2,1,0:T(8,128)(2,1)}, bf16[8,64,256]{2,1,0:T(8,128)(2,1)}) custom-call(s32[1]{0:T(128)} %bitcast.y_ref, bf16[16,400,128]{2,1,0:T(8,128)(2,1)} %copy-done.1, bf16[768,512]{1,0:T(8,128)(2,1)} %get-tuple-element.41.normed_hbm), custom_call_target="tpu_custom_call" | custom-call | flops 402653184 | bytes 8388608 | tf_op jit(solution)/shard_map/pallas_call | solution.py:459
  127.5 1.4 collective-permute-start
  128.9 3.3 %shard_map.124 = bf16[768,512]{1,0:T(8,128)(2,1)} custom-call(bf16[16,384,128]{2,1,0:T(8,128)(2,1)} %copy-done.2, bf16[768,512]{1,0:T(8,128)(2,1)} %x_ref.5, bf16[2,512,256]{2,1,0:T(8,128)(2,1)} %w4_ref.3), custom_call_target="tpu_custom_call" | custom-call | flops 64424509440 | bytes 3670016 | tf_op jit(solution)/shard_map/pallas_call | solution.py:47
  132.2 0.0 collective-permute-done.1.fourth_other
  132.2 0.0 copy-start.6
  132.2 4.3 %collective-permute-done.first_other = bf16[8,64,256]{2,1,0:T(8,128)(2,1)S(1)} collective-permute-done((bf16[8,64,256]{2,1,0:T(8,128)(2,1)}, bf16[8,64,256]{2,1,0:T(8,128)(2,1)S(1)}, u32[]{:S(2)}, u32[]{:S(2)}) %collective-permute-start) | collective-permute-done | bytes 262176 | tf_op jit(solution)/shard_map/ppermute | solution.py:472
  136.5 0.0 copy-start.7
  136.5 0.0 copy-done.6
  136.5 0.7 copy-done.7
  137.2 2.1 %shard_map.128 = bf16[8,128,256]{2,1,0:T(8,128)(2,1)} custom-call(bf16[8,64,256]{2,1,0:T(8,128)(2,1)} %get-tuple-element.42.first_own, bf16[8,64,256]{2,1,0:T(8,128)(2,1)} %copy-done.7, bf16[8,64,256]{2,1,0:T(8,128)(2,1)} %get-tuple-element.44.fourth_own, bf16[8,64,256]{2,1,0:T(8,128)(2,1)} %copy-done.6), custom_call_target="tpu_custom_call" | custom-call | bytes 1572864 | tf_op jit(solution)/shard_map/pallas_call | solution.py:47
  139.4 8.5 %all-to-all-start.4 = ((bf16[8,128,256]{2,1,0:T(8,128)(2,1)}), bf16[8,128,256]{2,1,0:T(8,128)(2,1)S(1)}, u32[]{:S(2)}, u32[]{:S(2)}) async-start(bf16[8,128,256]{2,1,0:T(8,128)(2,1)} %shard_map.128), calls=%async_computation.4 | async-start | bytes 1048576 | tf_op jit(solution)/shard_map/all_to_all | solution.py:474
  147.8 0.0 reduce-scatter.2.cloned.1.call-done.own_ref
  147.9 1.0 slice_bitcast_fusion
  148.8 1.4 collective-permute-start.2
  150.2 4.3 %shard_map.125 = bf16[768,512]{1,0:T(8,128)(2,1)} custom-call(bf16[16,400,128]{2,1,0:T(8,128)(2,1)} %copy-done.1, bf16[16,400,128]{2,1,0:T(8,128)(2,1)} %copy-done, bf16[768,512]{1,0:T(8,128)(2,1)} %x_ref.5, f32[1,512]{1,0:T(1,128)} %bitcast.6, bf16[2,256,512]{2,1,0:T(8,128)(2,1)} %w1_ref.1, bf16[768,512]{1,0:T(8,128)(2,1)} %cot_ref.5), custom_call_target="tpu_custom_call" | custom-call | flops 64424509440 | bytes 8388608 | tf_op jit(solution)/shard_map/pallas_call | solution.py:475
  154.5 2.2 %collective-permute-done.2.other_ref = bf16[64,2048]{1,0:T(8,128)(2,1)S(1)} collective-permute-done((bf16[64,2048]{1,0:T(8,128)(2,1)S(1)}, bf16[64,2048]{1,0:T(8,128)(2,1)S(1)}, u32[]{:S(2)}, u32[]{:S(2)}) %collective-permute-start.2) | collective-permute-done | bytes 262176 | tf_op jit(solution)/shard_map/ppermute | solution.py:484
  156.7 0.0 copy-start.5
  156.7 0.7 copy-done.5
  157.4 1.9 %shard_map.129 = (f32[1,64,1024]{2,1,0:T(8,128)}, f32[1,64,1024]{2,1,0:T(8,128)}) custom-call(bf16[1,2,64,2048]{3,2,1,0:T(8,128)(2,1)} %reduce-scatter.2.cloned.1.call-done.own_ref, bf16[64,2048]{1,0:T(8,128)(2,1)} %copy-done.5), custom_call_target="tpu_custom_call" | custom-call | bytes 1310720 | tf_op jit(solution)/shard_map/pallas_call | solution.py:47
  159.4 6.0 %all-to-all-done.4.recv_ref = bf16[8,128,256]{2,1,0:T(8,128)(2,1)S(1)} async-done(((bf16[8,128,256]{2,1,0:T(8,128)(2,1)}), bf16[8,128,256]{2,1,0:T(8,128)(2,1)S(1)}, u32[]{:S(2)}, u32[]{:S(2)}) %all-to-all-start.4) | async-done | bytes 524320 | tf_op jit(solution)/shard_map/all_to_all | solution.py:474
  165.4 0.0 copy-start.3
  165.4 0.8 copy-done.3
  166.2 1.7 shard_map.130
Async XLA Ops:
  11.0 27.1 %all-to-all-start = ((bf16[16,400,128]{2,1,0:T(8,128)(2,1)}), bf16[16,400,128]{2,1,0:T(8,128)(2,1)S(1)}, u32[]{:S(2)}, u32[]{:S(2)}) async-start(bf16[16,400,128]{2,1,0:T(8,128)(2,1)} %shard_map.118), calls=%async_computation | async-start | bytes 3276800 | tf_op jit(solution)/shard_map/all_to_all | solution.py:376
  38.2 13.4 %copy-start = (bf16[16,400,128]{2,1,0:T(8,128)(2,1)}, bf16[16,400,128]{2,1,0:T(8,128)(2,1)S(1)}, u32[]{:S(2)}) copy-start(bf16[16,400,128]{2,1,0:T(8,128)(2,1)S(1)} %all-to-all-done.recv_hbm.stats_ref) | copy-start | bytes 4915204
  38.2 27.7 %all-to-all-start.1 = ((bf16[16,384,128]{2,1,0:T(8,128)(2,1)}), bf16[16,384,128]{2,1,0:T(8,128)(2,1)S(1)}, u32[]{:S(2)}, u32[]{:S(2)}) async-start(bf16[16,384,128]{2,1,0:T(8,128)(2,1)} %shard_map.119), calls=%async_computation.1 | async-start | bytes 3145728 | tf_op jit(solution)/shard_map/all_to_all | solution.py:376
  65.8 8.8 %copy-start.4 = (bf16[16,384,128]{2,1,0:T(8,128)(2,1)}, bf16[16,384,128]{2,1,0:T(8,128)(2,1)S(1)}, u32[]{:S(2)}) copy-start(bf16[16,384,128]{2,1,0:T(8,128)(2,1)S(1)} %all-to-all-done.1.dthird_hbm) | copy-start | bytes 4718596
  65.8 27.6 %all-to-all-start.2 = ((bf16[16,384,128]{2,1,0:T(8,128)(2,1)}), bf16[16,384,128]{2,1,0:T(8,128)(2,1)S(1)}, u32[]{:S(2)}, u32[]{:S(2)}) async-start(bf16[16,384,128]{2,1,0:T(8,128)(2,1)} %get-tuple-element.38), calls=%async_computation.2 | async-start | bytes 3145728 | tf_op jit(solution)/shard_map/all_to_all | solution.py:376
  74.4 73.5 %reduce-scatter.2.cloned.1.call-start = ((), (), s32[]{:S(2)}) async-start(), calls=%async_computation.6 | async-start | bytes 4718592 | tf_op jit(solution)/shard_map/reduce_scatter | solution.py:439
  93.5 1.2 copy-start.2
  94.7 28.5 %all-to-all-start.3 = ((bf16[16,400,128]{2,1,0:T(8,128)(2,1)}), bf16[16,400,128]{2,1,0:T(8,128)(2,1)S(1)}, u32[]{:S(2)}, u32[]{:S(2)}) async-start(bf16[16,400,128]{2,1,0:T(8,128)(2,1)} %shard_map.123), calls=%async_computation.3 | async-start | bytes 3276800 | tf_op jit(solution)/shard_map/all_to_all | solution.py:376
  106.7 25.5 %collective-permute-start.1 = (bf16[8,64,256]{2,1,0:T(8,128)(2,1)}, bf16[8,64,256]{2,1,0:T(8,128)(2,1)S(1)}, u32[]{:S(2)}, u32[]{:S(2)}) collective-permute-start(bf16[8,64,256]{2,1,0:T(8,128)(2,1)} %get-tuple-element.45), channel_id=1, source_target_pairs={{0,128},{16,144},{32,160},{48,176},{64,192},{80,208},{96,224},{112... | collective-permute-start | bytes 786440 | tf_op jit(solution)/shard_map/ppermute | solution.py:457
  123.1 1.2 copy-start.1
  127.5 9.0 %collective-permute-start = (bf16[8,64,256]{2,1,0:T(8,128)(2,1)}, bf16[8,64,256]{2,1,0:T(8,128)(2,1)S(1)}, u32[]{:S(2)}, u32[]{:S(2)}) collective-permute-start(bf16[8,64,256]{2,1,0:T(8,128)(2,1)} %get-tuple-element.43), channel_id=1, source_target_pairs={{0,128},{16,144},{32,160},{48,176},{64,192},{80,208},{96,224},{112... | collective-permute-start | bytes 786440 | tf_op jit(solution)/shard_map/ppermute | solution.py:472
  132.2 4.3 %copy-start.6 = (bf16[8,64,256]{2,1,0:T(8,128)(2,1)}, bf16[8,64,256]{2,1,0:T(8,128)(2,1)S(1)}, u32[]{:S(2)}) copy-start(bf16[8,64,256]{2,1,0:T(8,128)(2,1)S(1)} %collective-permute-done.1.fourth_other) | copy-start | bytes 786436
  136.5 0.7 copy-start.7
  139.4 26.0 %all-to-all-start.4 = ((bf16[8,128,256]{2,1,0:T(8,128)(2,1)}), bf16[8,128,256]{2,1,0:T(8,128)(2,1)S(1)}, u32[]{:S(2)}, u32[]{:S(2)}) async-start(bf16[8,128,256]{2,1,0:T(8,128)(2,1)} %shard_map.128), calls=%async_computation.4 | async-start | bytes 1048576 | tf_op jit(solution)/shard_map/all_to_all | solution.py:474
  148.8 7.9 %collective-permute-start.2 = (bf16[64,2048]{1,0:T(8,128)(2,1)S(1)}, bf16[64,2048]{1,0:T(8,128)(2,1)S(1)}, u32[]{:S(2)}, u32[]{:S(2)}) collective-permute-start(bf16[64,2048]{1,0:T(8,128)(2,1)S(1)} %slice_bitcast_fusion), channel_id=1, source_target_pairs={{0,128},{16,144},{32,160},{48,176},{64,192},{80,208},{96,224},{112... | collective-permute-start | bytes 786440 | tf_op jit(solution)/shard_map/ppermute | solution.py:484
  156.7 0.7 copy-start.5
  165.4 0.8 copy-start.3
Sparse Core Ops, SparseCore 0:
  88.2 58.0 reduce-scatter.1

commit v8 on v7

--- a/solution.py
+++ b/solution.py
@@ -20,7 +20,11 @@
 STATS = 16
 STEP = 256
 LATE = 160
+TOKEN = 1
+FOURTH = 200
+TIE = 6
 VMEM = 58 * 1024 * 1024
+SMALL = 16 * 1024 * 1024
 
 epsilon = 1e-05
 root_scale = math.sqrt(2.0 / math.pi)
@@ -39,7 +43,7 @@
     return lax.dot_general(a, b, dims, preferred_element_type=F32)
 
 
-def call(kernel, out_shape, args, scratch=(), flops=0, **extra):
+def call(kernel, out_shape, args, scratch=(), flops=0, limit=None, **extra):
     outs = out_shape if isinstance(out_shape, (list, tuple)) else [out_shape]
     moved = sum(a.size * a.dtype.itemsize for a in args) + sum(
         math.prod(o.shape) * o.dtype.itemsize for o in outs
@@ -50,7 +54,7 @@
         in_specs=[pl.BlockSpec(memory_space=pltpu.VMEM)] * len(args),
         out_specs=jax.tree.map(lambda _: pl.BlockSpec(memory_space=pltpu.VMEM), out_shape),
         scratch_shapes=list(scratch),
-        compiler_params=pltpu.CompilerParams(vmem_limit_bytes=VMEM),
+        compiler_params=pltpu.CompilerParams(vmem_limit_bytes=limit or VMEM),
         cost_estimate=pl.CostEstimate(flops=int(flops), bytes_accessed=int(moved), transcendentals=0),
         **extra,
     )(*args)
@@ -277,28 +281,36 @@
         out_ref[:, feats] = (x_ref[:, feats].astype(F32) + branch).astype(BF16)
 
 
-def fourth_kernel(y_ref, recv_ref, cot_ref, x_ref, gain_ref, stats_ref, own_ref, other_ref, normed_ref):
+def fourth_kernel(place_ref, recv_ref, cot_ref, x_ref, gain_ref, stats_ref, *refs):
+    out_refs, normed_ref, block_ref = refs[:-2], refs[-2], refs[-1]
     chunks = cot_ref.shape[0] // LANES
-    z_size = own_ref.shape[0]
+    z_size = len(out_refs)
     rows = HB * EB // PEERS
+    y = place_ref[0]
     for a in range(2):
         grad = dot(model_rows(recv_ref, chunks, a), cot_ref[:, a * BS : (a + 1) * BS], NN).astype(BF16)
         grad = grad.reshape(PEERS, rows, BS)
-        part = slice(a * rows, (a + 1) * rows)
-        own_ref[:, part, :] = jnp.where(y_ref[0] == 0, grad[:z_size], grad[z_size:])
-        other_ref[:, part, :] = jnp.where(y_ref[0] == 0, grad[z_size:], grad[:z_size])
+        own = slice(a * rows, (a + 1) * rows)
+        block_ref[:, own, :] = jnp.where(y == 0, grad[:z_size], grad[z_size:])
+        other = slice((2 + a) * rows, (3 + a) * rows)
+        block_ref[:, other, :] = jnp.where(y == 0, grad[z_size:], grad[:z_size])
+    for k, out_ref in enumerate(out_refs):
+        out_ref[...] = block_ref[lax.rem(place_ref[1] + k, z_size)]
     inverse = lax.rsqrt(columns(stat_sum(stats_ref[...]), chunks) / MODEL_WIDTH + epsilon)
     normed_ref[...] = (x_ref[...].astype(F32) * inverse * gain_ref[...]).astype(BF16)
 
 
-def pair_kernel(first_own, first_other, fourth_own, fourth_other, out_ref):
-    out_ref[:, :PAIR, :] = (first_own[...].astype(F32) + first_other[...].astype(F32)).astype(BF16)
-    out_ref[:, PAIR:, :] = (fourth_own[...].astype(F32) + fourth_other[...].astype(F32)).astype(BF16)
-
-
-def first_kernel(y_ref, recv_hbm, normed_hbm, own_ref, other_ref, recv_ref, normed_ref, sems):
+def fourth_sum_kernel(*refs):
+    total = refs[0][...].astype(F32)
+    for ref in refs[1:-2]:
+        total = total + ref[...].astype(F32)
+    half = total.shape[0] // 2
+    refs[-2][...] = total[:half]
+    refs[-1][...] = total[half:].astype(BF16)
+
+
+def first_kernel(recv_hbm, normed_hbm, out_ref, recv_ref, normed_ref, sems):
     chunks = normed_ref.shape[0] // LANES
-    z_size = own_ref.shape[0]
     loads = Copies(sems)
     loads.start(normed_hbm, normed_ref)
     loads.start(recv_hbm.at[:, pl.ds(0, chunks * PAIR)], recv_ref)
@@ -309,10 +321,8 @@
         grad = dot(dfirst, normed_ref[:, a * BS : (a + 1) * BS], NN).astype(BF16).T
         for half in range(2):
             base = (2 * a + half) * rows
-            value = grad[:, half * BS : (half + 1) * BS].reshape(PEERS, rows, BS)
-            part = slice(base, base + rows)
-            own_ref[:, part, :] = jnp.where(y_ref[0] == 0, value[:z_size], value[z_size:])
-            other_ref[:, part, :] = jnp.where(y_ref[0] == 0, value[z_size:], value[:z_size])
+            value = grad[:, half * BS : (half + 1) * BS]
+            out_ref[:, base : base + rows, :] = value.reshape(PEERS, rows, BS)
 
 
 def token_kernel(recv_ref, stats_ref, x_ref, gain_ref, w1_ref, cot_ref, out_ref):
@@ -328,20 +338,21 @@
         out_ref[:, feats] = (cot_ref[:, feats].astype(F32) + inverse * change).astype(BF16)
 
 
-def sum_kernel(scale, recv_ref, first_ref, fourth_ref):
+def first_total_kernel(scale, recv_ref, first_ref):
     total = jnp.sum(recv_ref[...].astype(F32), axis=0) * scale
     _, rows, _ = first_ref.shape
     for a in range(2):
         for half in range(2):
             base = (2 * a + half) * rows
             first_ref[a, :, half * BS : (half + 1) * BS] = total[base : base + rows]
-    fourth_ref[...] = total[PAIR:].reshape(fourth_ref.shape)
-
-
-def finish_kernel(scale, own_ref, other_ref, second_ref, third_ref):
+
+
+def finish_kernel(scale, own_ref, other_ref, own4_ref, other4_ref, second_ref, third_ref, fourth_ref):
     total = (own_ref[0, 0].astype(F32) + other_ref[...].astype(F32)) * scale
     second_ref[0] = total[:, :HBS]
     third_ref[0] = total[:, HBS:]
+    total = (own4_ref[...] + other4_ref[...].astype(F32)) * scale
+    fourth_ref[...] = total.reshape(fourth_ref.shape)
 
 
 def shards(tokens, gain, w_first, w_second, w_third, w_fourth, cotangent):
@@ -352,7 +363,8 @@
     z_size = dp // 2
     z_groups = [[y * z_size + z for z in range(z_size)] for y in range(2)]
     y_pairs = [(i, (i + z_size) % dp) for i in range(dp)]
-    y_index = (lax.axis_index("dp") // z_size).astype(jnp.int32)[None]
+    place = lax.axis_index("dp")
+    place = jnp.stack([place // z_size, place % z_size]).astype(jnp.int32)
     shape = jax.ShapeDtypeStruct
     hidden_flops = 2 * HBS * HBS * element_count
     model_flops = 2 * local_width * HB * EB * element_count
@@ -435,7 +447,7 @@
         ],
         compiler_params=params,
         cost_estimate=cost(3 * hidden_flops),
-    )(y_index, recv, dthird, pre, act, w_third)
+    )(place, recv, dthird, pre, act, w_third)
     hidden = lax.psum_scatter(hidden, "dp", scatter_dimension=0, axis_index_groups=z_groups, tiled=True)
     send = call(dmixed_kernel, stats_sent, (dpre, inner, w_second), flops=hidden_flops)
     send, third = lax.optimization_barrier((send, third))
@@ -444,23 +456,22 @@
     stats_spec = pl.BlockSpec((PEERS, STATS, LANES), lambda i: (0, rows // STATS, 0))
     all_tokens = whole(*tokens.shape)
     row = whole(1, local_width)
-    part = shape((z_size, PAIR, BS), BF16)
-    own, other, normed = pl.pallas_call(
+    block = shape((2 * PAIR, BS), BF16)
+    *blocks, normed = pl.pallas_call(
         fourth_kernel,
-        out_shape=[part, part, shape(tokens.shape, BF16)],
+        out_shape=[block] * z_size + [shape(tokens.shape, BF16)],
         grid=(1,),
         in_specs=[smem, whole(*plain_sent.shape), all_tokens, all_tokens, row, stats_spec],
-        out_specs=[whole(*part.shape), whole(*part.shape), all_tokens],
+        out_specs=[whole(*block.shape)] * z_size + [all_tokens],
+        scratch_shapes=[pltpu.VMEM((z_size,) + block.shape, BF16)],
         compiler_params=params,
-        cost_estimate=cost(model_flops),
-    )(y_index, third, cotangent, tokens, gain_row, recv)
-    fourths = (own, lax.ppermute(other, "dp", y_pairs))
-    output = call(output_kernel, shape(tokens.shape, BF16), (third, tokens, w_fourth), flops=LATE * model_flops)
-    own, other = pl.pallas_call(
+        cost_estimate=cost(FOURTH * model_flops),
+    )(place, third, cotangent, tokens, gain_row, recv)
+    first = pl.pallas_call(
         first_kernel,
-        out_shape=[part, part],
-        in_specs=[smem, hbm, hbm],
-        out_specs=[vmem, vmem],
+        out_shape=shape((PEERS, PAIR, BS), BF16),
+        in_specs=[hbm, hbm],
+        out_specs=vmem,
         scratch_shapes=[
             pltpu.VMEM(plain_sent.shape, BF16),
             pltpu.VMEM(tokens.shape, BF16),
@@ -468,10 +479,17 @@
         ],
         compiler_params=params,
         cost_estimate=cost(model_flops),
-    )(y_index, back, normed)
-    firsts = (own, lax.ppermute(other, "dp", y_pairs))
-    both = call(pair_kernel, shape((z_size, 2 * PAIR, BS), BF16), firsts + fourths)
-    both = lax.all_to_all(both, "dp", 0, 0, axis_index_groups=z_groups, tiled=True)
+    )(back, normed)
+    late, third, first = lax.optimization_barrier((blocks[TIE:], third, first))
+    blocks[TIE:] = late
+    first = lax.all_to_all(first, "dp", 0, 0, tiled=True)
+    for k in range(1, z_size):
+        shift = [(g[z], g[(z + k) % z_size]) for g in z_groups for z in range(z_size)]
+        blocks[k] = lax.ppermute(blocks[k], "dp", shift)
+    part = (PAIR, BS)
+    own4, other4 = call(fourth_sum_kernel, [shape(part, F32), shape(part, BF16)], tuple(blocks), limit=SMALL)
+    other4 = lax.ppermute(other4, "dp", y_pairs)
+    output = call(output_kernel, shape(tokens.shape, BF16), (third, tokens, w_fourth), flops=LATE * model_flops)
     token_gradient = pl.pallas_call(
         token_kernel,
         out_shape=shape(tokens.shape, BF16),
@@ -479,16 +497,23 @@
         in_specs=[whole(*stats_sent.shape), stats_spec, all_tokens, row, whole(*w_first.shape), all_tokens],
         out_specs=all_tokens,
         compiler_params=params,
-        cost_estimate=cost(LATE * model_flops),
+        cost_estimate=cost(TOKEN * model_flops),
     )(back, recv, tokens, gain_row, w_first, cotangent)
+    hidden, own4 = lax.optimization_barrier((hidden, own4))
     other = lax.ppermute(hidden[0, 1], "dp", y_pairs)
     part = shape((1, HBS // dp, HBS), F32)
-    grad_second, grad_third = call(functools.partial(finish_kernel, scale), [part, part], (hidden, other))
-    both, grad_second, grad_third = lax.optimization_barrier((both, grad_second, grad_third))
-    grad_first, grad_fourth = call(
-        functools.partial(sum_kernel, scale),
-        [shape((2, BS // dp, HB * EB), F32), shape((2, HB * EB // dp, BS), F32)],
-        (both,),
+    grad_second, grad_third, grad_fourth = call(
+        functools.partial(finish_kernel, scale),
+        [part, part, shape((2, HB * EB // dp, BS), F32)],
+        (hidden, other, own4, other4),
+        limit=SMALL,
+    )
+    first, grad_second, grad_third = lax.optimization_barrier((first, grad_second, grad_third))
+    grad_first = call(
+        functools.partial(first_total_kernel, scale),
+        shape((2, BS // dp, HB * EB), F32),
+        (first,),
+        limit=SMALL,
     )
     return output, token_gradient, grad_first, grad_second, grad_third, grad_fourth
 

time: 177 us -> 192 us (1.085)
  starting transfers between devices: 45.7 us -> 59.9 us
  waiting for transfers between devices: 50.3 us -> 56.9 us
  Pallas kernels: 59.1 us -> 55.7 us
  local copies, waits for them, and re-layouts: 5.57 us -> 3.33 us
    reduce_scatter x1, waiting for transfers between devices: 0.01 us -> 29.6 us  [shards(): lax.psum_scatter(hidden, 'dp', scatter_dimension=0, axis_index_groups=z_g...]
    ppermute x2 -> x8, starting transfers between devices: 2.66 us -> 22.8 us  [the longest x7 22 us: shards(): blocks[k] = lax.ppermute(blocks[k], 'dp', shift)]
    all_to_all x4, waiting for transfers between devices: 37.7 us -> 23.7 us  [exchange(): return lax.all_to_all(value, 'tensor', 0, 0, tiled=True)]
    all_to_all x1, waiting for transfers between devices: 6 us -> 0.01 us  [shards(): first = lax.all_to_all(first, 'dp', 0, 0, tiled=True)]
    all_to_all x1, starting transfers between devices: 8.46 us -> 3.58 us  [shards(): first = lax.all_to_all(first, 'dp', 0, 0, tiled=True)]
    pallas_call x7, Pallas kernels: 22.1 us -> 17.8 us  [call(): pl.pallas_call(kernel, out_shape=out_shape, in_specs=[pl.BlockSpec(memory...]
    unnamed x16, local copies, waits for them, and re-layouts: 4.6 us -> 2.36 us
    ppermute x1, waiting for transfers between devices: 2.23 us -> 0.01 us  [shards(): other = lax.ppermute(hidden[0, 1], 'dp', y_pairs)]
  transfers between devices with their start and end apart: 9 -> 15, of which waited for: 7 -> 6; matrix products, arithmetic and copies ran while one was open for 1% -> 1% of each run, Pallas kernels for 31% -> 27%
where the time goes in v8:
time: 192 us; the launch traced here: 191 us
  starting transfers between devices  59.9 us (31%)
  waiting for transfers between devices  56.9 us (30%)
  Pallas kernels  55.7 us (29%)
  between operations  14.2 us (7%)
  local copies, waits for them, and re-layouts  3.33 us (2%)
    all_to_all x4, starting transfers between devices, exchange(): return lax.all_to_all(value, 'tensor', 0, 0, tiled=True)  32 us
    reduce_scatter x1, waiting for transfers between devices, shards(): lax.psum_scatter(hidden, 'dp', scatter_dimension=0, axis_index_groups=z_g...  29.6 us
    all_to_all x4, waiting for transfers between devices, exchange(): return lax.all_to_all(value, 'tensor', 0, 0, tiled=True)  23.7 us
    ppermute x7, starting transfers between devices, shards(): blocks[k] = lax.ppermute(blocks[k], 'dp', shift)  22 us
    pallas_call x7, Pallas kernels, call(): pl.pallas_call(kernel, out_shape=out_shape, in_specs=[pl.BlockSpec(memory...  17.8 us
    pallas_call x1, Pallas kernels, shards(): pl.pallas_call(backward_kernel, out_shape=[grads, stepped, shape((1, elem...  14 us
    pallas_call x1, Pallas kernels, shards(): pl.pallas_call(forward_kernel, out_shape=[pre_shape, stepped, plain_sent]...  8.92 us
    pallas_call x1, Pallas kernels, shards(): pl.pallas_call(token_kernel, out_shape=shape(tokens.shape, BF16), grid=(1...  4.3 us
  transfers between devices with their start and end apart: 15, of which 6 were waited for; matrix products, arithmetic and copies ran while one was open for 1% of the time, Pallas kernels for 27%

profile of v8, /device:TPU:18, one launch (start us, length us, event | category | flops | bytes accessed | tf_op | source)
XLA Modules:
  0.0 190.8 jit_solution(6476140169341332059)
XLA Ops:
  7.2 3.8 %shard_map.118 = bf16[16,400,128]{2,1,0:T(8,128)(2,1)} custom-call(bf16[768,512]{1,0:T(8,128)(2,1)} %x_ref.5, f32[1,512]{1,0:T(1,128)} %bitcast.5, bf16[2,256,512]{2,1,0:T(8,128)(2,1)} %w1_ref.1), custom_call_target="tpu_custom_call" | custom-call | flops 402653184 | bytes 8388608 | tf_op jit(solution)/shard_map/pallas_call | solution.py:390
  11.0 7.3 %all-to-all-start = ((bf16[16,400,128]{2,1,0:T(8,128)(2,1)}), bf16[16,400,128]{2,1,0:T(8,128)(2,1)S(1)}, u32[]{:S(2)}, u32[]{:S(2)}) async-start(bf16[16,400,128]{2,1,0:T(8,128)(2,1)} %shard_map.118), calls=%async_computation | async-start | bytes 3276800 | tf_op jit(solution)/shard_map/all_to_all | solution.py:388
  18.3 3.1 %shard_map.119 = bf16[16,384,128]{2,1,0:T(8,128)(2,1)} custom-call(bf16[2,512,256]{2,1,0:T(8,128)(2,1)} %w4_ref.3, bf16[768,512]{1,0:T(8,128)(2,1)} %cot_ref.5), custom_call_target="tpu_custom_call" | custom-call | flops 402653184 | bytes 2883584 | tf_op jit(solution)/shard_map/pallas_call | solution.py:51
  21.3 16.8 %all-to-all-done.recv_hbm.stats_ref = bf16[16,400,128]{2,1,0:T(8,128)(2,1)S(1)} async-done(((bf16[16,400,128]{2,1,0:T(8,128)(2,1)}), bf16[16,400,128]{2,1,0:T(8,128)(2,1)S(1)}, u32[]{:S(2)}, u32[]{:S(2)}) %all-to-all-start) | async-done | bytes 1638432 | tf_op jit(solution)/shard_map/all_to_all | solution.py:388
  38.1 0.0 copy-start.3
  38.1 8.6 %all-to-all-start.1 = ((bf16[16,384,128]{2,1,0:T(8,128)(2,1)}), bf16[16,384,128]{2,1,0:T(8,128)(2,1)S(1)}, u32[]{:S(2)}, u32[]{:S(2)}) async-start(bf16[16,384,128]{2,1,0:T(8,128)(2,1)} %shard_map.119), calls=%async_computation.1 | async-start | bytes 3145728 | tf_op jit(solution)/shard_map/all_to_all | solution.py:388
  46.7 4.8 %shard_map.120 = (bf16[1024,1024]{1,0:T(8,128)(2,1)}, bf16[1024,1024]{1,0:T(8,128)(2,1)}) custom-call(bf16[1,1024,1024]{2,1,0:T(8,128)(2,1)} %w2_ref.3, bf16[1,1024,1024]{2,1,0:T(8,128)(2,1)} %w3_hbm.1), custom_call_target="tpu_custom_call" | custom-call | bytes 8388608 | tf_op jit(solution)/shard_map/pallas_call | solution.py:51
  51.5 0.0 copy-done.3
  51.5 8.9 %shard_map.121 = (f32[3,1024,256]{2,1,0:T(8,128)}, bf16[3,1024,256]{2,1,0:T(8,128)(2,1)}, bf16[16,384,128]{2,1,0:T(8,128)(2,1)}) custom-call(bf16[16,400,128]{2,1,0:T(8,128)(2,1)} %copy-done.3, bf16[1024,1024]{1,0:T(8,128)(2,1)} %get-tuple-element.42.w2t_hbm, bf16[1024,1024]{1,0:T(8,128)(2,1)} %get-tuple-element.43.w3t_hbm), custom_call_target="tpu_custom_call" | custom-call | flops 3221225472 | bytes 8388608 | tf_op jit(solution)/shard_map/pallas_call | solution.py:411
  60.5 5.3 %all-to-all-done.1.dthird_hbm = bf16[16,384,128]{2,1,0:T(8,128)(2,1)S(1)} async-done(((bf16[16,384,128]{2,1,0:T(8,128)(2,1)}), bf16[16,384,128]{2,1,0:T(8,128)(2,1)S(1)}, u32[]{:S(2)}, u32[]{:S(2)}) %all-to-all-start.1) | async-done | bytes 1572896 | tf_op jit(solution)/shard_map/all_to_all | solution.py:388
  65.8 0.0 copy-start.5
  65.8 8.6 %all-to-all-start.2 = ((bf16[16,384,128]{2,1,0:T(8,128)(2,1)}), bf16[16,384,128]{2,1,0:T(8,128)(2,1)S(1)}, u32[]{:S(2)}, u32[]{:S(2)}) async-start(bf16[16,384,128]{2,1,0:T(8,128)(2,1)} %get-tuple-element.49), calls=%async_computation.2 | async-start | bytes 3145728 | tf_op jit(solution)/shard_map/all_to_all | solution.py:388
  74.3 0.2 reduce-scatter.2.cloned.1.call-start
  74.6 0.6 pad_add_fusion.y_ref.place_ref
  75.2 0.0 copy-done.5
  75.2 14.0 %shard_map.122 = (bf16[8,2,64,2048]{3,2,1,0:T(8,128)(2,1)}, bf16[3,1024,256]{2,1,0:T(8,128)(2,1)}, f32[1,768]{1,0:T(1,128)}) custom-call(s32[2]{0:T(128)} %pad_add_fusion.y_ref.place_ref, bf16[16,400,128]{2,1,0:T(8,128)(2,1)} %copy-done.3, bf16[16,384,128]{2,1,0:T(8,128)(2,1)} %copy-done.5, f32[3,1024,256]{2,1,0:T(8,128)} %get-tuple-element.44.pre_hbm, ...), custom_call_target="tpu_custom_call" | custom-call | flops 4831838208 | bytes 8388608 | tf_op jit(solution)/shard_map/pallas_call | solution.py:431
  89.3 0.0 reduce-scatter.2.cloned.1.call-update
  89.3 5.1 %shard_map.123 = bf16[16,400,128]{2,1,0:T(8,128)(2,1)} custom-call(bf16[3,1024,256]{2,1,0:T(8,128)(2,1)} %get-tuple-element.46.dpre_ref, f32[1,768]{1,0:T(1,128)} %get-tuple-element.47.inner_ref, bf16[1,1024,1024]{2,1,0:T(8,128)(2,1)} %w2_ref.3), custom_call_target="tpu_custom_call" | custom-call | flops 1610612736 | bytes 5311488 | tf_op jit(solution)/shard_map/pallas_call | solution.py:51
  94.4 0.0 all-to-all-done.2.recv_ref
  94.4 0.0 copy-start.4
  94.4 1.2 copy-done.4
  95.5 7.6 %all-to-all-start.3 = ((bf16[16,400,128]{2,1,0:T(8,128)(2,1)}), bf16[16,400,128]{2,1,0:T(8,128)(2,1)S(1)}, u32[]{:S(2)}, u32[]{:S(2)}) async-start(bf16[16,400,128]{2,1,0:T(8,128)(2,1)} %shard_map.123), calls=%async_computation.3 | async-start | bytes 3276800 | tf_op jit(solution)/shard_map/all_to_all | solution.py:388
  103.2 3.7 %shard_map.124 = (bf16[128,256]{1,0:T(8,128)(2,1)}, bf16[128,256]{1,0:T(8,128)(2,1)}, bf16[128,256]{1,0:T(8,128)(2,1)}, bf16[128,256]{1,0:T(8,128)(2,1)}, bf16[1...) custom-call(s32[2]{0:T(128)} %pad_add_fusion.y_ref.place_ref, ...), custom_call_target="tpu_custom_call" | custom-call | flops 80530636800 | bytes 8388608 | tf_op jit(solution)/shard_map/pallas_call | solution.py:460
  106.8 0.0 copy-start.7
  106.8 0.0 copy-start.6
  106.8 1.8 collective-permute-start
  108.7 3.2 %collective-permute-start.1 = (bf16[128,256]{1,0:T(8,128)(2,1)}, bf16[128,256]{1,0:T(8,128)(2,1)S(1)}, u32[]{:S(2)}, u32[]{:S(2)}) collective-permute-start(bf16[128,256]{1,0:T(8,128)(2,1)} %get-tuple-element.60), channel_id=1, source_target_pairs={{0,32},{16,48},{32,64},{48,80},{64,96},{80,112},{96,0},{112,16},{1... | collective-permute-start | bytes 196616 | tf_op jit(solution)/shard_map/ppermute | solution.py:488
  111.9 4.0 %collective-permute-start.2 = (bf16[128,256]{1,0:T(8,128)(2,1)}, bf16[128,256]{1,0:T(8,128)(2,1)S(1)}, u32[]{:S(2)}, u32[]{:S(2)}) collective-permute-start(bf16[128,256]{1,0:T(8,128)(2,1)} %get-tuple-element.61), channel_id=1, source_target_pairs={{0,48},{16,64},{32,80},{48,96},{64,112},{80,0},{96,16},{112,32},{1... | collective-permute-start | bytes 196616 | tf_op jit(solution)/shard_map/ppermute | solution.py:488
  116.0 0.6 collective-permute-start.3
  116.5 4.9 %collective-permute-start.4 = (bf16[128,256]{1,0:T(8,128)(2,1)}, bf16[128,256]{1,0:T(8,128)(2,1)S(1)}, u32[]{:S(2)}, u32[]{:S(2)}) collective-permute-start(bf16[128,256]{1,0:T(8,128)(2,1)} %get-tuple-element.63), channel_id=1, source_target_pairs={{0,80},{16,96},{32,112},{48,0},{64,16},{80,32},{96,48},{112,64},{1... | collective-permute-start | bytes 196616 | tf_op jit(solution)/shard_map/ppermute | solution.py:488
  121.4 1.6 all-to-all-done.3.recv_hbm.recv_ref
  123.0 0.0 copy-start.2
  123.0 1.2 copy-done.2
  124.2 0.0 copy-start.1
  124.2 3.1 %shard_map.125 = bf16[16,64,256]{2,1,0:T(8,128)(2,1)} custom-call(bf16[16,400,128]{2,1,0:T(8,128)(2,1)} %copy-done.2, bf16[768,512]{1,0:T(8,128)(2,1)} %get-tuple-element.54.normed_hbm), custom_call_target="tpu_custom_call" | custom-call | flops 402653184 | bytes 8388608 | tf_op jit(solution)/shard_map/pallas_call | solution.py:470
  127.3 0.0 collective-permute-done.refs_1_
  127.3 0.0 copy-done.7
  127.4 6.4 %collective-permute-start.5 = (bf16[128,256]{1,0:T(8,128)(2,1)S(1)}, bf16[128,256]{1,0:T(8,128)(2,1)S(1)}, u32[]{:S(2)}, u32[]{:S(2)}) collective-permute-start(bf16[128,256]{1,0:T(8,128)(2,1)S(1)} %copy-done.7), channel_id=1, source_target_pairs={{0,96},{16,112},{32,0},{48,16},{64,32},{80,48},{96,64},{112,80},{1... | collective-permute-start | bytes 196616 | tf_op jit(solution)/shard_map/ppermute | solution.py:488
  133.8 0.0 collective-permute-done.1.refs_2_
  133.8 0.0 copy-done.6
  133.8 1.0 collective-permute-start.6
  134.8 3.6 %all-to-all-start.4 = ((bf16[16,64,256]{2,1,0:T(8,128)(2,1)}), bf16[16,64,256]{2,1,0:T(8,128)(2,1)S(1)}, u32[]{:S(2)}, u32[]{:S(2)}) async-start(bf16[16,64,256]{2,1,0:T(8,128)(2,1)} %shard_map.125), calls=%async_computation.4 | async-start | bytes 1048576 | tf_op jit(solution)/shard_map/all_to_all | solution.py:485
  138.3 0.0 collective-permute-done.2.refs_3_
  138.3 0.0 collective-permute-done.3.refs_4_
  138.4 0.0 collective-permute-done.4.refs_5_
  138.4 0.1 collective-permute-done.5.refs_6_
  138.4 3.6 %collective-permute-done.6.refs_7_ = bf16[128,256]{1,0:T(8,128)(2,1)S(1)} collective-permute-done((bf16[128,256]{1,0:T(8,128)(2,1)S(1)}, bf16[128,256]{1,0:T(8,128)(2,1)S(1)}, u32[]{:S(2)}, u32[]{:S(2)}) %collective-permute-start.6) | collective-permute-done | bytes 65568 | tf_op jit(solution)/shard_map/ppermute | solution.py:488
  142.0 0.0 copy-done.1
  142.0 0.1 shard_map.128
  142.1 29.6 %reduce-scatter.2.cloned.1.call-done.own_ref = bf16[1,2,64,2048]{3,2,1,0:T(8,128)(2,1)} async-done(((bf16[8,2,64,2048]{3,2,1,0:T(8,128)(2,1)}), bf16[1,2,64,2048]{3,2,1,0:T(8,128)(2,1)}) %reduce-scatter.2.cloned.1.call-update) | async-done | bytes 524304 | tf_op jit(solution)/shard_map/reduce_scatter | solution.py:451
  171.7 1.0 slice_bitcast_fusion
  172.7 1.3 collective-permute-start.7
  173.9 3.3 %shard_map.126 = bf16[768,512]{1,0:T(8,128)(2,1)} custom-call(bf16[16,384,128]{2,1,0:T(8,128)(2,1)} %copy-done.4, bf16[768,512]{1,0:T(8,128)(2,1)} %x_ref.5, bf16[2,512,256]{2,1,0:T(8,128)(2,1)} %w4_ref.3), custom_call_target="tpu_custom_call" | custom-call | flops 64424509440 | bytes 3670016 | tf_op jit(solution)/shard_map/pallas_call | solution.py:51
  177.2 0.0 copy-start
  177.2 0.8 collective-permute-start.8
  178.0 4.3 %shard_map.127 = bf16[768,512]{1,0:T(8,128)(2,1)} custom-call(bf16[16,400,128]{2,1,0:T(8,128)(2,1)} %copy-done.2, bf16[16,400,128]{2,1,0:T(8,128)(2,1)} %copy-done.3, bf16[768,512]{1,0:T(8,128)(2,1)} %x_ref.5, f32[1,512]{1,0:T(1,128)} %bitcast.7, bf16[2,256,512]{2,1,0:T(8,128)(2,1)} %w1_ref.1, bf16[768,512]{1,0:T(8,128)(2,1)} %cot_ref.5), custom_call_target="tpu_custom_call" | custom-call | flops 402653184 | bytes 8388608 | tf_op jit(solution)/shard_map/pallas_call | solution.py:493
  182.3 0.0 collective-permute-done.8.other4_ref
  182.3 0.0 collective-permute-done.7.other_ref
  182.3 0.0 copy-done
  182.4 0.8 shard_map.129
  183.2 0.0 all-to-all-done.4.recv_ref
  183.2 0.7 shard_map.130
Async XLA Ops:
  11.0 27.1 %all-to-all-start = ((bf16[16,400,128]{2,1,0:T(8,128)(2,1)}), bf16[16,400,128]{2,1,0:T(8,128)(2,1)S(1)}, u32[]{:S(2)}, u32[]{:S(2)}) async-start(bf16[16,400,128]{2,1,0:T(8,128)(2,1)} %shard_map.118), calls=%async_computation | async-start | bytes 3276800 | tf_op jit(solution)/shard_map/all_to_all | solution.py:388
  38.1 13.4 %copy-start.3 = (bf16[16,400,128]{2,1,0:T(8,128)(2,1)}, bf16[16,400,128]{2,1,0:T(8,128)(2,1)S(1)}, u32[]{:S(2)}) copy-start(bf16[16,400,128]{2,1,0:T(8,128)(2,1)S(1)} %all-to-all-done.recv_hbm.stats_ref) | copy-start | bytes 4915204
  38.1 27.7 %all-to-all-start.1 = ((bf16[16,384,128]{2,1,0:T(8,128)(2,1)}), bf16[16,384,128]{2,1,0:T(8,128)(2,1)S(1)}, u32[]{:S(2)}, u32[]{:S(2)}) async-start(bf16[16,384,128]{2,1,0:T(8,128)(2,1)} %shard_map.119), calls=%async_computation.1 | async-start | bytes 3145728 | tf_op jit(solution)/shard_map/all_to_all | solution.py:388
  65.8 9.5 %copy-start.5 = (bf16[16,384,128]{2,1,0:T(8,128)(2,1)}, bf16[16,384,128]{2,1,0:T(8,128)(2,1)S(1)}, u32[]{:S(2)}) copy-start(bf16[16,384,128]{2,1,0:T(8,128)(2,1)S(1)} %all-to-all-done.1.dthird_hbm) | copy-start | bytes 4718596
  65.8 28.6 %all-to-all-start.2 = ((bf16[16,384,128]{2,1,0:T(8,128)(2,1)}), bf16[16,384,128]{2,1,0:T(8,128)(2,1)S(1)}, u32[]{:S(2)}, u32[]{:S(2)}) async-start(bf16[16,384,128]{2,1,0:T(8,128)(2,1)} %get-tuple-element.49), calls=%async_computation.2 | async-start | bytes 3145728 | tf_op jit(solution)/shard_map/all_to_all | solution.py:388
  74.3 97.4 %reduce-scatter.2.cloned.1.call-start = ((), (), s32[]{:S(2)}) async-start(), calls=%async_computation.6 | async-start | bytes 4718592 | tf_op jit(solution)/shard_map/reduce_scatter | solution.py:451
  94.4 1.2 copy-start.4
  95.5 27.5 %all-to-all-start.3 = ((bf16[16,400,128]{2,1,0:T(8,128)(2,1)}), bf16[16,400,128]{2,1,0:T(8,128)(2,1)S(1)}, u32[]{:S(2)}, u32[]{:S(2)}) async-start(bf16[16,400,128]{2,1,0:T(8,128)(2,1)} %shard_map.123), calls=%async_computation.3 | async-start | bytes 3276800 | tf_op jit(solution)/shard_map/all_to_all | solution.py:388
  106.8 20.5 %copy-start.7 = (bf16[128,256]{1,0:T(8,128)(2,1)S(1)}, bf16[128,256]{1,0:T(8,128)(2,1)}, u32[]{:S(2)}) copy-start(bf16[128,256]{1,0:T(8,128)(2,1)} %get-tuple-element.64) | copy-start | bytes 196612
  106.8 26.9 %copy-start.6 = (bf16[128,256]{1,0:T(8,128)(2,1)S(1)}, bf16[128,256]{1,0:T(8,128)(2,1)}, u32[]{:S(2)}) copy-start(bf16[128,256]{1,0:T(8,128)(2,1)} %get-tuple-element.65) | copy-start | bytes 196612
  106.8 20.5 %collective-permute-start = (bf16[128,256]{1,0:T(8,128)(2,1)}, bf16[128,256]{1,0:T(8,128)(2,1)S(1)}, u32[]{:S(2)}, u32[]{:S(2)}) collective-permute-start(bf16[128,256]{1,0:T(8,128)(2,1)} %get-tuple-element.59), channel_id=1, source_target_pairs={{0,16},{16,32},{32,48},{48,64},{64,80},{80,96},{96,112},{112,0},{1... | collective-permute-start | bytes 196616 | tf_op jit(solution)/shard_map/ppermute | solution.py:488
  108.7 25.1 %collective-permute-start.1 = (bf16[128,256]{1,0:T(8,128)(2,1)}, bf16[128,256]{1,0:T(8,128)(2,1)S(1)}, u32[]{:S(2)}, u32[]{:S(2)}) collective-permute-start(bf16[128,256]{1,0:T(8,128)(2,1)} %get-tuple-element.60), channel_id=1, source_target_pairs={{0,32},{16,48},{32,64},{48,80},{64,96},{80,112},{96,0},{112,16},{1... | collective-permute-start | bytes 196616 | tf_op jit(solution)/shard_map/ppermute | solution.py:488
  111.9 26.4 %collective-permute-start.2 = (bf16[128,256]{1,0:T(8,128)(2,1)}, bf16[128,256]{1,0:T(8,128)(2,1)S(1)}, u32[]{:S(2)}, u32[]{:S(2)}) collective-permute-start(bf16[128,256]{1,0:T(8,128)(2,1)} %get-tuple-element.61), channel_id=1, source_target_pairs={{0,48},{16,64},{32,80},{48,96},{64,112},{80,0},{96,16},{112,32},{1... | collective-permute-start | bytes 196616 | tf_op jit(solution)/shard_map/ppermute | solution.py:488
  116.0 22.4 %collective-permute-start.3 = (bf16[128,256]{1,0:T(8,128)(2,1)}, bf16[128,256]{1,0:T(8,128)(2,1)S(1)}, u32[]{:S(2)}, u32[]{:S(2)}) collective-permute-start(bf16[128,256]{1,0:T(8,128)(2,1)} %get-tuple-element.62), channel_id=1, source_target_pairs={{0,64},{16,80},{32,96},{48,112},{64,0},{80,16},{96,32},{112,48},{1... | collective-permute-start | bytes 196616 | tf_op jit(solution)/shard_map/ppermute | solution.py:488
  116.5 21.8 %collective-permute-start.4 = (bf16[128,256]{1,0:T(8,128)(2,1)}, bf16[128,256]{1,0:T(8,128)(2,1)S(1)}, u32[]{:S(2)}, u32[]{:S(2)}) collective-permute-start(bf16[128,256]{1,0:T(8,128)(2,1)} %get-tuple-element.63), channel_id=1, source_target_pairs={{0,80},{16,96},{32,112},{48,0},{64,16},{80,32},{96,48},{112,64},{1... | collective-permute-start | bytes 196616 | tf_op jit(solution)/shard_map/ppermute | solution.py:488
  123.0 1.2 copy-start.2
  124.2 17.8 %copy-start.1 = (bf16[128,256]{1,0:T(8,128)(2,1)S(1)}, bf16[128,256]{1,0:T(8,128)(2,1)}, u32[]{:S(2)}) copy-start(bf16[128,256]{1,0:T(8,128)(2,1)} %get-tuple-element.58.refs_0_) | copy-start | bytes 196612
  127.4 11.1 %collective-permute-start.5 = (bf16[128,256]{1,0:T(8,128)(2,1)S(1)}, bf16[128,256]{1,0:T(8,128)(2,1)S(1)}, u32[]{:S(2)}, u32[]{:S(2)}) collective-permute-start(bf16[128,256]{1,0:T(8,128)(2,1)S(1)} %copy-done.7), channel_id=1, source_target_pairs={{0,96},{16,112},{32,0},{48,16},{64,32},{80,48},{96,64},{112,80},{1... | collective-permute-start | bytes 196616 | tf_op jit(solution)/shard_map/ppermute | solution.py:488
  133.8 8.2 %collective-permute-start.6 = (bf16[128,256]{1,0:T(8,128)(2,1)S(1)}, bf16[128,256]{1,0:T(8,128)(2,1)S(1)}, u32[]{:S(2)}, u32[]{:S(2)}) collective-permute-start(bf16[128,256]{1,0:T(8,128)(2,1)S(1)} %copy-done.6), channel_id=1, source_target_pairs={{0,112},{16,0},{32,16},{48,32},{64,48},{80,64},{96,80},{112,96},{1... | collective-permute-start | bytes 196616 | tf_op jit(solution)/shard_map/ppermute | solution.py:488
  134.8 48.5 %all-to-all-start.4 = ((bf16[16,64,256]{2,1,0:T(8,128)(2,1)}), bf16[16,64,256]{2,1,0:T(8,128)(2,1)S(1)}, u32[]{:S(2)}, u32[]{:S(2)}) async-start(bf16[16,64,256]{2,1,0:T(8,128)(2,1)} %shard_map.125), calls=%async_computation.4 | async-start | bytes 1048576 | tf_op jit(solution)/shard_map/all_to_all | solution.py:485
  172.7 9.7 %collective-permute-start.7 = (bf16[64,2048]{1,0:T(8,128)(2,1)S(1)}, bf16[64,2048]{1,0:T(8,128)(2,1)S(1)}, u32[]{:S(2)}, u32[]{:S(2)}) collective-permute-start(bf16[64,2048]{1,0:T(8,128)(2,1)S(1)} %slice_bitcast_fusion), channel_id=1, source_target_pairs={{0,128},{16,144},{32,160},{48,176},{64,192},{80,208},{96,224},{112... | collective-permute-start | bytes 786440 | tf_op jit(solution)/shard_map/ppermute | solution.py:503
  177.2 5.2 %copy-start = (bf16[1,2,64,2048]{3,2,1,0:T(8,128)(2,1)S(1)}, bf16[1,2,64,2048]{3,2,1,0:T(8,128)(2,1)}, u32[]{:S(2)}) copy-start(bf16[1,2,64,2048]{3,2,1,0:T(8,128)(2,1)} %reduce-scatter.2.cloned.1.call-done.own_ref) | copy-start | bytes 1572868
  177.2 5.1 %collective-permute-start.8 = (bf16[64,256]{1,0:T(8,128)(2,1)S(1)}, bf16[64,256]{1,0:T(8,128)(2,1)S(1)}, u32[]{:S(2)}, u32[]{:S(2)}) collective-permute-start(bf16[64,256]{1,0:T(8,128)(2,1)S(1)} %get-tuple-element.69), channel_id=1, source_target_pairs={{0,128},{16,144},{32,160},{48,176},{64,192},{80,208},{96,224},{112... | collective-permute-start | bytes 98312 | tf_op jit(solution)/shard_map/ppermute | solution.py:491
Sparse Core Ops, SparseCore 0:
  89.4 82.2 reduce-scatter.1

commit v9 on v7

--- a/solution.py
+++ b/solution.py
@@ -21,6 +21,8 @@
 STEP = 256
 LATE = 160
 VMEM = 58 * 1024 * 1024
+SMALL = 16 * 1024 * 1024
+FIRST = 24 * 1024 * 1024
 
 epsilon = 1e-05
 root_scale = math.sqrt(2.0 / math.pi)
@@ -39,7 +41,7 @@
     return lax.dot_general(a, b, dims, preferred_element_type=F32)
 
 
-def call(kernel, out_shape, args, scratch=(), flops=0, **extra):
+def call(kernel, out_shape, args, scratch=(), flops=0, limit=None, **extra):
     outs = out_shape if isinstance(out_shape, (list, tuple)) else [out_shape]
     moved = sum(a.size * a.dtype.itemsize for a in args) + sum(
         math.prod(o.shape) * o.dtype.itemsize for o in outs
@@ -50,7 +52,7 @@
         in_specs=[pl.BlockSpec(memory_space=pltpu.VMEM)] * len(args),
         out_specs=jax.tree.map(lambda _: pl.BlockSpec(memory_space=pltpu.VMEM), out_shape),
         scratch_shapes=list(scratch),
-        compiler_params=pltpu.CompilerParams(vmem_limit_bytes=VMEM),
+        compiler_params=pltpu.CompilerParams(vmem_limit_bytes=limit or VMEM),
         cost_estimate=pl.CostEstimate(flops=int(flops), bytes_accessed=int(moved), transcendentals=0),
         **extra,
     )(*args)
@@ -225,6 +227,7 @@
         inner_ref[:, i * STEP : (i + 1) * STEP] = jnp.sum(dpre * pre, axis=0, keepdims=True)
         dpre_ref[i] = dpre.astype(BF16)
         scaled_ref[i] = (dpre * reciprocal(stats, i)).astype(BF16)
+    stores.start(dpre_ref, dpre_hbm)
     act_load.wait()
     mixed_load.wait()
     dthird = hidden_rows(dthird_ref)
@@ -242,7 +245,6 @@
         second = dot(mixed, scaled, NT).astype(BF16)
         grads_ref[z, r // 2, :, :HBS] = second.reshape(half, part_rows, HBS)
         stores.start(grads_ref.at[z, r // 2], grads_hbm.at[z, lax.rem(r // 2 + y, y_size)])
-    stores.start(dpre_ref, dpre_hbm)
     stores.wait()
 
 
@@ -466,11 +468,11 @@
             pltpu.VMEM(tokens.shape, BF16),
             pltpu.SemaphoreType.DMA((2,)),
         ],
-        compiler_params=params,
+        compiler_params=pltpu.CompilerParams(vmem_limit_bytes=FIRST),
         cost_estimate=cost(model_flops),
     )(y_index, back, normed)
     firsts = (own, lax.ppermute(other, "dp", y_pairs))
-    both = call(pair_kernel, shape((z_size, 2 * PAIR, BS), BF16), firsts + fourths)
+    both = call(pair_kernel, shape((z_size, 2 * PAIR, BS), BF16), firsts + fourths, limit=SMALL)
     both = lax.all_to_all(both, "dp", 0, 0, axis_index_groups=z_groups, tiled=True)
     token_gradient = pl.pallas_call(
         token_kernel,
@@ -483,12 +485,13 @@
     )(back, recv, tokens, gain_row, w_first, cotangent)
     other = lax.ppermute(hidden[0, 1], "dp", y_pairs)
     part = shape((1, HBS // dp, HBS), F32)
-    grad_second, grad_third = call(functools.partial(finish_kernel, scale), [part, part], (hidden, other))
+    grad_second, grad_third = call(functools.partial(finish_kernel, scale), [part, part], (hidden, other), limit=SMALL)
     both, grad_second, grad_third = lax.optimization_barrier((both, grad_second, grad_third))
     grad_first, grad_fourth = call(
         functools.partial(sum_kernel, scale),
         [shape((2, BS // dp, HB * EB), F32), shape((2, HB * EB // dp, BS), F32)],
         (both,),
+        limit=SMALL,
     )
     return output, token_gradient, grad_first, grad_second, grad_third, grad_fourth
 

time: 177 us -> 171 us (0.966)
  Pallas kernels: 59.1 us -> 52.9 us
  waiting for transfers between devices: 50.3 us -> 52.5 us
    pallas_call x7, Pallas kernels: 22.1 us -> 18.7 us  [call(): pl.pallas_call(kernel, out_shape=out_shape, in_specs=[pl.BlockSpec(memory...]
    pallas_call x1, Pallas kernels: 3.17 us -> 0.82 us  [shards(): pl.pallas_call(first_kernel, out_shape=[part, part], in_specs=[smem, hbm,...]
    unnamed x16 -> x14, local copies, waits for them, and re-layouts: 4.6 us -> 2.88 us
  transfers between devices with their start and end apart: 9 -> 9, of which waited for: 7 -> 8; matrix products, arithmetic and copies ran while one was open for 1% -> 1% of each run, Pallas kernels for 31% -> 29%
where the time goes in v9:
time: 171 us; the launch traced here: 169 us
  Pallas kernels  52.9 us (31%)
  waiting for transfers between devices  52.5 us (31%)
  starting transfers between devices  45.6 us (27%)
  between operations  14.1 us (8%)
  local copies, waits for them, and re-layouts  3.84 us (2%)
    all_to_all x4, waiting for transfers between devices, exchange(): return lax.all_to_all(value, 'tensor', 0, 0, tiled=True)  38.2 us
    all_to_all x4, starting transfers between devices, exchange(): return lax.all_to_all(value, 'tensor', 0, 0, tiled=True)  33 us
    pallas_call x7, Pallas kernels, call(): pl.pallas_call(kernel, out_shape=out_shape, in_specs=[pl.BlockSpec(memory...  18.7 us
    pallas_call x1, Pallas kernels, shards(): pl.pallas_call(backward_kernel, out_shape=[grads, stepped, shape((1, elem...  12.8 us
    pallas_call x1, Pallas kernels, shards(): pl.pallas_call(forward_kernel, out_shape=[pre_shape, stepped, plain_sent]...  8.93 us
    all_to_all x1, starting transfers between devices, shards(): lax.all_to_all(both, 'dp', 0, 0, axis_index_groups=z_groups, tiled=True)  8.46 us
    all_to_all x1, waiting for transfers between devices, shards(): lax.all_to_all(both, 'dp', 0, 0, axis_index_groups=z_groups, tiled=True)  5.79 us
    pallas_call x1, Pallas kernels, shards(): pl.pallas_call(token_kernel, out_shape=shape(tokens.shape, BF16), grid=(1...  4.3 us
  transfers between devices with their start and end apart: 9, of which 8 were waited for; matrix products, arithmetic and copies ran while one was open for 1% of the time, Pallas kernels for 29%

profile of v9, /device:TPU:18, one launch (start us, length us, event | category | flops | bytes accessed | tf_op | source)
XLA Modules:
  0.0 169.0 jit_solution(17531250644497329249)
XLA Ops:
  7.2 3.8 %shard_map.118 = bf16[16,400,128]{2,1,0:T(8,128)(2,1)} custom-call(bf16[768,512]{1,0:T(8,128)(2,1)} %x_ref.5, f32[1,512]{1,0:T(1,128)} %bitcast.4, bf16[2,256,512]{2,1,0:T(8,128)(2,1)} %w1_ref.1), custom_call_target="tpu_custom_call" | custom-call | flops 402653184 | bytes 8388608 | tf_op jit(solution)/shard_map/pallas_call | solution.py:380
  11.0 7.3 %all-to-all-start = ((bf16[16,400,128]{2,1,0:T(8,128)(2,1)}), bf16[16,400,128]{2,1,0:T(8,128)(2,1)S(1)}, u32[]{:S(2)}, u32[]{:S(2)}) async-start(bf16[16,400,128]{2,1,0:T(8,128)(2,1)} %shard_map.118), calls=%async_computation | async-start | bytes 3276800 | tf_op jit(solution)/shard_map/all_to_all | solution.py:378
  18.3 3.0 %shard_map.119 = bf16[16,384,128]{2,1,0:T(8,128)(2,1)} custom-call(bf16[2,512,256]{2,1,0:T(8,128)(2,1)} %w4_ref.3, bf16[768,512]{1,0:T(8,128)(2,1)} %cot_ref.5), custom_call_target="tpu_custom_call" | custom-call | flops 402653184 | bytes 2883584 | tf_op jit(solution)/shard_map/pallas_call | solution.py:49
  21.3 16.8 %all-to-all-done.recv_hbm.stats_ref = bf16[16,400,128]{2,1,0:T(8,128)(2,1)S(1)} async-done(((bf16[16,400,128]{2,1,0:T(8,128)(2,1)}), bf16[16,400,128]{2,1,0:T(8,128)(2,1)S(1)}, u32[]{:S(2)}, u32[]{:S(2)}) %all-to-all-start) | async-done | bytes 1638432 | tf_op jit(solution)/shard_map/all_to_all | solution.py:378
  38.1 0.0 copy-start.4
  38.1 8.6 %all-to-all-start.1 = ((bf16[16,384,128]{2,1,0:T(8,128)(2,1)}), bf16[16,384,128]{2,1,0:T(8,128)(2,1)S(1)}, u32[]{:S(2)}, u32[]{:S(2)}) async-start(bf16[16,384,128]{2,1,0:T(8,128)(2,1)} %shard_map.119), calls=%async_computation.1 | async-start | bytes 3145728 | tf_op jit(solution)/shard_map/all_to_all | solution.py:378
  46.7 4.8 %shard_map.120 = (bf16[1024,1024]{1,0:T(8,128)(2,1)}, bf16[1024,1024]{1,0:T(8,128)(2,1)}) custom-call(bf16[1,1024,1024]{2,1,0:T(8,128)(2,1)} %w2_ref.3, bf16[1,1024,1024]{2,1,0:T(8,128)(2,1)} %w3_hbm.1), custom_call_target="tpu_custom_call" | custom-call | bytes 8388608 | tf_op jit(solution)/shard_map/pallas_call | solution.py:49
  51.5 0.0 copy-done.4
  51.5 8.9 %shard_map.121 = (f32[3,1024,256]{2,1,0:T(8,128)}, bf16[3,1024,256]{2,1,0:T(8,128)(2,1)}, bf16[16,384,128]{2,1,0:T(8,128)(2,1)}) custom-call(bf16[16,400,128]{2,1,0:T(8,128)(2,1)} %copy-done.4, bf16[1024,1024]{1,0:T(8,128)(2,1)} %get-tuple-element.31.w2t_hbm, bf16[1024,1024]{1,0:T(8,128)(2,1)} %get-tuple-element.32.w3t_hbm), custom_call_target="tpu_custom_call" | custom-call | flops 3221225472 | bytes 8388608 | tf_op jit(solution)/shard_map/pallas_call | solution.py:401
  60.5 5.3 %all-to-all-done.1.dthird_hbm = bf16[16,384,128]{2,1,0:T(8,128)(2,1)S(1)} async-done(((bf16[16,384,128]{2,1,0:T(8,128)(2,1)}), bf16[16,384,128]{2,1,0:T(8,128)(2,1)S(1)}, u32[]{:S(2)}, u32[]{:S(2)}) %all-to-all-start.1) | async-done | bytes 1572896 | tf_op jit(solution)/shard_map/all_to_all | solution.py:378
  65.8 0.0 copy-start.6
  65.8 8.6 %all-to-all-start.2 = ((bf16[16,384,128]{2,1,0:T(8,128)(2,1)}), bf16[16,384,128]{2,1,0:T(8,128)(2,1)S(1)}, u32[]{:S(2)}, u32[]{:S(2)}) async-start(bf16[16,384,128]{2,1,0:T(8,128)(2,1)} %get-tuple-element.38), calls=%async_computation.2 | async-start | bytes 3145728 | tf_op jit(solution)/shard_map/all_to_all | solution.py:378
  74.4 0.2 reduce-scatter.2.cloned.1.call-start
  74.6 0.0 copy-done.6
  74.6 12.8 %shard_map.122 = (bf16[8,2,64,2048]{3,2,1,0:T(8,128)(2,1)}, bf16[3,1024,256]{2,1,0:T(8,128)(2,1)}, f32[1,768]{1,0:T(1,128)}) custom-call(s32[1]{0:T(128)} %bitcast.y_ref, bf16[16,400,128]{2,1,0:T(8,128)(2,1)} %copy-done.4, bf16[16,384,128]{2,1,0:T(8,128)(2,1)} %copy-done.6, f32[3,1024,256]{2,1,0:T(8,128)} %get-tuple-element.33.pre_hbm, ...), custom_call_target="tpu_custom_call" | custom-call | flops 4831838208 | bytes 8388608 | tf_op jit(solution)/shard_map/pallas_call | solution.py:421
  87.4 0.0 reduce-scatter.2.cloned.1.call-update
  87.5 5.1 %shard_map.123 = bf16[16,400,128]{2,1,0:T(8,128)(2,1)} custom-call(bf16[3,1024,256]{2,1,0:T(8,128)(2,1)} %get-tuple-element.35.dpre_ref, f32[1,768]{1,0:T(1,128)} %get-tuple-element.36.inner_ref, bf16[1,1024,1024]{2,1,0:T(8,128)(2,1)} %w2_ref.3), custom_call_target="tpu_custom_call" | custom-call | flops 1610612736 | bytes 5311488 | tf_op jit(solution)/shard_map/pallas_call | solution.py:49
  92.5 0.9 all-to-all-done.2.recv_ref
  93.4 0.0 copy-start.5
  93.4 1.2 copy-done.5
  94.6 8.6 %all-to-all-start.3 = ((bf16[16,400,128]{2,1,0:T(8,128)(2,1)}), bf16[16,400,128]{2,1,0:T(8,128)(2,1)S(1)}, u32[]{:S(2)}, u32[]{:S(2)}) async-start(bf16[16,400,128]{2,1,0:T(8,128)(2,1)} %shard_map.123), calls=%async_computation.3 | async-start | bytes 3276800 | tf_op jit(solution)/shard_map/all_to_all | solution.py:378
  103.2 3.5 %shard_map.126 = (bf16[8,64,256]{2,1,0:T(8,128)(2,1)}, bf16[8,64,256]{2,1,0:T(8,128)(2,1)}, bf16[768,512]{1,0:T(8,128)(2,1)}) custom-call(s32[1]{0:T(128)} %bitcast.y_ref, bf16[16,384,128]{2,1,0:T(8,128)(2,1)} %copy-done.5, bf16[768,512]{1,0:T(8,128)(2,1)} %cot_ref.5, bf16[768,512]{1,0:T(8,128)(2,1)} %x_ref.5, f32[1,512]{1,0:T(1,128)} %bitcast.5, ...), custom_call_target="tpu_custom_call" | custom-call | flops 402653184 | bytes 8388608 | tf_op jit(solution)/shard_map/pallas_call | solution.py:450
  106.7 1.3 collective-permute-start.1
  108.0 15.1 %all-to-all-done.3.recv_ref.recv_hbm = bf16[16,400,128]{2,1,0:T(8,128)(2,1)S(1)} async-done(((bf16[16,400,128]{2,1,0:T(8,128)(2,1)}), bf16[16,400,128]{2,1,0:T(8,128)(2,1)S(1)}, u32[]{:S(2)}, u32[]{:S(2)}) %all-to-all-start.3) | async-done | bytes 1638432 | tf_op jit(solution)/shard_map/all_to_all | solution.py:378
  123.1 0.0 copy-start
  123.1 0.0 copy-start.2
  123.1 1.7 copy-done.2
  124.8 0.8 shard_map.127
  125.6 0.0 copy-start.3
  125.6 1.4 collective-permute-start
  127.0 3.3 %shard_map.124 = bf16[768,512]{1,0:T(8,128)(2,1)} custom-call(bf16[16,384,128]{2,1,0:T(8,128)(2,1)} %copy-done.5, bf16[768,512]{1,0:T(8,128)(2,1)} %x_ref.5, bf16[2,512,256]{2,1,0:T(8,128)(2,1)} %w4_ref.3), custom_call_target="tpu_custom_call" | custom-call | flops 64424509440 | bytes 3670016 | tf_op jit(solution)/shard_map/pallas_call | solution.py:49
  130.3 0.0 copy-done
  130.3 0.0 collective-permute-done.1.fourth_other
  130.3 4.2 %collective-permute-done.first_other = bf16[8,64,256]{2,1,0:T(8,128)(2,1)S(1)} collective-permute-done((bf16[8,64,256]{2,1,0:T(8,128)(2,1)S(1)}, bf16[8,64,256]{2,1,0:T(8,128)(2,1)S(1)}, u32[]{:S(2)}, u32[]{:S(2)}) %collective-permute-start) | collective-permute-done | bytes 262176 | tf_op jit(solution)/shard_map/ppermute | solution.py:474
  134.5 0.0 copy-done.3
  134.5 0.9 shard_map.128
  135.4 8.5 %all-to-all-start.4 = ((bf16[8,128,256]{2,1,0:T(8,128)(2,1)}), bf16[8,128,256]{2,1,0:T(8,128)(2,1)S(1)}, u32[]{:S(2)}, u32[]{:S(2)}) async-start(bf16[8,128,256]{2,1,0:T(8,128)(2,1)} %shard_map.128), calls=%async_computation.4 | async-start | bytes 1048576 | tf_op jit(solution)/shard_map/all_to_all | solution.py:476
  143.9 1.7 %reduce-scatter.2.cloned.1.call-done.own_ref = bf16[1,2,64,2048]{3,2,1,0:T(8,128)(2,1)} async-done(((bf16[8,2,64,2048]{3,2,1,0:T(8,128)(2,1)}), bf16[1,2,64,2048]{3,2,1,0:T(8,128)(2,1)}) %reduce-scatter.2.cloned.1.call-update) | async-done | bytes 524304 | tf_op jit(solution)/shard_map/reduce_scatter | solution.py:441
  145.6 1.0 slice_bitcast_fusion
  146.6 0.0 copy-start.1
  146.6 1.3 collective-permute-start.2
  147.9 4.3 %shard_map.125 = bf16[768,512]{1,0:T(8,128)(2,1)} custom-call(bf16[16,400,128]{2,1,0:T(8,128)(2,1)} %copy-done, bf16[16,400,128]{2,1,0:T(8,128)(2,1)} %copy-done.4, bf16[768,512]{1,0:T(8,128)(2,1)} %x_ref.5, f32[1,512]{1,0:T(1,128)} %bitcast.6, bf16[2,256,512]{2,1,0:T(8,128)(2,1)} %w1_ref.1, bf16[768,512]{1,0:T(8,128)(2,1)} %cot_ref.5), custom_call_target="tpu_custom_call" | custom-call | flops 64424509440 | bytes 8388608 | tf_op jit(solution)/shard_map/pallas_call | solution.py:477
  152.2 2.6 %collective-permute-done.2.other_ref = bf16[64,2048]{1,0:T(8,128)(2,1)S(1)} collective-permute-done((bf16[64,2048]{1,0:T(8,128)(2,1)S(1)}, bf16[64,2048]{1,0:T(8,128)(2,1)S(1)}, u32[]{:S(2)}, u32[]{:S(2)}) %collective-permute-start.2) | collective-permute-done | bytes 262176 | tf_op jit(solution)/shard_map/ppermute | solution.py:486
  154.8 0.0 copy-done.1
  154.8 0.8 shard_map.129
  155.6 5.8 %all-to-all-done.4.recv_ref = bf16[8,128,256]{2,1,0:T(8,128)(2,1)S(1)} async-done(((bf16[8,128,256]{2,1,0:T(8,128)(2,1)}), bf16[8,128,256]{2,1,0:T(8,128)(2,1)S(1)}, u32[]{:S(2)}, u32[]{:S(2)}) %all-to-all-start.4) | async-done | bytes 524320 | tf_op jit(solution)/shard_map/all_to_all | solution.py:476
  161.4 0.7 shard_map.130
Async XLA Ops:
  11.0 27.1 %all-to-all-start = ((bf16[16,400,128]{2,1,0:T(8,128)(2,1)}), bf16[16,400,128]{2,1,0:T(8,128)(2,1)S(1)}, u32[]{:S(2)}, u32[]{:S(2)}) async-start(bf16[16,400,128]{2,1,0:T(8,128)(2,1)} %shard_map.118), calls=%async_computation | async-start | bytes 3276800 | tf_op jit(solution)/shard_map/all_to_all | solution.py:378
  38.1 13.4 %copy-start.4 = (bf16[16,400,128]{2,1,0:T(8,128)(2,1)}, bf16[16,400,128]{2,1,0:T(8,128)(2,1)S(1)}, u32[]{:S(2)}) copy-start(bf16[16,400,128]{2,1,0:T(8,128)(2,1)S(1)} %all-to-all-done.recv_hbm.stats_ref) | copy-start | bytes 4915204
  38.1 27.7 %all-to-all-start.1 = ((bf16[16,384,128]{2,1,0:T(8,128)(2,1)}), bf16[16,384,128]{2,1,0:T(8,128)(2,1)S(1)}, u32[]{:S(2)}, u32[]{:S(2)}) async-start(bf16[16,384,128]{2,1,0:T(8,128)(2,1)} %shard_map.119), calls=%async_computation.1 | async-start | bytes 3145728 | tf_op jit(solution)/shard_map/all_to_all | solution.py:378
  65.8 8.8 %copy-start.6 = (bf16[16,384,128]{2,1,0:T(8,128)(2,1)}, bf16[16,384,128]{2,1,0:T(8,128)(2,1)S(1)}, u32[]{:S(2)}) copy-start(bf16[16,384,128]{2,1,0:T(8,128)(2,1)S(1)} %all-to-all-done.1.dthird_hbm) | copy-start | bytes 4718596
  65.8 27.6 %all-to-all-start.2 = ((bf16[16,384,128]{2,1,0:T(8,128)(2,1)}), bf16[16,384,128]{2,1,0:T(8,128)(2,1)S(1)}, u32[]{:S(2)}, u32[]{:S(2)}) async-start(bf16[16,384,128]{2,1,0:T(8,128)(2,1)} %get-tuple-element.38), calls=%async_computation.2 | async-start | bytes 3145728 | tf_op jit(solution)/shard_map/all_to_all | solution.py:378
  74.4 71.3 %reduce-scatter.2.cloned.1.call-start = ((), (), s32[]{:S(2)}) async-start(), calls=%async_computation.6 | async-start | bytes 4718592 | tf_op jit(solution)/shard_map/reduce_scatter | solution.py:441
  93.4 1.2 copy-start.5
  94.6 28.5 %all-to-all-start.3 = ((bf16[16,400,128]{2,1,0:T(8,128)(2,1)}), bf16[16,400,128]{2,1,0:T(8,128)(2,1)S(1)}, u32[]{:S(2)}, u32[]{:S(2)}) async-start(bf16[16,400,128]{2,1,0:T(8,128)(2,1)} %shard_map.123), calls=%async_computation.3 | async-start | bytes 3276800 | tf_op jit(solution)/shard_map/all_to_all | solution.py:378
  106.7 23.6 %collective-permute-start.1 = (bf16[8,64,256]{2,1,0:T(8,128)(2,1)}, bf16[8,64,256]{2,1,0:T(8,128)(2,1)S(1)}, u32[]{:S(2)}, u32[]{:S(2)}) collective-permute-start(bf16[8,64,256]{2,1,0:T(8,128)(2,1)} %get-tuple-element.45), channel_id=1, source_target_pairs={{0,128},{16,144},{32,160},{48,176},{64,192},{80,208},{96,224},{112... | collective-permute-start | bytes 786440 | tf_op jit(solution)/shard_map/ppermute | solution.py:459
  123.1 7.2 %copy-start = (bf16[16,400,128]{2,1,0:T(8,128)(2,1)}, bf16[16,400,128]{2,1,0:T(8,128)(2,1)S(1)}, u32[]{:S(2)}) copy-start(bf16[16,400,128]{2,1,0:T(8,128)(2,1)S(1)} %all-to-all-done.3.recv_ref.recv_hbm) | copy-start | bytes 4915204
  123.1 1.7 copy-start.2
  125.6 8.9 %copy-start.3 = (bf16[8,64,256]{2,1,0:T(8,128)(2,1)S(1)}, bf16[8,64,256]{2,1,0:T(8,128)(2,1)}, u32[]{:S(2)}) copy-start(bf16[8,64,256]{2,1,0:T(8,128)(2,1)} %get-tuple-element.44.fourth_own) | copy-start | bytes 786436
  125.6 8.9 %collective-permute-start = (bf16[8,64,256]{2,1,0:T(8,128)(2,1)S(1)}, bf16[8,64,256]{2,1,0:T(8,128)(2,1)S(1)}, u32[]{:S(2)}, u32[]{:S(2)}) collective-permute-start(bf16[8,64,256]{2,1,0:T(8,128)(2,1)S(1)} %get-tuple-element.43), channel_id=1, source_target_pairs={{0,128},{16,144},{32,160},{48,176},{64,192},{80,208},{96,224},{112... | collective-permute-start | bytes 786440 | tf_op jit(solution)/shard_map/ppermute | solution.py:474
  135.4 26.0 %all-to-all-start.4 = ((bf16[8,128,256]{2,1,0:T(8,128)(2,1)}), bf16[8,128,256]{2,1,0:T(8,128)(2,1)S(1)}, u32[]{:S(2)}, u32[]{:S(2)}) async-start(bf16[8,128,256]{2,1,0:T(8,128)(2,1)} %shard_map.128), calls=%async_computation.4 | async-start | bytes 1048576 | tf_op jit(solution)/shard_map/all_to_all | solution.py:476
  146.6 8.2 %copy-start.1 = (bf16[1,2,64,2048]{3,2,1,0:T(8,128)(2,1)S(1)}, bf16[1,2,64,2048]{3,2,1,0:T(8,128)(2,1)}, u32[]{:S(2)}) copy-start(bf16[1,2,64,2048]{3,2,1,0:T(8,128)(2,1)} %reduce-scatter.2.cloned.1.call-done.own_ref) | copy-start | bytes 1572868
  146.6 8.2 %collective-permute-start.2 = (bf16[64,2048]{1,0:T(8,128)(2,1)S(1)}, bf16[64,2048]{1,0:T(8,128)(2,1)S(1)}, u32[]{:S(2)}, u32[]{:S(2)}) collective-permute-start(bf16[64,2048]{1,0:T(8,128)(2,1)S(1)} %slice_bitcast_fusion), channel_id=1, source_target_pairs={{0,128},{16,144},{32,160},{48,176},{64,192},{80,208},{96,224},{112... | collective-permute-start | bytes 786440 | tf_op jit(solution)/shard_map/ppermute | solution.py:486
Sparse Core Ops, SparseCore 0:
  87.6 58.0 reduce-scatter.1

commit v10 on v9

--- a/solution.py
+++ b/solution.py
@@ -159,8 +159,8 @@
 
 
 def forward_kernel(
-    recv_hbm, w2t_hbm, w3t_hbm, pre_hbm, act_hbm, out_hbm,
-    recv_ref, w2t_ref, w3t_ref, pre_ref, act_ref, out_ref, in_sems, out_sems,
+    recv_hbm, w2t_hbm, w3t_hbm, slope_hbm, act_hbm, out_hbm,
+    recv_ref, w2t_ref, w3t_ref, slope_ref, act_ref, out_ref, in_sems, out_sems,
 ):
     steps = act_ref.shape[0]
     rows = steps * 2 * PAIR
@@ -179,11 +179,15 @@
     for i in range(steps):
         row_loads[i].wait()
         pre = dot(w2t_ref[...], hidden_rows(recv_ref.at[:, parts[i]]), NN) * reciprocal(stats, i)
-        pre_ref[i] = pre
-        stores.start(pre_ref.at[i], pre_hbm.at[i])
-        hyper = jnp.tanh(pre * (root_scale + (root_scale * cubic_term) * (pre * pre)))
+        square = pre * pre
+        hyper = jnp.tanh(pre * (root_scale + (root_scale * cubic_term) * square))
         half = 0.5 * pre
         act_ref[i] = (half + half * hyper).astype(BF16)
+        slope = (0.5 + 0.5 * hyper) + half * (1.0 - hyper * hyper) * (
+            root_scale + (3.0 * root_scale * cubic_term) * square
+        )
+        slope_ref[i] = slope.astype(BF16)
+        stores.start(slope_ref.at[i], slope_hbm.at[i])
     stores.start(act_ref, act_hbm)
     w3t_load.wait()
     for i in range(steps):
@@ -194,8 +198,8 @@
 
 
 def backward_kernel(
-    y_ref, recv_hbm, dthird_hbm, pre_hbm, act_hbm, w3_hbm, grads_hbm, dpre_hbm, inner_ref,
-    recv_ref, dthird_ref, pre_ref, act_ref, w3_ref, dpre_ref, scaled_ref, grads_ref, in_sems, out_sems,
+    y_ref, recv_hbm, dthird_hbm, slope_hbm, act_hbm, w3_hbm, grads_hbm, dpre_hbm,
+    recv_ref, dthird_ref, slope_ref, act_ref, w3_ref, dpre_ref, scaled_ref, grads_ref, in_sems, out_sems,
 ):
     steps = act_ref.shape[0]
     rows = steps * 2 * PAIR
@@ -207,7 +211,7 @@
     stats_load = loads.start(recv_hbm.at[:, rest], recv_ref.at[:, rest])
     w3_load = loads.start(w3_hbm, w3_ref)
     third_loads = [loads.start(dthird_hbm.at[:, part], dthird_ref.at[:, part]) for part in parts]
-    pre_loads = [loads.start(pre_hbm.at[i], pre_ref.at[i]) for i in range(steps)]
+    slope_loads = [loads.start(slope_hbm.at[i], slope_ref.at[i]) for i in range(steps)]
     act_load = loads.start(act_hbm, act_ref)
     mixed_load = loads.start(recv_hbm.at[:, pl.ds(0, rows)], recv_ref.at[:, pl.ds(0, rows)])
     stats_load.wait()
@@ -215,16 +219,9 @@
     w3_load.wait()
     for i in range(steps):
         third_loads[i].wait()
-        pre_loads[i].wait()
+        slope_loads[i].wait()
         dact = dot(w3_ref[0], hidden_rows(dthird_ref.at[:, parts[i]]), NN)
-        pre = pre_ref[i]
-        square = pre * pre
-        hyper = jnp.tanh(pre * (root_scale + (root_scale * cubic_term) * square))
-        slope = (0.5 + 0.5 * hyper) + (0.5 * pre) * (1.0 - hyper * hyper) * (
-            root_scale + (3.0 * root_scale * cubic_term) * square
-        )
-        dpre = dact * slope
-        inner_ref[:, i * STEP : (i + 1) * STEP] = jnp.sum(dpre * pre, axis=0, keepdims=True)
+        dpre = dact * slope_ref[i].astype(F32)
         dpre_ref[i] = dpre.astype(BF16)
         scaled_ref[i] = (dpre * reciprocal(stats, i)).astype(BF16)
     stores.start(dpre_ref, dpre_hbm)
@@ -248,13 +245,19 @@
     stores.wait()
 
 
-def dmixed_kernel(dpre_ref, inner_ref, w2_ref, out_ref):
+def dmixed_kernel(dpre_ref, recv_ref, w2_ref, out_ref):
     steps = dpre_ref.shape[0]
+    rows = steps * 2 * PAIR
+    stats = stat_sum(recv_ref[:, rows:, :])
+    inner = []
     for i in range(steps):
-        dmixed = dot(w2_ref[0], dpre_ref[i], NN).astype(BF16)
-        out_ref[:, i * 2 * PAIR : (i + 1) * 2 * PAIR, :] = by_peer(dmixed)
-    rest = stat_rows(inner_ref[...], 2 * steps)
-    out_ref[:, steps * 2 * PAIR :, :] = jnp.broadcast_to(rest[None], (PEERS, STATS, LANES))
+        part = slice(i * 2 * PAIR, (i + 1) * 2 * PAIR)
+        dmixed = dot(w2_ref[0], dpre_ref[i], NN)
+        out_ref[:, part, :] = by_peer(dmixed.astype(BF16))
+        mixed = hidden_rows(recv_ref.at[:, part]).astype(F32)
+        inner.append(jnp.sum(dmixed * mixed, axis=0, keepdims=True) * reciprocal(stats, i))
+    rest = stat_rows(jnp.concatenate(inner, axis=1), 2 * steps)
+    out_ref[:, rows:, :] = jnp.broadcast_to(rest[None], (PEERS, STATS, LANES))
 
 
 def model_rows(ref, chunks, a):
@@ -397,17 +400,16 @@
     dthird = exchange(lax.optimization_barrier((send, recv))[0])
     turned = shape((HBS, HBS), BF16)
     w_second_t, w_third_t = call(turn_kernel, [turned, turned], (w_second, w_third))
-    pre_shape = shape(stepped.shape, F32)
-    pre, act, send = pl.pallas_call(
+    slope, act, send = pl.pallas_call(
         forward_kernel,
-        out_shape=[pre_shape, stepped, plain_sent],
+        out_shape=[stepped, stepped, plain_sent],
         in_specs=[hbm] * 3,
         out_specs=[hbm] * 3,
         scratch_shapes=[
             pltpu.VMEM(stats_sent.shape, BF16),
             pltpu.VMEM(turned.shape, BF16),
             pltpu.VMEM(turned.shape, BF16),
-            pltpu.VMEM(stepped.shape, F32),
+            pltpu.VMEM(stepped.shape, BF16),
             pltpu.VMEM(stepped.shape, BF16),
             pltpu.VMEM(plain_sent.shape, BF16),
             pltpu.SemaphoreType.DMA((steps + 3,)),
@@ -418,15 +420,15 @@
     )(recv, w_second_t, w_third_t)
     third = exchange(lax.optimization_barrier((send, dthird))[0])
     grads = shape((z_size, 2, HBS // dp, 2 * HBS), BF16)
-    hidden, dpre, inner = pl.pallas_call(
+    hidden, dpre = pl.pallas_call(
         backward_kernel,
-        out_shape=[grads, stepped, shape((1, element_count), F32)],
+        out_shape=[grads, stepped],
         in_specs=[smem] + [hbm] * 5,
-        out_specs=[hbm, hbm, vmem],
+        out_specs=[hbm, hbm],
         scratch_shapes=[
             pltpu.VMEM(stats_sent.shape, BF16),
             pltpu.VMEM(plain_sent.shape, BF16),
-            pltpu.VMEM(stepped.shape, F32),
+            pltpu.VMEM(stepped.shape, BF16),
             pltpu.VMEM(stepped.shape, BF16),
             pltpu.VMEM(w_third.shape, BF16),
             pltpu.VMEM(stepped.shape, BF16),
@@ -437,9 +439,9 @@
         ],
         compiler_params=params,
         cost_estimate=cost(3 * hidden_flops),
-    )(y_index, recv, dthird, pre, act, w_third)
+    )(y_index, recv, dthird, slope, act, w_third)
     hidden = lax.psum_scatter(hidden, "dp", scatter_dimension=0, axis_index_groups=z_groups, tiled=True)
-    send = call(dmixed_kernel, stats_sent, (dpre, inner, w_second), flops=hidden_flops)
+    send = call(dmixed_kernel, stats_sent, (dpre, recv, w_second), flops=hidden_flops)
     send, third = lax.optimization_barrier((send, third))
     back = exchange(send)
 

time: 171 us -> 171 us (level)
    reduce_scatter x1, waiting for transfers between devices: 1.75 us -> 0.01 us  [shards(): lax.psum_scatter(hidden, 'dp', scatter_dimension=0, axis_index_groups=z_g...]
    all_to_all x1, waiting for transfers between devices: 5.79 us -> 7.52 us  [shards(): lax.all_to_all(both, 'dp', 0, 0, axis_index_groups=z_groups, tiled=True)]
  transfers between devices with their start and end apart: 9 -> 9, of which waited for: 8 -> 7; matrix products, arithmetic and copies ran while one was open for 1% -> 1% of each run, Pallas kernels for 29% -> 29%
where the time goes in v10:
time: 171 us; the launch traced here: 169 us
  Pallas kernels  52.7 us (31%)
  waiting for transfers between devices  52.6 us (31%)
  starting transfers between devices  45.7 us (27%)
  between operations  14.1 us (8%)
  local copies, waits for them, and re-layouts  3.84 us (2%)
    all_to_all x4, waiting for transfers between devices, exchange(): return lax.all_to_all(value, 'tensor', 0, 0, tiled=True)  38.3 us
    all_to_all x4, starting transfers between devices, exchange(): return lax.all_to_all(value, 'tensor', 0, 0, tiled=True)  33 us
    pallas_call x7, Pallas kernels, call(): pl.pallas_call(kernel, out_shape=out_shape, in_specs=[pl.BlockSpec(memory...  19.3 us
    pallas_call x1, Pallas kernels, shards(): pl.pallas_call(backward_kernel, out_shape=[grads, stepped], in_specs=[sme...  11 us
    pallas_call x1, Pallas kernels, shards(): pl.pallas_call(forward_kernel, out_shape=[stepped, stepped, plain_sent],...  9.91 us
    all_to_all x1, starting transfers between devices, shards(): lax.all_to_all(both, 'dp', 0, 0, axis_index_groups=z_groups, tiled=True)  8.49 us
    all_to_all x1, waiting for transfers between devices, shards(): lax.all_to_all(both, 'dp', 0, 0, axis_index_groups=z_groups, tiled=True)  7.52 us
    pallas_call x1, Pallas kernels, shards(): pl.pallas_call(token_kernel, out_shape=shape(tokens.shape, BF16), grid=(1...  4.3 us
  transfers between devices with their start and end apart: 9, of which 7 were waited for; matrix products, arithmetic and copies ran while one was open for 1% of the time, Pallas kernels for 29%

profile of v10, /device:TPU:18, one launch (start us, length us, event | category | flops | bytes accessed | tf_op | source)
XLA Modules:
  0.0 168.9 jit_solution(12281424656373638047)
XLA Ops:
  7.2 3.8 %shard_map.118 = bf16[16,400,128]{2,1,0:T(8,128)(2,1)} custom-call(bf16[768,512]{1,0:T(8,128)(2,1)} %x_ref.5, f32[1,512]{1,0:T(1,128)} %bitcast.4, bf16[2,256,512]{2,1,0:T(8,128)(2,1)} %w1_ref.1), custom_call_target="tpu_custom_call" | custom-call | flops 402653184 | bytes 8388608 | tf_op jit(solution)/shard_map/pallas_call | solution.py:383
  11.0 7.3 %all-to-all-start = ((bf16[16,400,128]{2,1,0:T(8,128)(2,1)}), bf16[16,400,128]{2,1,0:T(8,128)(2,1)S(1)}, u32[]{:S(2)}, u32[]{:S(2)}) async-start(bf16[16,400,128]{2,1,0:T(8,128)(2,1)} %shard_map.118), calls=%async_computation | async-start | bytes 3276800 | tf_op jit(solution)/shard_map/all_to_all | solution.py:381
  18.3 3.1 %shard_map.119 = bf16[16,384,128]{2,1,0:T(8,128)(2,1)} custom-call(bf16[2,512,256]{2,1,0:T(8,128)(2,1)} %w4_ref.3, bf16[768,512]{1,0:T(8,128)(2,1)} %cot_ref.5), custom_call_target="tpu_custom_call" | custom-call | flops 402653184 | bytes 2883584 | tf_op jit(solution)/shard_map/pallas_call | solution.py:49
  21.3 16.8 %all-to-all-done.recv_hbm.recv_ref.stats_ref = bf16[16,400,128]{2,1,0:T(8,128)(2,1)S(1)} async-done(((bf16[16,400,128]{2,1,0:T(8,128)(2,1)}), bf16[16,400,128]{2,1,0:T(8,128)(2,1)S(1)}, u32[]{:S(2)}, u32[]{:S(2)}) %all-to-all-start) | async-done | bytes 1638432 | tf_op jit(solution)/shard_map/all_to_all | solution.py:381
  38.1 0.0 copy-start.4
  38.1 8.6 %all-to-all-start.1 = ((bf16[16,384,128]{2,1,0:T(8,128)(2,1)}), bf16[16,384,128]{2,1,0:T(8,128)(2,1)S(1)}, u32[]{:S(2)}, u32[]{:S(2)}) async-start(bf16[16,384,128]{2,1,0:T(8,128)(2,1)} %shard_map.119), calls=%async_computation.1 | async-start | bytes 3145728 | tf_op jit(solution)/shard_map/all_to_all | solution.py:381
  46.7 4.8 %shard_map.120 = (bf16[1024,1024]{1,0:T(8,128)(2,1)}, bf16[1024,1024]{1,0:T(8,128)(2,1)}) custom-call(bf16[1,1024,1024]{2,1,0:T(8,128)(2,1)} %w2_ref.3, bf16[1,1024,1024]{2,1,0:T(8,128)(2,1)} %w3_hbm.1), custom_call_target="tpu_custom_call" | custom-call | bytes 8388608 | tf_op jit(solution)/shard_map/pallas_call | solution.py:49
  51.6 0.0 copy-done.4
  51.6 9.9 %shard_map.121 = (bf16[3,1024,256]{2,1,0:T(8,128)(2,1)}, bf16[3,1024,256]{2,1,0:T(8,128)(2,1)}, bf16[16,384,128]{2,1,0:T(8,128)(2,1)}) custom-call(bf16[16,400,128]{2,1,0:T(8,128)(2,1)} %copy-done.4, bf16[1024,1024]{1,0:T(8,128)(2,1)} %get-tuple-element.30.w2t_hbm, bf16[1024,1024]{1,0:T(8,128)(2,1)} %get-tuple-element.31.w3t_hbm), custom_call_target="tpu_custom_call" | custom-call | flops 3221225472 | bytes 8388608 | tf_op jit(solution)/shard_map/pallas_call | solution.py:403
  61.5 4.3 %all-to-all-done.1.dthird_hbm = bf16[16,384,128]{2,1,0:T(8,128)(2,1)S(1)} async-done(((bf16[16,384,128]{2,1,0:T(8,128)(2,1)}), bf16[16,384,128]{2,1,0:T(8,128)(2,1)S(1)}, u32[]{:S(2)}, u32[]{:S(2)}) %all-to-all-start.1) | async-done | bytes 1572896 | tf_op jit(solution)/shard_map/all_to_all | solution.py:381
  65.8 0.0 copy-start.6
  65.8 8.6 %all-to-all-start.2 = ((bf16[16,384,128]{2,1,0:T(8,128)(2,1)}), bf16[16,384,128]{2,1,0:T(8,128)(2,1)S(1)}, u32[]{:S(2)}, u32[]{:S(2)}) async-start(bf16[16,384,128]{2,1,0:T(8,128)(2,1)} %get-tuple-element.36), calls=%async_computation.2 | async-start | bytes 3145728 | tf_op jit(solution)/shard_map/all_to_all | solution.py:381
  74.4 0.2 reduce-scatter.2.cloned.1.call-start
  74.6 0.0 copy-done.6
  74.6 11.0 %shard_map.122 = (bf16[8,2,64,2048]{3,2,1,0:T(8,128)(2,1)}, bf16[3,1024,256]{2,1,0:T(8,128)(2,1)}) custom-call(s32[1]{0:T(128)} %bitcast.y_ref, bf16[16,400,128]{2,1,0:T(8,128)(2,1)} %copy-done.4, bf16[16,384,128]{2,1,0:T(8,128)(2,1)} %copy-done.6, bf16[3,1024,256]{2,1,0:T(8,128)(2,1)} %get-tuple-element.32.slope_hbm, ...), custom_call_target="tpu_custom_call" | custom-call | flops 4831838208 | bytes 8388608 | tf_op jit(solution)/shard_map/pallas_call | solution.py:423
  85.7 0.0 reduce-scatter.2.cloned.1.call-update
  85.7 5.6 %shard_map.123 = bf16[16,400,128]{2,1,0:T(8,128)(2,1)} custom-call(bf16[3,1024,256]{2,1,0:T(8,128)(2,1)} %get-tuple-element.34.dpre_ref, bf16[16,400,128]{2,1,0:T(8,128)(2,1)} %copy-done.4, bf16[1,1024,1024]{2,1,0:T(8,128)(2,1)} %w2_ref.3), custom_call_target="tpu_custom_call" | custom-call | flops 1610612736 | bytes 6946816 | tf_op jit(solution)/shard_map/pallas_call | solution.py:49
  91.3 2.1 %all-to-all-done.2.recv_ref = bf16[16,384,128]{2,1,0:T(8,128)(2,1)S(1)} async-done(((bf16[16,384,128]{2,1,0:T(8,128)(2,1)}), bf16[16,384,128]{2,1,0:T(8,128)(2,1)S(1)}, u32[]{:S(2)}, u32[]{:S(2)}) %all-to-all-start.2) | async-done | bytes 1572896 | tf_op jit(solution)/shard_map/all_to_all | solution.py:381
  93.4 0.0 copy-start.5
  93.4 1.1 copy-done.5
  94.6 8.6 %all-to-all-start.3 = ((bf16[16,400,128]{2,1,0:T(8,128)(2,1)}), bf16[16,400,128]{2,1,0:T(8,128)(2,1)S(1)}, u32[]{:S(2)}, u32[]{:S(2)}) async-start(bf16[16,400,128]{2,1,0:T(8,128)(2,1)} %shard_map.123), calls=%async_computation.3 | async-start | bytes 3276800 | tf_op jit(solution)/shard_map/all_to_all | solution.py:381
  103.1 3.5 %shard_map.126 = (bf16[8,64,256]{2,1,0:T(8,128)(2,1)}, bf16[8,64,256]{2,1,0:T(8,128)(2,1)}, bf16[768,512]{1,0:T(8,128)(2,1)}) custom-call(s32[1]{0:T(128)} %bitcast.y_ref, bf16[16,384,128]{2,1,0:T(8,128)(2,1)} %copy-done.5, bf16[768,512]{1,0:T(8,128)(2,1)} %cot_ref.5, bf16[768,512]{1,0:T(8,128)(2,1)} %x_ref.5, f32[1,512]{1,0:T(1,128)} %bitcast.5, ...), custom_call_target="tpu_custom_call" | custom-call | flops 402653184 | bytes 8388608 | tf_op jit(solution)/shard_map/pallas_call | solution.py:452
  106.7 1.3 collective-permute-start.1
  108.0 15.1 %all-to-all-done.3.recv_ref.recv_hbm = bf16[16,400,128]{2,1,0:T(8,128)(2,1)S(1)} async-done(((bf16[16,400,128]{2,1,0:T(8,128)(2,1)}), bf16[16,400,128]{2,1,0:T(8,128)(2,1)S(1)}, u32[]{:S(2)}, u32[]{:S(2)}) %all-to-all-start.3) | async-done | bytes 1638432 | tf_op jit(solution)/shard_map/all_to_all | solution.py:381
  123.1 0.0 copy-start
  123.1 0.0 copy-start.2
  123.1 1.7 %copy-done.2 = bf16[768,512]{1,0:T(8,128)(2,1)S(1)} copy-done((bf16[768,512]{1,0:T(8,128)(2,1)S(1)}, bf16[768,512]{1,0:T(8,128)(2,1)}, u32[]{:S(2)}) %copy-start.2) | copy-done | bytes 786456
  124.8 0.8 shard_map.127
  125.6 0.0 copy-start.3
  125.6 1.3 collective-permute-start
  127.0 3.3 %shard_map.124 = bf16[768,512]{1,0:T(8,128)(2,1)} custom-call(bf16[16,384,128]{2,1,0:T(8,128)(2,1)} %copy-done.5, bf16[768,512]{1,0:T(8,128)(2,1)} %x_ref.5, bf16[2,512,256]{2,1,0:T(8,128)(2,1)} %w4_ref.3), custom_call_target="tpu_custom_call" | custom-call | flops 64424509440 | bytes 3670016 | tf_op jit(solution)/shard_map/pallas_call | solution.py:49
  130.2 0.0 copy-done
  130.2 0.0 collective-permute-done.1.fourth_other
  130.2 4.2 %collective-permute-done.first_other = bf16[8,64,256]{2,1,0:T(8,128)(2,1)S(1)} collective-permute-done((bf16[8,64,256]{2,1,0:T(8,128)(2,1)S(1)}, bf16[8,64,256]{2,1,0:T(8,128)(2,1)S(1)}, u32[]{:S(2)}, u32[]{:S(2)}) %collective-permute-start) | collective-permute-done | bytes 262176 | tf_op jit(solution)/shard_map/ppermute | solution.py:476
  134.4 0.0 copy-done.3
  134.4 0.9 shard_map.128
  135.4 8.5 %all-to-all-start.4 = ((bf16[8,128,256]{2,1,0:T(8,128)(2,1)}), bf16[8,128,256]{2,1,0:T(8,128)(2,1)S(1)}, u32[]{:S(2)}, u32[]{:S(2)}) async-start(bf16[8,128,256]{2,1,0:T(8,128)(2,1)} %shard_map.128), calls=%async_computation.4 | async-start | bytes 1048576 | tf_op jit(solution)/shard_map/all_to_all | solution.py:478
  143.8 0.0 reduce-scatter.2.cloned.1.call-done.own_ref
  143.9 1.0 slice_bitcast_fusion
  144.8 0.0 copy-start.1
  144.8 1.4 collective-permute-start.2
  146.2 4.3 %shard_map.125 = bf16[768,512]{1,0:T(8,128)(2,1)} custom-call(bf16[16,400,128]{2,1,0:T(8,128)(2,1)} %copy-done, bf16[16,400,128]{2,1,0:T(8,128)(2,1)} %copy-done.4, bf16[768,512]{1,0:T(8,128)(2,1)} %x_ref.5, f32[1,512]{1,0:T(1,128)} %bitcast.6, bf16[2,256,512]{2,1,0:T(8,128)(2,1)} %w1_ref.1, bf16[768,512]{1,0:T(8,128)(2,1)} %cot_ref.5), custom_call_target="tpu_custom_call" | custom-call | flops 64424509440 | bytes 8388608 | tf_op jit(solution)/shard_map/pallas_call | solution.py:479
  150.5 2.5 %collective-permute-done.2.other_ref = bf16[64,2048]{1,0:T(8,128)(2,1)S(1)} collective-permute-done((bf16[64,2048]{1,0:T(8,128)(2,1)S(1)}, bf16[64,2048]{1,0:T(8,128)(2,1)S(1)}, u32[]{:S(2)}, u32[]{:S(2)}) %collective-permute-start.2) | collective-permute-done | bytes 262176 | tf_op jit(solution)/shard_map/ppermute | solution.py:488
  153.0 0.0 copy-done.1
  153.0 0.8 shard_map.129
  153.9 7.5 %all-to-all-done.4.recv_ref = bf16[8,128,256]{2,1,0:T(8,128)(2,1)S(1)} async-done(((bf16[8,128,256]{2,1,0:T(8,128)(2,1)}), bf16[8,128,256]{2,1,0:T(8,128)(2,1)S(1)}, u32[]{:S(2)}, u32[]{:S(2)}) %all-to-all-start.4) | async-done | bytes 524320 | tf_op jit(solution)/shard_map/all_to_all | solution.py:478
  161.4 0.7 shard_map.130
Async XLA Ops:
  11.0 27.1 %all-to-all-start = ((bf16[16,400,128]{2,1,0:T(8,128)(2,1)}), bf16[16,400,128]{2,1,0:T(8,128)(2,1)S(1)}, u32[]{:S(2)}, u32[]{:S(2)}) async-start(bf16[16,400,128]{2,1,0:T(8,128)(2,1)} %shard_map.118), calls=%async_computation | async-start | bytes 3276800 | tf_op jit(solution)/shard_map/all_to_all | solution.py:381
  38.1 13.4 %copy-start.4 = (bf16[16,400,128]{2,1,0:T(8,128)(2,1)}, bf16[16,400,128]{2,1,0:T(8,128)(2,1)S(1)}, u32[]{:S(2)}) copy-start(bf16[16,400,128]{2,1,0:T(8,128)(2,1)S(1)} %all-to-all-done.recv_hbm.recv_ref.stats_ref) | copy-start | bytes 4915204
  38.1 27.7 %all-to-all-start.1 = ((bf16[16,384,128]{2,1,0:T(8,128)(2,1)}), bf16[16,384,128]{2,1,0:T(8,128)(2,1)S(1)}, u32[]{:S(2)}, u32[]{:S(2)}) async-start(bf16[16,384,128]{2,1,0:T(8,128)(2,1)} %shard_map.119), calls=%async_computation.1 | async-start | bytes 3145728 | tf_op jit(solution)/shard_map/all_to_all | solution.py:381
  65.8 8.8 %copy-start.6 = (bf16[16,384,128]{2,1,0:T(8,128)(2,1)}, bf16[16,384,128]{2,1,0:T(8,128)(2,1)S(1)}, u32[]{:S(2)}) copy-start(bf16[16,384,128]{2,1,0:T(8,128)(2,1)S(1)} %all-to-all-done.1.dthird_hbm) | copy-start | bytes 4718596
  65.8 27.6 %all-to-all-start.2 = ((bf16[16,384,128]{2,1,0:T(8,128)(2,1)}), bf16[16,384,128]{2,1,0:T(8,128)(2,1)S(1)}, u32[]{:S(2)}, u32[]{:S(2)}) async-start(bf16[16,384,128]{2,1,0:T(8,128)(2,1)} %get-tuple-element.36), calls=%async_computation.2 | async-start | bytes 3145728 | tf_op jit(solution)/shard_map/all_to_all | solution.py:381
  74.4 69.5 %reduce-scatter.2.cloned.1.call-start = ((), (), s32[]{:S(2)}) async-start(), calls=%async_computation.6 | async-start | bytes 4718592 | tf_op jit(solution)/shard_map/reduce_scatter | solution.py:443
  93.4 1.1 copy-start.5
  94.6 28.5 %all-to-all-start.3 = ((bf16[16,400,128]{2,1,0:T(8,128)(2,1)}), bf16[16,400,128]{2,1,0:T(8,128)(2,1)S(1)}, u32[]{:S(2)}, u32[]{:S(2)}) async-start(bf16[16,400,128]{2,1,0:T(8,128)(2,1)} %shard_map.123), calls=%async_computation.3 | async-start | bytes 3276800 | tf_op jit(solution)/shard_map/all_to_all | solution.py:381
  106.7 23.6 %collective-permute-start.1 = (bf16[8,64,256]{2,1,0:T(8,128)(2,1)}, bf16[8,64,256]{2,1,0:T(8,128)(2,1)S(1)}, u32[]{:S(2)}, u32[]{:S(2)}) collective-permute-start(bf16[8,64,256]{2,1,0:T(8,128)(2,1)} %get-tuple-element.43), channel_id=1, source_target_pairs={{0,128},{16,144},{32,160},{48,176},{64,192},{80,208},{96,224},{112... | collective-permute-start | bytes 786440 | tf_op jit(solution)/shard_map/ppermute | solution.py:461
  123.1 7.2 %copy-start = (bf16[16,400,128]{2,1,0:T(8,128)(2,1)}, bf16[16,400,128]{2,1,0:T(8,128)(2,1)S(1)}, u32[]{:S(2)}) copy-start(bf16[16,400,128]{2,1,0:T(8,128)(2,1)S(1)} %all-to-all-done.3.recv_ref.recv_hbm) | copy-start | bytes 4915204
  123.1 1.7 %copy-start.2 = (bf16[768,512]{1,0:T(8,128)(2,1)S(1)}, bf16[768,512]{1,0:T(8,128)(2,1)}, u32[]{:S(2)}) copy-start(bf16[768,512]{1,0:T(8,128)(2,1)} %get-tuple-element.39.normed_hbm) | copy-start | bytes 2359300
  125.6 8.8 %copy-start.3 = (bf16[8,64,256]{2,1,0:T(8,128)(2,1)S(1)}, bf16[8,64,256]{2,1,0:T(8,128)(2,1)}, u32[]{:S(2)}) copy-start(bf16[8,64,256]{2,1,0:T(8,128)(2,1)} %get-tuple-element.42.fourth_own) | copy-start | bytes 786436
  125.6 8.8 %collective-permute-start = (bf16[8,64,256]{2,1,0:T(8,128)(2,1)S(1)}, bf16[8,64,256]{2,1,0:T(8,128)(2,1)S(1)}, u32[]{:S(2)}, u32[]{:S(2)}) collective-permute-start(bf16[8,64,256]{2,1,0:T(8,128)(2,1)S(1)} %get-tuple-element.41), channel_id=1, source_target_pairs={{0,128},{16,144},{32,160},{48,176},{64,192},{80,208},{96,224},{112... | collective-permute-start | bytes 786440 | tf_op jit(solution)/shard_map/ppermute | solution.py:476
  135.4 26.0 %all-to-all-start.4 = ((bf16[8,128,256]{2,1,0:T(8,128)(2,1)}), bf16[8,128,256]{2,1,0:T(8,128)(2,1)S(1)}, u32[]{:S(2)}, u32[]{:S(2)}) async-start(bf16[8,128,256]{2,1,0:T(8,128)(2,1)} %shard_map.128), calls=%async_computation.4 | async-start | bytes 1048576 | tf_op jit(solution)/shard_map/all_to_all | solution.py:478
  144.8 8.2 %copy-start.1 = (bf16[1,2,64,2048]{3,2,1,0:T(8,128)(2,1)S(1)}, bf16[1,2,64,2048]{3,2,1,0:T(8,128)(2,1)}, u32[]{:S(2)}) copy-start(bf16[1,2,64,2048]{3,2,1,0:T(8,128)(2,1)} %reduce-scatter.2.cloned.1.call-done.own_ref) | copy-start | bytes 1572868
  144.8 8.2 %collective-permute-start.2 = (bf16[64,2048]{1,0:T(8,128)(2,1)S(1)}, bf16[64,2048]{1,0:T(8,128)(2,1)S(1)}, u32[]{:S(2)}, u32[]{:S(2)}) collective-permute-start(bf16[64,2048]{1,0:T(8,128)(2,1)S(1)} %slice_bitcast_fusion), channel_id=1, source_target_pairs={{0,128},{16,144},{32,160},{48,176},{64,192},{80,208},{96,224},{112... | collective-permute-start | bytes 786440 | tf_op jit(solution)/shard_map/ppermute | solution.py:488
Sparse Core Ops, SparseCore 0:
  85.8 58.0 reduce-scatter.1

commit v11 on v10

--- a/solution.py
+++ b/solution.py
@@ -89,39 +89,26 @@
             copy.wait()
 
 
-def head_kernel(x_hbm, gain_ref, w1_hbm, out_hbm, x_ref, w1_ref, out_ref, in_sems, out_sems):
-    steps = x_ref.shape[0] // STEP
-    loads, stores = Copies(in_sems), Copies(out_sems)
-    w1_load = loads.start(w1_hbm, w1_ref)
-    parts = [pl.ds(i * STEP, STEP) for i in range(steps)]
-    x_loads = [loads.start(x_hbm.at[part], x_ref.at[part]) for part in parts]
-    w1_load.wait()
-    turned = [w1_ref[a].T for a in range(2)]
-    totals = []
-    for i in range(steps):
-        x_loads[i].wait()
-        x = x_ref[parts[i], :].astype(F32)
-        scaled = (x * gain_ref[...]).astype(BF16)
-        base = i * 2 * PAIR
-        for a in range(2):
-            first = dot(turned[a], scaled[:, a * BS : (a + 1) * BS], NT).astype(BF16)
-            for k in range(2):
-                start = base + k * PAIR + a * EB
-                value = first[:, k * LANES : (k + 1) * LANES]
-                out_ref[:, start : start + EB, :] = value.reshape(PEERS, EB, LANES)
-        part = pl.ds(base, 2 * PAIR)
-        stores.start(out_ref.at[:, part], out_hbm.at[:, part])
-        squares = x * x
-        folded = squares[:, :LANES]
-        for k in range(1, squares.shape[1] // LANES):
-            folded = folded + squares[:, k * LANES : (k + 1) * LANES]
-        totals.append(jnp.sum(folded.T, axis=0, keepdims=True))
-    rows = steps * 2 * PAIR
-    stats = stat_rows(jnp.concatenate(totals, axis=1), 2 * steps)
-    out_ref[:, rows:, :] = jnp.broadcast_to(stats[None], (PEERS, STATS, LANES))
-    part = pl.ds(rows, STATS)
-    stores.start(out_ref.at[:, part], out_hbm.at[:, part])
-    stores.wait()
+def first_factor_kernel(x_ref, gain_ref, w1_ref, out_ref, squares_ref):
+    a = pl.program_id(0)
+    chunks = x_ref.shape[0] // LANES
+    x = x_ref[...].astype(F32)
+    first = dot(w1_ref[0].T, (x * gain_ref[...]).astype(BF16), NT).astype(BF16)
+    base = pl.multiple_of(a * EB, EB)
+    for i in range(chunks):
+        part = slice(i * LANES, (i + 1) * LANES)
+        out_ref[:, pl.ds(i * PAIR + base, EB), :] = first[:, part].reshape(PEERS, EB, LANES)
+    squares = x * x
+    total = jnp.sum((squares[:, :LANES] + squares[:, LANES:]).T, axis=0, keepdims=True)
+
+    @pl.when(a == 0)
+    def _():
+        squares_ref[...] = total
+
+    @pl.when(a == 1)
+    def _():
+        rows = stat_rows(squares_ref[...] + total, chunks)
+        out_ref[:, chunks * PAIR :, :] = jnp.broadcast_to(rows[None], (PEERS, STATS, LANES))
 
 
 def dgathered_kernel(w4_ref, cot_ref, out_ref):
@@ -381,17 +368,16 @@
         return lax.all_to_all(value, "tensor", 0, 0, tiled=True)
 
     send = pl.pallas_call(
-        head_kernel,
+        first_factor_kernel,
         out_shape=stats_sent,
-        in_specs=[hbm, vmem, hbm],
-        out_specs=hbm,
-        scratch_shapes=[
-            pltpu.VMEM(tokens.shape, BF16),
-            pltpu.VMEM(w_first.shape, BF16),
-            pltpu.VMEM(stats_sent.shape, BF16),
-            pltpu.SemaphoreType.DMA((steps + 1,)),
-            pltpu.SemaphoreType.DMA((steps + 1,)),
+        grid=(2,),
+        in_specs=[
+            pl.BlockSpec((element_count, BS), lambda a: (0, a)),
+            pl.BlockSpec((1, BS), lambda a: (0, a)),
+            pl.BlockSpec((1, BS, HB * EB), lambda a: (a, 0, 0)),
         ],
+        out_specs=whole(*stats_sent.shape),
+        scratch_shapes=[pltpu.VMEM((1, element_count), F32)],
         compiler_params=params,
         cost_estimate=cost(model_flops),
     )(tokens, gain_row, w_first)

time: 171 us -> 171 us (level)
  no operation moved by 1% of the time
where the time goes in v11:
time: 171 us; the launch traced here: 168 us
  waiting for transfers between devices  52.6 us (31%)
  Pallas kernels  52.2 us (31%)
  starting transfers between devices  45.7 us (27%)
  between operations  14.1 us (8%)
  local copies, waits for them, and re-layouts  3.84 us (2%)
    all_to_all x4, waiting for transfers between devices, exchange(): return lax.all_to_all(value, 'tensor', 0, 0, tiled=True)  38.3 us
    all_to_all x4, starting transfers between devices, exchange(): return lax.all_to_all(value, 'tensor', 0, 0, tiled=True)  33 us
    pallas_call x7, Pallas kernels, call(): pl.pallas_call(kernel, out_shape=out_shape, in_specs=[pl.BlockSpec(memory...  19.3 us
    pallas_call x1, Pallas kernels, shards(): pl.pallas_call(backward_kernel, out_shape=[grads, stepped], in_specs=[sme...  11 us
    pallas_call x1, Pallas kernels, shards(): pl.pallas_call(forward_kernel, out_shape=[stepped, stepped, plain_sent],...  9.91 us
    all_to_all x1, starting transfers between devices, shards(): lax.all_to_all(both, 'dp', 0, 0, axis_index_groups=z_groups, tiled=True)  8.48 us
    all_to_all x1, waiting for transfers between devices, shards(): lax.all_to_all(both, 'dp', 0, 0, axis_index_groups=z_groups, tiled=True)  7.51 us
    pallas_call x1, Pallas kernels, shards(): pl.pallas_call(token_kernel, out_shape=shape(tokens.shape, BF16), grid=(1...  4.3 us
  transfers between devices with their start and end apart: 9, of which 7 were waited for; matrix products, arithmetic and copies ran while one was open for 1% of the time, Pallas kernels for 29%

profile of v11, /device:TPU:18, one launch (start us, length us, event | category | flops | bytes accessed | tf_op | source)
XLA Modules:
  0.0 168.4 jit_solution(1132227063167657666)
XLA Ops:
  7.2 3.3 %shard_map.118 = bf16[16,400,128]{2,1,0:T(8,128)(2,1)} custom-call(bf16[768,512]{1,0:T(8,128)(2,1)} %x_ref.7, f32[1,512]{1,0:T(1,128)} %bitcast.4, bf16[2,256,512]{2,1,0:T(8,128)(2,1)} %w1_ref.3), custom_call_target="tpu_custom_call" | custom-call | flops 402653184 | bytes 8388608 | tf_op jit(solution)/shard_map/pallas_call | solution.py:370
  10.4 7.3 %all-to-all-start = ((bf16[16,400,128]{2,1,0:T(8,128)(2,1)}), bf16[16,400,128]{2,1,0:T(8,128)(2,1)S(1)}, u32[]{:S(2)}, u32[]{:S(2)}) async-start(bf16[16,400,128]{2,1,0:T(8,128)(2,1)} %shard_map.118), calls=%async_computation | async-start | bytes 3276800 | tf_op jit(solution)/shard_map/all_to_all | solution.py:368
  17.7 3.0 %shard_map.119 = bf16[16,384,128]{2,1,0:T(8,128)(2,1)} custom-call(bf16[2,512,256]{2,1,0:T(8,128)(2,1)} %w4_ref.3, bf16[768,512]{1,0:T(8,128)(2,1)} %cot_ref.5), custom_call_target="tpu_custom_call" | custom-call | flops 402653184 | bytes 2883584 | tf_op jit(solution)/shard_map/pallas_call | solution.py:49
  20.7 16.8 %all-to-all-done.recv_hbm.recv_ref.stats_ref = bf16[16,400,128]{2,1,0:T(8,128)(2,1)S(1)} async-done(((bf16[16,400,128]{2,1,0:T(8,128)(2,1)}), bf16[16,400,128]{2,1,0:T(8,128)(2,1)S(1)}, u32[]{:S(2)}, u32[]{:S(2)}) %all-to-all-start) | async-done | bytes 1638432 | tf_op jit(solution)/shard_map/all_to_all | solution.py:368
  37.5 0.0 copy-start.4
  37.5 8.6 %all-to-all-start.1 = ((bf16[16,384,128]{2,1,0:T(8,128)(2,1)}), bf16[16,384,128]{2,1,0:T(8,128)(2,1)S(1)}, u32[]{:S(2)}, u32[]{:S(2)}) async-start(bf16[16,384,128]{2,1,0:T(8,128)(2,1)} %shard_map.119), calls=%async_computation.1 | async-start | bytes 3145728 | tf_op jit(solution)/shard_map/all_to_all | solution.py:368
  46.1 4.8 %shard_map.120 = (bf16[1024,1024]{1,0:T(8,128)(2,1)}, bf16[1024,1024]{1,0:T(8,128)(2,1)}) custom-call(bf16[1,1024,1024]{2,1,0:T(8,128)(2,1)} %w2_ref.3, bf16[1,1024,1024]{2,1,0:T(8,128)(2,1)} %w3_hbm.1), custom_call_target="tpu_custom_call" | custom-call | bytes 8388608 | tf_op jit(solution)/shard_map/pallas_call | solution.py:49
  51.0 0.0 copy-done.4
  51.0 9.9 %shard_map.121 = (bf16[3,1024,256]{2,1,0:T(8,128)(2,1)}, bf16[3,1024,256]{2,1,0:T(8,128)(2,1)}, bf16[16,384,128]{2,1,0:T(8,128)(2,1)}) custom-call(bf16[16,400,128]{2,1,0:T(8,128)(2,1)} %copy-done.4, bf16[1024,1024]{1,0:T(8,128)(2,1)} %get-tuple-element.30.w2t_hbm, bf16[1024,1024]{1,0:T(8,128)(2,1)} %get-tuple-element.31.w3t_hbm), custom_call_target="tpu_custom_call" | custom-call | flops 3221225472 | bytes 8388608 | tf_op jit(solution)/shard_map/pallas_call | solution.py:389
  60.9 4.3 %all-to-all-done.1.dthird_hbm = bf16[16,384,128]{2,1,0:T(8,128)(2,1)S(1)} async-done(((bf16[16,384,128]{2,1,0:T(8,128)(2,1)}), bf16[16,384,128]{2,1,0:T(8,128)(2,1)S(1)}, u32[]{:S(2)}, u32[]{:S(2)}) %all-to-all-start.1) | async-done | bytes 1572896 | tf_op jit(solution)/shard_map/all_to_all | solution.py:368
  65.2 0.0 copy-start.6
  65.2 8.6 %all-to-all-start.2 = ((bf16[16,384,128]{2,1,0:T(8,128)(2,1)}), bf16[16,384,128]{2,1,0:T(8,128)(2,1)S(1)}, u32[]{:S(2)}, u32[]{:S(2)}) async-start(bf16[16,384,128]{2,1,0:T(8,128)(2,1)} %get-tuple-element.36), calls=%async_computation.2 | async-start | bytes 3145728 | tf_op jit(solution)/shard_map/all_to_all | solution.py:368
  73.8 0.2 reduce-scatter.2.cloned.1.call-start
  74.0 0.0 copy-done.6
  74.0 11.0 %shard_map.122 = (bf16[8,2,64,2048]{3,2,1,0:T(8,128)(2,1)}, bf16[3,1024,256]{2,1,0:T(8,128)(2,1)}) custom-call(s32[1]{0:T(128)} %bitcast.y_ref, bf16[16,400,128]{2,1,0:T(8,128)(2,1)} %copy-done.4, bf16[16,384,128]{2,1,0:T(8,128)(2,1)} %copy-done.6, bf16[3,1024,256]{2,1,0:T(8,128)(2,1)} %get-tuple-element.32.slope_hbm, ...), custom_call_target="tpu_custom_call" | custom-call | flops 4831838208 | bytes 8388608 | tf_op jit(solution)/shard_map/pallas_call | solution.py:409
  85.1 0.0 reduce-scatter.2.cloned.1.call-update
  85.1 5.6 %shard_map.123 = bf16[16,400,128]{2,1,0:T(8,128)(2,1)} custom-call(bf16[3,1024,256]{2,1,0:T(8,128)(2,1)} %get-tuple-element.34.dpre_ref, bf16[16,400,128]{2,1,0:T(8,128)(2,1)} %copy-done.4, bf16[1,1024,1024]{2,1,0:T(8,128)(2,1)} %w2_ref.3), custom_call_target="tpu_custom_call" | custom-call | flops 1610612736 | bytes 6946816 | tf_op jit(solution)/shard_map/pallas_call | solution.py:49
  90.7 2.1 %all-to-all-done.2.recv_ref = bf16[16,384,128]{2,1,0:T(8,128)(2,1)S(1)} async-done(((bf16[16,384,128]{2,1,0:T(8,128)(2,1)}), bf16[16,384,128]{2,1,0:T(8,128)(2,1)S(1)}, u32[]{:S(2)}, u32[]{:S(2)}) %all-to-all-start.2) | async-done | bytes 1572896 | tf_op jit(solution)/shard_map/all_to_all | solution.py:368
  92.9 0.0 copy-start.5
  92.9 1.1 copy-done.5
  94.0 8.6 %all-to-all-start.3 = ((bf16[16,400,128]{2,1,0:T(8,128)(2,1)}), bf16[16,400,128]{2,1,0:T(8,128)(2,1)S(1)}, u32[]{:S(2)}, u32[]{:S(2)}) async-start(bf16[16,400,128]{2,1,0:T(8,128)(2,1)} %shard_map.123), calls=%async_computation.3 | async-start | bytes 3276800 | tf_op jit(solution)/shard_map/all_to_all | solution.py:368
  102.6 3.5 %shard_map.126 = (bf16[8,64,256]{2,1,0:T(8,128)(2,1)}, bf16[8,64,256]{2,1,0:T(8,128)(2,1)}, bf16[768,512]{1,0:T(8,128)(2,1)}) custom-call(s32[1]{0:T(128)} %bitcast.y_ref, bf16[16,384,128]{2,1,0:T(8,128)(2,1)} %copy-done.5, bf16[768,512]{1,0:T(8,128)(2,1)} %cot_ref.5, bf16[768,512]{1,0:T(8,128)(2,1)} %x_ref.7, f32[1,512]{1,0:T(1,128)} %bitcast.5, ...), custom_call_target="tpu_custom_call" | custom-call | flops 402653184 | bytes 8388608 | tf_op jit(solution)/shard_map/pallas_call | solution.py:438
  106.1 1.3 collective-permute-start.1
  107.4 15.1 %all-to-all-done.3.recv_ref.recv_hbm = bf16[16,400,128]{2,1,0:T(8,128)(2,1)S(1)} async-done(((bf16[16,400,128]{2,1,0:T(8,128)(2,1)}), bf16[16,400,128]{2,1,0:T(8,128)(2,1)S(1)}, u32[]{:S(2)}, u32[]{:S(2)}) %all-to-all-start.3) | async-done | bytes 1638432 | tf_op jit(solution)/shard_map/all_to_all | solution.py:368
  122.5 0.0 copy-start
  122.5 0.0 copy-start.2
  122.5 1.7 %copy-done.2 = bf16[768,512]{1,0:T(8,128)(2,1)S(1)} copy-done((bf16[768,512]{1,0:T(8,128)(2,1)S(1)}, bf16[768,512]{1,0:T(8,128)(2,1)}, u32[]{:S(2)}) %copy-start.2) | copy-done | bytes 786456
  124.2 0.8 shard_map.127
  125.0 0.0 copy-start.3
  125.0 1.4 collective-permute-start
  126.4 3.3 %shard_map.124 = bf16[768,512]{1,0:T(8,128)(2,1)} custom-call(bf16[16,384,128]{2,1,0:T(8,128)(2,1)} %copy-done.5, bf16[768,512]{1,0:T(8,128)(2,1)} %x_ref.7, bf16[2,512,256]{2,1,0:T(8,128)(2,1)} %w4_ref.3), custom_call_target="tpu_custom_call" | custom-call | flops 64424509440 | bytes 3670016 | tf_op jit(solution)/shard_map/pallas_call | solution.py:49
  129.7 0.0 copy-done
  129.7 0.0 collective-permute-done.1.fourth_other
  129.7 4.2 %collective-permute-done.first_other = bf16[8,64,256]{2,1,0:T(8,128)(2,1)S(1)} collective-permute-done((bf16[8,64,256]{2,1,0:T(8,128)(2,1)S(1)}, bf16[8,64,256]{2,1,0:T(8,128)(2,1)S(1)}, u32[]{:S(2)}, u32[]{:S(2)}) %collective-permute-start) | collective-permute-done | bytes 262176 | tf_op jit(solution)/shard_map/ppermute | solution.py:462
  133.9 0.0 copy-done.3
  133.9 0.9 shard_map.128
  134.8 8.5 %all-to-all-start.4 = ((bf16[8,128,256]{2,1,0:T(8,128)(2,1)}), bf16[8,128,256]{2,1,0:T(8,128)(2,1)S(1)}, u32[]{:S(2)}, u32[]{:S(2)}) async-start(bf16[8,128,256]{2,1,0:T(8,128)(2,1)} %shard_map.128), calls=%async_computation.4 | async-start | bytes 1048576 | tf_op jit(solution)/shard_map/all_to_all | solution.py:464
  143.3 0.0 reduce-scatter.2.cloned.1.call-done.own_ref
  143.3 1.0 slice_bitcast_fusion
  144.3 0.0 copy-start.1
  144.3 1.4 collective-permute-start.2
  145.6 4.3 %shard_map.125 = bf16[768,512]{1,0:T(8,128)(2,1)} custom-call(bf16[16,400,128]{2,1,0:T(8,128)(2,1)} %copy-done, bf16[16,400,128]{2,1,0:T(8,128)(2,1)} %copy-done.4, bf16[768,512]{1,0:T(8,128)(2,1)} %x_ref.7, f32[1,512]{1,0:T(1,128)} %bitcast.6, bf16[2,256,512]{2,1,0:T(8,128)(2,1)} %w1_ref.3, bf16[768,512]{1,0:T(8,128)(2,1)} %cot_ref.5), custom_call_target="tpu_custom_call" | custom-call | flops 64424509440 | bytes 8388608 | tf_op jit(solution)/shard_map/pallas_call | solution.py:465
  149.9 2.5 %collective-permute-done.2.other_ref = bf16[64,2048]{1,0:T(8,128)(2,1)S(1)} collective-permute-done((bf16[64,2048]{1,0:T(8,128)(2,1)S(1)}, bf16[64,2048]{1,0:T(8,128)(2,1)S(1)}, u32[]{:S(2)}, u32[]{:S(2)}) %collective-permute-start.2) | collective-permute-done | bytes 262176 | tf_op jit(solution)/shard_map/ppermute | solution.py:474
  152.5 0.0 copy-done.1
  152.5 0.8 shard_map.129
  153.3 7.5 %all-to-all-done.4.recv_ref = bf16[8,128,256]{2,1,0:T(8,128)(2,1)S(1)} async-done(((bf16[8,128,256]{2,1,0:T(8,128)(2,1)}), bf16[8,128,256]{2,1,0:T(8,128)(2,1)S(1)}, u32[]{:S(2)}, u32[]{:S(2)}) %all-to-all-start.4) | async-done | bytes 524320 | tf_op jit(solution)/shard_map/all_to_all | solution.py:464
  160.8 0.7 shard_map.130
Async XLA Ops:
  10.4 27.1 %all-to-all-start = ((bf16[16,400,128]{2,1,0:T(8,128)(2,1)}), bf16[16,400,128]{2,1,0:T(8,128)(2,1)S(1)}, u32[]{:S(2)}, u32[]{:S(2)}) async-start(bf16[16,400,128]{2,1,0:T(8,128)(2,1)} %shard_map.118), calls=%async_computation | async-start | bytes 3276800 | tf_op jit(solution)/shard_map/all_to_all | solution.py:368
  37.5 13.4 %copy-start.4 = (bf16[16,400,128]{2,1,0:T(8,128)(2,1)}, bf16[16,400,128]{2,1,0:T(8,128)(2,1)S(1)}, u32[]{:S(2)}) copy-start(bf16[16,400,128]{2,1,0:T(8,128)(2,1)S(1)} %all-to-all-done.recv_hbm.recv_ref.stats_ref) | copy-start | bytes 4915204
  37.5 27.7 %all-to-all-start.1 = ((bf16[16,384,128]{2,1,0:T(8,128)(2,1)}), bf16[16,384,128]{2,1,0:T(8,128)(2,1)S(1)}, u32[]{:S(2)}, u32[]{:S(2)}) async-start(bf16[16,384,128]{2,1,0:T(8,128)(2,1)} %shard_map.119), calls=%async_computation.1 | async-start | bytes 3145728 | tf_op jit(solution)/shard_map/all_to_all | solution.py:368
  65.2 8.8 %copy-start.6 = (bf16[16,384,128]{2,1,0:T(8,128)(2,1)}, bf16[16,384,128]{2,1,0:T(8,128)(2,1)S(1)}, u32[]{:S(2)}) copy-start(bf16[16,384,128]{2,1,0:T(8,128)(2,1)S(1)} %all-to-all-done.1.dthird_hbm) | copy-start | bytes 4718596
  65.2 27.6 %all-to-all-start.2 = ((bf16[16,384,128]{2,1,0:T(8,128)(2,1)}), bf16[16,384,128]{2,1,0:T(8,128)(2,1)S(1)}, u32[]{:S(2)}, u32[]{:S(2)}) async-start(bf16[16,384,128]{2,1,0:T(8,128)(2,1)} %get-tuple-element.36), calls=%async_computation.2 | async-start | bytes 3145728 | tf_op jit(solution)/shard_map/all_to_all | solution.py:368
  73.8 69.5 %reduce-scatter.2.cloned.1.call-start = ((), (), s32[]{:S(2)}) async-start(), calls=%async_computation.6 | async-start | bytes 4718592 | tf_op jit(solution)/shard_map/reduce_scatter | solution.py:429
  92.9 1.1 copy-start.5
  94.0 28.5 %all-to-all-start.3 = ((bf16[16,400,128]{2,1,0:T(8,128)(2,1)}), bf16[16,400,128]{2,1,0:T(8,128)(2,1)S(1)}, u32[]{:S(2)}, u32[]{:S(2)}) async-start(bf16[16,400,128]{2,1,0:T(8,128)(2,1)} %shard_map.123), calls=%async_computation.3 | async-start | bytes 3276800 | tf_op jit(solution)/shard_map/all_to_all | solution.py:368
  106.1 23.6 %collective-permute-start.1 = (bf16[8,64,256]{2,1,0:T(8,128)(2,1)}, bf16[8,64,256]{2,1,0:T(8,128)(2,1)S(1)}, u32[]{:S(2)}, u32[]{:S(2)}) collective-permute-start(bf16[8,64,256]{2,1,0:T(8,128)(2,1)} %get-tuple-element.43), channel_id=1, source_target_pairs={{0,128},{16,144},{32,160},{48,176},{64,192},{80,208},{96,224},{112... | collective-permute-start | bytes 786440 | tf_op jit(solution)/shard_map/ppermute | solution.py:447
  122.5 7.2 %copy-start = (bf16[16,400,128]{2,1,0:T(8,128)(2,1)}, bf16[16,400,128]{2,1,0:T(8,128)(2,1)S(1)}, u32[]{:S(2)}) copy-start(bf16[16,400,128]{2,1,0:T(8,128)(2,1)S(1)} %all-to-all-done.3.recv_ref.recv_hbm) | copy-start | bytes 4915204
  122.5 1.7 %copy-start.2 = (bf16[768,512]{1,0:T(8,128)(2,1)S(1)}, bf16[768,512]{1,0:T(8,128)(2,1)}, u32[]{:S(2)}) copy-start(bf16[768,512]{1,0:T(8,128)(2,1)} %get-tuple-element.39.normed_hbm) | copy-start | bytes 2359300
  125.0 8.9 %copy-start.3 = (bf16[8,64,256]{2,1,0:T(8,128)(2,1)S(1)}, bf16[8,64,256]{2,1,0:T(8,128)(2,1)}, u32[]{:S(2)}) copy-start(bf16[8,64,256]{2,1,0:T(8,128)(2,1)} %get-tuple-element.42.fourth_own) | copy-start | bytes 786436
  125.0 8.8 %collective-permute-start = (bf16[8,64,256]{2,1,0:T(8,128)(2,1)S(1)}, bf16[8,64,256]{2,1,0:T(8,128)(2,1)S(1)}, u32[]{:S(2)}, u32[]{:S(2)}) collective-permute-start(bf16[8,64,256]{2,1,0:T(8,128)(2,1)S(1)} %get-tuple-element.41), channel_id=1, source_target_pairs={{0,128},{16,144},{32,160},{48,176},{64,192},{80,208},{96,224},{112... | collective-permute-start | bytes 786440 | tf_op jit(solution)/shard_map/ppermute | solution.py:462
  134.8 26.0 %all-to-all-start.4 = ((bf16[8,128,256]{2,1,0:T(8,128)(2,1)}), bf16[8,128,256]{2,1,0:T(8,128)(2,1)S(1)}, u32[]{:S(2)}, u32[]{:S(2)}) async-start(bf16[8,128,256]{2,1,0:T(8,128)(2,1)} %shard_map.128), calls=%async_computation.4 | async-start | bytes 1048576 | tf_op jit(solution)/shard_map/all_to_all | solution.py:464
  144.3 8.2 %copy-start.1 = (bf16[1,2,64,2048]{3,2,1,0:T(8,128)(2,1)S(1)}, bf16[1,2,64,2048]{3,2,1,0:T(8,128)(2,1)}, u32[]{:S(2)}) copy-start(bf16[1,2,64,2048]{3,2,1,0:T(8,128)(2,1)} %reduce-scatter.2.cloned.1.call-done.own_ref) | copy-start | bytes 1572868
  144.3 8.2 %collective-permute-start.2 = (bf16[64,2048]{1,0:T(8,128)(2,1)S(1)}, bf16[64,2048]{1,0:T(8,128)(2,1)S(1)}, u32[]{:S(2)}, u32[]{:S(2)}) collective-permute-start(bf16[64,2048]{1,0:T(8,128)(2,1)S(1)} %slice_bitcast_fusion), channel_id=1, source_target_pairs={{0,128},{16,144},{32,160},{48,176},{64,192},{80,208},{96,224},{112... | collective-permute-start | bytes 786440 | tf_op jit(solution)/shard_map/ppermute | solution.py:474
Sparse Core Ops, SparseCore 0:
  85.2 58.0 reduce-scatter.1
